TPU v7x, 32 devices: a whole 2x2x4 slice. The times are simulated.
32 devices in a mesh: seg: 8 (over y, x, core), stretch: 4 (over z).
Axes of the slice: x: 2, y: 2, z: 4, core: 2. Of those that a mesh axis runs over, the one named last changes fastest.
Arguments:
- stream_in: bfloat16 [2, 8, 512, 1024], P(None, 'seg', 'stretch'), may hold values from -6 to 6
- cotangent: bfloat16 [2, 8, 512, 1024], P(None, 'seg', 'stretch'), may hold values from -6 to 6
- previous_mix: float32 [2, 8, 1024], P(None, 'seg'), may hold values from -6 to 6
- previous_ffn: float32 [2, 8, 1024], P(None, 'seg'), may hold values from -6 to 6
- state_num: float32 [2, 8, 1024], P(None, 'seg'), may hold values from -6 to 6
- state_den: float32 [2, 8, 1024], P(None, 'seg'), may hold values from 1 to 4
- state_exp: float32 [2, 8, 1024], P(None, 'seg'), may hold values from 1 to 5
- gain_one: bfloat16 [1024], P('seg'), may hold values from 0.5 to 1.5
- bias_one: bfloat16 [1024], P('seg'), may hold values from -1.5 to 1.5
- gain_two: bfloat16 [1024], P('seg'), may hold values from 0.5 to 1.5
- bias_two: bfloat16 [1024], P('seg'), may hold values from -1.5 to 1.5
- mix_key: bfloat16 [1024], P('seg'), may hold values from 0 to 1
- mix_value: bfloat16 [1024], P('seg'), may hold values from 0 to 1
- mix_recept: bfloat16 [1024], P('seg'), may hold values from 0 to 1
- time_decay: bfloat16 [1024], P('seg'), may hold values from -11 to -3.390625
- time_first: bfloat16 [1024], P('seg'), may hold values from -1 to 1
- chan_mix_key: bfloat16 [1024], P('seg'), may hold values from 0 to 1
- chan_mix_recept: bfloat16 [1024], P('seg'), may hold values from 0 to 1
- att_key: bfloat16 [1024, 1024], P('seg'), may hold values from -0.1875 to 0.1875
- att_value: bfloat16 [1024, 1024], P('seg'), may hold values from -0.1875 to 0.1875
- att_recept: bfloat16 [1024, 1024], P('seg'), may hold values from -0.1875 to 0.1875
- att_output: bfloat16 [1024, 1024], P('seg'), may hold values from -2 to 2
- chan_key: bfloat16 [1024, 4096], P('seg'), may hold values from -0.1875 to 0.1875
- chan_value: bfloat16 [4096, 1024], P('seg'), may hold values from -0.09375 to 0.09375
- chan_recept: bfloat16 [1024, 1024], P('seg'), may hold values from -0.1875 to 0.1875
Outputs:
- block_out: bfloat16 [2, 8, 512, 1024], P(None, 'seg', 'stretch')
- grad_stream: bfloat16 [2, 8, 512, 1024], P(None, 'seg', 'stretch')
- grad_gain_one: float32 [1024], P(('seg', 'stretch'))
- grad_bias_one: float32 [1024], P(('seg', 'stretch'))
- grad_gain_two: float32 [1024], P(('seg', 'stretch'))
- grad_bias_two: float32 [1024], P(('seg', 'stretch'))
- grad_mix_key: float32 [1024], P(('seg', 'stretch'))
- grad_mix_value: float32 [1024], P(('seg', 'stretch'))
- grad_mix_recept: float32 [1024], P(('seg', 'stretch'))
- grad_time_decay: float32 [1024], P(('seg', 'stretch'))
- grad_time_first: float32 [1024], P(('seg', 'stretch'))
- grad_chan_mix_key: float32 [1024], P(('seg', 'stretch'))
- grad_chan_mix_recept: float32 [1024], P(('seg', 'stretch'))
- grad_att_key: float32 [1024, 1024], P(('seg', 'stretch'))
- grad_att_value: float32 [1024, 1024], P(('seg', 'stretch'))
- grad_att_recept: float32 [1024, 1024], P(('seg', 'stretch'))
- grad_att_output: float32 [1024, 1024], P(('seg', 'stretch'))
- grad_chan_key: float32 [1024, 4096], P(('seg', 'stretch'))
- grad_chan_value: float32 [4096, 1024], P(('seg', 'stretch'))
- grad_chan_recept: float32 [1024, 1024], P(('seg', 'stretch'))
- grad_state_num: float32 [2, 8, 1024], P(None, 'seg')
- grad_state_den: float32 [2, 8, 1024], P(None, 'seg')
- grad_state_exp: float32 [2, 8, 1024], P(None, 'seg')
- grad_previous_mix: float32 [2, 8, 1024], P(None, 'seg')
- grad_previous_ffn: float32 [2, 8, 1024], P(None, 'seg')
- final_mean: float32 [2, 8, 1024], P(None, 'seg')
- final_log: float32 [2, 8, 1024], P(None, 'seg')
All inputs are finite; a program needn't handle non-finite values.
Results may differ from a plain program's by a relative error of at most 0.025.
Values may be sent and summed in bfloat16 or wider, within the bound.
No kernel may reach another device: no remote copies, remote signals or barrier semaphores. Data moves between devices by JAX's collectives and lax.ppermute only.
A program may use at most 192 MiB of HBM per device.

v0:
```python
import jax
import jax.numpy as jnp
from jax import lax
from jax.sharding import PartitionSpec as P

epsilon = 1e-05
highest = lax.Precision.HIGHEST
bottom = -1e30


def from_behind(value, axis, steps):
    count = lax.axis_size(axis)
    first, last = (max(0, -steps), min(count, count - steps))
    return lax.ppermute(value, axis, [(source, source + steps) for source in range(first, last)])


def entering_2(value, axis, combine, identity, reverse):
    count, mine = (lax.axis_size(axis), lax.axis_index(axis))
    everything = jax.tree.map(lambda part: lax.all_gather(part, axis), value)
    start = jax.tree.map(
        lambda part, zero: jnp.broadcast_to(jnp.asarray(zero, part.dtype), part.shape),
        value,
        identity,
    )

    def entering_turn(k, before):
        at = count - 1 - k if reverse else k
        reached = at > mine if reverse else at < mine
        new = combine(before, jax.tree.map(lambda part: part[at], everything))
        return jax.tree.map(lambda a, b: jnp.where(reached, a, b), new, before)

    return lax.fori_loop(0, count, entering_turn, start)


def for_sending(value):
    return jax.tree.map(lambda a: a.astype(jnp.bfloat16) if a.dtype == jnp.float32 else a, value)


def combined_all(value, axis, combine):
    everything = jax.tree.map(lambda part: lax.all_gather(part, axis), value)
    first = jax.tree.map(lambda part: part[0], everything)

    def combined_turn(k, so_far):
        return combine(so_far, jax.tree.map(lambda part: part[k], everything))

    return lax.fori_loop(1, lax.axis_size(axis), combined_turn, first)


def merged(value, axis, combine):
    everything = jax.tree.map(
        lambda part, kind: lax.all_gather(part.astype(kind), axis),
        value,
        jax.tree.map(lambda a: jnp.bfloat16 if a.dtype == jnp.float32 else a.dtype, value),
    )

    def take(k):
        return jax.tree.map(lambda part, own: part[k].astype(own.dtype), everything, value)

    return lax.fori_loop(
        1, lax.axis_size(axis), lambda k, so_far: combine(so_far, take(k)), take(0)
    )


def matmul_nt(left, right):
    return lax.dot_general(
        left, right, (((1,), (1,)), ((), ())), preferred_element_type=jnp.float32
    )


def matmul_tn(left, right):
    return lax.dot_general(
        left, right, (((0,), (0,)), ((), ())), preferred_element_type=jnp.float32
    )


def norm_forward(matrix_rows, gain_vec, bias_vec):
    centre = matrix_rows - jnp.mean(matrix_rows, axis=1, keepdims=True)
    inverse = lax.rsqrt(jnp.mean(centre * centre, axis=1, keepdims=True) + epsilon)
    normal_rows = centre * inverse
    return (normal_rows * gain_vec + bias_vec, normal_rows, inverse)


def norm_backward(upstream, normal_rows, inverse, gain_vec):
    scaled = upstream * gain_vec
    back_rows = inverse * (
        scaled
        - jnp.mean(scaled, axis=1, keepdims=True)
        - normal_rows * jnp.mean(scaled * normal_rows, axis=1, keepdims=True)
    )
    return (back_rows, jnp.sum(upstream * normal_rows, axis=0), jnp.sum(upstream, axis=0))


def merge_terms(one_side, other_side):
    largest_logit = jnp.maximum(one_side[2], other_side[2])
    left_part = jnp.exp(one_side[2] - largest_logit)
    right_part = jnp.exp(other_side[2] - largest_logit)
    head = (
        one_side[0] * left_part + other_side[0] * right_part,
        one_side[1] * left_part + other_side[1] * right_part,
        largest_logit,
    )
    return head + tuple(
        (lhs_part + rhs_part for lhs_part, rhs_part in zip(one_side[3:], other_side[3:]))
    )


def add_tuples(running, extra):
    if running is None:
        return extra
    return tuple((lhs_part + rhs_part for lhs_part, rhs_part in zip(running, extra)))


def stretch_summary(widened_lookup_lines, widened_payload_lines, fading_rate_param):
    length = widened_lookup_lines.shape[0]
    places = lax.broadcasted_iota(jnp.int32, (length, 1), 0).astype(jnp.float32)
    exponent = widened_lookup_lines + (length - 1.0 - places) * fading_rate_param
    largest_logit = jnp.max(exponent, axis=0)
    weights = jnp.exp(exponent - largest_logit)
    return (
        jnp.sum(weights * widened_payload_lines, axis=0),
        jnp.sum(weights, axis=0),
        largest_logit,
    )


def span_mixing(
    widened_lookup_lines,
    widened_payload_lines,
    fading_rate_param,
    reward_channels,
    incoming_numerator,
    incoming_denominator,
    incoming_maximum,
):
    length = widened_lookup_lines.shape[0]
    places = lax.broadcasted_iota(jnp.int32, (length, 1), 0).astype(jnp.float32)
    row_ids = lax.broadcasted_iota(jnp.int32, (length, length), 0)
    col_ids = lax.broadcasted_iota(jnp.int32, (length, length), 1)
    lower = (col_ids < row_ids).astype(jnp.float32)
    shifted = widened_lookup_lines - places * fading_rate_param
    maxima = jnp.max(shifted, axis=0)
    factor = jnp.exp(shifted - maxima)
    cumulative_numerator = jnp.dot(
        lower, factor * widened_payload_lines, precision=highest, preferred_element_type=jnp.float32
    )
    cumulative_denominator = jnp.dot(
        lower, factor, precision=highest, preferred_element_type=jnp.float32
    )
    nearby_logit = (places - 1.0) * fading_rate_param + maxima
    opening_logit = places * fading_rate_param + incoming_maximum
    reward_logit = reward_channels + widened_lookup_lines
    largest_logit = jnp.maximum(jnp.maximum(nearby_logit, opening_logit), reward_logit)
    local_portion = jnp.exp(nearby_logit - largest_logit)
    start_portion = jnp.exp(opening_logit - largest_logit)
    reward_contribution = jnp.exp(reward_logit - largest_logit)
    return (
        cumulative_numerator * local_portion
        + incoming_numerator * start_portion
        + widened_payload_lines * reward_contribution
    ) / (
        cumulative_denominator * local_portion
        + incoming_denominator * start_portion
        + reward_contribution
    )


def body(
    stream_in,
    cotangent,
    previous_mix,
    previous_ffn,
    state_num,
    state_den,
    state_exp,
    gain_one,
    bias_one,
    gain_two,
    bias_two,
    mix_key,
    mix_value,
    mix_recept,
    time_decay,
    time_first,
    chan_mix_key,
    chan_mix_recept,
    att_key,
    att_value,
    att_recept,
    att_output,
    chan_key,
    chan_value,
    chan_recept,
):
    shards = (
        gain_one,
        bias_one,
        gain_two,
        bias_two,
        mix_key,
        mix_value,
        mix_recept,
        time_decay,
        time_first,
        chan_mix_key,
        chan_mix_recept,
        att_key,
        att_value,
        att_recept,
        att_output,
        chan_key,
        chan_value,
        chan_recept,
    )
    batches = stream_in.shape[0]
    length = stream_in.shape[2]
    stretches = lax.axis_size("stretch")
    position = lax.axis_index("stretch")
    at_start = position == 0
    later_count = (stretches - 1 - position).astype(jnp.float32)
    earlier_count = position.astype(jnp.float32)
    summed = None
    block_rows = []
    stream_grads = []
    total_terms = []
    state_terms = []
    stretch_span = None
    for micro_index in range(batches):
        gathered = (
            lax.all_gather(shards[0], "seg", axis=0, tiled=True),
            lax.all_gather(shards[1], "seg", axis=0, tiled=True),
            lax.all_gather(shards[2], "seg", axis=0, tiled=True),
            lax.all_gather(shards[3], "seg", axis=0, tiled=True),
            lax.all_gather(shards[4], "seg", axis=0, tiled=True),
            lax.all_gather(shards[5], "seg", axis=0, tiled=True),
            lax.all_gather(shards[6], "seg", axis=0, tiled=True),
            lax.all_gather(shards[7], "seg", axis=0, tiled=True),
            lax.all_gather(shards[8], "seg", axis=0, tiled=True),
            lax.all_gather(shards[9], "seg", axis=0, tiled=True),
            lax.all_gather(shards[10], "seg", axis=0, tiled=True),
            lax.all_gather(shards[11], "seg", axis=0, tiled=True),
            lax.all_gather(shards[12], "seg", axis=0, tiled=True),
            lax.all_gather(shards[13], "seg", axis=0, tiled=True),
            lax.all_gather(shards[14], "seg", axis=0, tiled=True),
            lax.all_gather(shards[15], "seg", axis=0, tiled=True),
            lax.all_gather(shards[16], "seg", axis=0, tiled=True),
            lax.all_gather(shards[17], "seg", axis=0, tiled=True),
        )
        vectors = [member.astype(jnp.float32) for member in gathered[:11]]
        (
            norm_gain_a,
            norm_bias_a,
            norm_gain_b,
            norm_bias_b,
            mixing_key,
            mixing_value,
            mixing_recept,
            decay_log,
            reward_channels,
            chan_mixing_key,
            chan_mixing_recept,
        ) = vectors
        (
            key_matrix,
            value_matrix,
            recept_matrix,
            output_matrix,
            hidden_matrix,
            back_matrix,
            gate_matrix,
        ) = gathered[11:]
        stream_rows = stream_in[micro_index, 0].astype(jnp.float32)
        normed_att, unit_att, inverse_att = norm_forward(stream_rows, norm_gain_a, norm_bias_a)
        edge_att = from_behind(normed_att[length - 1 :], "stretch", 1)
        entry_att = jnp.where(at_start, previous_mix[micro_index, 0], edge_att[0])
        before_att = jnp.concatenate([entry_att[None], normed_att[:-1]], axis=0)
        key_in = (normed_att * mixing_key + before_att * (1.0 - mixing_key)).astype(jnp.bfloat16)
        value_in = (normed_att * mixing_value + before_att * (1.0 - mixing_value)).astype(
            jnp.bfloat16
        )
        recept_in = (normed_att * mixing_recept + before_att * (1.0 - mixing_recept)).astype(
            jnp.bfloat16
        )
        widened_lookup_lines = jnp.dot(key_in, key_matrix, preferred_element_type=jnp.float32)
        widened_payload_lines = jnp.dot(value_in, value_matrix, preferred_element_type=jnp.float32)
        recs_f = jnp.dot(recept_in, recept_matrix, preferred_element_type=jnp.float32)
        fading_rate_param = -jnp.exp(decay_log)
        stretch_span = fading_rate_param * length
        summary, pull_summary = jax.vjp(
            stretch_summary, widened_lookup_lines, widened_payload_lines, fading_rate_param
        )
        zeros_vec = jnp.zeros_like(fading_rate_param)
        empty = (zeros_vec, zeros_vec, jnp.full_like(fading_rate_param, bottom))
        earlier_whole = entering_2(
            (summary[0], summary[1], summary[2] + later_count * stretch_span),
            "stretch",
            merge_terms,
            empty,
            False,
        )
        earlier = (
            earlier_whole[0],
            earlier_whole[1],
            earlier_whole[2] - (later_count + 1.0) * stretch_span,
        )
        entering = merge_terms(
            (
                state_num[micro_index, 0],
                state_den[micro_index, 0],
                state_exp[micro_index, 0] + earlier_count * stretch_span,
            ),
            earlier,
        )
        blended, mixing_pullback = jax.vjp(
            span_mixing,
            widened_lookup_lines,
            widened_payload_lines,
            fading_rate_param,
            reward_channels,
            entering[0],
            entering[1],
            entering[2],
        )
        total_terms.append((summary[0], summary[1], summary[2] + later_count * stretch_span))
        sig_recept = jax.nn.sigmoid(recs_f)
        gated = (sig_recept * blended).astype(jnp.bfloat16)
        middle = stream_rows + jnp.dot(gated, output_matrix, preferred_element_type=jnp.float32)
        normed_ffn, unit_ffn, inverse_ffn = norm_forward(middle, norm_gain_b, norm_bias_b)
        edge_ffn = from_behind(normed_ffn[length - 1 :], "stretch", 1)
        entry_ffn = jnp.where(at_start, previous_ffn[micro_index, 0], edge_ffn[0])
        before_ffn = jnp.concatenate([entry_ffn[None], normed_ffn[:-1]], axis=0)
        fkey_in = (normed_ffn * chan_mixing_key + before_ffn * (1.0 - chan_mixing_key)).astype(
            jnp.bfloat16
        )
        frec_in = (
            normed_ffn * chan_mixing_recept + before_ffn * (1.0 - chan_mixing_recept)
        ).astype(jnp.bfloat16)
        pre_act = jnp.dot(fkey_in, hidden_matrix, preferred_element_type=jnp.float32)
        active = jax.nn.relu(pre_act)
        hidden = (active * active).astype(jnp.bfloat16)
        chan_val = jnp.dot(hidden, back_matrix, preferred_element_type=jnp.float32)
        chan_gate = jnp.dot(frec_in, gate_matrix, preferred_element_type=jnp.float32)
        sig_gate = jax.nn.sigmoid(chan_gate)
        block_rows.append((middle + sig_gate * chan_val).astype(jnp.bfloat16))
        upstream = cotangent[micro_index, 0].astype(jnp.float32)
        d_fval = (upstream * sig_gate).astype(jnp.bfloat16)
        d_frec = (upstream * chan_val * sig_gate * (1.0 - sig_gate)).astype(jnp.bfloat16)
        d_hidden = matmul_nt(d_fval, back_matrix)
        d_pre = (d_hidden * 2.0 * active).astype(jnp.bfloat16)
        d_fkey_in = matmul_nt(d_pre, hidden_matrix)
        d_frec_in = matmul_nt(d_frec, gate_matrix)
        gap_ffn = normed_ffn - before_ffn
        d_before_ffn = d_fkey_in * (1.0 - chan_mixing_key) + d_frec_in * (1.0 - chan_mixing_recept)
        from_next_ffn = from_behind(d_before_ffn[:1], "stretch", -1)
        d_normed_ffn = (
            d_fkey_in * chan_mixing_key
            + d_frec_in * chan_mixing_recept
            + jnp.concatenate([d_before_ffn[1:], from_next_ffn], axis=0)
        )
        row_ffn = jnp.where(at_start, d_before_ffn[0], 0.0)
        back_ffn_rows, grad_gain_b, grad_bias_b = norm_backward(
            d_normed_ffn, unit_ffn, inverse_ffn, norm_gain_b
        )
        d_middle = upstream + back_ffn_rows
        d_branch = d_middle.astype(jnp.bfloat16)
        d_gated = matmul_nt(d_branch, output_matrix)
        weighted_value_gradient = d_gated * sig_recept
        d_recs = (d_gated * blended * sig_recept * (1.0 - sig_recept)).astype(jnp.bfloat16)
        (
            key_mixing_gradient,
            value_mixing_gradient,
            decay_mixing_gradient,
            reward_sensitivity,
            incoming_numerator_gradient,
            incoming_denominator_gradient,
            discarded_maximum,
        ) = mixing_pullback(weighted_value_gradient)
        back_term = (
            incoming_numerator_gradient,
            incoming_denominator_gradient,
            earlier_count * stretch_span - entering[2],
        )
        later_whole = entering_2(back_term, "stretch", merge_terms, empty, True)
        later = (
            later_whole[0],
            later_whole[1],
            later_whole[2] - (earlier_count + 1.0) * stretch_span,
        )
        lift_next = jnp.exp(later[2] + summary[2])
        d_summary = (
            later[0] * lift_next,
            later[1] * lift_next,
            (later[0] * summary[0] + later[1] * summary[1]) * lift_next,
        )
        dk_summ, dv_summ, dw_summ = pull_summary(d_summary)
        dw_chain = (
            length
            * (later[0] * entering[0] + later[1] * entering[1])
            * jnp.exp(later[2] + entering[2] + stretch_span)
        )
        d_rate = decay_mixing_gradient + dw_summ + dw_chain
        state_terms.append(
            (
                incoming_numerator_gradient,
                incoming_denominator_gradient,
                earlier_count * stretch_span - entering[2],
                row_ffn,
            )
        )
        d_keys = (key_mixing_gradient + dk_summ).astype(jnp.bfloat16)
        d_vals = (value_mixing_gradient + dv_summ).astype(jnp.bfloat16)
        d_key_in = matmul_nt(d_keys, key_matrix)
        d_value_in = matmul_nt(d_vals, value_matrix)
        d_recept_in = matmul_nt(d_recs, recept_matrix)
        gap_att = normed_att - before_att
        d_before_att = (
            d_key_in * (1.0 - mixing_key)
            + d_value_in * (1.0 - mixing_value)
            + d_recept_in * (1.0 - mixing_recept)
        )
        from_next_att = from_behind(d_before_att[:1], "stretch", -1)
        d_normed_att = (
            d_key_in * mixing_key
            + d_value_in * mixing_value
            + d_recept_in * mixing_recept
            + jnp.concatenate([d_before_att[1:], from_next_att], axis=0)
        )
        state_terms[-1] = state_terms[-1] + (jnp.where(at_start, d_before_att[0], 0.0),)
        back_att_rows, grad_gain_a, grad_bias_a = norm_backward(
            d_normed_att, unit_att, inverse_att, norm_gain_a
        )
        stream_grads.append((d_middle + back_att_rows).astype(jnp.bfloat16))
        local = (
            grad_gain_a,
            grad_bias_a,
            grad_gain_b,
            grad_bias_b,
            jnp.sum(d_key_in * gap_att, axis=0),
            jnp.sum(d_value_in * gap_att, axis=0),
            jnp.sum(d_recept_in * gap_att, axis=0),
            d_rate * fading_rate_param,
            reward_sensitivity,
            jnp.sum(d_fkey_in * gap_ffn, axis=0),
            jnp.sum(d_frec_in * gap_ffn, axis=0),
            matmul_tn(key_in, d_keys),
            matmul_tn(value_in, d_vals),
            matmul_tn(recept_in, d_recs),
            matmul_tn(gated, d_branch),
            matmul_tn(fkey_in, d_pre),
            matmul_tn(hidden, d_fval),
            matmul_tn(frec_in, d_frec),
        )
        summed = add_tuples(summed, local)
    group_total = jax.tree.map(
        lambda part: part.astype(jnp.float32),
        lax.psum_scatter(for_sending(summed), "seg", scatter_dimension=0, tiled=True),
    )
    summed = jax.tree.map(
        lambda part: part.astype(jnp.float32),
        lax.psum_scatter(for_sending(group_total), "stretch", scatter_dimension=0, tiled=True),
    )
    stacked_total = tuple(
        (jnp.stack([term[index_pos] for term in total_terms]) for index_pos in range(3))
    )
    merged_total = combined_all(stacked_total, "stretch", merge_terms)
    closing = merge_terms(
        (state_num[:, 0], state_den[:, 0], state_exp[:, 0] + stretches * stretch_span), merged_total
    )
    final_mean = (closing[0] / closing[1])[:, None]
    final_log = (closing[2] + jnp.log(closing[1]))[:, None]
    stacked_state = tuple(
        (jnp.stack([term[index_pos] for term in state_terms]) for index_pos in range(5))
    )
    merged_state = merged(stacked_state, "stretch", merge_terms)
    lift_init = jnp.exp(merged_state[2] + state_exp[:, 0])
    grad_state_num = merged_state[0] * lift_init
    grad_state_den = merged_state[1] * lift_init
    grad_state_exp = state_num[:, 0] * grad_state_num + state_den[:, 0] * grad_state_den
    grad_previous_ffn = merged_state[3]
    grad_previous_mix = merged_state[4]
    block_out = jnp.stack(block_rows)[:, None]
    grad_stream = jnp.stack(stream_grads)[:, None]
    return (
        block_out,
        grad_stream,
        summed[0],
        summed[1],
        summed[2],
        summed[3],
        summed[4],
        summed[5],
        summed[6],
        summed[7],
        summed[8],
        summed[9],
        summed[10],
        summed[11],
        summed[12],
        summed[13],
        summed[14],
        summed[15],
        summed[16],
        summed[17],
        grad_state_num[:, None],
        grad_state_den[:, None],
        grad_state_exp[:, None],
        grad_previous_mix[:, None],
        grad_previous_ffn[:, None],
        final_mean,
        final_log,
    )


def solution(mesh):
    return jax.shard_map(
        body,
        mesh=mesh,
        in_specs=(
            P(None, "seg", "stretch", None),
            P(None, "seg", "stretch", None),
            P(None, "seg", None),
            P(None, "seg", None),
            P(None, "seg", None),
            P(None, "seg", None),
            P(None, "seg", None),
            P("seg"),
            P("seg"),
            P("seg"),
            P("seg"),
            P("seg"),
            P("seg"),
            P("seg"),
            P("seg"),
            P("seg"),
            P("seg"),
            P("seg"),
            P("seg", None),
            P("seg", None),
            P("seg", None),
            P("seg", None),
            P("seg", None),
            P("seg", None),
            P("seg", None),
        ),
        out_specs=(
            P(None, "seg", "stretch", None),
            P(None, "seg", "stretch", None),
            P(("seg", "stretch")),
            P(("seg", "stretch")),
            P(("seg", "stretch")),
            P(("seg", "stretch")),
            P(("seg", "stretch")),
            P(("seg", "stretch")),
            P(("seg", "stretch")),
            P(("seg", "stretch")),
            P(("seg", "stretch")),
            P(("seg", "stretch")),
            P(("seg", "stretch")),
            P(("seg", "stretch"), None),
            P(("seg", "stretch"), None),
            P(("seg", "stretch"), None),
            P(("seg", "stretch"), None),
            P(("seg", "stretch"), None),
            P(("seg", "stretch"), None),
            P(("seg", "stretch"), None),
            P(None, "seg", None),
            P(None, "seg", None),
            P(None, "seg", None),
            P(None, "seg", None),
            P(None, "seg", None),
            P(None, "seg", None),
            P(None, "seg", None),
        ),
        check_vma=False,
    )
```

profile of v0, /device:TPU:9, one launch (start us, length us, event | category | flops | bytes accessed | tf_op | source)
XLA Modules:
  0.0 852.2 jit_solution(14177147229784541951)
XLA Ops:
  11.4 9.2 %all-gather.15 = bf16[8,1,128]{2,1,0:T(2,128)(2,1)S(1)} all-gather(bf16[1,1,128]{2,1,0:T(2,128)(2,1)S(1)} %bitcast.580), channel_id=1, replica_groups=mesh['seg'=8,'stretch'=4] {'seg'}, dimensions={0}, use_global_device_ids=true | all-gather | bytes 2304 | tf_op jit(solution)/shard_map/all_gather | solution.py:229
  20.6 8.7 %all-gather.16 = bf16[8,1,128]{2,1,0:T(2,128)(2,1)S(1)} all-gather(bf16[1,1,128]{2,1,0:T(2,128)(2,1)S(1)} %bitcast.581), channel_id=1, replica_groups=mesh['seg'=8,'stretch'=4] {'seg'}, dimensions={0}, use_global_device_ids=true | all-gather | bytes 2304 | tf_op jit(solution)/shard_map/all_gather | solution.py:230
  30.2 3.2 collective-permute-start.2
  33.4 3.2 collective-permute-start
  37.3 8.3 all-gather.18
  45.6 8.7 %all-gather.20 = bf16[8,1,128]{2,1,0:T(2,128)(2,1)S(1)} all-gather(bf16[1,1,128]{2,1,0:T(2,128)(2,1)S(1)} %bitcast.583), channel_id=1, replica_groups=mesh['seg'=8,'stretch'=4] {'seg'}, dimensions={0}, use_global_device_ids=true | all-gather | bytes 2304 | tf_op jit(solution)/shard_map/all_gather | solution.py:234
  54.3 7.8 all-gather.17
  62.1 8.7 %all-gather.25 = bf16[8,1,128]{2,1,0:T(2,128)(2,1)S(1)} all-gather(bf16[1,1,128]{2,1,0:T(2,128)(2,1)S(1)} %bitcast.585), channel_id=1, replica_groups=mesh['seg'=8,'stretch'=4] {'seg'}, dimensions={0}, use_global_device_ids=true | all-gather | bytes 2304 | tf_op jit(solution)/shard_map/all_gather | solution.py:238
  70.9 7.8 all-gather.24
  78.7 8.7 %all-gather.19 = bf16[8,1,128]{2,1,0:T(2,128)(2,1)S(1)} all-gather(bf16[1,1,128]{2,1,0:T(2,128)(2,1)S(1)} %bitcast.587), channel_id=1, replica_groups=mesh['seg'=8,'stretch'=4] {'seg'}, dimensions={0}, use_global_device_ids=true | all-gather | bytes 2304 | tf_op jit(solution)/shard_map/all_gather | solution.py:236
  90.5 7.8 all-gather.22
  98.3 8.7 %all-gather.23 = bf16[8,1,128]{2,1,0:T(2,128)(2,1)S(1)} all-gather(bf16[1,1,128]{2,1,0:T(2,128)(2,1)S(1)} %bitcast.589), channel_id=1, replica_groups=mesh['seg'=8,'stretch'=4] {'seg'}, dimensions={0}, use_global_device_ids=true | all-gather | bytes 2304 | tf_op jit(solution)/shard_map/all_gather | solution.py:232
  107.7 7.8 all-gather.21
  118.6 8.7 %all-gather = f32[4096]{0:T(1024)S(1)} all-gather(f32[1024]{0:T(1024)S(1)} %multiply_add_fusion.23), channel_id=2, replica_groups=mesh['seg'=8,'stretch'=4] {'stretch'}, dimensions={0}, use_global_device_ids=true | all-gather | bytes 20480 | tf_op jit(solution)/shard_map/all_gather | solution.py:19
  131.4 10.4 %all-gather.5 = f32[4096]{0:T(1024)S(1)} all-gather(f32[1024]{0:T(1024)S(1)} %get-tuple-element.1363), channel_id=7, replica_groups=mesh['seg'=8,'stretch'=4] {'stretch'}, dimensions={0}, use_global_device_ids=true | all-gather | bytes 20480 | tf_op jit(solution)/shard_map/all_gather | solution.py:19
  141.8 10.2 %all-gather.4 = f32[4096]{0:T(1024)S(1)} all-gather(f32[1024]{0:T(1024)S(1)} %get-tuple-element.1364), channel_id=6, replica_groups=mesh['seg'=8,'stretch'=4] {'stretch'}, dimensions={0}, use_global_device_ids=true | all-gather | bytes 20480 | tf_op jit(solution)/shard_map/all_gather | solution.py:19
  152.7 9.9 %all-gather.1 = f32[4096]{0:T(1024)S(1)} all-gather(f32[1024]{0:T(1024)S(1)} %get-tuple-element.1388), channel_id=3, replica_groups=mesh['seg'=8,'stretch'=4] {'stretch'}, dimensions={0}, use_global_device_ids=true | all-gather | bytes 20480 | tf_op jit(solution)/shard_map/all_gather | solution.py:19
  162.6 10.6 %all-gather.2 = f32[4096]{0:T(1024)S(1)} all-gather(f32[1024]{0:T(1024)S(1)} %get-tuple-element.1389), channel_id=4, replica_groups=mesh['seg'=8,'stretch'=4] {'stretch'}, dimensions={0}, use_global_device_ids=true | all-gather | bytes 20480 | tf_op jit(solution)/shard_map/all_gather | solution.py:19
  174.1 9.9 %all-gather.6 = f32[4096]{0:T(1024)S(1)} all-gather(f32[1024]{0:T(1024)S(1)} %get-tuple-element.1531), channel_id=8, replica_groups=mesh['seg'=8,'stretch'=4] {'stretch'}, dimensions={0}, use_global_device_ids=true | all-gather | bytes 20480 | tf_op jit(solution)/shard_map/all_gather | solution.py:19
  184.6 10.8 %all-gather.3 = f32[4096]{0:T(1024)S(1)} all-gather(f32[1024]{0:T(1024)S(1)} %get-tuple-element.1674), channel_id=5, replica_groups=mesh['seg'=8,'stretch'=4] {'stretch'}, dimensions={0}, use_global_device_ids=true | all-gather | bytes 20480 | tf_op jit(solution)/shard_map/all_gather | solution.py:19
  198.4 4.3 multiply_convert_fusion.5
  205.7 3.1 while.121
  210.8 4.6 convert_reduce_fusion.3
  216.9 3.0 collective-permute-start.3
  222.8 9.3 %all-gather.9 = f32[4096]{0:T(1024)S(1)} all-gather(f32[1024]{0:T(1024)S(1)} %get-tuple-element.1536), channel_id=11, replica_groups=mesh['seg'=8,'stretch'=4] {'stretch'}, dimensions={0}, use_global_device_ids=true | all-gather | bytes 20480 | tf_op jit(solution)/shard_map/all_gather | solution.py:19
  233.3 3.3 fusion.29
  237.9 6.2 convolution_maximum_fusion
  245.4 25.6 %all-gather.49.cloned.1.call-done = bf16[4096,1024]{1,0:T(8,128)(2,1)} async-done(((bf16[512,1024]{1,0:T(8,128)(2,1)}), bf16[4096,1024]{1,0:T(8,128)(2,1)}) %all-gather.49.cloned.1.call-update) | async-done | bytes 8388624 | tf_op jit(solution)/shard_map/all_gather | solution.py:245
  271.0 4.8 fusion.117
  292.9 3.9 fusion.17
  313.4 3.6 multiply_reduce_fusion.19
  331.5 10.9 %all-gather.8 = f32[4096]{0:T(1024)S(1)} all-gather(f32[1024]{0:T(1024)S(1)} %get-tuple-element.1395), channel_id=10, replica_groups=mesh['seg'=8,'stretch'=4] {'stretch'}, dimensions={0}, use_global_device_ids=true | all-gather | bytes 20480 | tf_op jit(solution)/shard_map/all_gather | solution.py:19
  342.4 10.2 %all-gather.7 = f32[4096]{0:T(1024)S(1)} all-gather(f32[1024]{0:T(1024)S(1)} %get-tuple-element.1394), channel_id=9, replica_groups=mesh['seg'=8,'stretch'=4] {'stretch'}, dimensions={0}, use_global_device_ids=true | all-gather | bytes 20480 | tf_op jit(solution)/shard_map/all_gather | solution.py:19
  357.1 3.2 while.122
  362.2 3.0 fusion.196
  373.9 3.2 multiply_reduce_fusion.7
  377.1 10.3 %all-gather.10 = f32[4096]{0:T(1024)S(1)} all-gather(f32[1024]{0:T(1024)S(1)} %get-tuple-element.1342), channel_id=12, replica_groups=mesh['seg'=8,'stretch'=4] {'stretch'}, dimensions={0}, use_global_device_ids=true | all-gather | bytes 20480 | tf_op jit(solution)/shard_map/all_gather | solution.py:19
  387.4 9.9 %all-gather.11 = f32[4096]{0:T(1024)S(1)} all-gather(f32[1024]{0:T(1024)S(1)} %get-tuple-element.1341), channel_id=13, replica_groups=mesh['seg'=8,'stretch'=4] {'stretch'}, dimensions={0}, use_global_device_ids=true | all-gather | bytes 20480 | tf_op jit(solution)/shard_map/all_gather | solution.py:19
  397.4 3.2 while.123
  409.6 3.1 multiply_reduce_fusion.8
  416.3 9.5 %fusion.116 = f32[4096,1024]{1,0:T(8,128)} fusion(f32[128,4096]{1,0:T(8,128)S(1)} %convolution_maximum_fusion.1, f32[128,1024]{1,0:T(8,128)} %fusion.25, bf16[2,1,128,1024]{3,2,1,0:T(8,128)(2,1)} %param.38), kind=kOutput, calls=%fused_computation.308 | convolution fusion | flops 1075183616 | bytes 19660800 | tf_op jit(solution)/shard_map/dot_general | solution.py:71
  425.9 11.8 %add_convert_fusion = bf16[4096,1024]{1,0:T(8,128)(2,1)} fusion(f32[4096,1024]{1,0:T(8,128)} %fusion.116, f32[128,4096]{1,0:T(8,128)S(1)} %copy-done.3, f32[128,1024]{1,0:T(8,128)S(1)} %copy-done.67, bf16[2,1,128,1024]{3,2,1,0:T(8,128)(2,1)S(1)} %copy-done.65), kind=kOutput, calls=%fused_computation.59 | convolution fusion | flops 1083572224 | bytes 28049408 | tf_op jit(solution)/shard_map/dot_general | solution.py:71
  438.9 9.2 %fusion.204 = f32[1024,4096]{1,0:T(8,128)} fusion(bf16[128,1024]{1,0:T(8,128)(2,1)} %copy-done.84, bf16[128,4096]{1,0:T(8,128)(2,1)S(1)} %copy-done.34), kind=kOutput, calls=%fused_computation.490 | convolution fusion | flops 1073741824 | bytes 18087936 | tf_op jit(solution)/shard_map/dot_general | solution.py:71
  448.1 11.6 %add_convert_fusion.1 = bf16[1024,4096]{1,0:T(8,128)(2,1)} fusion(f32[1024,4096]{1,0:T(8,128)} %fusion.204, bf16[128,1024]{1,0:T(8,128)(2,1)S(1)} %copy-done.83, bf16[128,4096]{1,0:T(8,128)(2,1)S(1)} %copy-done.36), kind=kOutput, calls=%fused_computation.60 | convolution fusion | flops 1082130432 | bytes 26476544 | tf_op jit(solution)/shard_map/dot_general | solution.py:71
  462.9 10.2 %all_gather.214 = bf16[4,2,1024]{2,1,0:T(2,128)(2,1)S(1)} all-gather(bf16[1,2,1024]{2,1,0:T(2,128)(2,1)S(1)} %pad_maximum_fusion.6), channel_id=1, replica_groups=mesh['seg'=8,'stretch'=4] {'stretch'}, dimensions={0}, use_global_device_ids=true | all-gather | bytes 20480 | tf_op jit(solution)/shard_map/all_gather | solution.py:51
  473.2 10.2 %all-gather.28 = f32[4,2,1024]{2,1,0:T(2,128)S(1)} all-gather(f32[1,2,1024]{2,1,0:T(2,128)S(1)} %maximum_bitcast_fusion.4), channel_id=16, replica_groups=mesh['seg'=8,'stretch'=4] {'stretch'}, dimensions={0}, use_global_device_ids=true | all-gather | bytes 40960 | tf_op jit(solution)/shard_map/all_gather | solution.py:40
  483.4 10.4 %all-gather.26 = f32[4,2,1024]{2,1,0:T(2,128)S(1)} all-gather(f32[1,2,1024]{2,1,0:T(2,128)S(1)} %maximum_bitcast_fusion.2), channel_id=14, replica_groups=mesh['seg'=8,'stretch'=4] {'stretch'}, dimensions={0}, use_global_device_ids=true | all-gather | bytes 40960 | tf_op jit(solution)/shard_map/all_gather | solution.py:40
  493.8 10.1 %all-gather.27 = f32[4,2,1024]{2,1,0:T(2,128)S(1)} all-gather(f32[1,2,1024]{2,1,0:T(2,128)S(1)} %maximum_bitcast_fusion.3), channel_id=15, replica_groups=mesh['seg'=8,'stretch'=4] {'stretch'}, dimensions={0}, use_global_device_ids=true | all-gather | bytes 40960 | tf_op jit(solution)/shard_map/all_gather | solution.py:40
  504.6 4.4 while.119
  510.7 10.6 %all_gather.215 = bf16[4,2,1024]{2,1,0:T(2,128)(2,1)S(1)} all-gather(bf16[1,2,1024]{2,1,0:T(2,128)(2,1)S(1)} %pad_maximum_fusion.7), channel_id=1, replica_groups=mesh['seg'=8,'stretch'=4] {'stretch'}, dimensions={0}, use_global_device_ids=true | all-gather | bytes 20480 | tf_op jit(solution)/shard_map/all_gather | solution.py:51
  529.1 10.7 %all_gather.212 = bf16[4,2,1024]{2,1,0:T(2,128)(2,1)} all-gather(bf16[1,2,1024]{2,1,0:T(2,128)(2,1)S(1)} %pad_maximum_fusion.4), channel_id=1, replica_groups=mesh['seg'=8,'stretch'=4] {'stretch'}, dimensions={0}, use_global_device_ids=true | all-gather | bytes 20480 | tf_op jit(solution)/shard_map/all_gather | solution.py:51
  548.9 4.3 multiply_add_fusion.10
  553.5 10.3 %all_gather.213 = bf16[4,2,1024]{2,1,0:T(2,128)(2,1)S(1)} all-gather(bf16[1,2,1024]{2,1,0:T(2,128)(2,1)S(1)} %pad_maximum_fusion.5), channel_id=1, replica_groups=mesh['seg'=8,'stretch'=4] {'stretch'}, dimensions={0}, use_global_device_ids=true | all-gather | bytes 20480 | tf_op jit(solution)/shard_map/all_gather | solution.py:51
  565.4 10.6 %all_gather.216 = bf16[4,2,1024]{2,1,0:T(2,128)(2,1)S(1)} all-gather(bf16[1,2,1024]{2,1,0:T(2,128)(2,1)S(1)} %pad_maximum_fusion.8), channel_id=1, replica_groups=mesh['seg'=8,'stretch'=4] {'stretch'}, dimensions={0}, use_global_device_ids=true | all-gather | bytes 20480 | tf_op jit(solution)/shard_map/all_gather | solution.py:51
  576.1 4.5 while.118
  595.6 17.0 %reduce-scatter.35.cloned.1.call-done = bf16[512,1024]{1,0:T(8,128)(2,1)} async-done(((bf16[4096,1024]{1,0:T(8,128)(2,1)}), bf16[512,1024]{1,0:T(8,128)(2,1)}) %reduce-scatter.35.cloned.1.call-update) | async-done | bytes 1048592 | tf_op jit(solution)/shard_map/reduce_scatter | solution.py:455
  617.4 69.8 %reduce-scatter.31.cloned.1.call-done = bf16[128,4096]{1,0:T(8,128)(2,1)} async-done(((bf16[1024,4096]{1,0:T(8,128)(2,1)}), bf16[128,4096]{1,0:T(8,128)(2,1)}) %reduce-scatter.31.cloned.1.call-update) | async-done | bytes 1048592 | tf_op jit(solution)/shard_map/reduce_scatter | solution.py:455
  687.3 20.6 %all-reduce.22 = (bf16[1024]{0:T(1024)(128)(2,1)S(1)}, bf16[1024]{0:T(1024)(128)(2,1)S(1)}, bf16[1024]{0:T(1024)(128)(2,1)S(1)}, bf16[1024]{0:T(1024)(128)(2,1)S...) all-reduce(bf16[1024]{0:T(1024)(128)(2,1)S(1)} %add_convert_fusion., ...), channel_id=17, replica_groups=mesh['seg'=8,'stretch'=4] {'seg'}, use_global_device_ids=true, to_apply=%region_48.49.clone | all-reduce | flops 11264 | bytes 45056
  708.7 7.5 all-reduce.23
  727.8 17.3 %reduce-scatter.25.cloned.1.call-done = bf16[32,1024]{1,0:T(8,128)(2,1)} async-done(((bf16[128,1024]{1,0:T(8,128)(2,1)}), bf16[32,1024]{1,0:T(8,128)(2,1)}) %reduce-scatter.25.cloned.1.call-update) | async-done | bytes 65552 | tf_op jit(solution)/shard_map/reduce_scatter | solution.py:459
  746.5 18.5 %reduce-scatter.21.cloned.1.call-done = bf16[32,1024]{1,0:T(8,128)(2,1)} async-done(((bf16[128,1024]{1,0:T(8,128)(2,1)}), bf16[32,1024]{1,0:T(8,128)(2,1)}) %reduce-scatter.21.cloned.1.call-update) | async-done | bytes 65552 | tf_op jit(solution)/shard_map/reduce_scatter | solution.py:459
  766.6 18.8 %reduce-scatter.17.cloned.1.call-done = bf16[32,1024]{1,0:T(8,128)(2,1)} async-done(((bf16[128,1024]{1,0:T(8,128)(2,1)}), bf16[32,1024]{1,0:T(8,128)(2,1)}) %reduce-scatter.17.cloned.1.call-update) | async-done | bytes 65552 | tf_op jit(solution)/shard_map/reduce_scatter | solution.py:459
  786.9 28.3 %reduce-scatter.37.cloned.1.call-done = bf16[128,1024]{1,0:T(8,128)(2,1)} async-done(((bf16[512,1024]{1,0:T(8,128)(2,1)}), bf16[128,1024]{1,0:T(8,128)(2,1)}) %reduce-scatter.37.cloned.1.call-update) | async-done | bytes 262160 | tf_op jit(solution)/shard_map/reduce_scatter | solution.py:459
  816.9 26.4 %reduce-scatter.33.cloned.1.call-done = bf16[32,4096]{1,0:T(8,128)(2,1)} async-done(((bf16[128,4096]{1,0:T(8,128)(2,1)}), bf16[32,4096]{1,0:T(8,128)(2,1)}) %reduce-scatter.33.cloned.1.call-update) | async-done | bytes 262160 | tf_op jit(solution)/shard_map/reduce_scatter | solution.py:459
  (953 shorter events, 190.0 us)
Async XLA Ops:
  7.2 108.3 %all-gather.39.cloned.1.call-start = ((), (), s32[]{:S(2)}) async-start(), calls=%async_computation.15 | async-start | bytes 2359296 | tf_op jit(solution)/shard_map/all_gather | solution.py:240
  8.0 119.3 %all-gather.41.cloned.1.call-start = ((), (), s32[]{:S(2)}) async-start(), calls=%async_computation.16 | async-start | bytes 2359296 | tf_op jit(solution)/shard_map/all_gather | solution.py:241
  8.7 189.6 %all-gather.37.cloned.1.call-start = ((), (), s32[]{:S(2)}) async-start(), calls=%async_computation.14 | async-start | bytes 2359296 | tf_op jit(solution)/shard_map/all_gather | solution.py:242
  9.5 193.3 %all-gather.43.cloned.1.call-start = ((), (), s32[]{:S(2)}) async-start(), calls=%async_computation.17 | async-start | bytes 2359296 | tf_op jit(solution)/shard_map/all_gather | solution.py:243
  10.0 223.2 %all-gather.45.cloned.1.call-start = ((), (), s32[]{:S(2)}) async-start(), calls=%async_computation.18 | async-start | bytes 2359296 | tf_op jit(solution)/shard_map/all_gather | solution.py:246
  10.6 227.3 %all-gather.47.cloned.1.call-start = ((), (), s32[]{:S(2)}) async-start(), calls=%async_computation.19 | async-start | bytes 9437184 | tf_op jit(solution)/shard_map/all_gather | solution.py:244
  11.3 77.4 %copy-start.217 = (f32[2,1,1024]{2,1,0:T(1,128)S(1)}, f32[2,1,1024]{2,1,0:T(1,128)}, u32[]{:S(2)}) copy-start(f32[2,1,1024]{2,1,0:T(1,128)} %param.41) | copy-start | bytes 24580
  11.3 78.0 %copy-start.219 = (f32[2,1,1024]{2,1,0:T(1,128)S(1)}, f32[2,1,1024]{2,1,0:T(1,128)}, u32[]{:S(2)}) copy-start(f32[2,1,1024]{2,1,0:T(1,128)} %param.42) | copy-start | bytes 24580
  11.3 78.5 %copy-start.218 = (f32[2,1,1024]{2,1,0:T(1,128)S(1)}, f32[2,1,1024]{2,1,0:T(1,128)}, u32[]{:S(2)}) copy-start(f32[2,1,1024]{2,1,0:T(1,128)} %param.43) | copy-start | bytes 24580
  11.3 79.2 %copy-start.286 = (bf16[128]{0:T(256)(128)(2,1)S(1)}, bf16[128]{0:T(256)(128)(2,1)}, u32[]{:S(2)}) copy-start(bf16[128]{0:T(256)(128)(2,1)} %param.46) | copy-start | bytes 772
  11.3 87.0 %copy-start.287 = (bf16[128]{0:T(256)(128)(2,1)S(1)}, bf16[128]{0:T(256)(128)(2,1)}, u32[]{:S(2)}) copy-start(bf16[128]{0:T(256)(128)(2,1)} %param.47) | copy-start | bytes 772
  11.3 96.3 %copy-start.288 = (bf16[128]{0:T(256)(128)(2,1)S(1)}, bf16[128]{0:T(256)(128)(2,1)}, u32[]{:S(2)}) copy-start(bf16[128]{0:T(256)(128)(2,1)} %param.52) | copy-start | bytes 772
  11.3 104.1 %copy-start.255 = (f32[2,1,1024]{2,1,0:T(1,128)S(1)}, f32[2,1,1024]{2,1,0:T(1,128)}, u32[]{:S(2)}) copy-start(f32[2,1,1024]{2,1,0:T(1,128)} %param.39) | copy-start | bytes 24580
  11.3 259.6 %all-gather.49.cloned.1.call-start = ((), (), s32[]{:S(2)}) async-start(), calls=%async_computation.20 | async-start | bytes 9437184 | tf_op jit(solution)/shard_map/all_gather | solution.py:245
  29.5 97.8 %copy-start.224 = (f32[128]{0:T(128)}, f32[128]{0:T(128)S(1)}, u32[]{:S(2)}) copy-start(f32[128]{0:T(128)S(1)} %get-tuple-element.1692) | copy-start | bytes 1540
  29.5 100.2 %copy-start.220 = (f32[128]{0:T(128)}, f32[128]{0:T(128)S(1)}, u32[]{:S(2)}) copy-start(f32[128]{0:T(128)S(1)} %get-tuple-element.1691) | copy-start | bytes 1540
  29.8 97.5 %copy-start.232 = (f32[128]{0:T(128)}, f32[128]{0:T(128)S(1)}, u32[]{:S(2)}) copy-start(f32[128]{0:T(128)S(1)} %add_rsqrt_fusion.3) | copy-start | bytes 1540
  29.9 99.8 %copy-start.228 = (f32[128]{0:T(128)}, f32[128]{0:T(128)S(1)}, u32[]{:S(2)}) copy-start(f32[128]{0:T(128)S(1)} %add_rsqrt_fusion.1) | copy-start | bytes 1540
  30.2 99.6 %copy-start.18 = (f32[128,1024]{1,0:T(8,128)}, f32[128,1024]{1,0:T(8,128)S(1)}, u32[]{:S(2)}) copy-start(f32[128,1024]{1,0:T(8,128)S(1)} %get-tuple-element.1635) | copy-start | bytes 1572868
  30.2 168.2 %copy-start.21 = (f32[128,1024]{1,0:T(8,128)}, f32[128,1024]{1,0:T(8,128)S(1)}, u32[]{:S(2)}) copy-start(f32[128,1024]{1,0:T(8,128)S(1)} %get-tuple-element.1634) | copy-start | bytes 1572868
  30.2 85.2 %collective-permute-start.2 = (f32[1,1024]{1,0:T(1,128)S(1)}, f32[1,1024]{1,0:T(1,128)S(1)}, u32[]{:S(2)}, u32[]{:S(2)}) collective-permute-start(f32[1,1024]{1,0:T(1,128)S(1)} %slice.166), channel_id=1, source_target_pairs={{0,1},{1,2},{2,3},{4,5},{5,6},{6,7},{8,9},{9,10},{10,11},{12,13},{... | collective-permute-start | bytes 12296 | tf_op jit(solution)/shard_map/ppermute | solution.py:14
  33.4 82.0 %collective-permute-start = (f32[1,1024]{1,0:T(1,128)S(1)}, f32[1,1024]{1,0:T(1,128)S(1)}, u32[]{:S(2)}, u32[]{:S(2)}) collective-permute-start(f32[1,1024]{1,0:T(1,128)S(1)} %slice.162), channel_id=1, source_target_pairs={{0,1},{1,2},{2,3},{4,5},{5,6},{6,7},{8,9},{9,10},{10,11},{12,13},{... | collective-permute-start | bytes 12296 | tf_op jit(solution)/shard_map/ppermute | solution.py:14
  36.7 511.4 %reduce-scatter.39.cloned.1.call-start = ((), (), s32[]{:S(2)}) async-start(), calls=%async_computation.33 | async-start | bytes 2359296 | tf_op jit(solution)/shard_map/reduce_scatter | solution.py:455
  36.7 174.1 %copy-start.140 = (f32[128]{0:T(128)}, f32[128]{0:T(128)S(1)}, u32[]{:S(2)}) copy-start(f32[128]{0:T(128)S(1)} %iota_convert_fusion) | copy-start | bytes 1540
  45.6 72.9 %copy-start.128 = (f32[8,1,128]{2,1,0:T(1,128)}, f32[8,1,128]{2,1,0:T(1,128)S(1)}, u32[]{:S(2)}) copy-start(f32[8,1,128]{2,1,0:T(1,128)S(1)} %convert_element_type.619) | copy-start | bytes 12292
  54.3 75.4 %copy-start.130 = (f32[8,1,128]{2,1,0:T(1,128)}, f32[8,1,128]{2,1,0:T(1,128)S(1)}, u32[]{:S(2)}) copy-start(f32[8,1,128]{2,1,0:T(1,128)S(1)} %convert_element_type.621) | copy-start | bytes 12292
  62.1 148.7 %copy-start.133 = (f32[8,1,128]{2,1,0:T(1,128)}, f32[8,1,128]{2,1,0:T(1,128)S(1)}, u32[]{:S(2)}) copy-start(f32[8,1,128]{2,1,0:T(1,128)S(1)} %convert_element_type.618) | copy-start | bytes 12292
  70.8 161.9 %copy-start.160 = (f32[8,1,128]{2,1,0:T(1,128)}, f32[8,1,128]{2,1,0:T(1,128)S(1)}, u32[]{:S(2)}) copy-start(f32[8,1,128]{2,1,0:T(1,128)S(1)} %convert_element_type.626) | copy-start | bytes 12292
  87.4 123.4 %copy-start.147 = (f32[1024]{0:T(1024)}, f32[1024]{0:T(1024)S(1)}, u32[]{:S(2)}) copy-start(f32[1024]{0:T(1024)S(1)} %broadcast_subtract_fusion.4) | copy-start | bytes 12292
  89.2 106.3 %copy-start.197 = (f32[1,1,1024]{2,1,0:T(1,128)}, f32[1,1,1024]{2,1,0:T(1,128)S(1)}, u32[]{:S(2)}) copy-start(f32[1,1,1024]{2,1,0:T(1,128)S(1)} %get-tuple-element.1665) | copy-start | bytes 12292
  89.8 105.7 %copy-start.201 = (f32[1,1,1024]{2,1,0:T(1,128)}, f32[1,1,1024]{2,1,0:T(1,128)S(1)}, u32[]{:S(2)}) copy-start(f32[1,1,1024]{2,1,0:T(1,128)S(1)} %get-tuple-element.1669) | copy-start | bytes 12292
  98.3 118.1 %copy-start.158 = (f32[8,1,128]{2,1,0:T(1,128)}, f32[8,1,128]{2,1,0:T(1,128)S(1)}, u32[]{:S(2)}) copy-start(f32[8,1,128]{2,1,0:T(1,128)S(1)} %convert_element_type.623) | copy-start | bytes 12292
  115.5 82.9 %copy-start.136 = (f32[1,1024]{1,0:T(1,128)}, f32[1,1024]{1,0:T(1,128)S(1)}, u32[]{:S(2)}) copy-start(f32[1,1024]{1,0:T(1,128)S(1)} %get-tuple-element.1671) | copy-start | bytes 12292
  115.5 298.1 %copy-start.126 = (f32[1,1024]{1,0:T(1,128)}, f32[1,1024]{1,0:T(1,128)S(1)}, u32[]{:S(2)}) copy-start(f32[1,1024]{1,0:T(1,128)S(1)} %get-tuple-element.1672) | copy-start | bytes 12292
  118.6 79.8 %copy-start.7 = (f32[128,1024]{1,0:T(8,128)}, f32[128,1024]{1,0:T(8,128)S(1)}, u32[]{:S(2)}) copy-start(f32[128,1024]{1,0:T(8,128)S(1)} %get-tuple-element.1675) | copy-start | bytes 1572868
  130.8 79.3 %copy-start.30 = (f32[128,1024]{1,0:T(8,128)}, f32[128,1024]{1,0:T(8,128)S(1)}, u32[]{:S(2)}) copy-start(f32[128,1024]{1,0:T(8,128)S(1)} %get-tuple-element.1676) | copy-start | bytes 1572868
  130.8 67.6 %copy-start.171 = (f32[128]{0:T(128)S(1)}, f32[128]{0:T(128)}, u32[]{:S(2)}) copy-start(f32[128]{0:T(128)} %broadcast_add_fusion) | copy-start | bytes 1540
  209.5 114.5 %copy-start.150 = (f32[1024]{0:T(1024)}, f32[1024]{0:T(1024)S(1)}, u32[]{:S(2)}) copy-start(f32[1024]{0:T(1024)S(1)} %get-tuple-element.1659) | copy-start | bytes 12292
  209.5 114.5 %copy-start.152 = (f32[1024]{0:T(1024)}, f32[1024]{0:T(1024)S(1)}, u32[]{:S(2)}) copy-start(f32[1024]{0:T(1024)S(1)} %get-tuple-element.1660) | copy-start | bytes 12292
  216.9 15.8 %collective-permute-start.3 = (f32[1,1024]{1,0:T(1,128)S(1)}, f32[1,1024]{1,0:T(1,128)S(1)}, u32[]{:S(2)}, u32[]{:S(2)}) collective-permute-start(f32[1,1024]{1,0:T(1,128)S(1)} %slice.168), channel_id=1, source_target_pairs={{0,1},{1,2},{2,3},{4,5},{5,6},{6,7},{8,9},{9,10},{10,11},{12,13},{... | collective-permute-start | bytes 12296 | tf_op jit(solution)/shard_map/ppermute | solution.py:14
  219.9 12.8 %collective-permute-start.1 = (f32[1,1024]{1,0:T(1,128)S(1)}, f32[1,1024]{1,0:T(1,128)S(1)}, u32[]{:S(2)}, u32[]{:S(2)}) collective-permute-start(f32[1,1024]{1,0:T(1,128)S(1)} %slice.164), channel_id=1, source_target_pairs={{0,1},{1,2},{2,3},{4,5},{5,6},{6,7},{8,9},{9,10},{10,11},{12,13},{... | collective-permute-start | bytes 12296 | tf_op jit(solution)/shard_map/ppermute | solution.py:14
  303.1 10.2 %collective-permute-start.6 = (f32[1,1024]{1,0:T(1,128)S(1)}, f32[1,1024]{1,0:T(1,128)S(1)}, u32[]{:S(2)}, u32[]{:S(2)}) collective-permute-start(f32[1,1024]{1,0:T(1,128)S(1)} %slice.175), channel_id=1, source_target_pairs={{1,0},{2,1},{3,2},{5,4},{6,5},{7,6},{9,8},{10,9},{11,10},{13,12},{... | collective-permute-start | bytes 12296 | tf_op jit(solution)/shard_map/ppermute | solution.py:14
  305.2 8.0 collective-permute-start.4
  313.2 240.2 %reduce-scatter.27.cloned.1.call-start = ((), (), s32[]{:S(2)}) async-start(), calls=%async_computation.27 | async-start | bytes 2359296 | tf_op jit(solution)/shard_map/reduce_scatter | solution.py:455
  356.8 208.5 %reduce-scatter.23.cloned.1.call-start = ((), (), s32[]{:S(2)}) async-start(), calls=%async_computation.25 | async-start | bytes 2359296 | tf_op jit(solution)/shard_map/reduce_scatter | solution.py:455
  372.9 203.1 %reduce-scatter.19.cloned.1.call-start = ((), (), s32[]{:S(2)}) async-start(), calls=%async_computation.23 | async-start | bytes 2359296 | tf_op jit(solution)/shard_map/reduce_scatter | solution.py:455
  408.6 179.7 %reduce-scatter.15.cloned.1.call-start = ((), (), s32[]{:S(2)}) async-start(), calls=%async_computation.21 | async-start | bytes 2359296 | tf_op jit(solution)/shard_map/reduce_scatter | solution.py:455
  415.8 196.8 %reduce-scatter.35.cloned.1.call-start = ((), (), s32[]{:S(2)}) async-start(), calls=%async_computation.31 | async-start | bytes 9437184 | tf_op jit(solution)/shard_map/reduce_scatter | solution.py:455
  437.8 249.5 %reduce-scatter.31.cloned.1.call-start = ((), (), s32[]{:S(2)}) async-start(), calls=%async_computation.29 | async-start | bytes 9437184 | tf_op jit(solution)/shard_map/reduce_scatter | solution.py:455
  459.7 80.2 %copy-start.50 = (bf16[1024,1024]{1,0:T(8,128)(2,1)S(1)}, bf16[1024,1024]{1,0:T(8,128)(2,1)}, u32[]{:S(2)}) copy-start(bf16[1024,1024]{1,0:T(8,128)(2,1)} %all-gather.37.cloned.1.call-done) | copy-start | bytes 6291460
  459.7 80.1 %copy-start.91 = (bf16[128,1024]{1,0:T(8,128)(2,1)S(1)}, bf16[128,1024]{1,0:T(8,128)(2,1)}, u32[]{:S(2)}) copy-start(bf16[128,1024]{1,0:T(8,128)(2,1)} %get-tuple-element.1613) | copy-start | bytes 786436
  459.7 265.0 %reduce-scatter.41.cloned.1.call-start = ((), (), s32[]{:S(2)}) async-start(), calls=%async_computation.34 | async-start | bytes 327680 | tf_op jit(solution)/shard_map/reduce_scatter | solution.py:459
  548.1 178.2 %reduce-scatter.29.cloned.1.call-start = ((), (), s32[]{:S(2)}) async-start(), calls=%async_computation.28 | async-start | bytes 327680 | tf_op jit(solution)/shard_map/reduce_scatter | solution.py:459
  553.4 191.6 %reduce-scatter.25.cloned.1.call-start = ((), (), s32[]{:S(2)}) async-start(), calls=%async_computation.26 | async-start | bytes 327680 | tf_op jit(solution)/shard_map/reduce_scatter | solution.py:459
  565.3 199.7 %reduce-scatter.21.cloned.1.call-start = ((), (), s32[]{:S(2)}) async-start(), calls=%async_computation.24 | async-start | bytes 327680 | tf_op jit(solution)/shard_map/reduce_scatter | solution.py:459
  576.0 209.3 %reduce-scatter.17.cloned.1.call-start = ((), (), s32[]{:S(2)}) async-start(), calls=%async_computation.22 | async-start | bytes 327680 | tf_op jit(solution)/shard_map/reduce_scatter | solution.py:459
  582.3 30.4 %collective-permute-start.7 = (f32[1,1024]{1,0:T(1,128)S(1)}, f32[1,1024]{1,0:T(1,128)S(1)}, u32[]{:S(2)}, u32[]{:S(2)}) collective-permute-start(f32[1,1024]{1,0:T(1,128)S(1)} %slice.177), channel_id=1, source_target_pairs={{1,0},{2,1},{3,2},{5,4},{6,5},{7,6},{9,8},{10,9},{11,10},{13,12},{... | collective-permute-start | bytes 12296 | tf_op jit(solution)/shard_map/ppermute | solution.py:14
  584.3 28.5 %collective-permute-start.5 = (f32[1,1024]{1,0:T(1,128)S(1)}, f32[1,1024]{1,0:T(1,128)S(1)}, u32[]{:S(2)}, u32[]{:S(2)}) collective-permute-start(f32[1,1024]{1,0:T(1,128)S(1)} %slice.173), channel_id=1, source_target_pairs={{1,0},{2,1},{3,2},{5,4},{6,5},{7,6},{9,8},{10,9},{11,10},{13,12},{... | collective-permute-start | bytes 12296 | tf_op jit(solution)/shard_map/ppermute | solution.py:14
  588.3 226.8 %reduce-scatter.37.cloned.1.call-start = ((), (), s32[]{:S(2)}) async-start(), calls=%async_computation.32 | async-start | bytes 1310720 | tf_op jit(solution)/shard_map/reduce_scatter | solution.py:459
  612.7 230.7 %reduce-scatter.33.cloned.1.call-start = ((), (), s32[]{:S(2)}) async-start(), calls=%async_computation.30 | async-start | bytes 1310720 | tf_op jit(solution)/shard_map/reduce_scatter | solution.py:459
  616.6 70.7 %copy-start.259 = (bf16[1024]{0:T(1024)(128)(2,1)S(1)}, bf16[1024]{0:T(1024)(128)(2,1)}, u32[]{:S(2)}) copy-start(bf16[1024]{0:T(1024)(128)(2,1)} %add_convert_fusion.24) | copy-start | bytes 6148
  616.6 70.7 %copy-start.260 = (bf16[1024]{0:T(1024)(128)(2,1)S(1)}, bf16[1024]{0:T(1024)(128)(2,1)}, u32[]{:S(2)}) copy-start(bf16[1024]{0:T(1024)(128)(2,1)} %add_convert_fusion.23) | copy-start | bytes 6148
  616.6 70.7 %copy-start.261 = (bf16[1024]{0:T(1024)(128)(2,1)S(1)}, bf16[1024]{0:T(1024)(128)(2,1)}, u32[]{:S(2)}) copy-start(bf16[1024]{0:T(1024)(128)(2,1)} %add_convert_fusion.30) | copy-start | bytes 6148
  616.6 106.0 %copy-start.48 = (f32[128,1024]{1,0:T(8,128)S(1)}, f32[128,1024]{1,0:T(8,128)}, u32[]{:S(2)}) copy-start(f32[128,1024]{1,0:T(8,128)} %copy-done.46) | copy-start | bytes 1572868
  (259 other events, 2831.1 us)
Sparse Core Ops, SparseCore 0:
  10.0 29.4 all-gather.38
  41.4 27.9 all-gather.40
  71.2 27.8 all-gather.36
  100.9 27.8 all-gather.42
  130.6 27.8 all-gather.44
  160.2 54.3 all-gather.46
  216.5 54.3 all-gather.48
  313.3 41.5 reduce-scatter.38
  358.6 45.1 reduce-scatter.26
  406.9 41.1 reduce-scatter.22
  451.8 41.2 reduce-scatter.18
  496.2 41.2 reduce-scatter.14
  541.3 71.3 reduce-scatter.34
  616.0 71.2 reduce-scatter.30
  689.4 15.2 reduce-scatter.40
  706.9 18.3 reduce-scatter.28
  727.5 17.4 reduce-scatter.24
  747.1 17.8 reduce-scatter.20
  767.4 17.9 reduce-scatter.16
  787.5 27.5 reduce-scatter.36
  817.5 25.7 reduce-scatter.32
where the time goes:
time: 865 us; the launch traced here: 852 us
  blocking collectives  325 us (38%)
  waiting for transfers between devices  226 us (26%)
  matrix products  143 us (17%)
  other arithmetic  74.2 us (9%)
  local copies, waits for them, and re-layouts  42.7 us (5%)
  starting transfers between devices  21.7 us (3%)
  between operations  20 us (2%)
    all_gather x12, blocking collectives, entering_2(): everything = jax.tree.map(lambda part: lax.all_gather(part, axis), value)  121 us
    reduce_scatter x7, waiting for transfers between devices, body(): lax.psum_scatter(for_sending(group_total), 'stretch', scatter_dimension=0...  109 us
    reduce_scatter x7, waiting for transfers between devices, body(): lax.psum_scatter(for_sending(summed), 'seg', scatter_dimension=0, tiled=T...  86.9 us
    dot_general x14, matrix products, matmul_tn(): lax.dot_general(left, right, (((0,), (0,)), ((), ())), preferred_element_...  61.1 us
    all_gather x5, blocking collectives, merged(): lax.all_gather(part.astype(kind), axis)  52.4 us
    dot_general x14, matrix products, matmul_nt(): lax.dot_general(left, right, (((1,), (1,)), ((), ())), preferred_element_...  31.5 us
    all_gather x3, blocking collectives, combined_all(): everything = jax.tree.map(lambda part: lax.all_gather(part, axis), value)  30.7 us
    unnamed x2, blocking collectives  28.1 us
  transfers between devices with their start and end apart: 29, of which 8 were waited for; matrix products, arithmetic and copies ran while one was open for 25% of the time, Pallas kernels for 0%

commit v1 on v0

v1 whole, which is shorter than its diff:
```python
import jax
import jax.numpy as jnp
from jax import lax
from jax.sharding import PartitionSpec as P

epsilon = 1e-05
bf16 = jnp.bfloat16
f32 = jnp.float32


def hop(value, bit):
    count = lax.axis_size("seg")
    return lax.ppermute(value, "seg", [(i, i ^ bit) for i in range(count)])


def along(value, steps):
    count = lax.axis_size("stretch")
    first, last = (max(0, -steps), min(count, count - steps))
    return lax.ppermute(value, "stretch", [(i, i + steps) for i in range(first, last)])


def far_bits():
    bits, b = [], 2
    while b < lax.axis_size("seg"):
        bits.append(b)
        b *= 2
    return bits


def gather_pieces(own):
    half = own.shape[0] // 2
    held = {0: [own[:half], own[half:]]}
    whole = {0: own}
    rest = far_bits()
    for b in rest:
        whole[b] = hop(own, b)
        held[b] = [whole[b][:half], whole[b][half:]]
    for m in sorted(range(0, lax.axis_size("seg"), 2), key=lambda m: (bin(m).count("1"), m)):
        if m in held:
            continue
        bits = [b for b in rest if m & b]
        held[m] = [hop(held[m ^ bits[-1]][0], bits[-1]), hop(held[m ^ bits[0]][1], bits[0])]
    out = {}
    for m in sorted(held):
        pieces = [whole[m]] if m in whole else held[m]
        out[m] = pieces
        out[m ^ 1] = [hop(p, 1) for p in pieces]
    return out


def placed(pieces, first, rows, me):
    count = lax.axis_size("seg")
    some = next(iter(pieces.values()))
    buf = jnp.zeros((count * rows, some[0].shape[1]), some[0].dtype)
    for m, parts in pieces.items():
        base = (me ^ m) * rows
        at = 0
        for part in parts:
            lo, hi = max(first, at), min(first + rows, at + part.shape[0])
            if lo < hi:
                buf = lax.dynamic_update_slice_in_dim(
                    buf, part[lo - at : hi - at], base + (lo - first), 0
                )
            at += part.shape[0]
    return buf


def dot_nn(a, b):
    return jnp.dot(a, b, preferred_element_type=f32)


def dot_nt(a, b):
    return lax.dot_general(a, b, (((1,), (1,)), ((), ())), preferred_element_type=f32)


def dot_tn(a, b):
    return lax.dot_general(a, b, (((0,), (0,)), ((), ())), preferred_element_type=f32)


def paired(a, axis=0):
    return jnp.concatenate([a, hop(a, 1)], axis=axis)


def group_sum(items, me):
    count = lax.axis_size("seg")
    rest = far_bits()
    evens = list(range(0, count, 2))
    keep = {}
    parts = []
    for x, dy in items:
        w = x.shape[1] // count
        mine, other = [], []
        for m in evens:
            mine.append(lax.dynamic_slice_in_dim(x, (me ^ m) * w, w, 1))
            other.append(lax.dynamic_slice_in_dim(x, (me ^ m ^ 1) * w, w, 1))
        got = hop(jnp.concatenate(other, axis=1), 1)
        cols = {m: jnp.concatenate([mine[i], got[:, i * w : (i + 1) * w]], axis=0)
                for i, m in enumerate(evens)}
        half = dy.shape[1] // 2
        parts.append((cols, [paired(dy[:, :half]), paired(dy[:, half:])]))
    result = []
    for side in range(2):
        order = rest if side == 0 else rest[::-1]
        now = evens
        acc = None
        for b in order:
            send = [m for m in now if m & b]
            stay = [m for m in now if not m & b]
            def term(ms):
                outs = []
                for cols, dys in parts:
                    left = jnp.concatenate([cols[m] for m in ms], axis=1)
                    g = dot_tn(left, dys[side])
                    outs.append(g.reshape(len(ms), -1, dys[side].shape[1]))
                return jnp.concatenate(outs, axis=1) if len(outs) > 1 else outs[0]
            if acc is None:
                out = term(send).astype(bf16)
                kept = term(stay)
            else:
                out = jnp.stack([acc[now.index(m)] for m in send]).astype(bf16)
                kept = jnp.stack([acc[now.index(m)] for m in stay])
            got = hop(out, b)
            acc = kept + got.astype(f32)
            now = stay
        result.append(acc[0].astype(bf16))
    return jnp.concatenate(result, axis=1)


def stretch_sum(part):
    return lax.psum_scatter(part, "stretch", scatter_dimension=0, tiled=True).astype(f32)


def norm(rows):
    centre = rows - jnp.mean(rows, axis=-1, keepdims=True)
    inverse = lax.rsqrt(jnp.mean(centre * centre, axis=-1, keepdims=True) + epsilon)
    return centre * inverse, inverse


def norm_back(d, unit, inverse, gain):
    q = d * gain
    return inverse * (
        q
        - jnp.mean(q, axis=-1, keepdims=True)
        - unit * jnp.mean(q * unit, axis=-1, keepdims=True)
    )


def split(a):
    hi = a.astype(bf16)
    mid = (a - hi.astype(f32)).astype(bf16)
    return hi, mid


def tri(mat, a):
    hi, mid = split(a)
    def one(v):
        return jnp.einsum("ts,bsd->btd", mat, v, preferred_element_type=f32)
    return one(hi) + one(mid)


def body(
    stream_in, cotangent, previous_mix, previous_ffn, state_num, state_den, state_exp,
    gain_one, bias_one, gain_two, bias_two, mix_key, mix_value, mix_recept,
    time_decay, time_first, chan_mix_key, chan_mix_recept,
    att_key, att_value, att_recept, att_output, chan_key, chan_value, chan_recept,
):
    me = lax.axis_index("seg")
    position = lax.axis_index("stretch")
    stretches = lax.axis_size("stretch")
    at_start = position == 0
    batches, _, length, width = stream_in.shape
    tokens = batches * length
    shard = att_key.shape[0]
    fshard = chan_value.shape[0]

    def flat(a):
        return a.reshape(tokens, a.shape[-1])

    def cube(a):
        return a.reshape(batches, length, a.shape[-1])

    vecs = lax.all_gather(
        jnp.stack([gain_one, bias_one, gain_two, bias_two, mix_key, mix_value, mix_recept,
                   time_decay, time_first, chan_mix_key, chan_mix_recept]),
        "seg", axis=1, tiled=True).astype(f32)
    (g1, b1, g2, b2, mk, mv, mr, decay, first, cmk, cmr) = [vecs[i] for i in range(11)]

    stream = stream_in[:, 0].astype(f32)
    last_in = along(stream_in[:, 0, length - 1], 1)

    p_kvr = gather_pieces(jnp.concatenate([att_key, att_value, att_recept], axis=0))
    p_or = gather_pieces(jnp.concatenate([att_output, chan_recept], axis=0))
    p_ck = gather_pieces(chan_key)
    p_cv = gather_pieces(chan_value)
    w_k = placed(p_kvr, 0, shard, me)
    w_v = placed(p_kvr, shard, shard, me)
    w_r = placed(p_kvr, 2 * shard, shard, me)
    w_o = placed(p_or, 0, shard, me)
    w_c = placed(p_or, shard, shard, me)
    w_ck = placed(p_ck, 0, shard, me)
    w_cv = placed(p_cv, 0, fshard, me)

    na, inv_a = norm(stream)
    xa = na * g1 + b1
    edge_unit, _ = norm(last_in.astype(f32))
    entry = jnp.where(at_start, previous_mix[:, 0], edge_unit * g1 + b1)
    xs = jnp.concatenate([entry[:, None], xa[:, :-1]], axis=1)

    def mixed(a, shifted, mix):
        return flat((a * mix + shifted * (1.0 - mix)).astype(bf16))

    key_in, value_in, recept_in = mixed(xa, xs, mk), mixed(xa, xs, mv), mixed(xa, xs, mr)
    keys = cube(dot_nn(key_in, w_k))
    vals = cube(dot_nn(value_in, w_v))
    recs = cube(dot_nn(recept_in, w_r))

    rate = -jnp.exp(decay)
    span = rate * length
    places = lax.broadcasted_iota(jnp.int32, (length, 1), 0).astype(f32)
    row = lax.broadcasted_iota(jnp.int32, (length, length), 0)
    col = lax.broadcasted_iota(jnp.int32, (length, length), 1)
    lower = (col < row).astype(bf16)
    upper = (col > row).astype(bf16)
    shifted = keys - places * rate
    peak = jnp.max(shifted, axis=1, keepdims=True)
    factor = jnp.exp(shifted - peak)
    fv = factor * vals
    sum_num, sum_den = jnp.sum(fv, axis=1), jnp.sum(factor, axis=1)
    sum_exp = peak[:, 0] + (length - 1.0) * rate
    everyone = lax.all_gather(jnp.stack([sum_num, sum_den, sum_exp]), "stretch")

    def merge(upto):
        ids = jnp.arange(stretches)[:, None, None]
        gaps = (upto - 1 - ids).astype(f32)
        used = ids < upto
        logit = jnp.where(used, everyone[:, 2] + gaps * span, -jnp.inf)
        opening = state_exp[:, 0] + upto * span
        top = jnp.maximum(opening, jnp.max(logit, axis=0))
        weight = jnp.exp(logit - top)
        start = jnp.exp(opening - top)
        return (
            state_num[:, 0] * start + jnp.sum(weight * everyone[:, 0], axis=0),
            state_den[:, 0] * start + jnp.sum(weight * everyone[:, 1], axis=0),
            top,
        )

    ent_num, ent_den, ent_exp = merge(position)
    fin_num, fin_den, fin_exp = merge(jnp.int32(stretches))
    final_mean = (fin_num / fin_den)[:, None]
    final_log = (fin_exp + jnp.log(fin_den))[:, None]

    cum_num, cum_den = tri(lower, fv), tri(lower, factor)
    near = (places - 1.0) * rate + peak
    opening = places * rate + ent_exp[:, None]
    reward = first + keys
    top = jnp.maximum(jnp.maximum(near, opening), reward)
    p, o, e = jnp.exp(near - top), jnp.exp(opening - top), jnp.exp(reward - top)
    den = cum_den * p + ent_den[:, None] * o + e
    wkv = (cum_num * p + ent_num[:, None] * o + vals * e) / den
    sig = jax.nn.sigmoid(recs)
    gated = flat((sig * wkv).astype(bf16))
    middle = stream + cube(dot_nn(gated, w_o))

    nb, inv_b = norm(middle)
    xb = nb * g2 + b2
    edge_b = along(xb[:, length - 1], 1)
    entry_b = jnp.where(at_start, previous_ffn[:, 0], edge_b)
    xt = jnp.concatenate([entry_b[:, None], xb[:, :-1]], axis=1)
    fkey_in, frec_in = mixed(xb, xt, cmk), mixed(xb, xt, cmr)
    active = jax.nn.relu(dot_nn(fkey_in, w_ck))
    hidden = (active * active).astype(bf16)
    frec = cube(dot_nn(frec_in, w_c))
    fval = cube(dot_nn(hidden, w_cv))
    sigf = jax.nn.sigmoid(frec)
    block_out = (middle + sigf * fval).astype(bf16)[:, None]

    cot = cotangent[:, 0].astype(f32)
    d_fval = flat((cot * sigf).astype(bf16))
    d_frec = flat((cot * fval * sigf * (1.0 - sigf)).astype(bf16))
    d_pre = (dot_nt(d_fval, w_cv) * 2.0 * active).astype(bf16)
    part_cv = group_sum([(hidden, d_fval)], me)
    part_ck = group_sum([(fkey_in, d_pre)], me)
    d_fkey_in = cube(dot_nt(d_pre, w_ck))
    d_frec_in = cube(dot_nt(d_frec, w_c))
    gap_b = xb - xt
    gr_cmk = jnp.sum(d_fkey_in * gap_b, axis=(0, 1))
    gr_cmr = jnp.sum(d_frec_in * gap_b, axis=(0, 1))
    d_xt = d_fkey_in * (1.0 - cmk) + d_frec_in * (1.0 - cmr)
    next_b = along(d_xt[:, 0], -1)
    d_xb = d_fkey_in * cmk + d_frec_in * cmr + jnp.concatenate([d_xt[:, 1:], next_b[:, None]], axis=1)
    gr_g2 = jnp.sum(d_xb * nb, axis=(0, 1))
    gr_b2 = jnp.sum(d_xb, axis=(0, 1))
    d_middle = cot + norm_back(d_xb, nb, inv_b, g2)

    d_branch = flat(d_middle.astype(bf16))
    d_gated = cube(dot_nt(d_branch, w_o))
    d_recs = flat((d_gated * wkv * sig * (1.0 - sig)).astype(bf16))
    part_or = group_sum([(gated, d_branch), (frec_in, d_frec)], me)
    gn = d_gated * sig / den
    gd = -gn * wkv
    direct = e * (gn * vals + gd)
    gr_first = jnp.sum(direct, axis=(0, 1))
    go_n, go_d = gn * o, gd * o
    d_ent_num, d_ent_den = jnp.sum(go_n, axis=1), jnp.sum(go_d, axis=1)
    back = lax.all_gather(jnp.stack([d_ent_num, d_ent_den, ent_exp, d_xt[:, 0]]), "stretch")
    ids = jnp.arange(stretches)[:, None, None]
    lift = jnp.where(ids > position, jnp.exp(jnp.minimum(
        sum_exp - back[:, 2] + (ids - position - 1).astype(f32) * span, 0.0)), 0.0)
    s_num = jnp.sum(back[:, 0] * lift, axis=0)
    s_den = jnp.sum(back[:, 1] * lift, axis=0)
    carry = jnp.where(ids > position, jnp.exp(jnp.minimum(
        ent_exp + (ids - position).astype(f32) * span - back[:, 2], 0.0)), 0.0)
    d_rate = length * jnp.sum(
        ent_num * jnp.sum(back[:, 0] * carry, axis=0) + ent_den * jnp.sum(back[:, 1] * carry, axis=0),
        axis=0)
    raise_0 = jnp.exp(jnp.minimum(state_exp[:, 0] + ids.astype(f32) * span - back[:, 2], 0.0))
    grad_num = jnp.sum(back[:, 0] * raise_0, axis=0)
    grad_den = jnp.sum(back[:, 1] * raise_0, axis=0)
    grad_exp = state_num[:, 0] * grad_num + state_den[:, 0] * grad_den
    grad_previous_ffn = back[0, 3]

    pn, pd = gn * p, gd * p
    rn = tri(upper, pn) + s_num[:, None]
    rd = tri(upper, pd) + s_den[:, None]
    chain = factor * (rn * vals + rd)
    d_keys = flat((chain + direct).astype(bf16))
    d_vals = flat((factor * rn + gn * e).astype(bf16))
    d_rate = d_rate + jnp.sum(
        (places - 1.0) * (pn * cum_num + pd * cum_den)
        + places * (go_n * ent_num[:, None] + go_d * ent_den[:, None])
        - places * chain, axis=(0, 1))
    d_rate = d_rate + (length - 1.0) * jnp.sum(s_num * sum_num + s_den * sum_den, axis=0)
    gr_decay = d_rate * rate

    part_kvr = group_sum([(key_in, d_keys), (value_in, d_vals), (recept_in, d_recs)], me)
    d_key_in = cube(dot_nt(d_keys, w_k))
    d_value_in = cube(dot_nt(d_vals, w_v))
    d_recept_in = cube(dot_nt(d_recs, w_r))
    gap_a = xa - xs
    gr_mk = jnp.sum(d_key_in * gap_a, axis=(0, 1))
    gr_mv = jnp.sum(d_value_in * gap_a, axis=(0, 1))
    gr_mr = jnp.sum(d_recept_in * gap_a, axis=(0, 1))
    d_xs = d_key_in * (1.0 - mk) + d_value_in * (1.0 - mv) + d_recept_in * (1.0 - mr)
    heads = lax.all_gather(d_xs[:, 0], "stretch")
    grad_previous_mix = heads[0]
    next_a = jnp.where(position == stretches - 1, 0.0,
                       heads[jnp.minimum(position + 1, stretches - 1)])
    d_xa = (d_key_in * mk + d_value_in * mv + d_recept_in * mr
            + jnp.concatenate([d_xs[:, 1:], next_a[:, None]], axis=1))
    gr_g1 = jnp.sum(d_xa * na, axis=(0, 1))
    gr_b1 = jnp.sum(d_xa, axis=(0, 1))
    grad_stream = (d_middle + norm_back(d_xa, na, inv_a, g1)).astype(bf16)[:, None]

    out_cv = stretch_sum(part_cv)
    out_ck = stretch_sum(part_ck)
    out_or = [stretch_sum(part_or[:shard]), stretch_sum(part_or[shard:])]
    out_kvr = [stretch_sum(part_kvr[i * shard : (i + 1) * shard]) for i in range(3)]

    small = jnp.stack([gr_g1, gr_b1, gr_g2, gr_b2, gr_mk, gr_mv, gr_mr, gr_decay, gr_first,
                       gr_cmk, gr_cmr])
    small = lax.psum_scatter(small, "seg", scatter_dimension=1, tiled=True)
    small = lax.psum_scatter(small, "stretch", scatter_dimension=1, tiled=True)

    return (
        block_out, grad_stream, *[small[i] for i in range(11)],
        out_kvr[0], out_kvr[1], out_kvr[2], out_or[0], out_ck, out_cv, out_or[1],
        grad_num[:, None], grad_den[:, None], grad_exp[:, None],
        grad_previous_mix[:, None], grad_previous_ffn[:, None], final_mean, final_log,
    )


def solution(mesh):
    rows = P(None, "seg", "stretch", None)
    state = P(None, "seg", None)
    both = P(("seg", "stretch"))
    wide = P(("seg", "stretch"), None)
    return jax.shard_map(
        body,
        mesh=mesh,
        in_specs=(rows,) * 2 + (state,) * 5 + (P("seg"),) * 11 + (P("seg", None),) * 7,
        out_specs=(rows,) * 2 + (both,) * 11 + (wide,) * 7 + (state,) * 7,
        check_vma=False,
    )
```

time: 865 us -> 629 us (0.73)
  the two profiles are of different devices: /device:TPU:9 before, /device:TPU:0 now
where the time goes in v1:
time: 629 us; the launch traced here: 618 us
  waiting for transfers between devices  212 us (34%)
  local copies, waits for them, and re-layouts  117 us (19%)
  matrix products  90.8 us (14%)
  other arithmetic  75.7 us (12%)
  blocking collectives  53.5 us (9%)
  starting transfers between devices  51.8 us (8%)
  between operations  17.5 us (3%)
    ppermute x73, waiting for transfers between devices, hop(): return lax.ppermute(value, 'seg', [(i, i ^ bit) for i in range(count)])  147 us
    dynamic_update_slice x44, local copies, waits for them, and re-layouts, placed(): lax.dynamic_update_slice_in_dim(buf, part[lo - at:hi - at], base + (lo -...  45.1 us
    ppermute x73, starting transfers between devices, hop(): return lax.ppermute(value, 'seg', [(i, i ^ bit) for i in range(count)])  42.8 us
    dot_general x28, matrix products, dot_tn(): lax.dot_general(a, b, (((0,), (0,)), ((), ())), preferred_element_type=f32)  38.7 us
    reduce_scatter x7, waiting for transfers between devices, stretch_sum(): lax.psum_scatter(part, 'stretch', scatter_dimension=0, tiled=True)  33.3 us
    reduce_scatter x1, waiting for transfers between devices, body(): small = lax.psum_scatter(small, 'seg', scatter_dimension=1, tiled=True)  31.5 us
    dot_general x7, matrix products, dot_nn(): return jnp.dot(a, b, preferred_element_type=f32)  26.4 us
    dot_general x7, matrix products, dot_nt(): lax.dot_general(a, b, (((1,), (1,)), ((), ())), preferred_element_type=f32)  22.9 us
  transfers between devices with their start and end apart: 85, of which 26 were waited for; matrix products, arithmetic and copies ran while one was open for 38% of the time, Pallas kernels for 0%

profile of v1, /device:TPU:0, one launch (start us, length us, event | category | flops | bytes accessed | tf_op | source)
XLA Modules:
  0.0 618.2 jit_solution(11225748374694081169)
XLA Ops:
  12.3 2.9 collective-permute-start.11
  15.3 3.5 collective-permute-start
  20.4 11.2 %all_gather.18 = bf16[11,1024]{1,0:T(8,128)(2,1)S(1)} all-gather(bf16[11,128]{1,0:T(8,128)(2,1)S(1)} %stack.101), channel_id=1, replica_groups=mesh['seg'=8,'stretch'=4] {'seg'}, dimensions={1}, use_global_device_ids=true | all-gather | bytes 25344 | tf_op jit(solution)/shard_map/all_gather | solution.py:182
  33.4 4.3 broadcast_in_dim.53
  37.7 2.3 constant_dynamic-update-slice_fusion.19
  48.3 4.3 broadcast_in_dim.54
  65.0 1.9 slice_dynamic-update-slice_fusion.3
  68.4 1.9 slice_dynamic-update-slice_fusion.2
  71.6 11.2 %collective-permute-done.2 = bf16[384,1024]{1,0:T(8,128)(2,1)S(1)} collective-permute-done((bf16[384,1024]{1,0:T(8,128)(2,1)}, bf16[384,1024]{1,0:T(8,128)(2,1)S(1)}, u32[]{:S(2)}, u32[]{:S(2)}) %collective-permute-start.2) | collective-permute-done | bytes 786464 | tf_op jit(solution)/shard_map/ppermute | solution.py:13
  85.7 2.3 constant_dynamic-update-slice_fusion.18
  88.0 8.3 %collective-permute-done.13 = bf16[256,1024]{1,0:T(8,128)(2,1)S(1)} collective-permute-done((bf16[256,1024]{1,0:T(8,128)(2,1)}, bf16[256,1024]{1,0:T(8,128)(2,1)S(1)}, u32[]{:S(2)}, u32[]{:S(2)}) %collective-permute-start.13) | collective-permute-done | bytes 524320 | tf_op jit(solution)/shard_map/ppermute | solution.py:13
  98.6 24.9 %collective-permute-done.15 = bf16[128,1024]{1,0:T(8,128)(2,1)S(1)} collective-permute-done((bf16[128,1024]{1,0:T(8,128)(2,1)S(1)}, bf16[128,1024]{1,0:T(8,128)(2,1)S(1)}, u32[]{:S(2)}, u32[]{:S(2)}) %collective-permute-start.15) | collective-permute-done | bytes 262176 | tf_op jit(solution)/shard_map/ppermute | solution.py:13
  125.5 2.3 constant_dynamic-update-slice_fusion.17
  132.2 1.9 slice.633
  134.9 12.9 %collective-permute-done.32 = bf16[512,1024]{1,0:T(8,128)(2,1)S(1)} collective-permute-done((bf16[512,1024]{1,0:T(8,128)(2,1)S(1)}, bf16[512,1024]{1,0:T(8,128)(2,1)S(1)}, u32[]{:S(2)}, u32[]{:S(2)}) %collective-permute-start.32) | collective-permute-done | bytes 1048608 | tf_op jit(solution)/shard_map/ppermute | solution.py:13
  153.6 2.2 constant_dynamic-update-slice_fusion.7
  159.6 4.6 collective-permute-done.6
  165.5 2.1 collective-permute-done.9
  171.4 2.5 multiply_reduce_fusion.22
  173.9 13.8 %all-gather = f32[12,2,1024]{2,1,0:T(2,128)S(1)} all-gather(f32[3,2,1024]{2,1,0:T(2,128)S(1)} %pad_maximum_fusion.102), channel_id=2, replica_groups=mesh['seg'=8,'stretch'=4] {'stretch'}, dimensions={0}, use_global_device_ids=true | all-gather | bytes 122880 | tf_op jit(solution)/shard_map/all_gather | solution.py:230
  192.0 5.6 multiply_convert_fusion.2
  199.2 2.4 fusion.353
  203.8 3.4 collective-permute-start.17
  209.0 3.2 add_convert_fusion.3
  219.3 2.3 constant_dynamic-update-slice_fusion.16
  223.2 2.3 constant_dynamic-update-slice_fusion.6
  227.7 2.7 collective-permute-done.25
  231.8 9.2 %collective-permute-done.34 = bf16[256,1024]{1,0:T(8,128)(2,1)S(1)} collective-permute-done((bf16[256,1024]{1,0:T(8,128)(2,1)S(1)}, bf16[256,1024]{1,0:T(8,128)(2,1)S(1)}, u32[]{:S(2)}, u32[]{:S(2)}) %collective-permute-start.34) | collective-permute-done | bytes 524320 | tf_op jit(solution)/shard_map/ppermute | solution.py:13
  245.2 1.9 constant_dynamic-update-slice_fusion.12
  250.4 5.8 multiply_convert_fusion
  257.1 5.8 fusion.358
  262.8 3.5 fusion.65
  266.3 5.8 fusion.1
  272.2 5.7 fusion.359
  280.3 2.5 fusion.2
  282.8 7.0 %multiply_reduce_fusion = (f32[1024]{0:T(1024)}, f32[1024]{0:T(1024)}, f32[2,128,1024]{2,0,1:T(2,128)S(1)}) fusion(f32[2,128,1024]{2,1,0:T(8,128)S(1)} %fusion.2, f32[2,127,1024]{2,0,1:T(2,128)S(1)} %slice.626, f32[2,1,1024]{2,0,1:T(2,128)S(1)} %fusion.284, f32[2,128,1024]{2,1,0:T(8,128)S(1)} %bitcast.521, f32[1024]{0:T(1024)S(1)} %copy-done.179, ...), kind=kLoop, calls=%fused_computation.157 | loop fusion | flops 3405824 | bytes 5269504 | tf_op jit(solution)/shard_map/reduce_sum | solution.py:287
  295.5 5.2 multiply_reduce_fusion.5
  303.3 3.5 fusion.329
  308.0 14.7 %all-gather.1 = f32[16,2,1024]{2,1,0:T(2,128)S(1)} all-gather(f32[4,2,1024]{2,1,0:T(2,128)S(1)} %pad_maximum_fusion.101), channel_id=3, replica_groups=mesh['seg'=8,'stretch'=4] {'stretch'}, dimensions={0}, use_global_device_ids=true | all-gather | bytes 163840 | tf_op jit(solution)/shard_map/all_gather | solution.py:305
  325.8 2.2 subtract_reduce_fusion
  330.3 3.9 multiply_add_fusion
  337.8 13.8 %all-gather.2 = f32[8,1,1024]{2,1,0:T(1,128)} all-gather(f32[2,1,1024]{2,1,0:T(1,128)S(1)} %slice.643), channel_id=4, replica_groups=mesh['seg'=8,'stretch'=4] {'stretch'}, dimensions={0}, use_global_device_ids=true | all-gather | bytes 40960 | tf_op jit(solution)/shard_map/all_gather | solution.py:344
  356.1 4.7 fusion.112
  360.8 2.8 stack.118
  363.7 31.5 %reduce-scatter.12.cloned.1.call-done = f32[11,128]{1,0:T(8,128)} async-done(((f32[11,1024]{1,0:T(8,128)}), f32[11,128]{1,0:T(8,128)}) %reduce-scatter.12.cloned.1.call-update) | async-done | bytes 5648 | tf_op jit(solution)/shard_map/reduce_scatter | solution.py:361
  418.2 8.6 %collective-permute-done.56 = bf16[2,256,512]{2,1,0:T(8,128)(2,1)S(1)} collective-permute-done((bf16[2,256,512]{2,1,0:T(8,128)(2,1)S(1)}, bf16[2,256,512]{2,1,0:T(8,128)(2,1)S(1)}, u32[]{:S(2)}, u32[]{:S(2)}) %collective-permute-start.56) | collective-permute-done | bytes 524320 | tf_op jit(solution)/shard_map/ppermute | solution.py:13
  432.3 3.2 convolution_convert_fusion.1
  438.1 13.4 %collective-permute-done.61 = bf16[1,256,512]{2,1,0:T(8,128)(2,1)S(1)} collective-permute-done((bf16[1,256,512]{2,1,0:T(8,128)(2,1)S(1)}, bf16[1,256,512]{2,1,0:T(8,128)(2,1)S(1)}, u32[]{:S(2)}, u32[]{:S(2)}) %collective-permute-start.61) | collective-permute-done | bytes 262176 | tf_op jit(solution)/shard_map/ppermute | solution.py:13
  453.4 2.0 maximum_add_fusion
  460.6 3.2 convolution_convert_fusion
  463.9 4.0 collective-permute-done.46
  474.3 2.0 fusion.337
  476.4 3.0 convolution_convert_fusion.3
  480.8 3.7 fusion.50
  484.5 3.6 fusion.49
  488.4 6.5 %collective-permute-done.64 = bf16[2,128,2048]{2,1,0:T(8,128)(2,1)S(1)} collective-permute-done((bf16[2,128,2048]{2,1,0:T(8,128)(2,1)}, bf16[2,128,2048]{2,1,0:T(8,128)(2,1)S(1)}, u32[]{:S(2)}, u32[]{:S(2)}) %collective-permute-start.64) | collective-permute-done | bytes 1048608 | tf_op jit(solution)/shard_map/ppermute | solution.py:13
  495.9 2.3 convert_add_fusion.3
  503.0 2.8 convolution_convert_fusion.2
  507.3 6.0 collective-permute-done.65
  514.5 13.3 %collective-permute-done.68 = bf16[1,128,2048]{2,1,0:T(8,128)(2,1)} collective-permute-done((bf16[1,128,2048]{2,1,0:T(8,128)(2,1)}, bf16[1,128,2048]{2,1,0:T(8,128)(2,1)}, u32[]{:S(2)}, u32[]{:S(2)}) %collective-permute-start.68) | collective-permute-done | bytes 524320 | tf_op jit(solution)/shard_map/ppermute | solution.py:13
  539.5 9.3 %collective-permute-done.72 = bf16[1,512,512]{2,1,0:T(8,128)(2,1)S(1)} collective-permute-done((bf16[1,512,512]{2,1,0:T(8,128)(2,1)S(1)}, bf16[1,512,512]{2,1,0:T(8,128)(2,1)S(1)}, u32[]{:S(2)}, u32[]{:S(2)}) %collective-permute-start.72) | collective-permute-done | bytes 524320 | tf_op jit(solution)/shard_map/ppermute | solution.py:13
  549.0 2.3 collective-permute-done.75
  574.3 7.0 %reduce-scatter.22.cloned.1.call-done = bf16[32,4096]{1,0:T(8,128)(2,1)} async-done(((bf16[128,4096]{1,0:T(8,128)(2,1)}), bf16[32,4096]{1,0:T(8,128)(2,1)}) %reduce-scatter.22.cloned.1.call-update) | async-done | bytes 262160 | tf_op jit(solution)/shard_map/reduce_scatter | solution.py:130
  583.1 26.3 %reduce-scatter.24.cloned.1.call-done = bf16[128,1024]{1,0:T(8,128)(2,1)} async-done(((bf16[512,1024]{1,0:T(8,128)(2,1)}), bf16[128,1024]{1,0:T(8,128)(2,1)}) %reduce-scatter.24.cloned.1.call-update) | async-done | bytes 262160 | tf_op jit(solution)/shard_map/reduce_scatter | solution.py:130
  (823 shorter events, 205.6 us)
Async XLA Ops:
  7.2 388.1 %reduce-scatter.12.cloned.1.call-start = ((), (), s32[]{:S(2)}) async-start(), calls=%async_computation.9 | async-start | bytes 73728 | tf_op jit(solution)/shard_map/reduce_scatter | solution.py:361
  12.3 54.5 %collective-permute-start.11 = (bf16[256,1024]{1,0:T(8,128)(2,1)}, bf16[256,1024]{1,0:T(8,128)(2,1)}, u32[]{:S(2)}, u32[]{:S(2)}) collective-permute-start(bf16[256,1024]{1,0:T(8,128)(2,1)} %get-tuple-element.388), channel_id=1, source_target_pairs={{0,8},{4,12},{8,0},{12,4},{16,24},{20,28},{24,16},{28,20},{1,9},{5... | collective-permute-start | bytes 1572872 | tf_op jit(solution)/shard_map/ppermute | solution.py:13
  15.2 49.2 %collective-permute-start.10 = (bf16[256,1024]{1,0:T(8,128)(2,1)}, bf16[256,1024]{1,0:T(8,128)(2,1)}, u32[]{:S(2)}, u32[]{:S(2)}) collective-permute-start(bf16[256,1024]{1,0:T(8,128)(2,1)} %get-tuple-element.388), channel_id=1, source_target_pairs={{0,4},{4,0},{8,12},{12,8},{16,20},{20,16},{24,28},{28,24},{1,5},{5... | collective-permute-start | bytes 1572872 | tf_op jit(solution)/shard_map/ppermute | solution.py:13
  15.3 39.1 %collective-permute-start = (bf16[2,1024]{1,0:T(2,128)(2,1)S(1)}, bf16[2,1024]{1,0:T(2,128)(2,1)S(1)}, u32[]{:S(2)}, u32[]{:S(2)}) collective-permute-start(bf16[2,1024]{1,0:T(2,128)(2,1)S(1)} %bitcast.630), channel_id=1, source_target_pairs={{0,1},{1,2},{2,3},{4,5},{5,6},{6,7},{8,9},{9,10},{10,11},{12,13},{... | collective-permute-start | bytes 12296 | tf_op jit(solution)/shard_map/ppermute | solution.py:19
  18.8 66.8 %collective-permute-start.20 = (bf16[128,4096]{1,0:T(8,128)(2,1)}, bf16[128,4096]{1,0:T(8,128)(2,1)}, u32[]{:S(2)}, u32[]{:S(2)}) collective-permute-start(bf16[128,4096]{1,0:T(8,128)(2,1)} %param.47), channel_id=1, source_target_pairs={{0,4},{4,0},{8,12},{12,8},{16,20},{20,16},{24,28},{28,24},{1,5},{5... | collective-permute-start | bytes 3145736 | tf_op jit(solution)/shard_map/ppermute | solution.py:13
  62.3 20.6 %collective-permute-start.2 = (bf16[384,1024]{1,0:T(8,128)(2,1)}, bf16[384,1024]{1,0:T(8,128)(2,1)S(1)}, u32[]{:S(2)}, u32[]{:S(2)}) collective-permute-start(bf16[384,1024]{1,0:T(8,128)(2,1)} %get-tuple-element.395), channel_id=1, source_target_pairs={{0,8},{4,12},{8,0},{12,4},{16,24},{20,28},{24,16},{28,20},{1,9},{5... | collective-permute-start | bytes 2359304 | tf_op jit(solution)/shard_map/ppermute | solution.py:13
  64.5 20.6 %collective-permute-start.4 = (bf16[384,1024]{1,0:T(8,128)(2,1)}, bf16[384,1024]{1,0:T(8,128)(2,1)S(1)}, u32[]{:S(2)}, u32[]{:S(2)}) collective-permute-start(bf16[384,1024]{1,0:T(8,128)(2,1)} %get-tuple-element.395), channel_id=1, source_target_pairs={{0,16},{4,20},{8,24},{12,28},{16,0},{20,4},{24,8},{28,12},{1,17},{... | collective-permute-start | bytes 2359304 | tf_op jit(solution)/shard_map/ppermute | solution.py:13
  66.8 57.2 %collective-permute-start.21 = (bf16[128,4096]{1,0:T(8,128)(2,1)}, bf16[128,4096]{1,0:T(8,128)(2,1)}, u32[]{:S(2)}, u32[]{:S(2)}) collective-permute-start(bf16[128,4096]{1,0:T(8,128)(2,1)} %param.47), channel_id=1, source_target_pairs={{0,8},{4,12},{8,0},{12,4},{16,24},{20,28},{24,16},{28,20},{1,9},{5... | collective-permute-start | bytes 3145736 | tf_op jit(solution)/shard_map/ppermute | solution.py:13
  70.3 26.0 %collective-permute-start.13 = (bf16[256,1024]{1,0:T(8,128)(2,1)}, bf16[256,1024]{1,0:T(8,128)(2,1)S(1)}, u32[]{:S(2)}, u32[]{:S(2)}) collective-permute-start(bf16[256,1024]{1,0:T(8,128)(2,1)} %get-tuple-element.388), channel_id=1, source_target_pairs={{0,16},{4,20},{8,24},{12,28},{16,0},{20,4},{24,8},{28,12},{1,17},{... | collective-permute-start | bytes 1572872 | tf_op jit(solution)/shard_map/ppermute | solution.py:13
  82.8 14.0 %collective-permute-start.12 = (bf16[256,1024]{1,0:T(8,128)(2,1)}, bf16[256,1024]{1,0:T(8,128)(2,1)S(1)}, u32[]{:S(2)}, u32[]{:S(2)}) collective-permute-start(bf16[256,1024]{1,0:T(8,128)(2,1)} %collective-permute-done.11), channel_id=1, source_target_pairs={{0,4},{4,0},{8,12},{12,8},{16,20},{20,16},{24,28},{28,24},{1,5},{5... | collective-permute-start | bytes 1572872 | tf_op jit(solution)/shard_map/ppermute | solution.py:13
  85.1 45.2 %collective-permute-start.23 = (bf16[128,4096]{1,0:T(8,128)(2,1)}, bf16[128,4096]{1,0:T(8,128)(2,1)S(1)}, u32[]{:S(2)}, u32[]{:S(2)}) collective-permute-start(bf16[128,4096]{1,0:T(8,128)(2,1)} %param.47), channel_id=1, source_target_pairs={{0,16},{4,20},{8,24},{12,28},{16,0},{20,4},{24,8},{28,12},{1,17},{... | collective-permute-start | bytes 3145736 | tf_op jit(solution)/shard_map/ppermute | solution.py:13
  85.6 42.2 %collective-permute-start.29 = (bf16[512,1024]{1,0:T(8,128)(2,1)S(1)}, bf16[512,1024]{1,0:T(8,128)(2,1)S(1)}, u32[]{:S(2)}, u32[]{:S(2)}) collective-permute-start(bf16[512,1024]{1,0:T(8,128)(2,1)S(1)} %copy-done.36), channel_id=1, source_target_pairs={{0,4},{4,0},{8,12},{12,8},{16,20},{20,16},{24,28},{28,24},{1,5},{5... | collective-permute-start | bytes 3145736 | tf_op jit(solution)/shard_map/ppermute | solution.py:13
  96.3 27.2 %collective-permute-start.15 = (bf16[128,1024]{1,0:T(8,128)(2,1)S(1)}, bf16[128,1024]{1,0:T(8,128)(2,1)S(1)}, u32[]{:S(2)}, u32[]{:S(2)}) collective-permute-start(bf16[128,1024]{1,0:T(8,128)(2,1)S(1)} %get-tuple-element.359), channel_id=1, source_target_pairs={{0,16},{4,20},{8,24},{12,28},{16,0},{20,4},{24,8},{28,12},{1,17},{... | collective-permute-start | bytes 786440 | tf_op jit(solution)/shard_map/ppermute | solution.py:13
  96.8 31.0 %collective-permute-start.14 = (bf16[256,1024]{1,0:T(8,128)(2,1)S(1)}, bf16[256,1024]{1,0:T(8,128)(2,1)S(1)}, u32[]{:S(2)}, u32[]{:S(2)}) collective-permute-start(bf16[256,1024]{1,0:T(8,128)(2,1)S(1)} %collective-permute-done.13), channel_id=1, source_target_pairs={{0,4},{4,0},{8,12},{12,8},{16,20},{20,16},{24,28},{28,24},{1,5},{5... | collective-permute-start | bytes 1572872 | tf_op jit(solution)/shard_map/ppermute | solution.py:13
  123.5 24.3 %collective-permute-start.32 = (bf16[512,1024]{1,0:T(8,128)(2,1)S(1)}, bf16[512,1024]{1,0:T(8,128)(2,1)S(1)}, u32[]{:S(2)}, u32[]{:S(2)}) collective-permute-start(bf16[512,1024]{1,0:T(8,128)(2,1)S(1)} %copy-done.36), channel_id=1, source_target_pairs={{0,16},{4,20},{8,24},{12,28},{16,0},{20,4},{24,8},{28,12},{1,17},{... | collective-permute-start | bytes 3145736 | tf_op jit(solution)/shard_map/ppermute | solution.py:13
  124.0 26.2 %collective-permute-start.30 = (bf16[512,1024]{1,0:T(8,128)(2,1)S(1)}, bf16[512,1024]{1,0:T(8,128)(2,1)}, u32[]{:S(2)}, u32[]{:S(2)}) collective-permute-start(bf16[512,1024]{1,0:T(8,128)(2,1)S(1)} %copy-done.36), channel_id=1, source_target_pairs={{0,8},{4,12},{8,0},{12,4},{16,24},{20,28},{24,16},{28,20},{1,9},{5... | collective-permute-start | bytes 3145736 | tf_op jit(solution)/shard_map/ppermute | solution.py:13
  127.9 30.1 %collective-permute-start.3 = (bf16[384,1024]{1,0:T(8,128)(2,1)S(1)}, bf16[384,1024]{1,0:T(8,128)(2,1)S(1)}, u32[]{:S(2)}, u32[]{:S(2)}) collective-permute-start(bf16[384,1024]{1,0:T(8,128)(2,1)S(1)} %collective-permute-done.2), channel_id=1, source_target_pairs={{0,4},{4,0},{8,12},{12,8},{16,20},{20,16},{24,28},{28,24},{1,5},{5... | collective-permute-start | bytes 2359304 | tf_op jit(solution)/shard_map/ppermute | solution.py:13
  130.2 25.6 %collective-permute-start.18 = (bf16[128,1024]{1,0:T(8,128)(2,1)S(1)}, bf16[128,1024]{1,0:T(8,128)(2,1)S(1)}, u32[]{:S(2)}, u32[]{:S(2)}) collective-permute-start(bf16[128,1024]{1,0:T(8,128)(2,1)S(1)} %get-tuple-element.351), channel_id=1, source_target_pairs={{0,8},{4,12},{8,0},{12,4},{16,24},{20,28},{24,16},{28,20},{1,9},{5... | collective-permute-start | bytes 786440 | tf_op jit(solution)/shard_map/ppermute | solution.py:13
  131.5 33.2 %collective-permute-start.5 = (bf16[384,1024]{1,0:T(8,128)(2,1)S(1)}, bf16[384,1024]{1,0:T(8,128)(2,1)S(1)}, u32[]{:S(2)}, u32[]{:S(2)}) collective-permute-start(bf16[384,1024]{1,0:T(8,128)(2,1)S(1)} %collective-permute-done.4), channel_id=1, source_target_pairs={{0,4},{4,0},{8,12},{12,8},{16,20},{20,16},{24,28},{28,24},{1,5},{5... | collective-permute-start | bytes 2359304 | tf_op jit(solution)/shard_map/ppermute | solution.py:13
  147.8 16.3 %collective-permute-start.6 = (bf16[192,1024]{1,0:T(8,128)(2,1)S(1)}, bf16[192,1024]{1,0:T(8,128)(2,1)S(1)}, u32[]{:S(2)}, u32[]{:S(2)}) collective-permute-start(bf16[192,1024]{1,0:T(8,128)(2,1)S(1)} %slice.590), channel_id=1, source_target_pairs={{0,8},{4,12},{8,0},{12,4},{16,24},{20,28},{24,16},{28,20},{1,9},{5... | collective-permute-start | bytes 1179656 | tf_op jit(solution)/shard_map/ppermute | solution.py:13
  150.2 13.9 %collective-permute-start.8 = (bf16[192,1024]{1,0:T(8,128)(2,1)S(1)}, bf16[192,1024]{1,0:T(8,128)(2,1)S(1)}, u32[]{:S(2)}, u32[]{:S(2)}) collective-permute-start(bf16[192,1024]{1,0:T(8,128)(2,1)S(1)} %slice.599), channel_id=1, source_target_pairs={{0,16},{4,20},{8,24},{12,28},{16,0},{20,4},{24,8},{28,12},{1,17},{... | collective-permute-start | bytes 1179656 | tf_op jit(solution)/shard_map/ppermute | solution.py:13
  155.9 70.7 %collective-permute-start.26 = (bf16[64,4096]{1,0:T(8,128)(2,1)}, bf16[64,4096]{1,0:T(8,128)(2,1)}, u32[]{:S(2)}, u32[]{:S(2)}) collective-permute-start(bf16[64,4096]{1,0:T(8,128)(2,1)} %slice.634), channel_id=1, source_target_pairs={{0,8},{4,12},{8,0},{12,4},{16,24},{20,28},{24,16},{28,20},{1,9},{5... | collective-permute-start | bytes 1572872 | tf_op jit(solution)/shard_map/ppermute | solution.py:13
  158.0 61.3 %collective-permute-start.22 = (bf16[128,4096]{1,0:T(8,128)(2,1)}, bf16[128,4096]{1,0:T(8,128)(2,1)}, u32[]{:S(2)}, u32[]{:S(2)}) collective-permute-start(bf16[128,4096]{1,0:T(8,128)(2,1)} %collective-permute-done.21), channel_id=1, source_target_pairs={{0,4},{4,0},{8,12},{12,8},{16,20},{20,16},{24,28},{28,24},{1,5},{5... | collective-permute-start | bytes 3145736 | tf_op jit(solution)/shard_map/ppermute | solution.py:13
  164.2 57.5 %collective-permute-start.31 = (bf16[512,1024]{1,0:T(8,128)(2,1)}, bf16[512,1024]{1,0:T(8,128)(2,1)}, u32[]{:S(2)}, u32[]{:S(2)}) collective-permute-start(bf16[512,1024]{1,0:T(8,128)(2,1)} %collective-permute-done.30), channel_id=1, source_target_pairs={{0,4},{4,0},{8,12},{12,8},{16,20},{20,16},{24,28},{28,24},{1,5},{5... | collective-permute-start | bytes 3145736 | tf_op jit(solution)/shard_map/ppermute | solution.py:13
  167.6 36.1 %collective-permute-start.19 = (bf16[128,1024]{1,0:T(8,128)(2,1)S(1)}, bf16[128,1024]{1,0:T(8,128)(2,1)}, u32[]{:S(2)}, u32[]{:S(2)}) collective-permute-start(bf16[128,1024]{1,0:T(8,128)(2,1)S(1)} %collective-permute-done.18), channel_id=1, source_target_pairs={{0,4},{4,0},{8,12},{12,8},{16,20},{20,16},{24,28},{28,24},{1,5},{5... | collective-permute-start | bytes 786440 | tf_op jit(solution)/shard_map/ppermute | solution.py:13
  199.2 15.3 %collective-permute-start.52 = (bf16[256,512]{1,0:T(8,128)(2,1)}, bf16[256,512]{1,0:T(8,128)(2,1)S(1)}, u32[]{:S(2)}, u32[]{:S(2)}) collective-permute-start(bf16[256,512]{1,0:T(8,128)(2,1)} %pad_maximum_fusion.68), channel_id=1, source_target_pairs={{0,4},{4,0},{8,12},{12,8},{16,20},{20,16},{24,28},{28,24},{1,5},{5... | collective-permute-start | bytes 786440 | tf_op jit(solution)/shard_map/ppermute | solution.py:13
  215.6 14.8 %collective-permute-start.25 = (bf16[64,4096]{1,0:T(8,128)(2,1)S(1)}, bf16[64,4096]{1,0:T(8,128)(2,1)S(1)}, u32[]{:S(2)}, u32[]{:S(2)}) collective-permute-start(bf16[64,4096]{1,0:T(8,128)(2,1)S(1)} %copy-done.42), channel_id=1, source_target_pairs={{0,16},{4,20},{8,24},{12,28},{16,0},{20,4},{24,8},{28,12},{1,17},{... | collective-permute-start | bytes 1572872 | tf_op jit(solution)/shard_map/ppermute | solution.py:13
  218.0 13.8 %collective-permute-start.35 = (bf16[256,1024]{1,0:T(8,128)(2,1)S(1)}, bf16[256,1024]{1,0:T(8,128)(2,1)S(1)}, u32[]{:S(2)}, u32[]{:S(2)}) collective-permute-start(bf16[256,1024]{1,0:T(8,128)(2,1)S(1)} %copy-done.43), channel_id=1, source_target_pairs={{0,8},{4,12},{8,0},{12,4},{16,24},{20,28},{24,16},{28,20},{1,9},{5... | collective-permute-start | bytes 1572872 | tf_op jit(solution)/shard_map/ppermute | solution.py:13
  219.3 21.7 %collective-permute-start.24 = (bf16[128,4096]{1,0:T(8,128)(2,1)S(1)}, bf16[128,4096]{1,0:T(8,128)(2,1)S(1)}, u32[]{:S(2)}, u32[]{:S(2)}) collective-permute-start(bf16[128,4096]{1,0:T(8,128)(2,1)S(1)} %copy-done.27), channel_id=1, source_target_pairs={{0,4},{4,0},{8,12},{12,8},{16,20},{20,16},{24,28},{28,24},{1,5},{5... | collective-permute-start | bytes 3145736 | tf_op jit(solution)/shard_map/ppermute | solution.py:13
  221.7 19.3 %collective-permute-start.34 = (bf16[256,1024]{1,0:T(8,128)(2,1)S(1)}, bf16[256,1024]{1,0:T(8,128)(2,1)S(1)}, u32[]{:S(2)}, u32[]{:S(2)}) collective-permute-start(bf16[256,1024]{1,0:T(8,128)(2,1)S(1)} %copy-done.44), channel_id=1, source_target_pairs={{0,16},{4,20},{8,24},{12,28},{16,0},{20,4},{24,8},{28,12},{1,17},{... | collective-permute-start | bytes 1572872 | tf_op jit(solution)/shard_map/ppermute | solution.py:13
  226.6 16.7 %collective-permute-start.33 = (bf16[512,1024]{1,0:T(8,128)(2,1)S(1)}, bf16[512,1024]{1,0:T(8,128)(2,1)S(1)}, u32[]{:S(2)}, u32[]{:S(2)}) collective-permute-start(bf16[512,1024]{1,0:T(8,128)(2,1)S(1)} %copy-done.29), channel_id=1, source_target_pairs={{0,4},{4,0},{8,12},{12,8},{16,20},{20,16},{24,28},{28,24},{1,5},{5... | collective-permute-start | bytes 3145736 | tf_op jit(solution)/shard_map/ppermute | solution.py:13
  230.4 18.4 %collective-permute-start.28 = (bf16[64,4096]{1,0:T(8,128)(2,1)}, bf16[64,4096]{1,0:T(8,128)(2,1)S(1)}, u32[]{:S(2)}, u32[]{:S(2)}) collective-permute-start(bf16[64,4096]{1,0:T(8,128)(2,1)} %collective-permute-done.26), channel_id=1, source_target_pairs={{0,4},{4,0},{8,12},{12,8},{16,20},{20,16},{24,28},{28,24},{1,5},{5... | collective-permute-start | bytes 1572872 | tf_op jit(solution)/shard_map/ppermute | solution.py:13
  231.8 15.3 %collective-permute-start.27 = (bf16[64,4096]{1,0:T(8,128)(2,1)S(1)}, bf16[64,4096]{1,0:T(8,128)(2,1)S(1)}, u32[]{:S(2)}, u32[]{:S(2)}) collective-permute-start(bf16[64,4096]{1,0:T(8,128)(2,1)S(1)} %collective-permute-done.25), channel_id=1, source_target_pairs={{0,4},{4,0},{8,12},{12,8},{16,20},{20,16},{24,28},{28,24},{1,5},{5... | collective-permute-start | bytes 1572872 | tf_op jit(solution)/shard_map/ppermute | solution.py:13
  240.9 15.3 %collective-permute-start.37 = (bf16[256,1024]{1,0:T(8,128)(2,1)S(1)}, bf16[256,1024]{1,0:T(8,128)(2,1)S(1)}, u32[]{:S(2)}, u32[]{:S(2)}) collective-permute-start(bf16[256,1024]{1,0:T(8,128)(2,1)S(1)} %collective-permute-done.35), channel_id=1, source_target_pairs={{0,4},{4,0},{8,12},{12,8},{16,20},{20,16},{24,28},{28,24},{1,5},{5... | collective-permute-start | bytes 1572872 | tf_op jit(solution)/shard_map/ppermute | solution.py:13
  291.2 185.1 %collective-permute-start.70 = (bf16[256,512]{1,0:T(8,128)(2,1)}, bf16[256,512]{1,0:T(8,128)(2,1)}, u32[]{:S(2)}, u32[]{:S(2)}) collective-permute-start(bf16[256,512]{1,0:T(8,128)(2,1)} %get-tuple-element.291), channel_id=1, source_target_pairs={{0,4},{4,0},{8,12},{12,8},{16,20},{20,16},{24,28},{28,24},{1,5},{5... | collective-permute-start | bytes 786440 | tf_op jit(solution)/shard_map/ppermute | solution.py:13
  292.2 106.5 %collective-permute-start.59 = (bf16[256,512]{1,0:T(8,128)(2,1)}, bf16[256,512]{1,0:T(8,128)(2,1)}, u32[]{:S(2)}, u32[]{:S(2)}) collective-permute-start(bf16[256,512]{1,0:T(8,128)(2,1)} %get-tuple-element.303), channel_id=1, source_target_pairs={{0,4},{4,0},{8,12},{12,8},{16,20},{20,16},{24,28},{28,24},{1,5},{5... | collective-permute-start | bytes 786440 | tf_op jit(solution)/shard_map/ppermute | solution.py:13
  292.6 104.4 %collective-permute-start.55 = (bf16[256,512]{1,0:T(8,128)(2,1)}, bf16[256,512]{1,0:T(8,128)(2,1)}, u32[]{:S(2)}, u32[]{:S(2)}) collective-permute-start(bf16[256,512]{1,0:T(8,128)(2,1)} %get-tuple-element.304), channel_id=1, source_target_pairs={{0,4},{4,0},{8,12},{12,8},{16,20},{20,16},{24,28},{28,24},{1,5},{5... | collective-permute-start | bytes 786440 | tf_op jit(solution)/shard_map/ppermute | solution.py:13
  292.7 138.1 %collective-permute-start.63 = (bf16[256,2048]{1,0:T(8,128)(2,1)}, bf16[256,2048]{1,0:T(8,128)(2,1)}, u32[]{:S(2)}, u32[]{:S(2)}) collective-permute-start(bf16[256,2048]{1,0:T(8,128)(2,1)} %get-tuple-element.251), channel_id=1, source_target_pairs={{0,4},{4,0},{8,12},{12,8},{16,20},{20,16},{24,28},{28,24},{1,5},{5... | collective-permute-start | bytes 3145736 | tf_op jit(solution)/shard_map/ppermute | solution.py:13
  295.5 164.6 %collective-permute-start.66 = (bf16[256,2048]{1,0:T(8,128)(2,1)}, bf16[256,2048]{1,0:T(8,128)(2,1)}, u32[]{:S(2)}, u32[]{:S(2)}) collective-permute-start(bf16[256,2048]{1,0:T(8,128)(2,1)} %get-tuple-element.252), channel_id=1, source_target_pairs={{0,4},{4,0},{8,12},{12,8},{16,20},{20,16},{24,28},{28,24},{1,5},{5... | collective-permute-start | bytes 3145736 | tf_op jit(solution)/shard_map/ppermute | solution.py:13
  363.7 195.5 %reduce-scatter.28.cloned.1.call-start = ((), (), s32[]{:S(2)}) async-start(), calls=%async_computation.17 | async-start | bytes 81920
  396.7 170.1 %reduce-scatter.20.cloned.1.call-start = ((), (), s32[]{:S(2)}) async-start(), calls=%async_computation.13 | async-start | bytes 327680 | tf_op jit(solution)/shard_map/reduce_scatter | solution.py:130
  412.6 14.2 %collective-permute-start.56 = (bf16[2,256,512]{2,1,0:T(8,128)(2,1)S(1)}, bf16[2,256,512]{2,1,0:T(8,128)(2,1)S(1)}, u32[]{:S(2)}, u32[]{:S(2)}) collective-permute-start(bf16[2,256,512]{2,1,0:T(8,128)(2,1)S(1)} %pad_maximum_fusion.27), channel_id=1, source_target_pairs={{0,8},{4,12},{8,0},{12,4},{16,24},{20,28},{24,16},{28,20},{1,9},{5... | collective-permute-start | bytes 1572872 | tf_op jit(solution)/shard_map/ppermute | solution.py:13
  416.0 13.9 %collective-permute-start.60 = (bf16[2,256,512]{2,1,0:T(8,128)(2,1)S(1)}, bf16[2,256,512]{2,1,0:T(8,128)(2,1)S(1)}, u32[]{:S(2)}, u32[]{:S(2)}) collective-permute-start(bf16[2,256,512]{2,1,0:T(8,128)(2,1)S(1)} %pad_maximum_fusion.30), channel_id=1, source_target_pairs={{0,16},{4,20},{8,24},{12,28},{16,0},{20,4},{24,8},{28,12},{1,17},{... | collective-permute-start | bytes 1572872 | tf_op jit(solution)/shard_map/ppermute | solution.py:13
  426.8 25.6 %collective-permute-start.45 = (bf16[2,384,512]{2,1,0:T(8,128)(2,1)S(1)}, bf16[2,384,512]{2,1,0:T(8,128)(2,1)S(1)}, u32[]{:S(2)}, u32[]{:S(2)}) collective-permute-start(bf16[2,384,512]{2,1,0:T(8,128)(2,1)S(1)} %pad_maximum_fusion.17), channel_id=1, source_target_pairs={{0,8},{4,12},{8,0},{12,4},{16,24},{20,28},{24,16},{28,20},{1,9},{5... | collective-permute-start | bytes 2359304 | tf_op jit(solution)/shard_map/ppermute | solution.py:13
  430.8 20.6 %collective-permute-start.61 = (bf16[1,256,512]{2,1,0:T(8,128)(2,1)S(1)}, bf16[1,256,512]{2,1,0:T(8,128)(2,1)S(1)}, u32[]{:S(2)}, u32[]{:S(2)}) collective-permute-start(bf16[1,256,512]{2,1,0:T(8,128)(2,1)S(1)} %slice.872), channel_id=1, source_target_pairs={{0,8},{4,12},{8,0},{12,4},{16,24},{20,28},{24,16},{28,20},{1,9},{5... | collective-permute-start | bytes 786440 | tf_op jit(solution)/shard_map/ppermute | solution.py:13
  437.4 18.8 %collective-permute-start.50 = (bf16[2,384,512]{2,1,0:T(8,128)(2,1)S(1)}, bf16[2,384,512]{2,1,0:T(8,128)(2,1)}, u32[]{:S(2)}, u32[]{:S(2)}) collective-permute-start(bf16[2,384,512]{2,1,0:T(8,128)(2,1)S(1)} %pad_maximum_fusion.18), channel_id=1, source_target_pairs={{0,16},{4,20},{8,24},{12,28},{16,0},{20,4},{24,8},{28,12},{1,17},{... | collective-permute-start | bytes 2359304 | tf_op jit(solution)/shard_map/ppermute | solution.py:13
  451.4 51.6 %collective-permute-start.73 = (bf16[256,512]{1,0:T(8,128)(2,1)}, bf16[256,512]{1,0:T(8,128)(2,1)}, u32[]{:S(2)}, u32[]{:S(2)}) collective-permute-start(bf16[256,512]{1,0:T(8,128)(2,1)} %get-tuple-element.292), channel_id=1, source_target_pairs={{0,4},{4,0},{8,12},{12,8},{16,20},{20,16},{24,28},{28,24},{1,5},{5... | collective-permute-start | bytes 786440 | tf_op jit(solution)/shard_map/ppermute | solution.py:13
  452.4 115.9 %reduce-scatter.26.cloned.1.call-start = ((), (), s32[]{:S(2)}) async-start(), calls=%async_computation.16 | async-start | bytes 327680 | tf_op jit(solution)/shard_map/reduce_scatter | solution.py:130
  452.5 21.8 %collective-permute-start.69 = (bf16[256,2048]{1,0:T(8,128)(2,1)}, bf16[256,2048]{1,0:T(8,128)(2,1)}, u32[]{:S(2)}, u32[]{:S(2)}) collective-permute-start(bf16[256,2048]{1,0:T(8,128)(2,1)} %pad_maximum_fusion.9), channel_id=1, source_target_pairs={{0,4},{4,0},{8,12},{12,8},{16,20},{20,16},{24,28},{28,24},{1,5},{5... | collective-permute-start | bytes 3145736 | tf_op jit(solution)/shard_map/ppermute | solution.py:13
  456.2 11.7 %collective-permute-start.46 = (bf16[1,384,512]{2,1,0:T(8,128)(2,1)}, bf16[1,384,512]{2,1,0:T(8,128)(2,1)S(1)}, u32[]{:S(2)}, u32[]{:S(2)}) collective-permute-start(bf16[1,384,512]{2,1,0:T(8,128)(2,1)} %slice.871), channel_id=1, source_target_pairs={{0,16},{4,20},{8,24},{12,28},{16,0},{20,4},{24,8},{28,12},{1,17},{... | collective-permute-start | bytes 1179656 | tf_op jit(solution)/shard_map/ppermute | solution.py:13
  460.0 11.7 %collective-permute-start.51 = (bf16[1,384,512]{2,1,0:T(8,128)(2,1)}, bf16[1,384,512]{2,1,0:T(8,128)(2,1)}, u32[]{:S(2)}, u32[]{:S(2)}) collective-permute-start(bf16[1,384,512]{2,1,0:T(8,128)(2,1)} %slice.870), channel_id=1, source_target_pairs={{0,8},{4,12},{8,0},{12,4},{16,24},{20,28},{24,16},{28,20},{1,9},{5... | collective-permute-start | bytes 1179656 | tf_op jit(solution)/shard_map/ppermute | solution.py:13
  463.8 106.0 %reduce-scatter.16.cloned.1.call-start = ((), (), s32[]{:S(2)}) async-start(), calls=%async_computation.11 | async-start | bytes 327680 | tf_op jit(solution)/shard_map/reduce_scatter | solution.py:130
  468.6 26.3 %collective-permute-start.64 = (bf16[2,128,2048]{2,1,0:T(8,128)(2,1)}, bf16[2,128,2048]{2,1,0:T(8,128)(2,1)S(1)}, u32[]{:S(2)}, u32[]{:S(2)}) collective-permute-start(bf16[2,128,2048]{2,1,0:T(8,128)(2,1)} %bitcast.653), channel_id=1, source_target_pairs={{0,8},{4,12},{8,0},{12,4},{16,24},{20,28},{24,16},{28,20},{1,9},{5... | collective-permute-start | bytes 3145736 | tf_op jit(solution)/shard_map/ppermute | solution.py:13
  471.7 28.1 %collective-permute-start.67 = (bf16[2,128,2048]{2,1,0:T(8,128)(2,1)}, bf16[2,128,2048]{2,1,0:T(8,128)(2,1)}, u32[]{:S(2)}, u32[]{:S(2)}) collective-permute-start(bf16[2,128,2048]{2,1,0:T(8,128)(2,1)} %bitcast.654), channel_id=1, source_target_pairs={{0,16},{4,20},{8,24},{12,28},{16,0},{20,4},{24,8},{28,12},{1,17},{... | collective-permute-start | bytes 3145736 | tf_op jit(solution)/shard_map/ppermute | solution.py:13
  474.2 97.1 %reduce-scatter.14.cloned.1.call-start = ((), (), s32[]{:S(2)}) async-start(), calls=%async_computation.10 | async-start | bytes 327680 | tf_op jit(solution)/shard_map/reduce_scatter | solution.py:130
  479.4 54.7 %collective-permute-start.71 = (bf16[2,512,512]{2,1,0:T(8,128)(2,1)}, bf16[2,512,512]{2,1,0:T(8,128)(2,1)}, u32[]{:S(2)}, u32[]{:S(2)}) collective-permute-start(bf16[2,512,512]{2,1,0:T(8,128)(2,1)} %bitcast.141), channel_id=1, source_target_pairs={{0,8},{4,12},{8,0},{12,4},{16,24},{20,28},{24,16},{28,20},{1,9},{5... | collective-permute-start | bytes 3145736 | tf_op jit(solution)/shard_map/ppermute | solution.py:13
  488.1 84.7 %reduce-scatter.18.cloned.1.call-start = ((), (), s32[]{:S(2)}) async-start(), calls=%async_computation.12 | async-start | bytes 327680 | tf_op jit(solution)/shard_map/reduce_scatter | solution.py:130
  498.3 15.0 %collective-permute-start.65 = (bf16[1,128,2048]{2,1,0:T(8,128)(2,1)S(1)}, bf16[1,128,2048]{2,1,0:T(8,128)(2,1)}, u32[]{:S(2)}, u32[]{:S(2)}) collective-permute-start(bf16[1,128,2048]{2,1,0:T(8,128)(2,1)S(1)} %slice.869), channel_id=1, source_target_pairs={{0,16},{4,20},{8,24},{12,28},{16,0},{20,4},{24,8},{28,12},{1,17},{... | collective-permute-start | bytes 1572872 | tf_op jit(solution)/shard_map/ppermute | solution.py:13
  502.5 25.3 %collective-permute-start.68 = (bf16[1,128,2048]{2,1,0:T(8,128)(2,1)}, bf16[1,128,2048]{2,1,0:T(8,128)(2,1)}, u32[]{:S(2)}, u32[]{:S(2)}) collective-permute-start(bf16[1,128,2048]{2,1,0:T(8,128)(2,1)} %slice.868), channel_id=1, source_target_pairs={{0,8},{4,12},{8,0},{12,4},{16,24},{20,28},{24,16},{28,20},{1,9},{5... | collective-permute-start | bytes 1572872 | tf_op jit(solution)/shard_map/ppermute | solution.py:13
  505.8 31.3 %collective-permute-start.74 = (bf16[2,512,512]{2,1,0:T(8,128)(2,1)}, bf16[2,512,512]{2,1,0:T(8,128)(2,1)}, u32[]{:S(2)}, u32[]{:S(2)}) collective-permute-start(bf16[2,512,512]{2,1,0:T(8,128)(2,1)} %bitcast.144), channel_id=1, source_target_pairs={{0,16},{4,20},{8,24},{12,28},{16,0},{20,4},{24,8},{28,12},{1,17},{... | collective-permute-start | bytes 3145736 | tf_op jit(solution)/shard_map/ppermute | solution.py:13
  507.2 74.1 %reduce-scatter.22.cloned.1.call-start = ((), (), s32[]{:S(2)}) async-start(), calls=%async_computation.14 | async-start | bytes 1310720 | tf_op jit(solution)/shard_map/reduce_scatter | solution.py:130
  530.0 79.4 %reduce-scatter.24.cloned.1.call-start = ((), (), s32[]{:S(2)}) async-start(), calls=%async_computation.15 | async-start | bytes 1310720 | tf_op jit(solution)/shard_map/reduce_scatter | solution.py:130
  535.8 13.1 %collective-permute-start.72 = (bf16[1,512,512]{2,1,0:T(8,128)(2,1)S(1)}, bf16[1,512,512]{2,1,0:T(8,128)(2,1)S(1)}, u32[]{:S(2)}, u32[]{:S(2)}) collective-permute-start(bf16[1,512,512]{2,1,0:T(8,128)(2,1)S(1)} %slice.867), channel_id=1, source_target_pairs={{0,16},{4,20},{8,24},{12,28},{16,0},{20,4},{24,8},{28,12},{1,17},{... | collective-permute-start | bytes 1572872 | tf_op jit(solution)/shard_map/ppermute | solution.py:13
  538.8 12.6 %collective-permute-start.75 = (bf16[1,512,512]{2,1,0:T(8,128)(2,1)S(1)}, bf16[1,512,512]{2,1,0:T(8,128)(2,1)S(1)}, u32[]{:S(2)}, u32[]{:S(2)}) collective-permute-start(bf16[1,512,512]{2,1,0:T(8,128)(2,1)S(1)} %slice.866), channel_id=1, source_target_pairs={{0,8},{4,12},{8,0},{12,4},{16,24},{20,28},{24,16},{28,20},{1,9},{5... | collective-permute-start | bytes 1572872 | tf_op jit(solution)/shard_map/ppermute | solution.py:13
  (234 other events, 1709.9 us)
Sparse Core Ops, SparseCore 0:
  363.8 31.4 reduce-scatter.11
  398.2 19.0 reduce-scatter.27
  452.5 19.8 reduce-scatter.19
  474.6 17.7 reduce-scatter.25
  494.5 17.9 reduce-scatter.15
  514.7 17.9 reduce-scatter.13
  535.6 17.7 reduce-scatter.17
  555.8 25.4 reduce-scatter.21
  583.6 25.7 reduce-scatter.23

commit v2 on v1

v2 whole, which is shorter than its diff:
```python
import jax
import jax.numpy as jnp
from jax import lax
from jax.experimental import pallas as pl
from jax.experimental.pallas import tpu as pltpu
from jax.sharding import PartitionSpec as P

epsilon = 1e-05
bf16 = jnp.bfloat16
f32 = jnp.float32
ROWS = 64
STEP = 512
LANES = 512
LIMIT = 60
MIB = 2**20
G1, B1, G2, B2, MK, MV, MR, DECAY, FIRST, CMK, CMR = range(11)


def hop(value, bit):
    count = lax.axis_size("seg")
    return lax.ppermute(value, "seg", [(i, i ^ bit) for i in range(count)])


def along(value, steps):
    count = lax.axis_size("stretch")
    first, last = (max(0, -steps), min(count, count - steps))
    return lax.ppermute(value, "stretch", [(i, i + steps) for i in range(first, last)])


class Live:
    def __init__(self):
        self.__dict__["held"] = {}

    def __getattr__(self, name):
        return self.held[name]

    def __setattr__(self, name, value):
        self.held[name] = value

    def drop(self, *names):
        for name in names:
            del self.held[name]

    def sync(self):
        self.__dict__["held"] = lax.optimization_barrier(self.held)


def far_bits():
    bits, b = [], 2
    while b < lax.axis_size("seg"):
        bits.append(b)
        b *= 2
    return bits


def relative_order():
    count = lax.axis_size("seg")
    return list(range(0, count, 2)) + list(range(1, count, 2))


def first_stage(own):
    return {b: [hop(part, b) for part in own] for b in far_bits()}


def halves(parts):
    if len(parts) == 2:
        return parts
    half = parts[0].shape[0] // 2
    return [parts[0][:half], parts[0][half:]]


def second_stage(direct, held):
    rest = far_bits()
    held = dict(held)
    for m in sorted(range(0, lax.axis_size("seg"), 2), key=lambda m: (bin(m).count("1"), m)):
        if m == 0 or m in held:
            continue
        bits = [b for b in rest if m & b]
        held[m] = [hop(held[m ^ bits[-1]][0], bits[-1]), hop(held[m ^ bits[0]][1], bits[0])]
    return {m: held[m] for m in held if m not in direct}


def sibling(pieces):
    return {m ^ 1: [hop(p, 1) for p in parts] for m, parts in pieces.items()}


def plan(pieces, first, rows):
    steps, at = [], 0
    for m in relative_order():
        base = 0
        for part in pieces[m]:
            lo, hi = max(first, base), min(first + rows, base + part.shape[0])
            if lo < hi:
                steps.append((at, lo - base, hi - lo, m, lo - first))
            base += part.shape[0]
            at += 1
    return steps


def flat_pieces(pieces):
    return [part for m in relative_order() for part in pieces[m]]


class Loads:
    def __init__(self, sems):
        self.sems, self.used = sems, 0

    def start(self, src, dst):
        copy = pltpu.make_async_copy(src, dst, self.sems.at[self.used])
        self.used += 1
        copy.start()
        return copy

    def pieces(self, steps, refs, target, place):
        return [
            self.start(refs[piece].at[pl.ds(row, count)], target.at[pl.ds(place(m) + within, count)])
            for piece, row, count, m, within in steps
        ]


def wait(copies):
    for c in copies:
        c.wait()


def call(body, info, small, large, raw, outs, big_outs, scratch, copies, us, limit):
    n_small, n_large, n_raw = len(small), len(large), len(raw)
    n_out, n_big = len(outs), len(big_outs)

    def shape_of(array, index):
        return array.shape if index is None else array.shape[1:]

    def kernel(*refs):
        at = 0

        def take(n):
            nonlocal at
            at += n
            return refs[at - n : at]

        (info_ref,), small_refs, large_refs, raw_refs = take(1), take(n_small), take(n_large), take(n_raw)
        out_refs, big_refs = take(n_out), take(n_big)
        buffers, big_buffers, (sems,) = take(n_large), take(n_big), take(1)
        rest = take(len(refs) - at)
        loads = Loads(sems)
        pending = []
        for (array, index), ref, buf in zip(large, large_refs, buffers):
            pending.append(loads.start(ref if index is None else ref.at[index], buf))
        stored = {}

        def get(k):
            if pending[k] is not None:
                pending[k].wait()
                pending[k] = None
            return buffers[k]

        def put(k):
            stored[k] = loads.start(big_buffers[k], big_refs[k])

        body(info_ref, small_refs, get, raw_refs, out_refs, big_buffers, put, rest, loads)
        for k in range(n_large):
            get(k)
        for k in range(n_big):
            if k not in stored:
                put(k)
        wait(stored.values())

    hbm = pl.BlockSpec(memory_space=pltpu.HBM)
    vmem = pl.BlockSpec(memory_space=pltpu.VMEM)
    return pl.pallas_call(
        kernel,
        out_shape=[jax.ShapeDtypeStruct(s, d) for s, d in (*outs, *big_outs)],
        in_specs=[pl.BlockSpec(memory_space=pltpu.SMEM)] + [vmem] * n_small + [hbm] * (n_large + n_raw),
        out_specs=[vmem] * n_out + [hbm] * n_big,
        scratch_shapes=[pltpu.VMEM(shape_of(a, i), a.dtype) for a, i in large]
        + [pltpu.VMEM(s, d) for s, d in big_outs]
        + [pltpu.SemaphoreType.DMA((max(1, n_large + n_big + copies),))]
        + list(scratch),
        compiler_params=pltpu.CompilerParams(vmem_limit_bytes=LIMIT * MIB),
        cost_estimate=pl.CostEstimate(
            flops=0, bytes_accessed=int(us * 1e3), transcendentals=0),
    )(info, *small, *[a for a, _ in large], *raw)


def natural(me, rows):
    return lambda m: pl.multiple_of(jnp.bitwise_xor(me, m) * rows, rows)


def dot_nn(a, b):
    return jnp.dot(a, b, preferred_element_type=f32)


def dot_nt(a, b):
    return lax.dot_general(a, b, (((1,), (1,)), ((), ())), preferred_element_type=f32)


def dot_tn(a, b):
    return lax.dot_general(a, b, (((0,), (0,)), ((), ())), preferred_element_type=f32)


def norm(rows):
    centre = rows - jnp.mean(rows, axis=-1, keepdims=True)
    inverse = lax.rsqrt(jnp.mean(centre * centre, axis=-1, keepdims=True) + epsilon)
    return centre * inverse, inverse


def norm_back(d, unit, inverse, gain):
    q = d * gain
    return inverse * (
        q
        - jnp.mean(q, axis=-1, keepdims=True)
        - unit * jnp.mean(q * unit, axis=-1, keepdims=True)
    )


def down_one(rows, entering):
    at = lax.broadcasted_iota(jnp.int32, rows.shape, 0)
    return jnp.where(at == 0, entering, pltpu.roll(rows, 1, 0))


def up_one(rows, entering):
    at = lax.broadcasted_iota(jnp.int32, rows.shape, 0)
    last = rows.shape[0] - 1
    return jnp.where(at == last, entering, pltpu.roll(rows, last, 0))


def fold(rows):
    total = rows[:8]
    for k in range(8, rows.shape[0], 8):
        total = total + rows[k : k + 8]
    return total


def columns(width, step):
    step = min(step, width)

    def run(body):
        @pl.loop(0, width // step)
        def _(n):
            body(pl.ds(pl.multiple_of(n * step, step), step))

    return run


def row_chunk(b, i, length):
    return pl.ds(pl.multiple_of(b * length + i * ROWS, ROWS), ROWS)


def two_part(mat, value):
    hi = value.astype(bf16)
    lo = (value - hi.astype(f32)).astype(bf16)
    return dot_nn(mat, hi) + dot_nn(mat, lo)


def triangle(length, strictly_before):
    row = lax.broadcasted_iota(jnp.int32, (length, length), 0)
    col = lax.broadcasted_iota(jnp.int32, (length, length), 1)
    keep = (col < row) if strictly_before else (col > row)
    return keep.astype(f32).astype(bf16)


def column_sums(out_ref, sum_ref):
    for k in range(sum_ref.shape[0]):
        out_ref[k : k + 1, :] = jnp.sum(sum_ref[k], axis=0, keepdims=True)


def pack(info, parts_a, parts_b, width):
    arrays = [p[0] for p in (*parts_a, *parts_b)]

    def kernel(*refs):
        ins, outs, sems = refs[: len(arrays)], refs[len(arrays) : -1], refs[-1]
        copies, n = [], 0
        for out, parts in zip(outs, (parts_a, parts_b)):
            at = 0
            for _, first, count in parts:
                copies.append(pltpu.make_async_copy(
                    ins[n].at[pl.ds(first, count)], out.at[pl.ds(at, count)], sems.at[n]))
                at += count
                n += 1
        for c in copies:
            c.start()
        wait(copies)

    return pl.pallas_call(
        kernel,
        out_shape=[jax.ShapeDtypeStruct((sum(p[2] for p in parts), width), bf16)
                   for parts in (parts_a, parts_b)],
        in_specs=[pl.BlockSpec(memory_space=pltpu.HBM)] * len(arrays),
        out_specs=[pl.BlockSpec(memory_space=pltpu.VMEM)] * 2,
        compiler_params=pltpu.CompilerParams(vmem_limit_bytes=LIMIT * MIB),
        scratch_shapes=[pltpu.SemaphoreType.DMA((len(arrays),))],
        cost_estimate=pl.CostEstimate(flops=0, bytes_accessed=3 * MIB, transcendentals=0),
    )(*arrays)


def time_in(info, stream, last, previous, given, pieces, spots, length, shard):
    tokens, width = stream.shape
    batches = tokens // length
    plans = [plan(pieces, spots[k], shard) for k in "kvr"]
    vplan = plan(pieces, spots["vec"], 16)
    order = relative_order()

    def body(info, small, get, raw, outs, big, put, scratch, loads):
        last_ref, prev_ref = small[:2]
        sum_ref, vec_ref, entry_ref = outs
        in_ref, kvr_ref = big
        w, vt = scratch
        place = natural(info[0], shard)
        vcopies = loads.pieces(vplan, raw, vt, lambda m: order.index(m) * 16)
        copies = [loads.pieces(plans[k], raw, w.at[k], place) for k in range(3)]
        wait(vcopies)
        if given is not None:
            vec_ref[...] = small[2][...]
        else:
            for at, m in enumerate(order):
                vec_ref[:, pl.ds(place(m), shard)] = vt[at * 16 : at * 16 + 16, :shard].astype(f32)
        unit, _ = norm(last_ref[...].astype(f32))
        edge = unit * vec_ref[G1 : G1 + 1] + vec_ref[B1 : B1 + 1]
        for b in range(batches):
            entry_ref[b : b + 1, :] = jnp.where(info[1] == 1, prev_ref[b], edge[b : b + 1])
        stream_ref = get(0)

        for b in range(batches):
            def step(i, before):
                r = row_chunk(b, i, length)
                na, _ = norm(stream_ref[r, :].astype(f32))
                xa = na * vec_ref[G1 : G1 + 1] + vec_ref[B1 : B1 + 1]
                xs = down_one(xa, before)
                for k, row in enumerate((MK, MV, MR)):
                    mix = vec_ref[row : row + 1]
                    in_ref[k, r, :] = (xa * mix + xs * (1.0 - mix)).astype(bf16)
                return xa[ROWS - 1 :]
            lax.fori_loop(0, length // ROWS, step, entry_ref[b : b + 1])
        put(0)
        for k in range(3):
            wait(copies[k])
            @columns(width, STEP)
            def _(n):
                kvr_ref[k, :, n] = dot_nn(in_ref[k], w[k, :, n])
        put(1)
        for b in range(batches):
            t = slice(b * length, (b + 1) * length)
            @columns(width, LANES)
            def _(n):
                rate = -jnp.exp(vec_ref[DECAY : DECAY + 1, n])
                at = lax.broadcasted_iota(jnp.int32, (length, 1), 0).astype(f32)
                shifted = kvr_ref[0, t, n] - at * rate
                peak = jnp.max(shifted, axis=0, keepdims=True)
                factor = jnp.exp(shifted - peak)
                sum_ref[b : b + 1, n] = jnp.sum(factor * kvr_ref[1, t, n], axis=0, keepdims=True)
                sum_ref[batches + b : batches + b + 1, n] = jnp.sum(factor, axis=0, keepdims=True)
                sum_ref[2 * batches + b : 2 * batches + b + 1, n] = peak + (length - 1.0) * rate

    extra = [] if given is None else [given]
    return call(
        body, info, [last, previous, *extra], [(stream, None)], flat_pieces(pieces),
        [((3 * batches, width), f32), ((16, width), f32), ((batches, width), f32)],
        [((3, tokens, width), bf16), ((3, tokens, width), f32)],
        [pltpu.VMEM((3, width, width), bf16), pltpu.VMEM((16 * len(order), width), bf16)],
        len(vplan) + sum(map(len, plans)), 9, 40)


def wkv_terms(kvr_ref, ent_ref, vec_ref, b, t, n, batches, length):
    rate = -jnp.exp(vec_ref[DECAY : DECAY + 1, n])
    at = lax.broadcasted_iota(jnp.int32, (length, 1), 0).astype(f32)
    keys = kvr_ref[0, t, n]
    shifted = keys - at * rate
    peak = jnp.max(shifted, axis=0, keepdims=True)
    factor = jnp.exp(shifted - peak)
    near = (at - 1.0) * rate + peak
    opening = at * rate + ent_ref[2 * batches + b : 2 * batches + b + 1, n]
    reward = vec_ref[FIRST : FIRST + 1, n] + keys
    top = jnp.maximum(jnp.maximum(near, opening), reward)
    return at, factor, jnp.exp(near - top), jnp.exp(opening - top), jnp.exp(reward - top)


def time_out(info, kvr, everyone, state, vec, stream, pieces, spots, length, shard):
    tokens, width = stream.shape
    batches = tokens // length
    stretches = everyone.shape[0]
    steps = plan(pieces, spots["o"], shard)

    def body(info, small, get, raw, outs, big, put, scratch, loads):
        every_ref, num_ref, den_ref, exp_ref, vec_ref = small
        ent_ref, mean_ref, log_ref, edge_ref = outs
        gated_ref, wkv_ref, rden_ref, mid_ref, xb_ref = big
        (w,) = scratch
        copies = loads.pieces(steps, raw, w, natural(info[0], shard))
        span = -jnp.exp(vec_ref[DECAY : DECAY + 1, :]) * float(length)

        def merge(upto, b):
            upto_f = upto.astype(f32) if upto is not stretches else float(stretches)
            logits = []
            for z in range(stretches):
                row = 2 * batches + b
                logit = every_ref[z, row : row + 1, :] + (upto_f - 1.0 - z) * span
                logits.append(logit if upto is stretches else jnp.where(z < upto, logit, -jnp.inf))
            opening = exp_ref[b] + upto_f * span
            top = opening
            for logit in logits:
                top = jnp.maximum(top, logit)
            start = jnp.exp(opening - top)
            num, den = num_ref[b] * start, den_ref[b] * start
            for z, logit in enumerate(logits):
                weight = jnp.exp(logit - top)
                num = num + weight * every_ref[z, b : b + 1, :]
                den = den + weight * every_ref[z, batches + b : batches + b + 1, :]
            return num, den, top

        for b in range(batches):
            for k, part in enumerate(merge(info[2], b)):
                ent_ref[k * batches + b : k * batches + b + 1, :] = part
            num, den, top = merge(stretches, b)
            mean_ref[b] = num / den
            log_ref[b] = top + jnp.log(den)

        lower = triangle(length, True)
        kvr_ref = get(0)
        for b in range(batches):
            t = slice(b * length, (b + 1) * length)
            @columns(width, LANES)
            def _(n):
                _, factor, p, o, e = wkv_terms(kvr_ref, ent_ref, vec_ref, b, t, n, batches, length)
                vals = kvr_ref[1, t, n]
                num = (two_part(lower, factor * vals) * p
                       + ent_ref[b : b + 1, n] * o + vals * e)
                den = (two_part(lower, factor) * p
                       + ent_ref[batches + b : batches + b + 1, n] * o + e)
                rden = 1.0 / den
                wkv = num * rden
                wkv_ref[t, n] = wkv
                rden_ref[t, n] = rden
                gated_ref[t, n] = (jax.nn.sigmoid(kvr_ref[2, t, n]) * wkv).astype(bf16)
        put(0)
        put(1)
        put(2)
        wait(copies)
        stream_ref = get(1)
        @columns(width, STEP)
        def _(n):
            mid_ref[:, n] = stream_ref[:, n].astype(f32) + dot_nn(gated_ref[...], w[:, n])
        put(3)
        @pl.loop(0, tokens // ROWS)
        def _(i):
            r = row_chunk(0, i, 0)
            nb, _ = norm(mid_ref[r, :])
            xb_ref[r, :] = nb * vec_ref[G2 : G2 + 1] + vec_ref[B2 : B2 + 1]
        for b in range(batches):
            last = (b + 1) * length - 1
            edge_ref[b : b + 1, :] = xb_ref[last : last + 1, :]

    one = ((tokens, width), f32)
    return call(
        body, info, [everyone, *state, vec], [(kvr, None), (stream, None)], flat_pieces(pieces),
        [((3 * batches, width), f32), ((batches, 1, width), f32), ((batches, 1, width), f32),
         ((batches, width), f32)],
        [((tokens, width), bf16), one, one, one, one],
        [pltpu.VMEM((width, width), bf16)], len(steps), 7, 40)


def chan_in(info, xb, edge, previous, vec, pieces_c, pieces_ck, spots, length, shard, fshard):
    tokens, width = xb.shape
    batches = tokens // length
    order = relative_order()
    wide = fshard * len(order)
    flat_c, flat_k = flat_pieces(pieces_c), flat_pieces(pieces_ck)
    steps_c, steps_k = plan(pieces_c, spots["c"], shard), plan(pieces_ck, 0, shard)

    def body(info, small, get, raw, outs, big, put, scratch, loads):
        edge_ref, prev_ref, vec_ref = small
        (entry_ref,) = outs
        in_ref, near_ref, far_ref, act_ref, frec_ref = big
        wk, wc = scratch
        raw_c, raw_k = raw[: len(flat_c)], raw[len(flat_c) :]
        place = natural(info[0], shard)
        copies_c = loads.pieces(steps_c, raw_c, wc, place)
        copies_k = loads.pieces(steps_k, raw_k, wk, place)
        for b in range(batches):
            entry_ref[b : b + 1, :] = jnp.where(info[1] == 1, prev_ref[b], edge_ref[b : b + 1, :])
        xb_ref = get(0)
        for b in range(batches):
            def step(i, before):
                r = row_chunk(b, i, length)
                x = xb_ref[r, :]
                xt = down_one(x, before)
                for k, row in enumerate((CMK, CMR)):
                    mix = vec_ref[row : row + 1]
                    in_ref[k, r, :] = (x * mix + xt * (1.0 - mix)).astype(bf16)
                return x[ROWS - 1 :]
            lax.fori_loop(0, length // ROWS, step, entry_ref[b : b + 1])
        put(0)
        wait(copies_c)
        @columns(width, STEP)
        def _(n):
            frec_ref[:, n] = dot_nn(in_ref[1], wc[:, n])
        put(4)
        wait(copies_k)
        part = min(STEP, fshard)
        for hid_ref, first in ((far_ref, len(order) // 2), (near_ref, 0)):
            for k in range(len(order) // 2):
                base = natural(info[0], fshard)(order[first + k])
                for q in range(fshard // part):
                    src = pl.ds(pl.multiple_of(base + q * part, part), part)
                    lo = k * fshard + q * part
                    act = jnp.maximum(dot_nn(in_ref[0], wk[:, src]), 0.0)
                    act_ref[:, first * fshard + lo : first * fshard + lo + part] = act.astype(bf16)
                    hid_ref[:, lo : lo + part] = (act * act).astype(bf16)
            put(2 if first else 1)

    return call(
        body, info, [edge, previous, vec], [(xb, None)], [*flat_c, *flat_k],
        [((batches, width), f32)],
        [((2, tokens, width), bf16), ((tokens, wide // 2), bf16), ((tokens, wide // 2), bf16),
         ((tokens, wide), bf16), ((tokens, width), f32)],
        [pltpu.VMEM((width, wide), bf16), pltpu.VMEM((width, width), bf16)],
        len(steps_c) + len(steps_k), 11, 40)


def chan_out(info, near, far, act, frec, mid, cot, pieces, fshard):
    tokens, width = mid.shape
    order = relative_order()
    wide = fshard * len(order)
    steps = plan(pieces, 0, fshard)

    def body(info, small, get, raw, outs, big, put, scratch, loads):
        out_ref, df_ref, dr_ref, dpre_ref = big
        w, fval = scratch
        copies = loads.pieces(steps, raw, w, lambda m: order.index(m) * fshard)
        near_ref, far_ref = get(0), get(1)
        wait(copies)
        @columns(width, STEP)
        def _(n):
            fval[:, n] = (dot_nn(near_ref[...], w[: wide // 2, n])
                          + dot_nn(far_ref[...], w[wide // 2 :, n]))
        frec_ref, mid_ref, cot_ref, act_ref = get(2), get(3), get(4), get(5)
        @pl.loop(0, tokens // ROWS)
        def _(i):
            r = row_chunk(0, i, 0)
            sig = jax.nn.sigmoid(frec_ref[r, :])
            cots, value = cot_ref[r, :].astype(f32), fval[r, :]
            out_ref[r, :] = (mid_ref[r, :] + sig * value).astype(bf16)
            df_ref[r, :] = (cots * sig).astype(bf16)
            dr_ref[r, :] = (cots * value * sig * (1.0 - sig)).astype(bf16)
        for k in range(3):
            put(k)
        part = min(STEP, fshard)
        for at, m in enumerate(order):
            base = natural(info[0], fshard)(m)
            for q in range(fshard // part):
                src = slice(at * fshard + q * part, at * fshard + (q + 1) * part)
                dst = pl.ds(pl.multiple_of(base + q * part, part), part)
                d = dot_nt(df_ref[...], w[src, :]) * (2.0 * act_ref[:, src].astype(f32))
                dpre_ref[:, dst] = d.astype(bf16)

    low = ((tokens, width), bf16)
    return call(
        body, info, [], [(a, None) for a in (near, far, frec, mid, cot, act)], flat_pieces(pieces), [],
        [low, low, low, ((tokens, wide), bf16)],
        [pltpu.VMEM((wide, width), bf16), pltpu.VMEM((tokens, width), f32)], len(steps), 13, 40)


def chan_back(info, dpre, dfrec, xb, entry, vec, pieces_c, pieces_ck, spots, length, shard, wide):
    tokens, width = xb.shape
    batches = tokens // length
    flat_c, flat_k = flat_pieces(pieces_c), flat_pieces(pieces_ck)
    steps_c, steps_k = plan(pieces_c, spots["c"], shard), plan(pieces_ck, 0, shard)

    def body(info, small, get, raw, outs, big, put, scratch, loads):
        entry_ref, vec_ref = small
        head_ref, total_ref = outs
        dxt_ref, dxb_ref = big
        wk, wc, df, dr, sum_ref = scratch
        raw_c, raw_k = raw[: len(flat_c)], raw[len(flat_c) :]
        place = natural(info[0], shard)
        copies_c = loads.pieces(steps_c, raw_c, wc, place)
        copies_k = loads.pieces(steps_k, raw_k, wk, place)
        dfrec_ref = get(0)
        wait(copies_c)
        @columns(width, STEP)
        def _(n):
            dr[:, n] = dot_nt(dfrec_ref[...], wc[n, :])
        dpre_ref = get(1)
        wait(copies_k)
        @columns(width, STEP)
        def _(n):
            df[:, n] = dot_nt(dpre_ref[...], wk[n, :])
        sum_ref[...] = jnp.zeros_like(sum_ref)
        xb_ref = get(2)
        for b in range(batches):
            def step(i, before):
                r = row_chunk(b, i, length)
                x = xb_ref[r, :]
                gap = x - down_one(x, before)
                a, c = df[r, :], dr[r, :]
                ck, cr = vec_ref[CMK : CMK + 1], vec_ref[CMR : CMR + 1]
                dxt_ref[r, :] = a * (1.0 - ck) + c * (1.0 - cr)
                dxb_ref[r, :] = a * ck + c * cr
                sum_ref[0] += fold(a * gap)
                sum_ref[1] += fold(c * gap)
                return x[ROWS - 1 :]
            lax.fori_loop(0, length // ROWS, step, entry_ref[b : b + 1])
            head_ref[b : b + 1, :] = dxt_ref[b * length : b * length + 1, :]
        column_sums(total_ref, sum_ref)

    one = ((tokens, width), f32)
    return call(
        body, info, [entry, vec], [(dfrec, None), (dpre, None), (xb, None)], [*flat_c, *flat_k],
        [((batches, width), f32), ((2, width), f32)], [one, one],
        [pltpu.VMEM((width, wide), bf16), pltpu.VMEM((width, width), bf16),
         pltpu.VMEM((tokens, width), f32), pltpu.VMEM((tokens, width), f32),
         pltpu.VMEM((2, 8, width), f32)],
        len(steps_c) + len(steps_k), 11, 40)


def mid_back(info, dxt, dxb, after, mid, cot, vec, kvr, wkv, rden, ent, pieces, spots, length, shard):
    tokens, width = mid.shape
    batches = tokens // length
    steps = plan(pieces, spots["o"], shard)

    def body(info, small, get, raw, outs, big, put, scratch, loads):
        after_ref, vec_ref, ent_ref = small
        dent_ref, total_ref = outs
        dmid_ref, dbr_ref, drec_ref, gn_ref = big
        w, sum_ref = scratch
        copies = loads.pieces(steps, raw, w, natural(info[0], shard))
        sum_ref[...] = jnp.zeros_like(sum_ref)
        dxt_ref, dxb_ref, mid_ref, cot_ref = get(0), get(1), get(2), get(3)
        for b in range(batches):
            def step(k, after_row):
                r = row_chunk(b, length // ROWS - 1 - k, length)
                nb, inverse = norm(mid_ref[r, :])
                dx = dxt_ref[r, :]
                d = dxb_ref[r, :] + up_one(dx, after_row)
                back = cot_ref[r, :].astype(f32) + norm_back(d, nb, inverse, vec_ref[G2 : G2 + 1])
                dmid_ref[r, :] = back
                dbr_ref[r, :] = back.astype(bf16)
                sum_ref[0] += fold(d * nb)
                sum_ref[1] += fold(d)
                return dx[:1]
            lax.fori_loop(0, length // ROWS, step, after_ref[b : b + 1])
        put(0)
        put(1)
        column_sums(total_ref, sum_ref)
        wait(copies)
        @columns(width, STEP)
        def _(n):
            gn_ref[:, n] = dot_nt(dbr_ref[...], w[n, :])
        kvr_ref, wkv_ref, rden_ref = get(4), get(5), get(6)
        for b in range(batches):
            t = slice(b * length, (b + 1) * length)
            @columns(width, LANES)
            def _(n):
                _, _, _, o, _ = wkv_terms(kvr_ref, ent_ref, vec_ref, b, t, n, batches, length)
                sig = jax.nn.sigmoid(kvr_ref[2, t, n])
                d = gn_ref[t, n] * sig
                wkvs = wkv_ref[t, n]
                drec_ref[t, n] = (d * wkvs * (1.0 - sig)).astype(bf16)
                gn = d * rden_ref[t, n]
                gn_ref[t, n] = gn
                go = gn * o
                dent_ref[b : b + 1, n] = jnp.sum(go, axis=0, keepdims=True)
                dent_ref[batches + b : batches + b + 1, n] = -jnp.sum(go * wkvs, axis=0, keepdims=True)

    one, low = ((tokens, width), f32), ((tokens, width), bf16)
    return call(
        body, info, [after, vec, ent], [(a, None) for a in (dxt, dxb, mid, cot, kvr, wkv, rden)],
        flat_pieces(pieces), [((2 * batches, width), f32), ((2, width), f32)], [one, low, low, one],
        [pltpu.VMEM((width, width), bf16), pltpu.VMEM((2, 8, width), f32)], len(steps), 9, 40)


def time_back(info, gn, wkv, kvr, ent, back, sums, state, drec, stream, entry, vec, pieces, spots,
              length, shard):
    tokens, width = stream.shape
    batches = tokens // length
    stretches = back.shape[0]
    plans = [plan(pieces, spots[k], shard) for k in "kvr"]

    def body(info, small, get, raw, outs, big, put, scratch, loads):
        ent_ref, back_ref, sums_ref, num_ref, den_ref, exp_ref, entry_ref, vec_ref = small
        gnum_ref, gden_ref, gexp_ref, gffn_ref, head_ref, total_ref, extra_ref = outs
        d_ref, dxs_ref, dxa_ref = big
        w, dins, sum_ref, later_ref, loc_ref = scratch
        place = natural(info[0], shard)
        copies = [loads.pieces(plans[k], raw, w.at[k], place) for k in range(3)]
        span = -jnp.exp(vec_ref[DECAY : DECAY + 1, :]) * float(length)
        pos = info[2].astype(f32)
        nums, dens, exps = (slice(k * batches, (k + 1) * batches) for k in range(3))
        zero = jnp.zeros((batches, width), f32)

        def state(ref):
            return jnp.concatenate([ref[b] for b in range(batches)], axis=0)

        later_n = later_d = carry_n = carry_d = grad_n = grad_d = zero
        for z in range(stretches):
            there = back_ref[z, exps, :]
            after = z > info[2]
            lift = jnp.where(after, jnp.exp(jnp.minimum(
                sums_ref[exps, :] - there + (z - 1.0 - pos) * span, 0.0)), 0.0)
            carry = jnp.where(after, jnp.exp(jnp.minimum(
                ent_ref[exps, :] - there + (z - pos) * span, 0.0)), 0.0)
            raised = jnp.exp(jnp.minimum(state(exp_ref) - there + float(z) * span, 0.0))
            dn, dd = back_ref[z, nums, :], back_ref[z, dens, :]
            later_n, later_d = later_n + dn * lift, later_d + dd * lift
            carry_n, carry_d = carry_n + dn * carry, carry_d + dd * carry
            grad_n, grad_d = grad_n + dn * raised, grad_d + dd * raised
        later_ref[nums, :], later_ref[dens, :] = later_n, later_d
        grad_e = state(num_ref) * grad_n + state(den_ref) * grad_d
        for b in range(batches):
            gnum_ref[b], gden_ref[b] = grad_n[b : b + 1], grad_d[b : b + 1]
            gexp_ref[b] = grad_e[b : b + 1]
            gffn_ref[b] = back_ref[0, 3 * batches + b : 3 * batches + b + 1, :]
        rate_part = (
            float(length) * (ent_ref[nums, :] * carry_n + ent_ref[dens, :] * carry_d)
            + (length - 1.0) * (later_n * sums_ref[nums, :] + later_d * sums_ref[dens, :]))

        upper = triangle(length, False)
        gn_ref, wkv_ref, kvr_ref, drec_ref = get(0), get(1), get(2), get(3)
        for b in range(batches):
            t = slice(b * length, (b + 1) * length)
            @columns(width, LANES)
            def _(n):
                at, factor, p, o, e = wkv_terms(kvr_ref, ent_ref, vec_ref, b, t, n, batches, length)
                vals, g = kvr_ref[1, t, n], gn_ref[t, n]
                gd = -g * wkv_ref[t, n]
                direct = e * (g * vals + gd)
                opened = o * (g * ent_ref[b : b + 1, n] + gd * ent_ref[batches + b : batches + b + 1, n])
                rn = two_part(upper, g * p) + later_ref[b : b + 1, n]
                rd = two_part(upper, gd * p) + later_ref[batches + b : batches + b + 1, n]
                chain = factor * (rn * vals + rd)
                d_ref[0, t, n] = (chain + direct).astype(bf16)
                d_ref[1, t, n] = (factor * rn + g * e).astype(bf16)
                d_ref[2, t, n] = drec_ref[t, n]
                loc_ref[b : b + 1, n] = jnp.sum(
                    opened - (at - 1.0) * direct - at * chain, axis=0, keepdims=True)
                loc_ref[batches + b : batches + b + 1, n] = jnp.sum(direct, axis=0, keepdims=True)
        put(0)
        rate_rows = rate_part + loc_ref[:batches, :]
        extra_ref[0:1, :] = jnp.sum(rate_rows, axis=0, keepdims=True) * -jnp.exp(
            vec_ref[DECAY : DECAY + 1, :])
        extra_ref[1:2, :] = jnp.sum(loc_ref[batches:, :], axis=0, keepdims=True)
        for k in range(3):
            wait(copies[k])
            @columns(width, STEP)
            def _(n):
                dins[k, :, n] = dot_nt(d_ref[k], w[k, n, :])
        sum_ref[...] = jnp.zeros_like(sum_ref)
        stream_ref = get(4)
        for b in range(batches):
            def step(i, before):
                r = row_chunk(b, i, length)
                na, _ = norm(stream_ref[r, :].astype(f32))
                xa = na * vec_ref[G1 : G1 + 1] + vec_ref[B1 : B1 + 1]
                gap = xa - down_one(xa, before)
                dxs = jnp.zeros((ROWS, width), f32)
                dxa = jnp.zeros((ROWS, width), f32)
                for k, row in enumerate((MK, MV, MR)):
                    d, mix = dins[k, r, :], vec_ref[row : row + 1]
                    dxs = dxs + d * (1.0 - mix)
                    dxa = dxa + d * mix
                    sum_ref[k] += fold(d * gap)
                dxs_ref[r, :] = dxs
                dxa_ref[r, :] = dxa
                return xa[ROWS - 1 :]
            lax.fori_loop(0, length // ROWS, step, entry_ref[b : b + 1])
            head_ref[b : b + 1, :] = dxs_ref[b * length : b * length + 1, :]
        column_sums(total_ref, sum_ref)

    one = ((tokens, width), f32)
    return call(
        body, info, [ent, back, sums, *state, entry, vec],
        [(a, None) for a in (gn, wkv, kvr, drec, stream)], flat_pieces(pieces),
        [((batches, 1, width), f32)] * 4
        + [((batches, width), f32), ((3, width), f32), ((2, width), f32)],
        [((3, tokens, width), bf16), one, one],
        [pltpu.VMEM((3, width, width), bf16), pltpu.VMEM((3, tokens, width), f32),
         pltpu.VMEM((3, 8, width), f32), pltpu.VMEM((2 * batches, width), f32),
         pltpu.VMEM((2 * batches, width), f32)],
        sum(map(len, plans)), 14, 40)


def in_back(info, dxs, dxa, after, dmid, stream, vec, length):
    tokens, width = stream.shape
    batches = tokens // length

    def body(info, small, get, raw, outs, big, put, scratch, loads):
        after_ref, vec_ref = small
        (out_ref,) = big
        (sum_ref,) = scratch
        dxs_ref, dxa_ref, dmid_ref, stream_ref = (get(k) for k in range(4))
        sum_ref[...] = jnp.zeros_like(sum_ref)
        for b in range(batches):
            def step(k, after_row):
                r = row_chunk(b, length // ROWS - 1 - k, length)
                na, inverse = norm(stream_ref[r, :].astype(f32))
                dx = dxs_ref[r, :]
                d = dxa_ref[r, :] + up_one(dx, after_row)
                back = norm_back(d, na, inverse, vec_ref[G1 : G1 + 1])
                out_ref[r, :] = (dmid_ref[r, :] + back).astype(bf16)
                sum_ref[0] += fold(d * na)
                sum_ref[1] += fold(d)
                return dx[:1]
            lax.fori_loop(0, length // ROWS, step, after_ref[b : b + 1])
        column_sums(outs[0], sum_ref)

    return call(
        body, info, [after, vec], [(a, None) for a in (dxs, dxa, dmid, stream)], [],
        [((2, width), f32)], [((tokens, width), bf16)],
        [pltpu.VMEM((2, 8, width), f32)], 0, 6, 40)


def grad_orders():
    rest = far_bits()
    evens = list(range(0, lax.axis_size("seg"), 2))
    return evens, [[[m for m in evens if m & b], [m for m in evens if not m & b]]
                   for b in (rest[0], rest[-1])]


def weight_grad(info, arrays, items, layout, us):
    count = lax.axis_size("seg")
    evens, orders = grad_orders()
    tokens, n_wide = arrays[items[0][2][0]].shape[-2:]
    half = n_wide // 2
    per = len(evens) // 2
    w = arrays[items[0][0][0]].shape[-1] // {"natural": count, "blocks": len(evens), "groups": 4 * per}[layout]
    joined = w < 256
    loaded = 4 if joined else len(evens)
    group = per * w

    def body(info, small, get, raw, outs, big, put, scratch, loads):
        x_all, dy_all = scratch

        def view(spec):
            which, lead = spec
            return raw[which] if lead is None else raw[which].at[lead]

        def columns_of(ref, which, m):
            if layout == "natural":
                return ref.at[:, pl.ds(natural(info[0], w)(m), w)]
            return ref.at[:, pl.ds(evens.index(m) * w, w)]

        copies = []
        for k, (x, x_sib, dy, dy_sib) in enumerate(items):
            now = []
            for at, part in ((0, dy), (tokens, dy_sib)):
                now.append(loads.start(view(part), dy_all.at[k, pl.ds(at, tokens)]))
            for at, part in ((0, x), (tokens, x_sib)):
                ref = view(part)
                rows = pl.ds(at, tokens)
                if not joined:
                    for n, m in enumerate(evens):
                        now.append(loads.start(columns_of(ref, n, m), x_all.at[k, n, rows]))
                elif layout == "groups":
                    for g in range(4):
                        now.append(loads.start(
                            ref.at[:, pl.ds(g * group, group)], x_all.at[k, g, rows]))
                else:
                    for g in range(4):
                        for n, m in enumerate(orders[g // 2][g % 2]):
                            now.append(loads.start(
                                columns_of(ref, n, m), x_all.at[k, g, rows, pl.ds(n * w, w)]))
            copies.append(now)
        step = min(512, half)
        for k in range(len(items)):
            wait(copies[k])
        for stay in range(2):
            for side in range(2):
                out = big[2 * side + stay]
                for k in range(len(items)):
                    for q in range(half // step):
                        dst = slice(q * step, (q + 1) * step)
                        dys = dy_all[k, :, side * half + q * step : side * half + (q + 1) * step]
                        if joined:
                            g = dot_tn(x_all[k, 2 * side + stay], dys).astype(bf16)
                            for at in range(per):
                                out[at, k * w : (k + 1) * w, dst] = g[at * w : (at + 1) * w]
                        else:
                            for at, m in enumerate(orders[side][stay]):
                                out[at, k * w : (k + 1) * w, dst] = dot_tn(
                                    x_all[k, evens.index(m)], dys).astype(bf16)
                put(2 * side + stay)

    shape = (per, len(items) * w, half)
    return call(
        body, info, [], [], arrays, [], [(shape, bf16)] * 4,
        [pltpu.VMEM((len(items), loaded, 2 * tokens, group if joined else w), bf16),
         pltpu.VMEM((len(items), 2 * tokens, n_wide), bf16)],
        len(items) * (2 + 2 * max(len(evens), 4 * per)), us, 40)


def grad_first(parts):
    rest = far_bits()
    return hop(parts[0], rest[0]), hop(parts[2], rest[-1])


def total(terms):
    out = terms[0].astype(f32)
    for t in terms[1:]:
        out = out + t.astype(f32)
    return out


def own_rows(parts, items):
    return parts[0].shape[1] // items // lax.axis_size("stretch")


def by_kernel(parts, items):
    return len(far_bits()) == 2 and own_rows(parts, items) % 16 == 0


def grad_sends(info, parts, got, items):
    if by_kernel(parts, items):
        large = [(parts[1], 1), (got[0], 1), (parts[3], 1), (got[1], 1)]
        shape = parts[0].shape[1:]

        def body(info, small, get, raw, outs, big, put, scratch, loads):
            for side in range(2):
                a, b = get(2 * side), get(2 * side + 1)
                big[side][...] = total([a[...], b[...]]).astype(bf16)
                put(side)

        return call(body, info, [], large, [], [], [(shape, bf16)] * 2, [], 0, 2, 24)
    out = []
    for side, order in enumerate((far_bits(), far_bits()[::-1])):
        stay = grad_orders()[1][side][1]
        out.append(jnp.stack([
            total([parts[2 * side + 1][k], got[side][k]])
            for k, m in enumerate(stay) if m & order[1]]).astype(bf16))
    return out


def grad_second(parts, sends, items):
    rest = far_bits()
    if by_kernel(parts, items):
        return [hop(sends[0], rest[1]), hop(sends[1], rest[0])]
    return sends


def grad_finish(info, parts, got, last, items):
    stretches = lax.axis_size("stretch")
    own = own_rows(parts, items)
    rows, half = parts[0].shape[1:]
    rest = far_bits()
    if by_kernel(parts, items):
        large = [(parts[1], 0), (got[0], 0), (last[0], None), (parts[3], 0), (got[1], 0), (last[1], None)]

        def body(info, small, get, raw, outs, big, put, scratch, loads):
            for side in range(2):
                refs = [get(3 * side + j) for j in range(3)]
                for z in range(stretches):
                    for k in range(items):
                        src = slice((k * stretches + z) * own, (k * stretches + z + 1) * own)
                        dst = slice((z * items + k) * own, (z * items + k + 1) * own)
                        big[0][dst, side * half : (side + 1) * half] = total(
                            [r[src, :] for r in refs]).astype(bf16)

        return call(body, info, [], large, [], [], [((rows, 2 * half), bf16)], [], 0, 2, 24)[0]
    sides = []
    for side, order in enumerate((rest, rest[::-1])):
        stay = grad_orders()[1][side][1]
        terms = {m: [parts[2 * side + 1][k], got[side][k]] for k, m in enumerate(stay)}
        out = last[side]
        for b in order[1:]:
            if out is None:
                out = jnp.stack([total(v) for m, v in terms.items() if m & b]).astype(bf16)
            back = hop(out, b)
            terms = {m: v for m, v in terms.items() if not m & b}
            terms = {m: [*v, back[k]] for k, (m, v) in enumerate(terms.items())}
            out = None
        sides.append(total(terms[0]))
    whole = jnp.concatenate(sides, axis=1).astype(bf16).reshape(items, stretches, own, 2 * half)
    return jnp.swapaxes(whole, 0, 1).reshape(rows, 2 * half)


def stretch_part(part):
    return lax.psum_scatter(part, "stretch", scatter_dimension=0, tiled=True)


def stretch_items(out, items):
    own = out.shape[0] // items
    return [out[k * own : (k + 1) * own].astype(f32) for k in range(items)]


def vector_sum(table):
    for axis in ("seg", "stretch"):
        at = lax.axis_index(axis)
        bit = lax.axis_size(axis) // 2
        while bit:
            lo, hi = jnp.split(table, 2, axis=1)
            upper = (at & bit) != 0
            count = lax.axis_size(axis)
            got = lax.ppermute(jnp.where(upper, lo, hi), axis, [(i, i ^ bit) for i in range(count)])
            table = jnp.where(upper, hi, lo) + got
            bit //= 2
    return table


def grouped_columns(x, me, w):
    return jnp.concatenate([
        lax.dynamic_slice_in_dim(x, (me ^ m) * w, w, 1)
        for side in grad_orders()[1] for blocks in side for m in blocks], axis=1)


def body(
    stream_in, cotangent, previous_mix, previous_ffn, state_num, state_den, state_exp,
    gain_one, bias_one, gain_two, bias_two, mix_key, mix_value, mix_recept,
    time_decay, time_first, chan_mix_key, chan_mix_recept,
    att_key, att_value, att_recept, att_output, chan_key, chan_value, chan_recept,
):
    mine = lax.axis_index("seg")
    position = lax.axis_index("stretch")
    stretches = lax.axis_size("stretch")
    batches, _, length, width = stream_in.shape
    tokens = batches * length
    shard = att_key.shape[0]
    fshard = chan_value.shape[0]
    wide = chan_key.shape[1]
    aligned = shard % 128 == 0
    info = jnp.stack([mine, (position == 0).astype(jnp.int32), position])

    stream = stream_in.reshape(tokens, width)
    cot = cotangent.reshape(tokens, width)
    state = (state_num, state_den, state_exp)
    vectors = [gain_one, bias_one, gain_two, bias_two, mix_key, mix_value, mix_recept,
               time_decay, time_first, chan_mix_key, chan_mix_recept]

    v = Live()
    vec_rows = jnp.pad(jnp.stack(vectors), ((0, 16 - len(vectors)), (0, width - shard)))
    spots = {"k": 0, "v": shard, "vec": 2 * shard, "c": 2 * shard + 16, "r": 3 * shard + 16,
             "o": 4 * shard + 16}
    cut = shard // 2
    v.own_tm = pack(
        info, [(att_key, 0, shard), (att_value, 0, shard), (vec_rows, 0, 16), (chan_recept, 0, cut)],
        [(chan_recept, cut, cut), (att_recept, 0, shard), (att_output, 0, shard)], width)
    v.ck, v.cv = chan_key, chan_value
    v.last_in = stream_in[:, 0, length - 1]
    v.sync()
    v.one_tm = first_stage(v.own_tm)
    v.last_in = along(v.last_in, 1)
    v.tm0 = sibling({0: v.own_tm})
    v.sync()
    v.tm6 = second_stage(v.one_tm, v.one_tm)
    v.tm2 = sibling(v.one_tm)
    v.sync()

    v.one_ck = first_stage([v.ck])
    tm = {0: v.own_tm, **v.one_tm, **v.tm6, **v.tm0, **v.tm2, **sibling(v.tm6)}
    given = None
    if not aligned:
        given = lax.all_gather(jnp.stack(vectors), "seg", axis=1, tiled=True).astype(f32)
        given = jnp.pad(given, ((0, 5), (0, 0)))
    v.sums, v.vec, v.entry, v.kvr_in, v.kvr = time_in(
        info, stream, v.last_in, previous_mix, given, tm, spots, length, shard)
    v.everyone = lax.all_gather(v.sums, "stretch")
    v.tm = tm
    v.held_ck = {m: halves(p) for m, p in v.one_ck.items()}
    v.drop("own_tm", "one_tm", "tm6", "tm0", "tm2")
    v.sync()

    v.ck6 = second_stage(v.one_ck, v.held_ck)
    v.one_cv = first_stage([v.cv])
    v.ent, v.mean, v.log, edge_b, v.gated, v.wkv, v.rden, v.mid, v.xb = time_out(
        info, v.kvr, v.everyone, state, v.vec, stream, v.tm, spots, length, shard)
    v.edge_b = along(edge_b, 1)
    v.ck0 = sibling({0: [v.ck]})
    v.ck2 = sibling(v.one_ck)
    v.held_cv = {m: halves(p) for m, p in v.one_cv.items()}
    v.drop("held_ck")
    v.sync()

    v.cv6 = second_stage(v.one_cv, v.held_cv)
    ck = {0: [v.ck], **v.one_ck, **v.ck6, **v.ck0, **v.ck2, **sibling(v.ck6)}
    v.entry_b, v.f_in, v.near, v.far, v.act, v.frec = chan_in(
        info, v.xb, v.edge_b, previous_ffn, v.vec, v.tm, ck, spots, length, shard, fshard)
    v.cv0 = sibling({0: [v.cv]})
    v.cv2 = sibling(v.one_cv)
    v.all_ck = ck
    v.drop("held_cv", "ck", "one_ck", "ck6", "ck0", "ck2")
    v.sync()
    cv = {0: [v.cv], **v.one_cv, **v.cv6, **v.cv0, **v.cv2, **sibling(v.cv6)}
    v.far_sib = hop(v.far, 1)
    v.f_sib = hop(v.f_in, 1)
    v.block_out, v.d_fval, v.d_frec, v.dpre = chan_out(
        info, v.near, v.far, v.act, v.frec, v.mid, cot, cv, fshard)
    v.g_sib = hop(v.gated, 1)
    v.kvr_sib = hop(v.kvr_in, 1)
    v.drop("cv", "one_cv", "cv6", "cv0", "cv2", "act", "frec", "far")
    v.sync()

    def pairs(*arrays):
        if aligned:
            return [a for pair in arrays for a in pair]
        return [grouped_columns(a, mine, shard) for pair in arrays for a in pair]

    layout = "natural" if aligned else "groups"
    flat = tuple((j, None) for j in range(4))
    v.parts_cv = weight_grad(info, [v.near, v.far_sib, v.d_fval, hop(v.d_fval, 1)], [flat], "blocks", 6)
    v.drop("near", "far_sib", "d_fval")
    v.sync()

    v.got_cv = grad_first(v.parts_cv)
    v.head_b, v.sums_c, v.dxt, v.dxb = chan_back(
        info, v.dpre, v.d_frec, v.xb, v.entry_b, v.vec, v.tm, v.all_ck, spots, length, shard, wide)
    v.next_b = along(v.head_b, -1)
    dpre_sib = hop(v.dpre, 1)
    if aligned:
        v.parts_ck = weight_grad(
            info, [v.f_in, v.f_sib, v.dpre, dpre_sib], [((0, 0), (1, 0), (2, None), (3, None))], layout, 7)
    else:
        v.parts_ck = weight_grad(
            info, [*pairs((v.f_in[0], v.f_sib[0])), v.dpre, dpre_sib], [flat], layout, 7)
    v.dfrec_sib = hop(v.d_frec, 1)
    v.drop("all_ck", "dpre", "xb", "entry_b")
    v.sync()
    v.sends_cv = grad_sends(info, v.parts_cv, v.got_cv, 1)
    v.sync()

    v.last_cv = grad_second(v.parts_cv, v.sends_cv, 1)
    v.got_ck = grad_first(v.parts_ck)
    dent, v.sums_m, v.dmid, dbr, v.drec, v.gn = mid_back(
        info, v.dxt, v.dxb, v.next_b, v.mid, cot, v.vec, v.kvr, v.wkv, v.rden, v.ent, v.tm, spots,
        length, shard)
    v.back = lax.all_gather(jnp.concatenate([dent, v.ent[2 * batches :], v.head_b], axis=0), "stretch")
    dbr_sib = hop(dbr, 1)
    if aligned:
        v.parts_oc = weight_grad(
            info, [v.gated, v.g_sib, dbr, dbr_sib, v.f_in, v.f_sib, v.d_frec, v.dfrec_sib],
            [flat, ((4, 1), (5, 1), (6, None), (7, None))], layout, 6)
    else:
        xs = pairs((v.gated, v.g_sib), (v.f_in[1], v.f_sib[1]))
        v.parts_oc = weight_grad(
            info, [*xs, dbr, dbr_sib, v.d_frec, v.dfrec_sib],
            [((2 * k, None), (2 * k + 1, None), (4 + 2 * k, None), (5 + 2 * k, None)) for k in range(2)],
            layout, 6)
    v.drop("dxt", "dxb", "mid", "next_b", "rden", "head_b", "gated", "g_sib", "f_in", "f_sib", "d_frec",
           "dfrec_sib", "sends_cv")
    v.sync()
    v.part_cv = grad_finish(info, v.parts_cv, v.got_cv, v.last_cv, 1)
    v.sends_ck = grad_sends(info, v.parts_ck, v.got_ck, 1)
    v.drop("parts_cv", "got_cv", "last_cv")
    v.sync()

    v.z_cv = stretch_part(v.part_cv)
    v.last_ck = grad_second(v.parts_ck, v.sends_ck, 1)
    v.got_oc = grad_first(v.parts_oc)
    *v.grads, v.head_a, v.sums_t, v.extra, v.d_kvr, v.dxs, v.dxa = time_back(
        info, v.gn, v.wkv, v.kvr, v.ent, v.back, v.sums, state, v.drec, stream, v.entry, v.vec,
        v.tm, spots, length, shard)
    dkvr_sib = hop(v.d_kvr, 1)
    if aligned:
        v.parts_kvr = weight_grad(
            info, [v.kvr_in, v.kvr_sib, v.d_kvr, dkvr_sib],
            [tuple((j, k) for j in range(4)) for k in range(3)], layout, 7)
    else:
        xs = pairs(*[(v.kvr_in[k], v.kvr_sib[k]) for k in range(3)])
        v.parts_kvr = weight_grad(
            info, [*xs, v.d_kvr, dkvr_sib],
            [((2 * k, None), (2 * k + 1, None), (6, k), (7, k)) for k in range(3)], layout, 7)
    v.drop("gn", "wkv", "kvr", "ent", "sums", "drec", "entry", "tm", "kvr_in", "kvr_sib", "d_kvr",
           "sends_ck", "part_cv")
    v.sync()
    v.part_ck = grad_finish(info, v.parts_ck, v.got_ck, v.last_ck, 1)
    v.sends_oc = grad_sends(info, v.parts_oc, v.got_oc, 2)
    v.drop("parts_ck", "got_ck", "last_ck")
    v.sync()

    v.z_ck = stretch_part(v.part_ck)
    v.got_kvr = grad_first(v.parts_kvr)
    v.last_oc = grad_second(v.parts_oc, v.sends_oc, 2)
    next_a = along(v.head_a, -1)
    v.sums_i, v.grad_stream = in_back(info, v.dxs, v.dxa, next_a, v.dmid, stream, v.vec, length)
    v.out_cv = stretch_items(v.z_cv, 1)
    v.drop("dxs", "dxa", "dmid", "part_ck", "z_cv")
    v.sync()
    v.part_oc = grad_finish(info, v.parts_oc, v.got_oc, v.last_oc, 2)
    v.sends_kvr = grad_sends(info, v.parts_kvr, v.got_kvr, 3)
    v.drop("parts_oc", "got_oc", "last_oc")
    v.sync()
    v.z_oc = stretch_part(v.part_oc)
    v.last_kvr = grad_second(v.parts_kvr, v.sends_kvr, 3)
    v.small = vector_sum(jnp.concatenate([v.sums_i, v.sums_m, v.sums_t, v.extra, v.sums_c], axis=0))
    v.out_ck = stretch_items(v.z_ck, 1)
    v.drop("part_oc", "z_ck")
    v.sync()
    v.part_kvr = grad_finish(info, v.parts_kvr, v.got_kvr, v.last_kvr, 3)
    v.sync()
    out_kvr = stretch_items(stretch_part(v.part_kvr), 3)
    out_oc = stretch_items(v.z_oc, 2)
    out_cv, out_ck, small = v.out_cv, v.out_ck, v.small
    grad_previous_mix = lax.all_gather(v.head_a, "stretch")[0]
    block_out, grad_stream = v.block_out, v.grad_stream

    shape = stream_in.shape
    return (
        block_out.reshape(shape), grad_stream.reshape(shape), *[small[i] for i in range(11)],
        *out_kvr, out_oc[0], *out_ck, *out_cv, out_oc[1],
        *v.grads[:3], grad_previous_mix[:, None], v.grads[3], v.mean, v.log,
    )


def solution(mesh):
    rows = P(None, "seg", "stretch", None)
    state = P(None, "seg", None)
    both = P(("seg", "stretch"))
    table = P(("seg", "stretch"), None)
    return jax.shard_map(
        body,
        mesh=mesh,
        in_specs=(rows,) * 2 + (state,) * 5 + (P("seg"),) * 11 + (P("seg", None),) * 7,
        out_specs=(rows,) * 2 + (both,) * 11 + (table,) * 7 + (state,) * 7,
        check_vma=False,
    )
```

time: 629 us -> 402 us (0.64)
  the two profiles are of different devices: /device:TPU:0 before, /device:TPU:9 now
where the time goes in v2:
time: 402 us; the launch traced here: 397 us
  Pallas kernels  133 us (33%)
  waiting for transfers between devices  117 us (29%)
  starting transfers between devices  75.8 us (19%)
  blocking collectives  34 us (8%)
  local copies, waits for them, and re-layouts  17.4 us (4%)
  between operations  14.7 us (4%)
  other arithmetic  5.7 us (1%)
    pallas_call x20, Pallas kernels, call(): pl.pallas_call(kernel, out_shape=[jax.ShapeDtypeStruct(s, d) for s, d in...  130 us
    ppermute x57, waiting for transfers between devices, hop(): return lax.ppermute(value, 'seg', [(i, i ^ bit) for i in range(count)])  94.2 us
    ppermute x57, starting transfers between devices, hop(): return lax.ppermute(value, 'seg', [(i, i ^ bit) for i in range(count)])  52.7 us
    reduce_scatter x4, waiting for transfers between devices, stretch_part(): return lax.psum_scatter(part, 'stretch', scatter_dimension=0, tiled=True)  15.4 us
    ppermute x4, starting transfers between devices, along(): lax.ppermute(value, 'stretch', [(i, i + steps) for i in range(first, last)])  12.6 us
    all_gather x1, blocking collectives, body(): v.everyone = lax.all_gather(v.sums, 'stretch')  11.6 us
    all_gather x1, blocking collectives, body(): lax.all_gather(jnp.concatenate([dent, v.ent[2 * batches:], v.head_b], axi...  11.4 us
    all_gather x1, blocking collectives, body(): grad_previous_mix = lax.all_gather(v.head_a, 'stretch')[0]  10.9 us
  transfers between devices with their start and end apart: 70, of which 33 were waited for; matrix products, arithmetic and copies ran while one was open for 3% of the time, Pallas kernels for 25%

profile of v2, /device:TPU:9, one launch (start us, length us, event | category | flops | bytes accessed | tf_op | source)
XLA Modules:
  0.0 397.0 jit_solution(15356500315188757707)
XLA Ops:
  8.0 1.5 stack.67
  10.2 2.4 shard_map.448
  15.4 1.5 collective-permute-start.5
  16.9 3.2 collective-permute-start
  20.1 1.4 collective-permute-done.refs_1_
  21.8 6.7 %collective-permute-done.2.refs_7_.refs_11_.refs_8_.refs_9_.refs_14_.refs_17_ = bf16[320,1024]{1,0:T(8,128)(2,1)S(1)} collective-permute-done((bf16[320,1024]{1,0:T(8,128)(2,1)}, bf16[320,1024]{1,0:T(8,128)(2,1)S(1)}, u32[]{:S(2)}, u32[]{:S(2)}) %collective-permute-start.2) | collective-permute-done | bytes 655392 | tf_op jit(solution)/shard_map/ppermute | solution.py:21
  28.5 2.7 collective-permute-start.6
  31.2 12.9 %collective-permute-done.4.refs_9_.refs_13_.refs_10_.refs_11_.refs_16_.refs_19_ = bf16[320,1024]{1,0:T(8,128)(2,1)S(1)} collective-permute-done((bf16[320,1024]{1,0:T(8,128)(2,1)}, bf16[320,1024]{1,0:T(8,128)(2,1)S(1)}, u32[]{:S(2)}, u32[]{:S(2)}) %collective-permute-start.4) | collective-permute-done | bytes 655392 | tf_op jit(solution)/shard_map/ppermute | solution.py:21
  44.1 2.2 collective-permute-start.8
  51.0 13.8 %collective-permute-done.12.refs_11_.refs_15_.refs_12_.refs_13_.refs_18_.refs_21_ = bf16[320,1024]{1,0:T(8,128)(2,1)} collective-permute-done((bf16[320,1024]{1,0:T(8,128)(2,1)S(1)}, bf16[320,1024]{1,0:T(8,128)(2,1)}, u32[]{:S(2)}, u32[]{:S(2)}) %collective-permute-start.12) | collective-permute-done | bytes 655392 | tf_op jit(solution)/shard_map/ppermute | solution.py:21
  66.7 1.8 collective-permute-start.13
  69.1 2.4 collective-permute-done.14.refs_19_.refs_23_.refs_20_.refs_21_.refs_26_.refs_29_
  71.6 8.6 %shard_map.449 = (f32[6,1024]{1,0:T(8,128)}, f32[16,1024]{1,0:T(8,128)}, f32[2,1024]{1,0:T(2,128)}, bf16[3,256,1024]{2,1,0:T(8,128)(2,1)}, f32[3,256,1024]{2,1,0:T(8,128)}) custom-call(s32[3]{0:T(128)} %pad_add_fusion.refs_0_, bf16[2,1024]{1,0:T(2,128)(2,1)} %copy-done.51, f32[2,1,1024]{2,1,0:T(1,128)} %refs_2_.3, bf16[256,1024]{1,0:T(8,128)(2,1)} %bitcast.52, ...), custom_call_target="tpu_custom_call" | custom-call | bytes 9000 | tf_op jit(solution)/shard_map/pallas_call | solution.py:170
  80.2 11.6 %all-gather.3.refs_1_ = f32[4,6,1024]{2,1,0:T(8,128)} all-gather(f32[1,6,1024]{2,1,0:T(8,128)} %bitcast.59), channel_id=2, replica_groups=mesh['seg'=8,'stretch'=4] {'stretch'}, dimensions={0}, use_global_device_ids=true | all-gather | bytes 122880 | tf_op jit(solution)/shard_map/all_gather | solution.py:1053
  91.8 1.9 slice.98
  93.7 1.9 slice.99
  96.5 8.2 %shard_map.450 = (f32[6,1024]{1,0:T(8,128)}, f32[2,1,1024]{2,1,0:T(1,128)}, f32[2,1,1024]{2,1,0:T(1,128)}, f32[2,1024]{1,0:T(2,128)}, bf16[256,1024]{1,0:T(8,128...) custom-call(s32[3]{0:T(128)} %pad_add_fusion.refs_0_, ...), custom_call_target="tpu_custom_call" | custom-call | bytes 7000 | tf_op jit(solution)/shard_map/pallas_call | solution.py:170
  104.7 2.9 collective-permute-start.22
  107.6 3.6 collective-permute-start.17
  111.3 3.0 collective-permute-start.19
  114.3 3.0 collective-permute-done.23.refs_8_
  118.5 1.9 slice.100
  120.3 1.9 slice.101
  122.2 6.5 %collective-permute-done.20.refs_24_.refs_25_ = bf16[64,4096]{1,0:T(8,128)(2,1)S(1)} collective-permute-done((bf16[64,4096]{1,0:T(8,128)(2,1)}, bf16[64,4096]{1,0:T(8,128)(2,1)S(1)}, u32[]{:S(2)}, u32[]{:S(2)}) %collective-permute-start.20) | collective-permute-done | bytes 524320 | tf_op jit(solution)/shard_map/ppermute | solution.py:21
  128.7 4.2 %collective-permute-start.25 = (bf16[64,4096]{1,0:T(8,128)(2,1)S(1)}, bf16[64,4096]{1,0:T(8,128)(2,1)S(1)}, u32[]{:S(2)}, u32[]{:S(2)}) collective-permute-start(bf16[64,4096]{1,0:T(8,128)(2,1)S(1)} %collective-permute-done.20.refs_24_.refs_25_), channel_id=1, source_target_pairs={{0,4},{4,0},{8,12},{12,8},{16,20},{20,16},{24,28},{28,24},{1,5},{5... | collective-permute-start | bytes 1572872 | tf_op jit(solution)/shard_map/ppermute | solution.py:21
  137.4 11.1 %shard_map.451 = (f32[2,1024]{1,0:T(2,128)}, bf16[2,256,1024]{2,1,0:T(8,128)(2,1)}, bf16[256,2048]{1,0:T(8,128)(2,1)}, bf16[256,2048]{1,0:T(8,128)(2,1)}, bf16[2...) custom-call(s32[3]{0:T(128)} %pad_add_fusion.refs_0_, f32[2,1024]{1,0:T(2,128)} %copy-done.42, f32[2,1,1024]{2,1,0:T(1,128)} %refs_2_.5, ...), custom_call_target="tpu_custom_call" | custom-call | bytes 11000 | tf_op jit(solution)/shard_map/pallas_call | solution.py:170
  151.8 3.6 collective-permute-done.32.refs_15_
  155.5 3.6 collective-permute-done.33.refs_16_
  159.9 13.0 %shard_map.452 = (bf16[256,1024]{1,0:T(8,128)(2,1)}, bf16[256,1024]{1,0:T(8,128)(2,1)}, bf16[256,1024]{1,0:T(8,128)(2,1)}, bf16[256,4096]{1,0:T(8,128)(2,1)}) custom-call(s32[3]{0:T(128)} %pad_add_fusion.refs_0_, bf16[256,2048]{1,0:T(8,128)(2,1)} %get-tuple-element.896.refs_1_, bf16[256,2048]{1,0:T(8,128)(2,1)} %get-tuple-element.824.refs_2_, ...), custom_call_target="tpu_custom_call" | custom-call | bytes 13000 | tf_op jit(solution)/shard_map/pallas_call | solution.py:170
  173.2 2.1 collective-permute-done.38.refs_4_
  175.3 6.0 %shard_map.453 = (bf16[2,512,512]{2,1,0:T(8,128)(2,1)}, bf16[2,512,512]{2,1,0:T(8,128)(2,1)}, bf16[2,512,512]{2,1,0:T(8,128)(2,1)}, bf16[2,512,512]{2,1,0:T(8,128)(2,1)}) custom-call(s32[3]{0:T(128)} %pad_add_fusion.refs_0_, bf16[256,2048]{1,0:T(8,128)(2,1)} %get-tuple-element.896.refs_1_, bf16[256,2048]{1,0:T(8,128)(2,1)} %collective-permute-done.35.refs_2_, ...), custom_call_target="tpu_custom_call" | custom-call | bytes 6000 | tf_op jit(solution)/shard_map/pallas_call | solution.py:170
  184.5 11.1 %shard_map.454 = (f32[2,1024]{1,0:T(2,128)}, f32[2,1024]{1,0:T(2,128)}, f32[256,1024]{1,0:T(8,128)}, f32[256,1024]{1,0:T(8,128)}) custom-call(s32[3]{0:T(128)} %pad_add_fusion.refs_0_, f32[2,1024]{1,0:T(2,128)} %get-tuple-element.926.refs_1_, f32[16,1024]{1,0:T(8,128)} %get-tuple-element.1240.refs_5_.refs_3_.refs_2_.refs_8_, ...), custom_call_target="tpu_custom_call" | custom-call | bytes 11000 | tf_op jit(solution)/shard_map/pallas_call | solution.py:170
  195.6 3.4 collective-permute-start.42
  199.0 6.6 %shard_map.455 = (bf16[2,128,2048]{2,1,0:T(8,128)(2,1)}, bf16[2,128,2048]{2,1,0:T(8,128)(2,1)}, bf16[2,128,2048]{2,1,0:T(8,128)(2,1)}, bf16[2,128,2048]{2,1,0:T(8,128)(2,1)}) custom-call(s32[3]{0:T(128)} %pad_add_fusion.refs_0_, bf16[2,256,1024]{2,1,0:T(8,128)(2,1)} %get-tuple-element.1082.refs_1_.refs_5_, bf16[2,256,1024]{2,1,0:T(8,128)(2,1)} %copy-done.17, ...), custom_call_target="tpu_custom_call" | custom-call | bytes 7000 | tf_op jit(solution)/shard_map/pallas_call | solution.py:170
  207.3 3.1 shard_map.456
  212.5 8.6 %shard_map.457 = (f32[4,1024]{1,0:T(4,128)}, f32[2,1024]{1,0:T(2,128)}, f32[256,1024]{1,0:T(8,128)}, bf16[256,1024]{1,0:T(8,128)(2,1)}, bf16[256,1024]{1,0:T(8,128)(2,1)}, /*index=5*/f32[256,1024]{1,0:T(8,128)}) custom-call(s32[3]{0:T(128)} %pad_add_fusion.refs_0_, f32[2,1024]{1,0:T(2,128)} %copy-done.43, ...), custom_call_target="tpu_custom_call" | custom-call | bytes 9000 | tf_op jit(solution)/shard_map/pallas_call | solution.py:170
  221.1 1.7 collective-permute-start.48
  225.8 11.4 %all-gather.1 = f32[32,1024]{1,0:T(8,128)} all-gather(f32[8,1024]{1,0:T(8,128)S(1)} %pad_maximum_fusion), channel_id=3, replica_groups=mesh['seg'=8,'stretch'=4] {'stretch'}, dimensions={0}, use_global_device_ids=true | all-gather | bytes 163840 | tf_op jit(solution)/shard_map/all_gather | solution.py:1122
  238.0 5.2 %shard_map.458 = (bf16[2,256,512]{2,1,0:T(8,128)(2,1)}, bf16[2,256,512]{2,1,0:T(8,128)(2,1)}, bf16[2,256,512]{2,1,0:T(8,128)(2,1)}, bf16[2,256,512]{2,1,0:T(8,128)(2,1)}) custom-call(s32[3]{0:T(128)} %pad_add_fusion.refs_0_, bf16[256,1024]{1,0:T(8,128)(2,1)} %get-tuple-element.1079.refs_1_, bf16[256,1024]{1,0:T(8,128)(2,1)} %collective-permute-done.36.refs_2_, ...), custom_call_target="tpu_custom_call" | custom-call | bytes 6000 | tf_op jit(solution)/shard_map/pallas_call | solution.py:170
  243.3 3.3 collective-permute-done.46.refs_3_
  247.9 3.1 shard_map.460
  251.1 3.8 shard_map.459
  255.2 13.3 %shard_map.461 = (f32[2,1,1024]{2,1,0:T(1,128)}, f32[2,1,1024]{2,1,0:T(1,128)}, f32[2,1,1024]{2,1,0:T(1,128)}, f32[2,1,1024]{2,1,0:T(1,128)}, f32[2,1024]{1,0:T(...) custom-call(s32[3]{0:T(128)} %pad_add_fusion.refs_0_, ...), custom_call_target="tpu_custom_call" | custom-call | bytes 14000 | tf_op jit(solution)/shard_map/pallas_call | solution.py:170
  268.5 2.4 collective-permute-start.53
  275.3 6.8 %shard_map.462 = (bf16[2,384,512]{2,1,0:T(8,128)(2,1)}, bf16[2,384,512]{2,1,0:T(8,128)(2,1)}, bf16[2,384,512]{2,1,0:T(8,128)(2,1)}, bf16[2,384,512]{2,1,0:T(8,128)(2,1)}) custom-call(s32[3]{0:T(128)} %pad_add_fusion.refs_0_, bf16[3,256,1024]{2,1,0:T(8,128)(2,1)} %get-tuple-element.1187.refs_1_, bf16[3,256,1024]{2,1,0:T(8,128)(2,1)} %collective-permute-done.37.refs_2_, ...), custom_call_target="tpu_custom_call" | custom-call | bytes 7000 | tf_op jit(solution)/shard_map/pallas_call | solution.py:170
  282.1 2.5 collective-permute-done.49.refs_2_
  284.6 11.1 %collective-permute-done.51.refs_3_ = bf16[128,2048]{1,0:T(8,128)(2,1)S(1)} collective-permute-done((bf16[128,2048]{1,0:T(8,128)(2,1)}, bf16[128,2048]{1,0:T(8,128)(2,1)S(1)}, u32[]{:S(2)}, u32[]{:S(2)}) %collective-permute-start.51) | collective-permute-done | bytes 524320 | tf_op jit(solution)/shard_map/ppermute | solution.py:21
  296.0 2.7 shard_map.464
  298.7 3.8 shard_map.463
  305.6 3.1 collective-permute-start.56
  310.9 5.6 %shard_map.465 = (f32[2,1024]{1,0:T(2,128)}, bf16[256,1024]{1,0:T(8,128)(2,1)}) custom-call(s32[3]{0:T(128)} %pad_add_fusion.refs_0_, f32[2,1024]{1,0:T(2,128)} %copy-done.44, f32[16,1024]{1,0:T(8,128)} %get-tuple-element.1240.refs_5_.refs_3_.refs_2_.refs_8_, f32[256,1024]{1,0:T(8,128)} %get-tuple-element.1241.refs_3_, ...), custom_call_target="tpu_custom_call" | custom-call | bytes 6000 | tf_op jit(solution)/shard_map/pallas_call | solution.py:170
  316.4 10.8 %collective-permute-done.57.refs_3_ = bf16[256,512]{1,0:T(8,128)(2,1)S(1)} collective-permute-done((bf16[256,512]{1,0:T(8,128)(2,1)}, bf16[256,512]{1,0:T(8,128)(2,1)S(1)}, u32[]{:S(2)}, u32[]{:S(2)}) %collective-permute-start.57) | collective-permute-done | bytes 262176 | tf_op jit(solution)/shard_map/ppermute | solution.py:21
  328.6 2.9 shard_map.467
  331.6 3.1 shard_map.466
  336.2 1.6 collective-permute-done.61
  339.1 1.6 collective-permute-done.62
  340.7 4.3 %collective-permute-start.63 = (f32[11,128]{1,0:T(8,128)S(1)}, f32[11,128]{1,0:T(8,128)S(1)}, u32[]{:S(2)}, u32[]{:S(2)}) collective-permute-start(f32[11,128]{1,0:T(8,128)S(1)} %slice_select_fusion.4), channel_id=1, source_target_pairs={{0,4},{4,0},{8,12},{12,8},{16,20},{20,16},{24,28},{28,24},{1,5},{5... | collective-permute-start | bytes 16904 | tf_op jit(solution)/shard_map/ppermute | solution.py:991
  345.9 2.1 collective-permute-start.64
  352.4 5.7 %collective-permute-done.59.refs_3_ = bf16[384,512]{1,0:T(8,128)(2,1)S(1)} collective-permute-done((bf16[384,512]{1,0:T(8,128)(2,1)S(1)}, bf16[384,512]{1,0:T(8,128)(2,1)S(1)}, u32[]{:S(2)}, u32[]{:S(2)}) %collective-permute-start.59) | collective-permute-done | bytes 393248 | tf_op jit(solution)/shard_map/ppermute | solution.py:21
  358.4 3.6 reduce-scatter.9.cloned.1.call-done
  362.0 3.5 shard_map.468
  365.5 10.9 %all-gather.4 = f32[4,2,1024]{2,1,0:T(2,128)S(1)} all-gather(f32[1,2,1024]{2,1,0:T(2,128)S(1)} %bitcast.60), channel_id=4, replica_groups=mesh['seg'=8,'stretch'=4] {'stretch'}, dimensions={0}, use_global_device_ids=true | all-gather | bytes 40960 | tf_op jit(solution)/shard_map/all_gather | solution.py:1189
  378.4 10.4 %reduce-scatter.11.cloned.1.call-done = bf16[96,1024]{1,0:T(8,128)(2,1)} async-done(((bf16[384,1024]{1,0:T(8,128)(2,1)}), bf16[96,1024]{1,0:T(8,128)(2,1)}) %reduce-scatter.11.cloned.1.call-update) | async-done | bytes 196624 | tf_op jit(solution)/shard_map/reduce_scatter | solution.py:975
  388.8 1.7 slice_convert_fusion
  (245 shorter events, 56.3 us)
Async XLA Ops:
  7.2 288.7 %reduce-scatter.5.cloned.1.call-start = ((), (), s32[]{:S(2)}) async-start(), calls=%async_computation.4 | async-start | bytes 1310720 | tf_op jit(solution)/shard_map/reduce_scatter | solution.py:975
  12.6 15.9 %collective-permute-start.2 = (bf16[320,1024]{1,0:T(8,128)(2,1)}, bf16[320,1024]{1,0:T(8,128)(2,1)S(1)}, u32[]{:S(2)}, u32[]{:S(2)}) collective-permute-start(bf16[320,1024]{1,0:T(8,128)(2,1)} %get-tuple-element.1154.refs_5_.refs_9_.refs_6_.refs_7_.refs_12_.refs_15_), channel_id=1, source_target_pairs={{0,8},{4,12},{8,0},{12,4},{16,24},{20,28},{24,16},{28,20},{1,9},{5... | collective-permute-start | bytes 1966088 | tf_op jit(solution)/shard_map/ppermute | solution.py:21
  13.9 30.2 %collective-permute-start.1 = (bf16[336,1024]{1,0:T(8,128)(2,1)}, bf16[336,1024]{1,0:T(8,128)(2,1)S(1)}, u32[]{:S(2)}, u32[]{:S(2)}) collective-permute-start(bf16[336,1024]{1,0:T(8,128)(2,1)} %get-tuple-element.1153.refs_4_.refs_8_.refs_5_.refs_6_.refs_11_.refs_14_), channel_id=1, source_target_pairs={{0,8},{4,12},{8,0},{12,4},{16,24},{20,28},{24,16},{28,20},{1,9},{5... | collective-permute-start | bytes 2064392 | tf_op jit(solution)/shard_map/ppermute | solution.py:21
  14.1 30.0 %collective-permute-start.3 = (bf16[336,1024]{1,0:T(8,128)(2,1)}, bf16[336,1024]{1,0:T(8,128)(2,1)S(1)}, u32[]{:S(2)}, u32[]{:S(2)}) collective-permute-start(bf16[336,1024]{1,0:T(8,128)(2,1)} %get-tuple-element.1153.refs_4_.refs_8_.refs_5_.refs_6_.refs_11_.refs_14_), channel_id=1, source_target_pairs={{0,16},{4,20},{8,24},{12,28},{16,0},{20,4},{24,8},{28,12},{1,17},{... | collective-permute-start | bytes 2064392 | tf_op jit(solution)/shard_map/ppermute | solution.py:21
  15.4 28.8 %collective-permute-start.5 = (bf16[336,1024]{1,0:T(8,128)(2,1)}, bf16[336,1024]{1,0:T(8,128)(2,1)S(1)}, u32[]{:S(2)}, u32[]{:S(2)}) collective-permute-start(bf16[336,1024]{1,0:T(8,128)(2,1)} %get-tuple-element.1153.refs_4_.refs_8_.refs_5_.refs_6_.refs_11_.refs_14_), channel_id=1, source_target_pairs={{0,4},{4,0},{8,12},{12,8},{16,20},{20,16},{24,28},{28,24},{1,5},{5... | collective-permute-start | bytes 2064392 | tf_op jit(solution)/shard_map/ppermute | solution.py:21
  16.9 4.6 %collective-permute-start = (bf16[2,1024]{1,0:T(2,128)(2,1)S(1)}, bf16[2,1024]{1,0:T(2,128)(2,1)S(1)}, u32[]{:S(2)}, u32[]{:S(2)}) collective-permute-start(bf16[2,1024]{1,0:T(2,128)(2,1)S(1)} %bitcast.61), channel_id=1, source_target_pairs={{0,1},{1,2},{2,3},{4,5},{5,6},{6,7},{8,9},{9,10},{10,11},{12,13},{... | collective-permute-start | bytes 12296 | tf_op jit(solution)/shard_map/ppermute | solution.py:27
  21.5 22.6 %collective-permute-start.4 = (bf16[320,1024]{1,0:T(8,128)(2,1)}, bf16[320,1024]{1,0:T(8,128)(2,1)S(1)}, u32[]{:S(2)}, u32[]{:S(2)}) collective-permute-start(bf16[320,1024]{1,0:T(8,128)(2,1)} %get-tuple-element.1154.refs_5_.refs_9_.refs_6_.refs_7_.refs_12_.refs_15_), channel_id=1, source_target_pairs={{0,16},{4,20},{8,24},{12,28},{16,0},{20,4},{24,8},{28,12},{1,17},{... | collective-permute-start | bytes 1966088 | tf_op jit(solution)/shard_map/ppermute | solution.py:21
  28.5 15.6 %collective-permute-start.6 = (bf16[320,1024]{1,0:T(8,128)(2,1)}, bf16[320,1024]{1,0:T(8,128)(2,1)S(1)}, u32[]{:S(2)}, u32[]{:S(2)}) collective-permute-start(bf16[320,1024]{1,0:T(8,128)(2,1)} %get-tuple-element.1154.refs_5_.refs_9_.refs_6_.refs_7_.refs_12_.refs_15_), channel_id=1, source_target_pairs={{0,4},{4,0},{8,12},{12,8},{16,20},{20,16},{24,28},{28,24},{1,5},{5... | collective-permute-start | bytes 1966088 | tf_op jit(solution)/shard_map/ppermute | solution.py:21
  44.1 4.3 %collective-permute-start.8 = (bf16[320,1024]{1,0:T(8,128)(2,1)S(1)}, bf16[320,1024]{1,0:T(8,128)(2,1)S(1)}, u32[]{:S(2)}, u32[]{:S(2)}) collective-permute-start(bf16[320,1024]{1,0:T(8,128)(2,1)S(1)} %collective-permute-done.2.refs_7_.refs_11_.refs_8_.refs_9_.refs_14_.refs_17_), channel_id=1, source_target_pairs={{0,4},{4,0},{8,12},{12,8},{16,20},{20,16},{24,28},{28,24},{1,5},{5... | collective-permute-start | bytes 1966088 | tf_op jit(solution)/shard_map/ppermute | solution.py:21
  46.4 18.4 %collective-permute-start.7 = (bf16[336,1024]{1,0:T(8,128)(2,1)S(1)}, bf16[336,1024]{1,0:T(8,128)(2,1)S(1)}, u32[]{:S(2)}, u32[]{:S(2)}) collective-permute-start(bf16[336,1024]{1,0:T(8,128)(2,1)S(1)} %collective-permute-done.1.refs_6_.refs_10_.refs_7_.refs_8_.refs_13_.refs_16_), channel_id=1, source_target_pairs={{0,4},{4,0},{8,12},{12,8},{16,20},{20,16},{24,28},{28,24},{1,5},{5... | collective-permute-start | bytes 2064392 | tf_op jit(solution)/shard_map/ppermute | solution.py:21
  46.4 18.3 %collective-permute-start.9 = (bf16[336,1024]{1,0:T(8,128)(2,1)S(1)}, bf16[336,1024]{1,0:T(8,128)(2,1)S(1)}, u32[]{:S(2)}, u32[]{:S(2)}) collective-permute-start(bf16[336,1024]{1,0:T(8,128)(2,1)S(1)} %collective-permute-done.3.refs_8_.refs_12_.refs_9_.refs_10_.refs_15_.refs_18_), channel_id=1, source_target_pairs={{0,4},{4,0},{8,12},{12,8},{16,20},{20,16},{24,28},{28,24},{1,5},{5... | collective-permute-start | bytes 2064392 | tf_op jit(solution)/shard_map/ppermute | solution.py:21
  46.9 17.9 %collective-permute-start.11 = (bf16[336,1024]{1,0:T(8,128)(2,1)S(1)}, bf16[336,1024]{1,0:T(8,128)(2,1)}, u32[]{:S(2)}, u32[]{:S(2)}) collective-permute-start(bf16[336,1024]{1,0:T(8,128)(2,1)S(1)} %collective-permute-done.1.refs_6_.refs_10_.refs_7_.refs_8_.refs_13_.refs_16_), channel_id=1, source_target_pairs={{0,16},{4,20},{8,24},{12,28},{16,0},{20,4},{24,8},{28,12},{1,17},{... | collective-permute-start | bytes 2064392 | tf_op jit(solution)/shard_map/ppermute | solution.py:21
  48.5 16.3 %collective-permute-start.12 = (bf16[320,1024]{1,0:T(8,128)(2,1)S(1)}, bf16[320,1024]{1,0:T(8,128)(2,1)}, u32[]{:S(2)}, u32[]{:S(2)}) collective-permute-start(bf16[320,1024]{1,0:T(8,128)(2,1)S(1)} %collective-permute-done.4.refs_9_.refs_13_.refs_10_.refs_11_.refs_16_.refs_19_), channel_id=1, source_target_pairs={{0,8},{4,12},{8,0},{12,4},{16,24},{20,28},{24,16},{28,20},{1,9},{5... | collective-permute-start | bytes 1966088 | tf_op jit(solution)/shard_map/ppermute | solution.py:21
  64.8 27.0 %collective-permute-start.15 = (bf16[128,4096]{1,0:T(8,128)(2,1)}, bf16[128,4096]{1,0:T(8,128)(2,1)}, u32[]{:S(2)}, u32[]{:S(2)}) collective-permute-start(bf16[128,4096]{1,0:T(8,128)(2,1)} %refs_22_), channel_id=1, source_target_pairs={{0,8},{4,12},{8,0},{12,4},{16,24},{20,28},{24,16},{28,20},{1,9},{5... | collective-permute-start | bytes 3145736 | tf_op jit(solution)/shard_map/ppermute | solution.py:21
  66.1 27.6 %collective-permute-start.16 = (bf16[128,4096]{1,0:T(8,128)(2,1)}, bf16[128,4096]{1,0:T(8,128)(2,1)}, u32[]{:S(2)}, u32[]{:S(2)}) collective-permute-start(bf16[128,4096]{1,0:T(8,128)(2,1)} %refs_22_), channel_id=1, source_target_pairs={{0,16},{4,20},{8,24},{12,28},{16,0},{20,4},{24,8},{28,12},{1,17},{... | collective-permute-start | bytes 3145736 | tf_op jit(solution)/shard_map/ppermute | solution.py:21
  66.7 4.8 %collective-permute-start.13 = (bf16[336,1024]{1,0:T(8,128)(2,1)}, bf16[336,1024]{1,0:T(8,128)(2,1)}, u32[]{:S(2)}, u32[]{:S(2)}) collective-permute-start(bf16[336,1024]{1,0:T(8,128)(2,1)} %collective-permute-done.11.refs_10_.refs_14_.refs_11_.refs_12_.refs_17_.refs_20_), channel_id=1, source_target_pairs={{0,4},{4,0},{8,12},{12,8},{16,20},{20,16},{24,28},{28,24},{1,5},{5... | collective-permute-start | bytes 2064392 | tf_op jit(solution)/shard_map/ppermute | solution.py:21
  68.5 3.0 collective-permute-start.14
  95.6 21.7 %collective-permute-start.23 = (bf16[512,1024]{1,0:T(8,128)(2,1)}, bf16[512,1024]{1,0:T(8,128)(2,1)}, u32[]{:S(2)}, u32[]{:S(2)}) collective-permute-start(bf16[512,1024]{1,0:T(8,128)(2,1)} %refs_7_), channel_id=1, source_target_pairs={{0,8},{4,12},{8,0},{12,4},{16,24},{20,28},{24,16},{28,20},{1,9},{5... | collective-permute-start | bytes 3145736 | tf_op jit(solution)/shard_map/ppermute | solution.py:21
  95.8 22.1 %collective-permute-start.24 = (bf16[512,1024]{1,0:T(8,128)(2,1)}, bf16[512,1024]{1,0:T(8,128)(2,1)}, u32[]{:S(2)}, u32[]{:S(2)}) collective-permute-start(bf16[512,1024]{1,0:T(8,128)(2,1)} %refs_7_), channel_id=1, source_target_pairs={{0,16},{4,20},{8,24},{12,28},{16,0},{20,4},{24,8},{28,12},{1,17},{... | collective-permute-start | bytes 3145736 | tf_op jit(solution)/shard_map/ppermute | solution.py:21
  104.7 6.6 %collective-permute-start.22 = (f32[2,1024]{1,0:T(2,128)}, f32[2,1024]{1,0:T(2,128)S(1)}, u32[]{:S(2)}, u32[]{:S(2)}) collective-permute-start(f32[2,1024]{1,0:T(2,128)} %get-tuple-element.752), channel_id=1, source_target_pairs={{0,1},{1,2},{2,3},{4,5},{5,6},{6,7},{8,9},{9,10},{10,11},{12,13},{... | collective-permute-start | bytes 24584 | tf_op jit(solution)/shard_map/ppermute | solution.py:27
  107.6 21.1 %collective-permute-start.17 = (bf16[128,4096]{1,0:T(8,128)(2,1)S(1)}, bf16[128,4096]{1,0:T(8,128)(2,1)S(1)}, u32[]{:S(2)}, u32[]{:S(2)}) collective-permute-start(bf16[128,4096]{1,0:T(8,128)(2,1)S(1)} %copy-done.11), channel_id=1, source_target_pairs={{0,4},{4,0},{8,12},{12,8},{16,20},{20,16},{24,28},{28,24},{1,5},{5... | collective-permute-start | bytes 3145736 | tf_op jit(solution)/shard_map/ppermute | solution.py:21
  111.2 17.5 %collective-permute-start.18 = (bf16[128,4096]{1,0:T(8,128)(2,1)}, bf16[128,4096]{1,0:T(8,128)(2,1)S(1)}, u32[]{:S(2)}, u32[]{:S(2)}) collective-permute-start(bf16[128,4096]{1,0:T(8,128)(2,1)} %collective-permute-done.15.refs_22_.refs_23_), channel_id=1, source_target_pairs={{0,4},{4,0},{8,12},{12,8},{16,20},{20,16},{24,28},{28,24},{1,5},{5... | collective-permute-start | bytes 3145736 | tf_op jit(solution)/shard_map/ppermute | solution.py:21
  111.3 17.4 %collective-permute-start.19 = (bf16[128,4096]{1,0:T(8,128)(2,1)}, bf16[128,4096]{1,0:T(8,128)(2,1)}, u32[]{:S(2)}, u32[]{:S(2)}) collective-permute-start(bf16[128,4096]{1,0:T(8,128)(2,1)} %collective-permute-done.16.refs_23_.refs_24_), channel_id=1, source_target_pairs={{0,4},{4,0},{8,12},{12,8},{16,20},{20,16},{24,28},{28,24},{1,5},{5... | collective-permute-start | bytes 3145736 | tf_op jit(solution)/shard_map/ppermute | solution.py:21
  117.3 11.4 %collective-permute-start.20 = (bf16[64,4096]{1,0:T(8,128)(2,1)}, bf16[64,4096]{1,0:T(8,128)(2,1)S(1)}, u32[]{:S(2)}, u32[]{:S(2)}) collective-permute-start(bf16[64,4096]{1,0:T(8,128)(2,1)} %slice.98), channel_id=1, source_target_pairs={{0,16},{4,20},{8,24},{12,28},{16,0},{20,4},{24,8},{28,12},{1,17},{... | collective-permute-start | bytes 1572872 | tf_op jit(solution)/shard_map/ppermute | solution.py:21
  117.9 10.8 %collective-permute-start.21 = (bf16[64,4096]{1,0:T(8,128)(2,1)}, bf16[64,4096]{1,0:T(8,128)(2,1)S(1)}, u32[]{:S(2)}, u32[]{:S(2)}) collective-permute-start(bf16[64,4096]{1,0:T(8,128)(2,1)} %slice.99), channel_id=1, source_target_pairs={{0,8},{4,12},{8,0},{12,4},{16,24},{20,28},{24,16},{28,20},{1,9},{5... | collective-permute-start | bytes 1572872 | tf_op jit(solution)/shard_map/ppermute | solution.py:21
  128.7 5.8 %collective-permute-start.25 = (bf16[64,4096]{1,0:T(8,128)(2,1)S(1)}, bf16[64,4096]{1,0:T(8,128)(2,1)S(1)}, u32[]{:S(2)}, u32[]{:S(2)}) collective-permute-start(bf16[64,4096]{1,0:T(8,128)(2,1)S(1)} %collective-permute-done.20.refs_24_.refs_25_), channel_id=1, source_target_pairs={{0,4},{4,0},{8,12},{12,8},{16,20},{20,16},{24,28},{28,24},{1,5},{5... | collective-permute-start | bytes 1572872 | tf_op jit(solution)/shard_map/ppermute | solution.py:21
  133.1 16.4 %collective-permute-start.27 = (bf16[512,1024]{1,0:T(8,128)(2,1)}, bf16[512,1024]{1,0:T(8,128)(2,1)}, u32[]{:S(2)}, u32[]{:S(2)}) collective-permute-start(bf16[512,1024]{1,0:T(8,128)(2,1)} %refs_7_), channel_id=1, source_target_pairs={{0,4},{4,0},{8,12},{12,8},{16,20},{20,16},{24,28},{28,24},{1,5},{5... | collective-permute-start | bytes 3145736 | tf_op jit(solution)/shard_map/ppermute | solution.py:21
  133.5 16.0 %collective-permute-start.28 = (bf16[512,1024]{1,0:T(8,128)(2,1)}, bf16[512,1024]{1,0:T(8,128)(2,1)}, u32[]{:S(2)}, u32[]{:S(2)}) collective-permute-start(bf16[512,1024]{1,0:T(8,128)(2,1)} %collective-permute-done.23.refs_8_), channel_id=1, source_target_pairs={{0,4},{4,0},{8,12},{12,8},{16,20},{20,16},{24,28},{28,24},{1,5},{5... | collective-permute-start | bytes 3145736 | tf_op jit(solution)/shard_map/ppermute | solution.py:21
  133.6 15.9 %collective-permute-start.29 = (bf16[512,1024]{1,0:T(8,128)(2,1)}, bf16[512,1024]{1,0:T(8,128)(2,1)}, u32[]{:S(2)}, u32[]{:S(2)}) collective-permute-start(bf16[512,1024]{1,0:T(8,128)(2,1)} %collective-permute-done.24.refs_9_), channel_id=1, source_target_pairs={{0,4},{4,0},{8,12},{12,8},{16,20},{20,16},{24,28},{28,24},{1,5},{5... | collective-permute-start | bytes 3145736 | tf_op jit(solution)/shard_map/ppermute | solution.py:21
  134.5 14.0 %collective-permute-start.30 = (bf16[256,1024]{1,0:T(8,128)(2,1)}, bf16[256,1024]{1,0:T(8,128)(2,1)}, u32[]{:S(2)}, u32[]{:S(2)}) collective-permute-start(bf16[256,1024]{1,0:T(8,128)(2,1)} %slice.100), channel_id=1, source_target_pairs={{0,16},{4,20},{8,24},{12,28},{16,0},{20,4},{24,8},{28,12},{1,17},{... | collective-permute-start | bytes 1572872 | tf_op jit(solution)/shard_map/ppermute | solution.py:21
  136.0 13.5 %collective-permute-start.31 = (bf16[256,1024]{1,0:T(8,128)(2,1)}, bf16[256,1024]{1,0:T(8,128)(2,1)}, u32[]{:S(2)}, u32[]{:S(2)}) collective-permute-start(bf16[256,1024]{1,0:T(8,128)(2,1)} %slice.101), channel_id=1, source_target_pairs={{0,8},{4,12},{8,0},{12,4},{16,24},{20,28},{24,16},{28,20},{1,9},{5... | collective-permute-start | bytes 1572872 | tf_op jit(solution)/shard_map/ppermute | solution.py:21
  149.5 23.5 %collective-permute-start.37 = (bf16[3,256,1024]{2,1,0:T(8,128)(2,1)}, bf16[3,256,1024]{2,1,0:T(8,128)(2,1)}, u32[]{:S(2)}, u32[]{:S(2)}) collective-permute-start(bf16[3,256,1024]{2,1,0:T(8,128)(2,1)} %get-tuple-element.1187.refs_1_), channel_id=1, source_target_pairs={{0,4},{4,0},{8,12},{12,8},{16,20},{20,16},{24,28},{28,24},{1,5},{5... | collective-permute-start | bytes 4718600 | tf_op jit(solution)/shard_map/ppermute | solution.py:21
  150.8 4.6 %collective-permute-start.32 = (bf16[256,1024]{1,0:T(8,128)(2,1)}, bf16[256,1024]{1,0:T(8,128)(2,1)S(1)}, u32[]{:S(2)}, u32[]{:S(2)}) collective-permute-start(bf16[256,1024]{1,0:T(8,128)(2,1)} %collective-permute-done.30.refs_10_), channel_id=1, source_target_pairs={{0,4},{4,0},{8,12},{12,8},{16,20},{20,16},{24,28},{28,24},{1,5},{5... | collective-permute-start | bytes 1572872 | tf_op jit(solution)/shard_map/ppermute | solution.py:21
  150.8 22.1 %collective-permute-start.34 = (bf16[2,256,1024]{2,1,0:T(8,128)(2,1)}, bf16[2,256,1024]{2,1,0:T(8,128)(2,1)S(1)}, u32[]{:S(2)}, u32[]{:S(2)}) collective-permute-start(bf16[2,256,1024]{2,1,0:T(8,128)(2,1)} %get-tuple-element.1082.refs_1_.refs_5_), channel_id=1, source_target_pairs={{0,4},{4,0},{8,12},{12,8},{16,20},{20,16},{24,28},{28,24},{1,5},{5... | collective-permute-start | bytes 3145736 | tf_op jit(solution)/shard_map/ppermute | solution.py:21
  151.3 21.7 %collective-permute-start.35 = (bf16[256,2048]{1,0:T(8,128)(2,1)}, bf16[256,2048]{1,0:T(8,128)(2,1)}, u32[]{:S(2)}, u32[]{:S(2)}) collective-permute-start(bf16[256,2048]{1,0:T(8,128)(2,1)} %get-tuple-element.824.refs_2_), channel_id=1, source_target_pairs={{0,4},{4,0},{8,12},{12,8},{16,20},{20,16},{24,28},{28,24},{1,5},{5... | collective-permute-start | bytes 3145736 | tf_op jit(solution)/shard_map/ppermute | solution.py:21
  151.3 7.8 %collective-permute-start.33 = (bf16[256,1024]{1,0:T(8,128)(2,1)}, bf16[256,1024]{1,0:T(8,128)(2,1)S(1)}, u32[]{:S(2)}, u32[]{:S(2)}) collective-permute-start(bf16[256,1024]{1,0:T(8,128)(2,1)} %collective-permute-done.31.refs_11_), channel_id=1, source_target_pairs={{0,4},{4,0},{8,12},{12,8},{16,20},{20,16},{24,28},{28,24},{1,5},{5... | collective-permute-start | bytes 1572872 | tf_op jit(solution)/shard_map/ppermute | solution.py:21
  155.4 17.6 %collective-permute-start.36 = (bf16[256,1024]{1,0:T(8,128)(2,1)}, bf16[256,1024]{1,0:T(8,128)(2,1)}, u32[]{:S(2)}, u32[]{:S(2)}) collective-permute-start(bf16[256,1024]{1,0:T(8,128)(2,1)} %get-tuple-element.1079.refs_1_), channel_id=1, source_target_pairs={{0,4},{4,0},{8,12},{12,8},{16,20},{20,16},{24,28},{28,24},{1,5},{5... | collective-permute-start | bytes 1572872 | tf_op jit(solution)/shard_map/ppermute | solution.py:21
  181.4 17.6 %collective-permute-start.43 = (bf16[256,4096]{1,0:T(8,128)(2,1)S(1)}, bf16[256,4096]{1,0:T(8,128)(2,1)}, u32[]{:S(2)}, u32[]{:S(2)}) collective-permute-start(bf16[256,4096]{1,0:T(8,128)(2,1)S(1)} %copy-done.10), channel_id=1, source_target_pairs={{0,4},{4,0},{8,12},{12,8},{16,20},{20,16},{24,28},{28,24},{1,5},{5... | collective-permute-start | bytes 6291464 | tf_op jit(solution)/shard_map/ppermute | solution.py:21
  181.6 24.7 %collective-permute-start.40 = (bf16[2,512,512]{2,1,0:T(8,128)(2,1)}, bf16[2,512,512]{2,1,0:T(8,128)(2,1)S(1)}, u32[]{:S(2)}, u32[]{:S(2)}) collective-permute-start(bf16[2,512,512]{2,1,0:T(8,128)(2,1)} %get-tuple-element.964), channel_id=1, source_target_pairs={{0,8},{4,12},{8,0},{12,4},{16,24},{20,28},{24,16},{28,20},{1,9},{5... | collective-permute-start | bytes 3145736 | tf_op jit(solution)/shard_map/ppermute | solution.py:21
  182.9 24.4 %collective-permute-start.41 = (bf16[2,512,512]{2,1,0:T(8,128)(2,1)}, bf16[2,512,512]{2,1,0:T(8,128)(2,1)}, u32[]{:S(2)}, u32[]{:S(2)}) collective-permute-start(bf16[2,512,512]{2,1,0:T(8,128)(2,1)} %get-tuple-element.965), channel_id=1, source_target_pairs={{0,16},{4,20},{8,24},{12,28},{16,0},{20,4},{24,8},{28,12},{1,17},{... | collective-permute-start | bytes 3145736 | tf_op jit(solution)/shard_map/ppermute | solution.py:21
  183.5 22.1 %collective-permute-start.39 = (bf16[256,1024]{1,0:T(8,128)(2,1)S(1)}, bf16[256,1024]{1,0:T(8,128)(2,1)}, u32[]{:S(2)}, u32[]{:S(2)}) collective-permute-start(bf16[256,1024]{1,0:T(8,128)(2,1)S(1)} %copy-done.26), channel_id=1, source_target_pairs={{0,4},{4,0},{8,12},{12,8},{16,20},{20,16},{24,28},{28,24},{1,5},{5... | collective-permute-start | bytes 1572872 | tf_op jit(solution)/shard_map/ppermute | solution.py:21
  195.6 10.0 %collective-permute-start.42 = (f32[2,1024]{1,0:T(2,128)}, f32[2,1024]{1,0:T(2,128)S(1)}, u32[]{:S(2)}, u32[]{:S(2)}) collective-permute-start(f32[2,1024]{1,0:T(2,128)} %get-tuple-element.1059), channel_id=1, source_target_pairs={{1,0},{2,1},{3,2},{5,4},{6,5},{7,6},{9,8},{10,9},{11,10},{13,12},{... | collective-permute-start | bytes 24584 | tf_op jit(solution)/shard_map/ppermute | solution.py:27
  210.5 36.1 %collective-permute-start.44 = (bf16[2,128,2048]{2,1,0:T(8,128)(2,1)}, bf16[2,128,2048]{2,1,0:T(8,128)(2,1)S(1)}, u32[]{:S(2)}, u32[]{:S(2)}) collective-permute-start(bf16[2,128,2048]{2,1,0:T(8,128)(2,1)} %get-tuple-element.1065), channel_id=1, source_target_pairs={{0,8},{4,12},{8,0},{12,4},{16,24},{20,28},{24,16},{28,20},{1,9},{5... | collective-permute-start | bytes 3145736 | tf_op jit(solution)/shard_map/ppermute | solution.py:21
  211.9 34.7 %collective-permute-start.45 = (bf16[2,128,2048]{2,1,0:T(8,128)(2,1)}, bf16[2,128,2048]{2,1,0:T(8,128)(2,1)S(1)}, u32[]{:S(2)}, u32[]{:S(2)}) collective-permute-start(bf16[2,128,2048]{2,1,0:T(8,128)(2,1)} %get-tuple-element.1066), channel_id=1, source_target_pairs={{0,16},{4,20},{8,24},{12,28},{16,0},{20,4},{24,8},{28,12},{1,17},{... | collective-permute-start | bytes 3145736 | tf_op jit(solution)/shard_map/ppermute | solution.py:21
  221.1 16.1 %collective-permute-start.48 = (bf16[256,1024]{1,0:T(8,128)(2,1)}, bf16[256,1024]{1,0:T(8,128)(2,1)S(1)}, u32[]{:S(2)}, u32[]{:S(2)}) collective-permute-start(bf16[256,1024]{1,0:T(8,128)(2,1)} %get-tuple-element.1081.refs_3_), channel_id=1, source_target_pairs={{0,4},{4,0},{8,12},{12,8},{16,20},{20,16},{24,28},{28,24},{1,5},{5... | collective-permute-start | bytes 1572872 | tf_op jit(solution)/shard_map/ppermute | solution.py:21
  222.8 23.8 %collective-permute-start.46 = (bf16[512,512]{1,0:T(8,128)(2,1)}, bf16[512,512]{1,0:T(8,128)(2,1)S(1)}, u32[]{:S(2)}, u32[]{:S(2)}) collective-permute-start(bf16[512,512]{1,0:T(8,128)(2,1)} %get-tuple-element.1071), channel_id=1, source_target_pairs={{0,16},{4,20},{8,24},{12,28},{16,0},{20,4},{24,8},{28,12},{1,17},{... | collective-permute-start | bytes 1572872 | tf_op jit(solution)/shard_map/ppermute | solution.py:21
  223.7 22.9 %collective-permute-start.47 = (bf16[512,512]{1,0:T(8,128)(2,1)}, bf16[512,512]{1,0:T(8,128)(2,1)S(1)}, u32[]{:S(2)}, u32[]{:S(2)}) collective-permute-start(bf16[512,512]{1,0:T(8,128)(2,1)} %get-tuple-element.1072), channel_id=1, source_target_pairs={{0,8},{4,12},{8,0},{12,4},{16,24},{20,28},{24,16},{28,20},{1,9},{5... | collective-permute-start | bytes 1572872 | tf_op jit(solution)/shard_map/ppermute | solution.py:21
  254.9 73.7 %reduce-scatter.7.cloned.1.call-start = ((), (), s32[]{:S(2)}) async-start(), calls=%async_computation.5 | async-start | bytes 1310720 | tf_op jit(solution)/shard_map/reduce_scatter | solution.py:975
  268.5 5.6 %collective-permute-start.53 = (bf16[3,256,1024]{2,1,0:T(8,128)(2,1)}, bf16[3,256,1024]{2,1,0:T(8,128)(2,1)S(1)}, u32[]{:S(2)}, u32[]{:S(2)}) collective-permute-start(bf16[3,256,1024]{2,1,0:T(8,128)(2,1)} %get-tuple-element.1189.refs_3_), channel_id=1, source_target_pairs={{0,4},{4,0},{8,12},{12,8},{16,20},{20,16},{24,28},{28,24},{1,5},{5... | collective-permute-start | bytes 4718600 | tf_op jit(solution)/shard_map/ppermute | solution.py:21
  270.9 13.7 %collective-permute-start.49 = (bf16[2,256,512]{2,1,0:T(8,128)(2,1)}, bf16[2,256,512]{2,1,0:T(8,128)(2,1)S(1)}, u32[]{:S(2)}, u32[]{:S(2)}) collective-permute-start(bf16[2,256,512]{2,1,0:T(8,128)(2,1)} %get-tuple-element.1174), channel_id=1, source_target_pairs={{0,8},{4,12},{8,0},{12,4},{16,24},{20,28},{24,16},{28,20},{1,9},{5... | collective-permute-start | bytes 1572872 | tf_op jit(solution)/shard_map/ppermute | solution.py:21
  271.0 13.6 %collective-permute-start.50 = (bf16[2,256,512]{2,1,0:T(8,128)(2,1)}, bf16[2,256,512]{2,1,0:T(8,128)(2,1)S(1)}, u32[]{:S(2)}, u32[]{:S(2)}) collective-permute-start(bf16[2,256,512]{2,1,0:T(8,128)(2,1)} %get-tuple-element.1175), channel_id=1, source_target_pairs={{0,16},{4,20},{8,24},{12,28},{16,0},{20,4},{24,8},{28,12},{1,17},{... | collective-permute-start | bytes 1572872 | tf_op jit(solution)/shard_map/ppermute | solution.py:21
  271.6 24.1 %collective-permute-start.51 = (bf16[128,2048]{1,0:T(8,128)(2,1)}, bf16[128,2048]{1,0:T(8,128)(2,1)S(1)}, u32[]{:S(2)}, u32[]{:S(2)}) collective-permute-start(bf16[128,2048]{1,0:T(8,128)(2,1)} %get-tuple-element.1181), channel_id=1, source_target_pairs={{0,16},{4,20},{8,24},{12,28},{16,0},{20,4},{24,8},{28,12},{1,17},{... | collective-permute-start | bytes 1572872 | tf_op jit(solution)/shard_map/ppermute | solution.py:21
  272.5 23.4 %collective-permute-start.52 = (bf16[128,2048]{1,0:T(8,128)(2,1)S(1)}, bf16[128,2048]{1,0:T(8,128)(2,1)}, u32[]{:S(2)}, u32[]{:S(2)}) collective-permute-start(bf16[128,2048]{1,0:T(8,128)(2,1)S(1)} %copy-done.52), channel_id=1, source_target_pairs={{0,8},{4,12},{8,0},{12,4},{16,24},{20,28},{24,16},{28,20},{1,9},{5... | collective-permute-start | bytes 1572872 | tf_op jit(solution)/shard_map/ppermute | solution.py:21
  302.5 59.5 %reduce-scatter.9.cloned.1.call-start = ((), (), s32[]{:S(2)}) async-start(), calls=%async_computation.6 | async-start | bytes 655360 | tf_op jit(solution)/shard_map/reduce_scatter | solution.py:975
  302.6 24.6 %collective-permute-start.54 = (bf16[2,384,512]{2,1,0:T(8,128)(2,1)}, bf16[2,384,512]{2,1,0:T(8,128)(2,1)S(1)}, u32[]{:S(2)}, u32[]{:S(2)}) collective-permute-start(bf16[2,384,512]{2,1,0:T(8,128)(2,1)} %get-tuple-element.1235), channel_id=1, source_target_pairs={{0,8},{4,12},{8,0},{12,4},{16,24},{20,28},{24,16},{28,20},{1,9},{5... | collective-permute-start | bytes 2359304 | tf_op jit(solution)/shard_map/ppermute | solution.py:21
  303.7 23.5 %collective-permute-start.55 = (bf16[2,384,512]{2,1,0:T(8,128)(2,1)}, bf16[2,384,512]{2,1,0:T(8,128)(2,1)S(1)}, u32[]{:S(2)}, u32[]{:S(2)}) collective-permute-start(bf16[2,384,512]{2,1,0:T(8,128)(2,1)} %get-tuple-element.1236), channel_id=1, source_target_pairs={{0,16},{4,20},{8,24},{12,28},{16,0},{20,4},{24,8},{28,12},{1,17},{... | collective-permute-start | bytes 2359304 | tf_op jit(solution)/shard_map/ppermute | solution.py:21
  304.3 22.9 %collective-permute-start.57 = (bf16[256,512]{1,0:T(8,128)(2,1)}, bf16[256,512]{1,0:T(8,128)(2,1)S(1)}, u32[]{:S(2)}, u32[]{:S(2)}) collective-permute-start(bf16[256,512]{1,0:T(8,128)(2,1)} %get-tuple-element.1249), channel_id=1, source_target_pairs={{0,16},{4,20},{8,24},{12,28},{16,0},{20,4},{24,8},{28,12},{1,17},{... | collective-permute-start | bytes 786440 | tf_op jit(solution)/shard_map/ppermute | solution.py:21
  305.2 22.1 %collective-permute-start.58 = (bf16[256,512]{1,0:T(8,128)(2,1)S(1)}, bf16[256,512]{1,0:T(8,128)(2,1)S(1)}, u32[]{:S(2)}, u32[]{:S(2)}) collective-permute-start(bf16[256,512]{1,0:T(8,128)(2,1)S(1)} %copy-done.55), channel_id=1, source_target_pairs={{0,8},{4,12},{8,0},{12,4},{16,24},{20,28},{24,16},{28,20},{1,9},{5... | collective-permute-start | bytes 786440 | tf_op jit(solution)/shard_map/ppermute | solution.py:21
  305.6 4.7 %collective-permute-start.56 = (f32[2,1024]{1,0:T(2,128)S(1)}, f32[2,1024]{1,0:T(2,128)S(1)}, u32[]{:S(2)}, u32[]{:S(2)}) collective-permute-start(f32[2,1024]{1,0:T(2,128)S(1)} %copy-done.49), channel_id=1, source_target_pairs={{1,0},{2,1},{3,2},{5,4},{6,5},{7,6},{9,8},{10,9},{11,10},{13,12},{... | collective-permute-start | bytes 24584 | tf_op jit(solution)/shard_map/ppermute | solution.py:27
  340.7 5.1 %collective-permute-start.63 = (f32[11,128]{1,0:T(8,128)S(1)}, f32[11,128]{1,0:T(8,128)S(1)}, u32[]{:S(2)}, u32[]{:S(2)}) collective-permute-start(f32[11,128]{1,0:T(8,128)S(1)} %slice_select_fusion.4), channel_id=1, source_target_pairs={{0,4},{4,0},{8,12},{12,8},{16,20},{20,16},{24,28},{28,24},{1,5},{5... | collective-permute-start | bytes 16904 | tf_op jit(solution)/shard_map/ppermute | solution.py:991
  345.0 43.8 %reduce-scatter.11.cloned.1.call-start = ((), (), s32[]{:S(2)}) async-start(), calls=%async_computation.7 | async-start | bytes 983040 | tf_op jit(solution)/shard_map/reduce_scatter | solution.py:975
  345.9 3.4 collective-permute-start.64
  348.0 10.1 %collective-permute-start.59 = (bf16[384,512]{1,0:T(8,128)(2,1)S(1)}, bf16[384,512]{1,0:T(8,128)(2,1)S(1)}, u32[]{:S(2)}, u32[]{:S(2)}) collective-permute-start(bf16[384,512]{1,0:T(8,128)(2,1)S(1)} %copy-done.54), channel_id=1, source_target_pairs={{0,16},{4,20},{8,24},{12,28},{16,0},{20,4},{24,8},{28,12},{1,17},{... | collective-permute-start | bytes 1179656 | tf_op jit(solution)/shard_map/ppermute | solution.py:21
  348.6 9.8 %collective-permute-start.60 = (bf16[384,512]{1,0:T(8,128)(2,1)S(1)}, bf16[384,512]{1,0:T(8,128)(2,1)S(1)}, u32[]{:S(2)}, u32[]{:S(2)}) collective-permute-start(bf16[384,512]{1,0:T(8,128)(2,1)S(1)} %copy-done.53), channel_id=1, source_target_pairs={{0,8},{4,12},{8,0},{12,4},{16,24},{20,28},{24,16},{28,20},{1,9},{5... | collective-permute-start | bytes 1179656 | tf_op jit(solution)/shard_map/ppermute | solution.py:21
  (62 other events, 591.0 us)
Sparse Core Ops, SparseCore 0:
  255.0 26.2 reduce-scatter.4
  302.7 25.8 reduce-scatter.6
  345.1 16.9 reduce-scatter.8
  365.7 23.0 reduce-scatter.10

commit v3 on v2

v3 whole, which is shorter than its diff:
```python
import jax
import jax.numpy as jnp
from jax import lax
from jax.experimental import pallas as pl
from jax.experimental.pallas import tpu as pltpu
from jax.sharding import PartitionSpec as P

epsilon = 1e-05
bf16 = jnp.bfloat16
f32 = jnp.float32
ROWS = 64
STEP = 512
LANES = 512
LIMIT = 60
MIB = 2**20
G1, B1, G2, B2, MK, MV, MR, DECAY, FIRST, CMK, CMR = range(11)


def hop(value, bit):
    count = lax.axis_size("seg")
    return lax.ppermute(value, "seg", [(i, i ^ bit) for i in range(count)])


def along(value, steps):
    count = lax.axis_size("stretch")
    first, last = (max(0, -steps), min(count, count - steps))
    return lax.ppermute(value, "stretch", [(i, i + steps) for i in range(first, last)])


def across(value, j):
    count = lax.axis_size("stretch")
    return lax.ppermute(value, "stretch", [(i, i ^ j) for i in range(count)])


def exchange(value):
    count = lax.axis_size("stretch")
    if count == 4:
        near, far = across(value, 1), across(value, 2)
        return [value, near, far, across(near, 2)]
    return lax.all_gather(value, "stretch")


def tie(value, *others):
    return lax.optimization_barrier((value, *others))[0]


class Live:
    def __init__(self):
        self.__dict__["held"] = {}

    def __getattr__(self, name):
        return self.held[name]

    def __setattr__(self, name, value):
        self.held[name] = value

    def drop(self, *names):
        for name in names:
            del self.held[name]

    def sync(self):
        self.__dict__["held"] = lax.optimization_barrier(self.held)


def far_bits():
    bits, b = [], 2
    while b < lax.axis_size("seg"):
        bits.append(b)
        b *= 2
    return bits


def relative_order():
    count = lax.axis_size("seg")
    return list(range(0, count, 2)) + list(range(1, count, 2))


def first_stage(own):
    return {b: [hop(part, b) for part in own] for b in far_bits()}


def second_stage(direct, held):
    rest = far_bits()
    held = dict(held)
    for m in sorted(range(0, lax.axis_size("seg"), 2), key=lambda m: (bin(m).count("1"), m)):
        if m == 0 or m in held:
            continue
        bits = [b for b in rest if m & b]
        held[m] = [hop(held[m ^ bits[-1]][0], bits[-1]), hop(held[m ^ bits[0]][1], bits[0])]
    return {m: held[m] for m in held if m not in direct}


def sibling(pieces):
    return {m ^ 1: [hop(p, 1) for p in parts] for m, parts in pieces.items()}


def plan(pieces, first, rows):
    steps, at = [], 0
    for m in relative_order():
        base = 0
        for part in pieces[m]:
            lo, hi = max(first, base), min(first + rows, base + part.shape[0])
            if lo < hi:
                steps.append((at, lo - base, hi - lo, m, lo - first))
            base += part.shape[0]
            at += 1
    return steps


def flat_pieces(pieces):
    return [part for m in relative_order() for part in pieces[m]]


class Loads:
    def __init__(self, sems):
        self.sems, self.used = sems, 0

    def start(self, src, dst):
        copy = pltpu.make_async_copy(src, dst, self.sems.at[self.used])
        self.used += 1
        copy.start()
        return copy

    def pieces(self, steps, refs, target, place):
        return [
            self.start(refs[piece].at[pl.ds(row, count)], target.at[pl.ds(place(m) + within, count)])
            for piece, row, count, m, within in steps
        ]


def wait(copies):
    for c in copies:
        c.wait()


def call(body, info, small, large, raw, outs, big_outs, scratch, copies, us, limit):
    n_small, n_large, n_raw = len(small), len(large), len(raw)
    n_out, n_big = len(outs), len(big_outs)

    def shape_of(array, index):
        return array.shape if index is None else array.shape[1:]

    def kernel(*refs):
        at = 0

        def take(n):
            nonlocal at
            at += n
            return refs[at - n : at]

        (info_ref,), small_refs, large_refs, raw_refs = take(1), take(n_small), take(n_large), take(n_raw)
        out_refs, big_refs = take(n_out), take(n_big)
        buffers, big_buffers, (sems,) = take(n_large), take(n_big), take(1)
        rest = take(len(refs) - at)
        loads = Loads(sems)
        pending = []
        for (array, index), ref, buf in zip(large, large_refs, buffers):
            pending.append(loads.start(ref if index is None else ref.at[index], buf))
        stored = {}

        def get(k):
            if pending[k] is not None:
                pending[k].wait()
                pending[k] = None
            return buffers[k]

        def put(k):
            stored[k] = loads.start(big_buffers[k], big_refs[k])

        body(info_ref, small_refs, get, raw_refs, out_refs, big_buffers, put, rest, loads)
        for k in range(n_large):
            get(k)
        for k in range(n_big):
            if k not in stored:
                put(k)
        wait(stored.values())

    hbm = pl.BlockSpec(memory_space=pltpu.HBM)
    vmem = pl.BlockSpec(memory_space=pltpu.VMEM)
    return pl.pallas_call(
        kernel,
        out_shape=[jax.ShapeDtypeStruct(s, d) for s, d in (*outs, *big_outs)],
        in_specs=[pl.BlockSpec(memory_space=pltpu.SMEM)] + [vmem] * n_small + [hbm] * (n_large + n_raw),
        out_specs=[vmem] * n_out + [hbm] * n_big,
        scratch_shapes=[pltpu.VMEM(shape_of(a, i), a.dtype) for a, i in large]
        + [pltpu.VMEM(s, d) for s, d in big_outs]
        + [pltpu.SemaphoreType.DMA((max(1, n_large + n_big + copies),))]
        + list(scratch),
        compiler_params=pltpu.CompilerParams(vmem_limit_bytes=LIMIT * MIB),
        cost_estimate=pl.CostEstimate(
            flops=0, bytes_accessed=int(us * 1e3), transcendentals=0),
    )(info, *small, *[a for a, _ in large], *raw)


def natural(me, rows):
    return lambda m: pl.multiple_of(jnp.bitwise_xor(me, m) * rows, rows)


def dot_nn(a, b):
    return jnp.dot(a, b, preferred_element_type=f32)


def dot_nt(a, b):
    return lax.dot_general(a, b, (((1,), (1,)), ((), ())), preferred_element_type=f32)


def dot_tn(a, b):
    return lax.dot_general(a, b, (((0,), (0,)), ((), ())), preferred_element_type=f32)


def norm(rows):
    centre = rows - jnp.mean(rows, axis=-1, keepdims=True)
    inverse = lax.rsqrt(jnp.mean(centre * centre, axis=-1, keepdims=True) + epsilon)
    return centre * inverse, inverse


def norm_back(d, unit, inverse, gain):
    q = d * gain
    return inverse * (
        q
        - jnp.mean(q, axis=-1, keepdims=True)
        - unit * jnp.mean(q * unit, axis=-1, keepdims=True)
    )


def down_one(rows, entering):
    at = lax.broadcasted_iota(jnp.int32, rows.shape, 0)
    return jnp.where(at == 0, entering, pltpu.roll(rows, 1, 0))


def up_one(rows, entering):
    at = lax.broadcasted_iota(jnp.int32, rows.shape, 0)
    last = rows.shape[0] - 1
    return jnp.where(at == last, entering, pltpu.roll(rows, last, 0))


def fold(rows):
    total = rows[:8]
    for k in range(8, rows.shape[0], 8):
        total = total + rows[k : k + 8]
    return total


def columns(width, step):
    step = min(step, width)

    def run(body):
        @pl.loop(0, width // step)
        def _(n):
            body(pl.ds(pl.multiple_of(n * step, step), step))

    return run


def row_chunk(b, i, length):
    return pl.ds(pl.multiple_of(b * length + i * ROWS, ROWS), ROWS)


def two_part(mat, value):
    hi = value.astype(bf16)
    lo = (value - hi.astype(f32)).astype(bf16)
    return dot_nn(mat, hi) + dot_nn(mat, lo)


def triangle(length, strictly_before):
    row = lax.broadcasted_iota(jnp.int32, (length, length), 0)
    col = lax.broadcasted_iota(jnp.int32, (length, length), 1)
    keep = (col < row) if strictly_before else (col > row)
    return keep.astype(f32).astype(bf16)


def column_sums(out_ref, sum_ref):
    for k in range(sum_ref.shape[0]):
        out_ref[k : k + 1, :] = jnp.sum(sum_ref[k], axis=0, keepdims=True)


def pack(parts_a, parts_b, vectors, width):
    arrays = [p[0] for p in (*parts_a, *parts_b) if p[0] is not None]
    shard = vectors[0].shape[0]

    def kernel(*refs):
        vec_refs, ins = refs[: len(vectors)], refs[len(vectors) : len(vectors) + len(arrays)]
        outs, (table, sems) = refs[len(vectors) + len(arrays) : -2], refs[-2:]
        copies, n = [], 0
        for out, parts in zip(outs, (parts_a, parts_b)):
            at = 0
            for array, first, count in parts:
                if array is None:
                    spot = (out, at)
                else:
                    copies.append(pltpu.make_async_copy(
                        ins[n].at[pl.ds(first, count)], out.at[pl.ds(at, count)], sems.at[n]))
                    copies[-1].start()
                    n += 1
                at += count
        table[...] = jnp.zeros_like(table)
        for k, ref in enumerate(vec_refs):
            table[k : k + 1, :shard] = ref[...].astype(f32)
        spot[0][spot[1] : spot[1] + 16, :] = table[...].astype(bf16)
        wait(copies)

    return pl.pallas_call(
        kernel,
        out_shape=[jax.ShapeDtypeStruct((sum(p[2] for p in parts), width), bf16)
                   for parts in (parts_a, parts_b)],
        in_specs=[pl.BlockSpec(memory_space=pltpu.VMEM)] * len(vectors)
        + [pl.BlockSpec(memory_space=pltpu.HBM)] * len(arrays),
        out_specs=[pl.BlockSpec(memory_space=pltpu.VMEM)] * 2,
        scratch_shapes=[pltpu.VMEM((16, width), f32), pltpu.SemaphoreType.DMA((len(arrays),))],
        compiler_params=pltpu.CompilerParams(vmem_limit_bytes=LIMIT * MIB),
        cost_estimate=pl.CostEstimate(flops=0, bytes_accessed=1000, transcendentals=0),
    )(*[x.reshape(1, shard) for x in vectors], *arrays)


def pack_wide(key, recept):
    rows, wide = key.shape
    width = recept.shape[1]
    each = recept.shape[0] * width // wide
    half = (rows + each) // 32 * 16

    def kernel(key_ref, recept_ref, top_ref, low_ref, sems):
        copies = [
            pltpu.make_async_copy(key_ref.at[pl.ds(0, half)], top_ref, sems.at[0]),
            pltpu.make_async_copy(
                key_ref.at[pl.ds(half, rows - half)], low_ref.at[pl.ds(0, rows - half)], sems.at[1])]
        for q in range(wide // width):
            copies.append(pltpu.make_async_copy(
                recept_ref.at[pl.ds(q * each, each)],
                low_ref.at[pl.ds(rows - half, each), pl.ds(q * width, width)], sems.at[2 + q]))
        for c in copies:
            c.start()
        wait(copies)

    return pl.pallas_call(
        kernel,
        out_shape=[jax.ShapeDtypeStruct((n, wide), bf16) for n in (half, rows + each - half)],
        in_specs=[pl.BlockSpec(memory_space=pltpu.HBM)] * 2,
        out_specs=[pl.BlockSpec(memory_space=pltpu.VMEM)] * 2,
        scratch_shapes=[pltpu.SemaphoreType.DMA((2 + wide // width,))],
        compiler_params=pltpu.CompilerParams(vmem_limit_bytes=LIMIT * MIB),
        cost_estimate=pl.CostEstimate(flops=0, bytes_accessed=1000, transcendentals=0),
    )(key, recept)


def recept_blocks(loads, steps, raw, w, info, shard, width, wide):
    each = shard * width // wide
    place = natural(info[0], shard)
    return [
        loads.start(raw[piece].at[pl.ds(row, count), pl.ds(q * width, width)],
                    w.at[pl.ds(place(m) + q * each + within, count)])
        for piece, row, count, m, within in steps
        for q in range(wide // width)
    ]


def time_in(info, stream, last, previous, given, pieces, spots, length, shard):
    tokens, width = stream.shape
    batches = tokens // length
    plans = [plan(pieces, spots[k], shard) for k in "kvr"]
    vplan = plan(pieces, spots["vec"], 16)
    order = relative_order()

    def body(info, small, get, raw, outs, big, put, scratch, loads):
        last_ref, prev_ref = small[:2]
        sum_ref, vec_ref, entry_ref = outs
        in_ref = big[0]
        w, vt = scratch
        place = natural(info[0], shard)
        vcopies = loads.pieces(vplan, raw, vt, lambda m: order.index(m) * 16)
        copies = [loads.pieces(plans[k], raw, w.at[k], place) for k in range(3)]
        wait(vcopies)
        if given is not None:
            vec_ref[...] = small[2][...]
        else:
            for at, m in enumerate(order):
                vec_ref[:, pl.ds(place(m), shard)] = vt[at * 16 : at * 16 + 16, :shard].astype(f32)
        unit, _ = norm(last_ref[...].astype(f32))
        edge = unit * vec_ref[G1 : G1 + 1] + vec_ref[B1 : B1 + 1]
        for b in range(batches):
            entry_ref[b : b + 1, :] = jnp.where(info[1] == 1, prev_ref[b], edge[b : b + 1])
        stream_ref = get(0)

        for b in range(batches):
            def step(i, before):
                r = row_chunk(b, i, length)
                na, _ = norm(stream_ref[r, :].astype(f32))
                xa = na * vec_ref[G1 : G1 + 1] + vec_ref[B1 : B1 + 1]
                xs = down_one(xa, before)
                for k, row in enumerate((MK, MV, MR)):
                    mix = vec_ref[row : row + 1]
                    in_ref[k, r, :] = (xa * mix + xs * (1.0 - mix)).astype(bf16)
                return xa[ROWS - 1 :]
            lax.fori_loop(0, length // ROWS, step, entry_ref[b : b + 1])
        put(0)
        def project(k):
            wait(copies[k])
            @columns(width, STEP)
            def _(n):
                big[1 + k][:, n] = dot_nn(in_ref[k], w[k, :, n])
            put(1 + k)
        project(0)
        project(1)
        keys_ref, vals_ref = big[1], big[2]
        for b in range(batches):
            t = slice(b * length, (b + 1) * length)
            @columns(width, LANES)
            def _(n):
                rate = -jnp.exp(vec_ref[DECAY : DECAY + 1, n])
                at = lax.broadcasted_iota(jnp.int32, (length, 1), 0).astype(f32)
                shifted = keys_ref[t, n] - at * rate
                peak = jnp.max(shifted, axis=0, keepdims=True)
                factor = jnp.exp(shifted - peak)
                sum_ref[b : b + 1, n] = jnp.sum(factor * vals_ref[t, n], axis=0, keepdims=True)
                sum_ref[batches + b : batches + b + 1, n] = jnp.sum(factor, axis=0, keepdims=True)
                sum_ref[2 * batches + b : 2 * batches + b + 1, n] = peak + (length - 1.0) * rate
        project(2)

    extra = [] if given is None else [given]
    return call(
        body, info, [last, previous, *extra], [(stream, None)], flat_pieces(pieces),
        [((3 * batches, width), f32), ((16, width), f32), ((batches, width), f32)],
        [((3, tokens, width), bf16)] + [((tokens, width), f32)] * 3,
        [pltpu.VMEM((3, width, width), bf16), pltpu.VMEM((16 * len(order), width), bf16)],
        len(vplan) + sum(map(len, plans)), 9, 40)


def wkv_terms(kvr_ref, ent_ref, vec_ref, b, t, n, batches, length):
    rate = -jnp.exp(vec_ref[DECAY : DECAY + 1, n])
    at = lax.broadcasted_iota(jnp.int32, (length, 1), 0).astype(f32)
    keys = kvr_ref[0][t, n]
    shifted = keys - at * rate
    peak = jnp.max(shifted, axis=0, keepdims=True)
    factor = jnp.exp(shifted - peak)
    near = (at - 1.0) * rate + peak
    opening = at * rate + ent_ref[2 * batches + b : 2 * batches + b + 1, n]
    reward = vec_ref[FIRST : FIRST + 1, n] + keys
    top = jnp.maximum(jnp.maximum(near, opening), reward)
    return at, factor, jnp.exp(near - top), jnp.exp(opening - top), jnp.exp(reward - top)


def time_out(info, kvr, everyone, state, vec, stream, pieces, spots, length, shard):
    tokens, width = stream.shape
    batches = tokens // length
    stretches = len(everyone)
    relative = isinstance(everyone, list)
    if not relative:
        everyone = [everyone]
    steps = plan(pieces, spots["o"], shard)

    def body(info, small, get, raw, outs, big, put, scratch, loads):
        every_ref, (num_ref, den_ref, exp_ref, vec_ref) = small[:-4], small[-4:]
        if not relative:
            every_ref = [every_ref[0].at[z] for z in range(stretches)]
        ent_ref, mean_ref, log_ref, edge_ref = outs
        gated_ref, wkv_ref, rden_ref, mid_ref, xb_ref = big
        (w,) = scratch
        copies = loads.pieces(steps, raw, w, natural(info[0], shard))
        span = -jnp.exp(vec_ref[DECAY : DECAY + 1, :]) * float(length)

        def merge(upto, b):
            upto_f = upto.astype(f32) if upto is not stretches else float(stretches)
            logits = []
            for j in range(stretches):
                row, z = 2 * batches + b, jnp.bitwise_xor(info[2], j) if relative else jnp.int32(j)
                logit = every_ref[j][row : row + 1, :] + (upto_f - 1.0 - z.astype(f32)) * span
                logits.append(logit if upto is stretches else jnp.where(z < upto, logit, -jnp.inf))
            opening = exp_ref[b] + upto_f * span
            top = opening
            for logit in logits:
                top = jnp.maximum(top, logit)
            start = jnp.exp(opening - top)
            num, den = num_ref[b] * start, den_ref[b] * start
            for j, logit in enumerate(logits):
                weight = jnp.exp(logit - top)
                num = num + weight * every_ref[j][b : b + 1, :]
                den = den + weight * every_ref[j][batches + b : batches + b + 1, :]
            return num, den, top

        for b in range(batches):
            for k, part in enumerate(merge(info[2], b)):
                ent_ref[k * batches + b : k * batches + b + 1, :] = part
            num, den, top = merge(stretches, b)
            mean_ref[b] = num / den
            log_ref[b] = top + jnp.log(den)

        lower = triangle(length, True)
        kvr_ref = [get(k) for k in range(3)]
        for b in range(batches):
            t = slice(b * length, (b + 1) * length)
            @columns(width, LANES)
            def _(n):
                _, factor, p, o, e = wkv_terms(kvr_ref, ent_ref, vec_ref, b, t, n, batches, length)
                vals = kvr_ref[1][t, n]
                num = (two_part(lower, factor * vals) * p
                       + ent_ref[b : b + 1, n] * o + vals * e)
                den = (two_part(lower, factor) * p
                       + ent_ref[batches + b : batches + b + 1, n] * o + e)
                rden = 1.0 / den
                wkv = num * rden
                wkv_ref[t, n] = wkv
                rden_ref[t, n] = rden
                gated_ref[t, n] = (jax.nn.sigmoid(kvr_ref[2][t, n]) * wkv).astype(bf16)
        put(0)
        put(1)
        put(2)
        wait(copies)
        stream_ref = get(3)
        @columns(width, STEP)
        def _(n):
            mid_ref[:, n] = stream_ref[:, n].astype(f32) + dot_nn(gated_ref[...], w[:, n])
        put(3)
        @pl.loop(0, tokens // ROWS)
        def _(i):
            r = row_chunk(0, i, 0)
            nb, _ = norm(mid_ref[r, :])
            xb_ref[r, :] = nb * vec_ref[G2 : G2 + 1] + vec_ref[B2 : B2 + 1]
        for b in range(batches):
            last = (b + 1) * length - 1
            edge_ref[b : b + 1, :] = xb_ref[last : last + 1, :]

    one = ((tokens, width), f32)
    return call(
        body, info, [*everyone, *state, vec], [(a, None) for a in (*kvr, stream)], flat_pieces(pieces),
        [((3 * batches, width), f32), ((batches, 1, width), f32), ((batches, 1, width), f32),
         ((batches, width), f32)],
        [((tokens, width), bf16), one, one, one, one],
        [pltpu.VMEM((width, width), bf16)], len(steps), 7, 40)


def key_blocks(loads, steps, raw, w, info, shard, fshard, wanted):
    order = relative_order()
    place = natural(info[0], shard)
    out = {}
    for m in wanted:
        cols = pl.ds(natural(info[0], fshard)(m), fshard)
        out[m] = [
            loads.start(raw[piece].at[pl.ds(row, count), cols],
                        w.at[pl.ds(place(m2) + within, count), pl.ds(order.index(m) * fshard, fshard)])
            for piece, row, count, m2, within in steps
        ]
    return out


def value_blocks(loads, raw, w, fshard, stretches):
    order = relative_order()
    others = [m for m in order if m % 2 == 0 and m]
    each = fshard // stretches
    out = {}
    for at, m in enumerate(order):
        own, gathered = raw[2 * (m % 2)], raw[2 * (m % 2) + 1]
        base = m - m % 2
        if base == 0:
            out[m] = [loads.start(own, w.at[pl.ds(at * fshard, fshard)])]
            continue
        out[m] = [
            loads.start(
                gathered.at[pl.ds((z * len(others) + others.index(base)) * each, each)],
                w.at[pl.ds(at * fshard + z * each, each)])
            for z in range(stretches)
        ]
    return out


def value_copies(stretches):
    count = lax.axis_size("seg")
    return 2 + (count - 2) * stretches


def chan_in(info, xb, edge, previous, vec, pieces_ck, length, shard, fshard):
    tokens, width = xb.shape
    batches = tokens // length
    order = relative_order()
    wide = fshard * len(order)
    steps_k = plan(pieces_ck, 0, shard)
    steps_c = plan(pieces_ck, shard, shard * width // wide)

    def body(info, small, get, raw, outs, big, put, scratch, loads):
        edge_ref, prev_ref, vec_ref = small
        (entry_ref,) = outs
        in_ref, near_ref, far_ref, act_ref, frec_ref = big
        wk, wc = scratch
        half = len(order) // 2
        turn = order[half:] + order[:half]
        blocks = key_blocks(loads, steps_k, raw, wk, info, shard, fshard, turn)
        copies_c = recept_blocks(loads, steps_c, raw, wc, info, shard, width, wide)
        for b in range(batches):
            entry_ref[b : b + 1, :] = jnp.where(info[1] == 1, prev_ref[b], edge_ref[b : b + 1, :])
        xb_ref = get(0)
        for b in range(batches):
            def step(i, before):
                r = row_chunk(b, i, length)
                x = xb_ref[r, :]
                xt = down_one(x, before)
                for k, row in enumerate((CMK, CMR)):
                    mix = vec_ref[row : row + 1]
                    in_ref[k, r, :] = (x * mix + xt * (1.0 - mix)).astype(bf16)
                return x[ROWS - 1 :]
            lax.fori_loop(0, length // ROWS, step, entry_ref[b : b + 1])
        put(0)
        for m in turn:
            wait(blocks[m])
            at = order.index(m)
            hid_ref, lo = (near_ref, at * fshard) if at < half else (far_ref, (at - half) * fshard)
            act = jnp.maximum(dot_nn(in_ref[0], wk[:, at * fshard : (at + 1) * fshard]), 0.0)
            act_ref[:, at * fshard : (at + 1) * fshard] = act.astype(bf16)
            hid_ref[:, lo : lo + fshard] = (act * act).astype(bf16)
            if m == turn[half - 1]:
                put(2)
        put(1)
        put(3)
        wait(copies_c)
        @columns(width, STEP)
        def _(n):
            frec_ref[:, n] = dot_nn(in_ref[1], wc[:, n])

    return call(
        body, info, [edge, previous, vec], [(xb, None)], flat_pieces(pieces_ck),
        [((batches, width), f32)],
        [((2, tokens, width), bf16), ((tokens, wide // 2), bf16), ((tokens, wide // 2), bf16),
         ((tokens, wide), bf16), ((tokens, width), f32)],
        [pltpu.VMEM((width, wide), bf16), pltpu.VMEM((width, width), bf16)],
        len(steps_c) * (wide // width) + len(steps_k) * len(order), 11, 40)


def chan_out(info, near, far, frec, mid, cot, cv, fshard):
    tokens, width = mid.shape
    order = relative_order()
    wide = fshard * len(order)
    stretches = lax.axis_size("stretch")

    def body(info, small, get, raw, outs, big, put, scratch, loads):
        out_ref, df_ref, dr_ref = big
        w, fval = scratch
        blocks = value_blocks(loads, raw, w, fshard, stretches)
        half = len(order) // 2
        for k in range(2):
            hid_ref = get(k)
            for m in order[k * half : (k + 1) * half]:
                wait(blocks[m])
            @columns(width, STEP)
            def _(n):
                part = dot_nn(hid_ref[...], w[k * wide // 2 : (k + 1) * wide // 2, n])
                fval[:, n] = part if k == 0 else fval[:, n] + part
        frec_ref, mid_ref, cot_ref = get(2), get(3), get(4)
        @pl.loop(0, tokens // ROWS)
        def _(i):
            r = row_chunk(0, i, 0)
            sig = jax.nn.sigmoid(frec_ref[r, :])
            cots, value = cot_ref[r, :].astype(f32), fval[r, :]
            df_ref[r, :] = (cots * sig).astype(bf16)
            out_ref[r, :] = (mid_ref[r, :] + sig * value).astype(bf16)
            dr_ref[r, :] = (cots * value * sig * (1.0 - sig)).astype(bf16)

    low = ((tokens, width), bf16)
    return call(
        body, info, [], [(a, None) for a in (near, far, frec, mid, cot)], cv, [], [low, low, low],
        [pltpu.VMEM((wide, width), bf16), pltpu.VMEM((tokens, width), f32)],
        value_copies(stretches), 7, 40)


def hidden_back(info, act, dfval, cv, fshard):
    tokens, width = dfval.shape
    order = relative_order()
    wide = fshard * len(order)
    stretches = lax.axis_size("stretch")

    def body(info, small, get, raw, outs, big, put, scratch, loads):
        (dpre_ref,) = big
        (wv,) = scratch
        values = value_blocks(loads, raw, wv, fshard, stretches)
        dfval_ref, act_ref = get(0), get(1)
        for at, m in enumerate(order):
            wait(values[m])
            block = slice(at * fshard, (at + 1) * fshard)
            d = dot_nt(dfval_ref[...], wv[block, :]) * (2.0 * act_ref[:, block].astype(f32))
            dpre_ref[:, block] = d.astype(bf16)

    return call(
        body, info, [], [(dfval, None), (act, None)], cv, [], [((tokens, wide), bf16)],
        [pltpu.VMEM((wide, width), bf16)], value_copies(stretches), 7, 40)[0]


def chan_back(info, dpre, dfrec, xb, entry, vec, pieces_ck, length, shard, fshard):
    tokens, width = xb.shape
    batches = tokens // length
    order = relative_order()
    wide = fshard * len(order)
    steps_k = plan(pieces_ck, 0, shard)
    steps_c = plan(pieces_ck, shard, shard * width // wide)

    def body(info, small, get, raw, outs, big, put, scratch, loads):
        entry_ref, vec_ref = small
        head_ref, total_ref = outs
        dxt_ref, dxb_ref = big
        wk, wc, df, dr, sum_ref = scratch
        copies_c = recept_blocks(loads, steps_c, raw, wc, info, shard, width, wide)
        keys = key_blocks(loads, steps_k, raw, wk, info, shard, fshard, order)
        dfrec_ref = get(0)
        wait(copies_c)
        @columns(width, STEP)
        def _(n):
            dr[:, n] = dot_nt(dfrec_ref[...], wc[n, :])
        dpre_ref = get(1)
        half = len(order) // 2
        for k in range(2):
            for m in order[k * half : (k + 1) * half]:
                wait(keys[m])
            part_of = slice(k * wide // 2, (k + 1) * wide // 2)
            @columns(width, STEP)
            def _(n):
                part = dot_nt(dpre_ref[:, part_of], wk[n, part_of])
                df[:, n] = part if k == 0 else df[:, n] + part
        sum_ref[...] = jnp.zeros_like(sum_ref)
        xb_ref = get(2)
        for b in range(batches):
            def step(i, before):
                r = row_chunk(b, i, length)
                x = xb_ref[r, :]
                gap = x - down_one(x, before)
                a, c = df[r, :], dr[r, :]
                ck, cr = vec_ref[CMK : CMK + 1], vec_ref[CMR : CMR + 1]
                dxt_ref[r, :] = a * (1.0 - ck) + c * (1.0 - cr)
                dxb_ref[r, :] = a * ck + c * cr
                sum_ref[0] += fold(a * gap)
                sum_ref[1] += fold(c * gap)
                return x[ROWS - 1 :]
            lax.fori_loop(0, length // ROWS, step, entry_ref[b : b + 1])
            head_ref[b : b + 1, :] = dxt_ref[b * length : b * length + 1, :]
        column_sums(total_ref, sum_ref)

    one = ((tokens, width), f32)
    return call(
        body, info, [entry, vec], [(a, None) for a in (dfrec, dpre, xb)], flat_pieces(pieces_ck),
        [((batches, width), f32), ((2, width), f32)], [one, one],
        [pltpu.VMEM((width, wide), bf16), pltpu.VMEM((width, width), bf16),
         pltpu.VMEM((tokens, width), f32), pltpu.VMEM((tokens, width), f32),
         pltpu.VMEM((2, 8, width), f32)],
        len(steps_c) * (wide // width) + len(steps_k) * len(order), 10, 40)


def mid_back(info, dxt, dxb, after, mid, cot, vec, kvr, wkv, rden, ent, pieces, spots, length, shard):
    tokens, width = mid.shape
    batches = tokens // length
    steps = plan(pieces, spots["o"], shard)

    def body(info, small, get, raw, outs, big, put, scratch, loads):
        after_ref, vec_ref, ent_ref = small
        dent_ref, total_ref = outs
        dmid_ref, low_ref, high_ref, rlow_ref, rhigh_ref, gn_ref = big
        w, sum_ref = scratch
        copies = loads.pieces(steps, raw, w, natural(info[0], shard))
        sum_ref[...] = jnp.zeros_like(sum_ref)
        dxt_ref, dxb_ref, mid_ref, cot_ref = get(0), get(1), get(2), get(3)
        for b in range(batches):
            def step(k, after_row):
                r = row_chunk(b, length // ROWS - 1 - k, length)
                nb, inverse = norm(mid_ref[r, :])
                dx = dxt_ref[r, :]
                d = dxb_ref[r, :] + up_one(dx, after_row)
                back = cot_ref[r, :].astype(f32) + norm_back(d, nb, inverse, vec_ref[G2 : G2 + 1])
                dmid_ref[r, :] = back
                low_ref[r, :] = back[:, : width // 2].astype(bf16)
                high_ref[r, :] = back[:, width // 2 :].astype(bf16)
                sum_ref[0] += fold(d * nb)
                sum_ref[1] += fold(d)
                return dx[:1]
            lax.fori_loop(0, length // ROWS, step, after_ref[b : b + 1])
        put(0)
        put(1)
        put(2)
        column_sums(total_ref, sum_ref)
        wait(copies)
        @columns(width, STEP)
        def _(n):
            gn_ref[:, n] = (dot_nt(low_ref[...], w[n, : width // 2])
                            + dot_nt(high_ref[...], w[n, width // 2 :]))
        kvr_ref = [get(4), None, get(5)]
        wkv_ref, rden_ref = get(6), get(7)
        lanes = min(LANES, width // 2)
        for b, half, q in [(b, h, q) for b in range(batches) for h in range(2)
                           for q in range(width // 2 // lanes)]:
            t = slice(b * length, (b + 1) * length)
            n = slice(half * width // 2 + q * lanes, half * width // 2 + (q + 1) * lanes)
            part, at_half = (rlow_ref, rhigh_ref)[half], slice(q * lanes, (q + 1) * lanes)
            if True:
                _, _, _, o, _ = wkv_terms(kvr_ref, ent_ref, vec_ref, b, t, n, batches, length)
                sig = jax.nn.sigmoid(kvr_ref[2][t, n])
                d = gn_ref[t, n] * sig
                wkvs = wkv_ref[t, n]
                part[t, at_half] = (d * wkvs * (1.0 - sig)).astype(bf16)
                gn = d * rden_ref[t, n]
                gn_ref[t, n] = gn
                go = gn * o
                dent_ref[b : b + 1, n] = jnp.sum(go, axis=0, keepdims=True)
                dent_ref[batches + b : batches + b + 1, n] = -jnp.sum(go * wkvs, axis=0, keepdims=True)

    one, half = ((tokens, width), f32), ((tokens, width // 2), bf16)
    return call(
        body, info, [after, vec, ent], [(a, None) for a in (dxt, dxb, mid, cot, kvr[0], kvr[2], wkv, rden)],
        flat_pieces(pieces), [((2 * batches, width), f32), ((2, width), f32)], [one, half, half, half, half, one],
        [pltpu.VMEM((width, width), bf16), pltpu.VMEM((2, 8, width), f32)], len(steps), 9, 40)


def time_back(info, gn, wkv, kvr, ent, back, sums, state, drec, stream, entry, vec, pieces, spots,
              length, shard):
    tokens, width = stream.shape
    batches = tokens // length
    stretches = len(back)
    relative = isinstance(back, list)
    if not relative:
        back = [back]
    plans = [plan(pieces, spots[k], shard) for k in "kvr"]

    def body(info, small, get, raw, outs, big, put, scratch, loads):
        back_ref = small[:-7]
        if not relative:
            back_ref = [back_ref[0].at[z] for z in range(stretches)]
        ent_ref, sums_ref, num_ref, den_ref, exp_ref, entry_ref, vec_ref = small[-7:]
        gnum_ref, gden_ref, gexp_ref, gffn_ref, head_ref, total_ref, extra_ref = outs
        d_ref, dxs_ref, dxa_ref = big
        w, dins, sum_ref, later_ref, loc_ref = scratch
        place = natural(info[0], shard)
        copies = [loads.pieces(plans[k], raw, w.at[k], place) for k in range(3)]
        span = -jnp.exp(vec_ref[DECAY : DECAY + 1, :]) * float(length)
        pos = info[2].astype(f32)
        nums, dens, exps = (slice(k * batches, (k + 1) * batches) for k in range(3))
        zero = jnp.zeros((batches, width), f32)

        def state(ref):
            return jnp.concatenate([ref[b] for b in range(batches)], axis=0)

        later_n = later_d = carry_n = carry_d = grad_n = grad_d = grad_f = zero
        for j in range(stretches):
            there = back_ref[j][exps, :]
            at_z = jnp.bitwise_xor(info[2], j) if relative else jnp.int32(j)
            z = at_z.astype(f32)
            after = at_z > info[2]
            lift = jnp.where(after, jnp.exp(jnp.minimum(
                sums_ref[exps, :] - there + (z - 1.0 - pos) * span, 0.0)), 0.0)
            carry = jnp.where(after, jnp.exp(jnp.minimum(
                ent_ref[exps, :] - there + (z - pos) * span, 0.0)), 0.0)
            raised = jnp.exp(jnp.minimum(state(exp_ref) - there + z * span, 0.0))
            dn, dd = back_ref[j][nums, :], back_ref[j][dens, :]
            grad_f = grad_f + jnp.where(at_z == 0, back_ref[j][3 * batches :, :], 0.0)
            later_n, later_d = later_n + dn * lift, later_d + dd * lift
            carry_n, carry_d = carry_n + dn * carry, carry_d + dd * carry
            grad_n, grad_d = grad_n + dn * raised, grad_d + dd * raised
        later_ref[nums, :], later_ref[dens, :] = later_n, later_d
        grad_e = state(num_ref) * grad_n + state(den_ref) * grad_d
        for b in range(batches):
            gnum_ref[b], gden_ref[b] = grad_n[b : b + 1], grad_d[b : b + 1]
            gexp_ref[b] = grad_e[b : b + 1]
            gffn_ref[b] = grad_f[b : b + 1]
        rate_part = (
            float(length) * (ent_ref[nums, :] * carry_n + ent_ref[dens, :] * carry_d)
            + (length - 1.0) * (later_n * sums_ref[nums, :] + later_d * sums_ref[dens, :]))

        upper = triangle(length, False)
        gn_ref, wkv_ref = get(0), get(1)
        kvr_ref = [get(2), get(3)]
        for b in range(batches):
            t = slice(b * length, (b + 1) * length)
            @columns(width, LANES)
            def _(n):
                at, factor, p, o, e = wkv_terms(kvr_ref, ent_ref, vec_ref, b, t, n, batches, length)
                vals, g = kvr_ref[1][t, n], gn_ref[t, n]
                gd = -g * wkv_ref[t, n]
                direct = e * (g * vals + gd)
                opened = o * (g * ent_ref[b : b + 1, n] + gd * ent_ref[batches + b : batches + b + 1, n])
                rn = two_part(upper, g * p) + later_ref[b : b + 1, n]
                rd = two_part(upper, gd * p) + later_ref[batches + b : batches + b + 1, n]
                chain = factor * (rn * vals + rd)
                d_ref[0, t, n] = (chain + direct).astype(bf16)
                d_ref[1, t, n] = (factor * rn + g * e).astype(bf16)
                loc_ref[b : b + 1, n] = jnp.sum(
                    opened - (at - 1.0) * direct - at * chain, axis=0, keepdims=True)
                loc_ref[batches + b : batches + b + 1, n] = jnp.sum(direct, axis=0, keepdims=True)
        put(0)
        rate_rows = rate_part + loc_ref[:batches, :]
        extra_ref[0:1, :] = jnp.sum(rate_rows, axis=0, keepdims=True) * -jnp.exp(
            vec_ref[DECAY : DECAY + 1, :])
        extra_ref[1:2, :] = jnp.sum(loc_ref[batches:, :], axis=0, keepdims=True)
        for k in range(2):
            wait(copies[k])
            @columns(width, STEP)
            def _(n):
                dins[k, :, n] = dot_nt(d_ref[k], w[k, n, :])
        low_ref, high_ref = get(5), get(6)
        wait(copies[2])
        @columns(width, STEP)
        def _(n):
            dins[2, :, n] = (dot_nt(low_ref[...], w[2, n, : width // 2])
                             + dot_nt(high_ref[...], w[2, n, width // 2 :]))
        sum_ref[...] = jnp.zeros_like(sum_ref)
        stream_ref = get(4)
        for b in range(batches):
            def step(i, before):
                r = row_chunk(b, i, length)
                na, _ = norm(stream_ref[r, :].astype(f32))
                xa = na * vec_ref[G1 : G1 + 1] + vec_ref[B1 : B1 + 1]
                gap = xa - down_one(xa, before)
                dxs = jnp.zeros((ROWS, width), f32)
                dxa = jnp.zeros((ROWS, width), f32)
                for k, row in enumerate((MK, MV, MR)):
                    d, mix = dins[k, r, :], vec_ref[row : row + 1]
                    dxs = dxs + d * (1.0 - mix)
                    dxa = dxa + d * mix
                    sum_ref[k] += fold(d * gap)
                dxs_ref[r, :] = dxs
                dxa_ref[r, :] = dxa
                return xa[ROWS - 1 :]
            lax.fori_loop(0, length // ROWS, step, entry_ref[b : b + 1])
            head_ref[b : b + 1, :] = dxs_ref[b * length : b * length + 1, :]
        column_sums(total_ref, sum_ref)

    one = ((tokens, width), f32)
    return call(
        body, info, [*back, ent, sums, *state, entry, vec],
        [(a, None) for a in (gn, wkv, kvr[0], kvr[1], stream, *drec)], flat_pieces(pieces),
        [((batches, 1, width), f32)] * 4
        + [((batches, width), f32), ((3, width), f32), ((2, width), f32)],
        [((2, tokens, width), bf16), one, one],
        [pltpu.VMEM((3, width, width), bf16), pltpu.VMEM((3, tokens, width), f32),
         pltpu.VMEM((3, 8, width), f32), pltpu.VMEM((2 * batches, width), f32),
         pltpu.VMEM((2 * batches, width), f32)],
        sum(map(len, plans)), 14, 40)


def in_back(info, dxs, dxa, after, dmid, stream, vec, length):
    tokens, width = stream.shape
    batches = tokens // length

    def body(info, small, get, raw, outs, big, put, scratch, loads):
        after_ref, vec_ref = small
        (out_ref,) = big
        (sum_ref,) = scratch
        dxs_ref, dxa_ref, dmid_ref, stream_ref = (get(k) for k in range(4))
        sum_ref[...] = jnp.zeros_like(sum_ref)
        for b in range(batches):
            def step(k, after_row):
                r = row_chunk(b, length // ROWS - 1 - k, length)
                na, inverse = norm(stream_ref[r, :].astype(f32))
                dx = dxs_ref[r, :]
                d = dxa_ref[r, :] + up_one(dx, after_row)
                back = norm_back(d, na, inverse, vec_ref[G1 : G1 + 1])
                out_ref[r, :] = (dmid_ref[r, :] + back).astype(bf16)
                sum_ref[0] += fold(d * na)
                sum_ref[1] += fold(d)
                return dx[:1]
            lax.fori_loop(0, length // ROWS, step, after_ref[b : b + 1])
        column_sums(outs[0], sum_ref)

    return call(
        body, info, [after, vec], [(a, None) for a in (dxs, dxa, dmid, stream)], [],
        [((2, width), f32)], [((tokens, width), bf16)],
        [pltpu.VMEM((2, 8, width), f32)], 0, 6, 40)


def weight_grad(info, arrays, items, layout, us, relative=False, stacked=False, under=()):
    count = lax.axis_size("seg")
    evens = list(range(0, count, 2))
    first = items[0][2]
    lead = first[0] if isinstance(first, list) else first
    tokens, n_wide = arrays[lead[0]].shape[-2:]
    n_wide *= len(first) if isinstance(first, list) else 1
    w = arrays[items[0][0][0]].shape[-1] // {"natural": count, "blocks": len(evens), "joined": len(evens)}[layout]
    pair = 2 if w < 256 else 1
    groups = [evens[1:][k : k + pair] for k in range(0, len(evens) - 1, pair)]
    groups[-1].append(0) if len(groups[-1]) < pair else groups.append([0])
    groups = [g for g in groups if g]
    stretches = lax.axis_size("stretch")
    each_z = w // stretches
    shapes = [(len(evens) * w, n_wide)] if stacked else [(len(items) * w, n_wide)] * len(evens)
    shares = [x.shape[0] // len(evens) for x in under]
    if under:
        shapes = [(len(items) * w + sum(shares), n_wide)] * len(evens)

    def body(info, small, get, raw, outs, big, put, scratch, loads):
        x_all, dy_all = scratch
        copies_under, at = [], len(items) * w
        for n, share in enumerate(shares):
            for k in range(len(evens)):
                copies_under.append(loads.start(
                    raw[len(arrays) + n].at[pl.ds(k * share, share)], big[k].at[pl.ds(at, share)]))
            at += share

        def view(spec):
            which, lead = spec
            return raw[which] if lead is None else raw[which].at[lead]

        def columns_of(ref, m):
            if layout == "natural":
                return ref.at[:, pl.ds(natural(info[0], w)(m), w)]
            return ref.at[:, pl.ds(evens.index(m) * w, w)]

        copies = []
        for k, (x, x_sib, dy, dy_sib) in enumerate(items):
            now = []
            for at, part in ((0, dy), (tokens, dy_sib)):
                if relative:
                    each = n_wide // count
                    for n, m in enumerate(relative_order()):
                        cols = natural(info[0], each)(m if at == 0 else m ^ 1)
                        now.append(loads.start(
                            view(part).at[:, pl.ds(n * each, each)],
                            dy_all.at[k, pl.ds(at, tokens), pl.ds(cols, each)]))
                    continue
                pieces = part if isinstance(part, list) else [part]
                each = n_wide // len(pieces)
                for n, piece in enumerate(pieces):
                    now.append(loads.start(
                        view(piece), dy_all.at[k, pl.ds(at, tokens), pl.ds(n * each, each)]))
            for at, part in ((0, x), (tokens, x_sib)):
                ref, rows = view(part), pl.ds(at, tokens)
                if layout == "joined":
                    for g, ms in enumerate(groups):
                        cols = pl.ds(g * pair * w, len(ms) * w)
                        now.append(loads.start(
                            ref.at[:, cols], x_all.at[k, g, rows, pl.ds(0, len(ms) * w)]))
                    continue
                for g, ms in enumerate(groups):
                    for n, m in enumerate(ms):
                        now.append(loads.start(
                            columns_of(ref, m), x_all.at[k, g, rows, pl.ds(n * w, w)]))
            copies.append(now)
        step = min(512, n_wide)
        for k in range(len(items)):
            wait(copies[k])
        for g, ms in enumerate(groups):
            for k in range(len(items)):
                for q in range(n_wide // step):
                    dst = slice(q * step, (q + 1) * step)
                    block = dot_tn(x_all[k, g, :, : len(ms) * w], dy_all[k, :, dst]).astype(bf16)
                    for n, m in enumerate(ms):
                        if not stacked:
                            big[evens.index(m)][k * w : (k + 1) * w, dst] = block[n * w : (n + 1) * w]
                            continue
                        for z in range(stretches):
                            row = (z * len(evens) + evens.index(m)) * each_z
                            big[0][row : row + each_z, dst] = block[n * w + z * each_z : n * w + (z + 1) * each_z]
            if g == 0:
                wait(copies_under)
            for m in ms if not stacked else []:
                put(evens.index(m))

    return call(
        body, info, [], [], [*arrays, *under], [], [(shape, bf16) for shape in shapes],
        [pltpu.VMEM((len(items), len(groups), 2 * tokens, pair * w), bf16),
         pltpu.VMEM((len(items), 2 * tokens, n_wide), bf16)],
        len(items) * (4 + 2 * len(evens) + 2 * count) + len(under) * len(evens), us, 40)


def grad_send(parts):
    return [hop(part, 2 * k) for k, part in enumerate(parts) if k]


def total(terms):
    out = terms[0].astype(f32)
    for t in terms[1:]:
        out = out + t.astype(f32)
    return out


def grad_finish(info, sets):
    stretches = lax.axis_size("stretch")
    n_wide = sets[0][0].shape[1]
    rows = sum(own.shape[0] for own, _, _ in sets)
    each = sets[0][0].shape[0] // sets[0][2] // stretches
    if each % 16:
        parts = [total([own, *got]).astype(bf16).reshape(items, stretches, each, n_wide)
                 for own, got, items in sets]
        return jnp.swapaxes(jnp.concatenate(parts, axis=0), 0, 1).reshape(rows, n_wide)
    flat = [(a, None) for own, got, _ in sets for a in (own, *got)]

    def body(info, small, get, raw, outs, big, put, scratch, loads):
        at, done = 0, 0
        for own, got, items in sets:
            refs = [get(at + k) for k in range(1 + len(got))]
            at += len(refs)
            for z in range(stretches):
                for k in range(items):
                    src = slice((k * stretches + z) * each, (k * stretches + z + 1) * each)
                    first = z * (rows // stretches) + (done + k) * each
                    big[0][first : first + each, :] = total([r[src, :] for r in refs]).astype(bf16)
            done += items

    return call(body, info, [], flat, [], [], [((rows, n_wide), bf16)], [], 0, 3, 24)[0]


def grad_pieces(info, own, got, items, each, under):
    stretches = lax.axis_size("stretch")
    rows, n_wide = own.shape
    width = each * stretches

    def body(info, small, get, raw, outs, big, put, scratch, loads):
        refs = [get(k) for k in range(1 + len(got))]
        first = items * width + under
        table = total([r[first : first + 16, :] for r in refs])
        half = n_wide // 2
        table = table[:, :half] + table[:, half:]
        hi = table.astype(bf16)
        lo = (table - hi.astype(f32)).astype(bf16)
        for j in list(range(1, stretches)) + [0]:
            z = jnp.bitwise_xor(info[2], j)
            for k in range(items):
                src = pl.ds(pl.multiple_of(k * width + z * each, each), each)
                big[j][k * each : (k + 1) * each, :] = total([r[src, :] for r in refs]).astype(bf16)
            big[j][items * each :, :half] = hi
            big[j][items * each :, half:] = lo
            put(j)
        middle = slice(items * width, first)
        big[stretches][...] = total([r[middle, :] for r in refs])

    return call(
        body, info, [], [(a, None) for a in (own, *got)], [], [],
        [((items * each + 16, n_wide), bf16)] * stretches + [((under, n_wide), f32)], [], 0, 3, 24)


def stretch_part(part):
    return lax.psum_scatter(part, "stretch", scatter_dimension=0, tiled=True)


def stretch_items(out, items):
    own = out.shape[0] // items
    return [out[k * own : (k + 1) * own].astype(f32) for k in range(items)]


def vector_rows(table, width):
    me, count = lax.axis_index("seg"), lax.axis_size("seg")
    own = table.shape[1] // count
    table = jnp.pad(table, ((0, 16 - table.shape[0]), (0, 0)))
    rows = []
    for m in range(0, count, 2):
        pair = lax.dynamic_slice_in_dim(table, (me ^ m) // 2 * (2 * own), 2 * own, 1)
        pair = jnp.pad(pair, ((0, 0), (0, width // 2 - 2 * own)))
        hi = pair.astype(bf16)
        rows.append(jnp.concatenate([hi, (pair - hi.astype(f32)).astype(bf16)], axis=1))
    return jnp.concatenate(rows, axis=0)


def vector_read(rows):
    half = rows.shape[1] // 2
    return rows[:, :half].astype(f32) + rows[:, half:].astype(f32)


def vector_own(pair, own):
    second = (lax.axis_index("seg") & 1) != 0
    lo, hi = pair[:, :own], pair[:, own : 2 * own]
    return jnp.where(second, hi, lo) + hop(jnp.where(second, lo, hi), 1)


def vector_finish(table):
    position, count = lax.axis_index("stretch"), lax.axis_size("stretch")
    bit = count // 2
    while bit:
        lo, hi = jnp.split(table, 2, axis=1)
        upper = (position & bit) != 0
        table = jnp.where(upper, hi, lo) + across(jnp.where(upper, lo, hi), bit)
        bit //= 2
    return table


def own_columns(x, me, w):
    ms = [*range(2, lax.axis_size("seg"), 2), 0]
    return jnp.concatenate([lax.dynamic_slice_in_dim(x, (me ^ m) * w, w, 1) for m in ms], axis=1)


def body(
    stream_in, cotangent, previous_mix, previous_ffn, state_num, state_den, state_exp,
    gain_one, bias_one, gain_two, bias_two, mix_key, mix_value, mix_recept,
    time_decay, time_first, chan_mix_key, chan_mix_recept,
    att_key, att_value, att_recept, att_output, chan_key, chan_value, chan_recept,
):
    mine = lax.axis_index("seg")
    position = lax.axis_index("stretch")
    stretches = lax.axis_size("stretch")
    batches, _, length, width = stream_in.shape
    tokens = batches * length
    shard = att_key.shape[0]
    fshard = chan_value.shape[0]
    wide = chan_key.shape[1]
    aligned = shard % 128 == 0
    count = lax.axis_size("seg")
    info = jnp.stack([mine, (position == 0).astype(jnp.int32), position])

    stream = stream_in.reshape(tokens, width)
    cot = cotangent.reshape(tokens, width)
    state = (state_num, state_den, state_exp)
    vectors = [gain_one, bias_one, gain_two, bias_two, mix_key, mix_value, mix_recept,
               time_decay, time_first, chan_mix_key, chan_mix_recept]

    v = Live()
    evens = list(range(0, count, 2))
    spots = {"k": 0, "v": shard, "vec": 2 * shard, "r": 2 * shard + 16, "o": 3 * shard + 16}
    each = fshard // stretches
    v.own_tm = pack(
        [(att_key, 0, shard), (att_value, 0, shard), (None, 0, 16)],
        [(att_recept, 0, shard), (att_output, 0, shard)], vectors, width)
    v.share = lax.dynamic_slice_in_dim(chan_value, position * each, each, 0)
    v.cv = chan_value
    v.last_in = stream_in[:, 0, length - 1]
    v.sync()
    v.shares = lax.all_gather(v.share, "seg", axis=0, tiled=True)
    v.one_tm = first_stage(v.own_tm)
    v.ck = pack_wide(tie(chan_key, *v.own_tm), chan_recept)
    v.tm0 = sibling({0: v.own_tm})
    v.last_in = along(tie(v.last_in, *v.tm0[1]), 1)
    v.sync()
    v.tm6 = second_stage(v.one_tm, v.one_tm)
    v.tm2 = sibling(v.one_tm)
    v.ck0 = sibling({0: v.ck})
    gathered_cv = lax.all_gather(
        jnp.concatenate([lax.dynamic_slice_in_dim(v.shares, (mine ^ m) * each, each, 0) for m in evens[1:]], axis=0),
        "stretch", axis=0, tiled=True)
    v.sync()
    v.tm6_sib = sibling(v.tm6)
    v.sync()

    v.one_ck = first_stage(v.ck)
    tm = {0: v.own_tm, **v.one_tm, **v.tm6, **v.tm0, **v.tm2, **v.tm6_sib}
    given = None
    if not aligned:
        given = lax.all_gather(jnp.stack(vectors), "seg", axis=1, tiled=True).astype(f32)
        given = jnp.pad(given, ((0, 5), (0, 0)))
    v.sums, v.vec, v.entry, v.kvr_in, *v.kvr = time_in(
        info, stream, v.last_in, previous_mix, given, tm, spots, length, shard)
    v.everyone = lax.all_gather(v.sums, "stretch")
    v.tm = tm
    v.drop("own_tm", "one_tm", "tm6", "tm0", "tm2", "tm6_sib", "share", "shares")
    v.sync()

    v.ck6 = second_stage(v.one_ck, v.one_ck)
    v.ent, v.mean, v.log, v.edge_b, v.gated, v.wkv, v.rden, v.mid, v.xb = time_out(
        info, v.kvr, v.everyone, state, v.vec, stream, v.tm, spots, length, shard)
    first_far = far_bits()[0]
    v.ck2 = sibling({first_far: v.one_ck[first_far]})
    v.edge_b = along(v.edge_b, 1)
    v.drop("everyone")
    v.sync()
    v.ck2 = {**v.ck2, **sibling({m: p for m, p in v.one_ck.items() if m != first_far})}
    v.all_ck = {0: v.ck, **v.one_ck, **v.ck6, **v.ck0, **v.ck2, **sibling(v.ck6)}
    v.gathered_cv = gathered_cv
    v.drop("ck", "one_ck", "ck6", "ck0", "ck2")
    v.sync()

    v.entry_b, v.f_in, v.near, v.far, v.act, v.frec = chan_in(
        info, v.xb, v.edge_b, previous_ffn, v.vec, v.all_ck, length, shard, fshard)
    v.all_cv = [v.cv, v.gathered_cv, hop(v.cv, 1), hop(v.gathered_cv, 1)]
    v.drop("cv", "gathered_cv")
    v.sync()
    v.block_out, v.d_fval, v.d_frec = chan_out(
        info, v.near, v.far, v.frec, v.mid, cot, v.all_cv, fshard)
    v.far_sib = hop(v.far, 1)
    v.f_sib = hop(v.f_in, 1)
    v.g_sib = hop(v.gated, 1)
    v.kvr_sib = hop(v.kvr_in, 1)
    v.drop("frec", "far")
    v.sync()

    def pairs(*arrays):
        if aligned:
            return [a for pair in arrays for a in pair]
        return [own_columns(a, mine, shard) for pair in arrays for a in pair]

    layout = "natural" if aligned else "joined"
    flat = tuple((j, None) for j in range(4))
    arrays = [v.near, v.far_sib, v.d_fval, hop(v.d_fval, 1)]
    v.stack_cv = weight_grad(info, arrays, [flat], "blocks", 6, stacked=True)[0]
    v.dfrec_sib = hop(v.d_frec, 1)
    v.drop("near", "far_sib")
    v.sync()

    z_cv = stretch_part(v.stack_cv)
    v.dpre = hidden_back(info, v.act, v.d_fval, v.all_cv, fshard)
    dpre_sib = hop(v.dpre, 1)
    v.head_b, v.sums_c, v.dxt, v.dxb = chan_back(
        info, v.dpre, v.d_frec, v.xb, v.entry_b, v.vec, v.all_ck, length, shard, fshard)
    v.next_b = along(v.head_b, -1)
    dpre = tie(v.dpre, v.dxt)
    if aligned:
        v.parts_ck = weight_grad(
            info, [v.f_in, v.f_sib, dpre, dpre_sib], [((0, 0), (1, 0), (2, None), (3, None))], layout, 7, True)
    else:
        v.parts_ck = weight_grad(
            info, [*pairs((v.f_in[0], v.f_sib[0])), dpre, dpre_sib], [flat], layout, 7, True)
    v.drop("all_ck", "all_cv", "xb", "entry_b", "act", "d_fval", "dpre", "stack_cv")
    v.sync()

    v.got_ck = grad_send(v.parts_ck)
    dent, v.sums_m, v.dmid, *lows, gn = mid_back(
        info, v.dxt, v.dxb, v.next_b, v.mid, cot, v.vec, v.kvr, v.wkv, v.rden, v.ent, v.tm, spots,
        length, shard)
    v.dbr, v.drec = lows[:2], lows[2:]
    back = lax.all_gather(jnp.concatenate([dent, v.ent[2 * batches :], v.head_b], axis=0), "stretch")
    *v.grads, v.head_a, v.sums_t, v.extra, v.d_kv, v.dxs, v.dxa = time_back(
        info, gn, v.wkv, v.kvr, v.ent, back, v.sums, state, v.drec, stream, v.entry, v.vec,
        v.tm, spots, length, shard)
    v.dbr_sib = [hop(a, 1) for a in v.dbr]
    v.drec_sib = [hop(a, 1) for a in v.drec]
    dys = [([(at, None), (at + 1, None)], [(at + 2, None), (at + 3, None)]) for at in (0, 4)]
    lows = [*v.dbr, *v.dbr_sib, *v.drec, *v.drec_sib, v.d_frec, v.dfrec_sib]
    last = ((8, None), (9, None))
    if aligned:
        v.parts_ocr = weight_grad(
            info, [*lows, tie(v.gated, v.d_kv), v.g_sib, v.f_in, v.f_sib, v.kvr_in, v.kvr_sib],
            [((10, None), (11, None), *dys[0]), ((12, 1), (13, 1), *last), ((14, 2), (15, 2), *dys[1])],
            layout, 6)
    else:
        xs = pairs((tie(v.gated, v.d_kv), v.g_sib), (v.f_in[1], v.f_sib[1]), (v.kvr_in[2], v.kvr_sib[2]))
        v.parts_ocr = weight_grad(
            info, [*lows, *xs],
            [((10, None), (11, None), *dys[0]), ((12, None), (13, None), *last),
             ((14, None), (15, None), *dys[1])], layout, 6)
    v.drop("wkv", "kvr", "ent", "sums", "entry", "tm", "dxt", "dxb", "mid", "rden", "next_b", "head_b")
    v.sync()
    v.dkv_sib = hop(v.d_kv, 1)
    v.next_a = along(v.head_a, -1)
    v.part_ck = grad_finish(info, [(v.parts_ck[0], v.got_ck, 1)])
    v.drop("gated", "g_sib", "dbr", "dbr_sib", "drec", "drec_sib", "f_in", "f_sib", "d_frec", "dfrec_sib",
           "parts_ck", "got_ck")
    v.z_cv = z_cv
    v.sync()

    v.got_ocr = grad_send(v.parts_ocr)
    z_ck = stretch_part(v.part_ck)
    sums_i, v.grad_stream = in_back(info, v.dxs, v.dxa, v.next_a, v.dmid, stream, v.vec, length)
    table = jnp.concatenate([sums_i, v.sums_m, v.sums_t, v.extra, v.sums_c], axis=0)
    under = [v.z_cv, vector_rows(table, width)]
    if aligned:
        v.parts_kv = weight_grad(
            info, [v.kvr_in, v.kvr_sib, v.d_kv, v.dkv_sib],
            [tuple((j, k) for j in range(4)) for k in range(2)], layout, 7, under=under)
    else:
        xs = pairs(*[(v.kvr_in[k], v.kvr_sib[k]) for k in range(2)])
        v.parts_kv = weight_grad(
            info, [*xs, v.d_kv, v.dkv_sib],
            [((2 * k, None), (2 * k + 1, None), (4, k), (5, k)) for k in range(2)], layout, 7, under=under)
    v.heads = lax.all_gather(v.head_a, "stretch")[0]
    v.drop("kvr_in", "kvr_sib", "d_kv", "dkv_sib", "dxs", "dxa", "dmid", "next_a", "part_ck",
           "sums_m", "sums_t", "extra", "sums_c", "z_cv")
    v.sync()

    v.got_kv = grad_send(v.parts_kv)
    z_ocr = stretch_part(grad_finish(info, [(v.parts_ocr[0], v.got_ocr, 3)]))
    v.z_ck = z_ck
    v.drop("parts_ocr", "got_ocr")
    v.sync()
    rows = shard // stretches
    by_hops = stretches == 4 and rows % 16 == 0
    if by_hops:
        *v.pieces, v.out_cv = grad_pieces(info, v.parts_kv[0], v.got_kv, 2, rows, each)
    else:
        whole = total([v.parts_kv[0], *v.got_kv])
        first = 2 * shard
        v.out_cv, v.table = whole[first : first + each], vector_read(whole[first + each :])
        v.part_kv = grad_finish(info, [(v.parts_kv[0][:first], [g[:first] for g in v.got_kv], 2)])
    v.z_ocr = z_ocr
    v.drop("parts_kv", "got_kv")
    v.sync()
    if by_hops:
        pieces = [v.pieces[0], *[across(v.pieces[j], j) for j in range(1, stretches)]]
        z_kv = total([p[: 2 * rows] for p in pieces])
        small = sum(vector_read(p[2 * rows : 2 * rows + 11]) for p in pieces)
        small = lax.dynamic_slice_in_dim(vector_own(small, shard), position * rows, rows, 1)
    else:
        z_kv = stretch_part(v.part_kv)
        small = vector_finish(vector_own(v.table[:11], shard))
    out_cv, out_ck = [v.out_cv], stretch_items(v.z_ck, 1)
    out_o, out_c, out_r = stretch_items(v.z_ocr, 3)
    out_k, out_v = stretch_items(z_kv, 2)
    grad_previous_mix = v.heads
    block_out, grad_stream = v.block_out, v.grad_stream

    shape = stream_in.shape
    return (
        block_out.reshape(shape), grad_stream.reshape(shape), *[small[i] for i in range(11)],
        out_k, out_v, out_r, out_o, *out_ck, *out_cv, out_c,
        *v.grads[:3], grad_previous_mix[:, None], v.grads[3], v.mean, v.log,
    )


def solution(mesh):
    rows = P(None, "seg", "stretch", None)
    state = P(None, "seg", None)
    both = P(("seg", "stretch"))
    table = P(("seg", "stretch"), None)
    return jax.shard_map(
        body,
        mesh=mesh,
        in_specs=(rows,) * 2 + (state,) * 5 + (P("seg"),) * 11 + (P("seg", None),) * 7,
        out_specs=(rows,) * 2 + (both,) * 11 + (table,) * 7 + (state,) * 7,
        check_vma=False,
    )
```

time: 402 us -> 369 us (0.918); the launches traced: 397 us -> 368 us
  starting transfers between devices: 75.8 us -> 48.6 us
  Pallas kernels: 133 us -> 127 us
    ppermute x57 -> x52, starting transfers between devices: 52.7 us -> 35.2 us  [hop(): return lax.ppermute(value, 'seg', [(i, i ^ bit) for i in range(count)])]
    reduce_scatter x4 -> x3, waiting for transfers between devices: 15.4 us -> 0.04 us  [stretch_part(): return lax.psum_scatter(part, 'stretch', scatter_dimension=0, tiled=True)]
    pallas_call x20 -> x16, Pallas kernels: 130 us -> 122 us  [call(): pl.pallas_call(kernel, out_shape=[jax.ShapeDtypeStruct(s, d) for s, d in...]
    ppermute x5 -> x3, starting transfers between devices: 10.2 us -> 2.71 us  [across(): return lax.ppermute(value, 'stretch', [(i, i ^ j) for i in range(count)])]
    slice x4 -> x2, local copies, waits for them, and re-layouts: 7.46 us -> 0.72 us  [the longest x1 0.72 us: stretch_items(): return [out[k * own:(k + 1) * own].astype(f32) for k in range(items)]]
    ppermute x5 -> x3, waiting for transfers between devices: 4.93 us -> 11.2 us  [across(): return lax.ppermute(value, 'stretch', [(i, i ^ j) for i in range(count)])]
    ppermute x57 -> x52, waiting for transfers between devices: 94.2 us -> 100 us  [hop(): return lax.ppermute(value, 'seg', [(i, i ^ bit) for i in range(count)])]
    unnamed x114 -> x102, local copies, waits for them, and re-layouts: 5.52 us -> 9.91 us
  transfers between devices with their start and end apart: 70 -> 64, of which waited for: 33 -> 21; matrix products, arithmetic and copies ran while one was open for 3% -> 2% of each run, Pallas kernels for 25% -> 34%
where the time goes in v3:
time: 369 us; the launch traced here: 368 us
  Pallas kernels  127 us (34%)
  waiting for transfers between devices  116 us (31%)
  starting transfers between devices  48.6 us (13%)
  blocking collectives  37.6 us (10%)
  local copies, waits for them, and re-layouts  16.5 us (4%)
  between operations  14.7 us (4%)
  other arithmetic  7.22 us (2%)
    pallas_call x16, Pallas kernels, call(): pl.pallas_call(kernel, out_shape=[jax.ShapeDtypeStruct(s, d) for s, d in...  122 us
    ppermute x52, waiting for transfers between devices, hop(): return lax.ppermute(value, 'seg', [(i, i ^ bit) for i in range(count)])  100 us
    ppermute x52, starting transfers between devices, hop(): return lax.ppermute(value, 'seg', [(i, i ^ bit) for i in range(count)])  35.2 us
    all_gather x1, blocking collectives, body(): lax.all_gather(jnp.concatenate([dent, v.ent[2 * batches:], v.head_b], axi...  14.6 us
    all_gather x1, blocking collectives, body(): v.everyone = lax.all_gather(v.sums, 'stretch')  13.2 us
    ppermute x3, waiting for transfers between devices, across(): return lax.ppermute(value, 'stretch', [(i, i ^ j) for i in range(count)])  11.2 us
    ppermute x4, starting transfers between devices, along(): lax.ppermute(value, 'stretch', [(i, i + steps) for i in range(first, last)])  10.6 us
    unnamed x102, local copies, waits for them, and re-layouts  9.91 us
  transfers between devices with their start and end apart: 64, of which 21 were waited for; matrix products, arithmetic and copies ran while one was open for 2% of the time, Pallas kernels for 34%

profile of v3, /device:TPU:9, one launch (start us, length us, event | category | flops | bytes accessed | tf_op | source)
XLA Modules:
  0.0 368.1 jit_solution(788025008284084524)
XLA Ops:
  8.0 1.7 constant_dynamic-slice_fusion.3
  9.7 3.0 shard_map.448
  13.6 1.2 collective-permute-start.3
  14.8 1.2 collective-permute-start.5
  17.1 3.2 collective-permute-start.2
  20.4 2.4 shard_map.449
  22.8 22.5 %collective-permute-done.4.refs_7_.refs_13_.refs_15_.refs_19_ = bf16[256,1024]{1,0:T(8,128)(2,1)S(1)} collective-permute-done((bf16[256,1024]{1,0:T(8,128)(2,1)}, bf16[256,1024]{1,0:T(8,128)(2,1)S(1)}, u32[]{:S(2)}, u32[]{:S(2)}) %collective-permute-start.4) | collective-permute-done | bytes 524320 | tf_op jit(solution)/shard_map/ppermute | solution.py:21
  45.3 1.8 collective-permute-done.6.refs_9_.refs_15_.refs_17_.refs_21_
  47.2 3.3 all-gather.8.cloned.1.call-done
  50.5 1.2 constant_dynamic-slice_fusion.2
  51.6 0.9 pad_maximum_fusion
  55.5 10.8 %collective-permute-done.14.refs_11_.refs_17_.refs_19_.refs_23_ = bf16[256,1024]{1,0:T(8,128)(2,1)S(1)} collective-permute-done((bf16[256,1024]{1,0:T(8,128)(2,1)S(1)}, bf16[256,1024]{1,0:T(8,128)(2,1)S(1)}, u32[]{:S(2)}, u32[]{:S(2)}) %collective-permute-start.14) | collective-permute-done | bytes 524320 | tf_op jit(solution)/shard_map/ppermute | solution.py:21
  66.3 1.0 collective-permute-start.9
  67.4 1.5 collective-permute-done.13.refs_10_.refs_16_.refs_18_.refs_22_
  71.1 2.3 collective-permute-done.16.refs_19_.refs_25_.refs_27_.refs_31_
  77.0 8.4 %shard_map.450 = (f32[6,1024]{1,0:T(8,128)}, f32[16,1024]{1,0:T(8,128)}, f32[2,1024]{1,0:T(2,128)}, bf16[3,256,1024]{2,1,0:T(8,128)(2,1)}, f32[256,1024]{1,0:T(8...) custom-call(s32[3]{0:T(128)} %pad_add_fusion.refs_0_, bf16[2,1024]{1,0:T(2,128)(2,1)} %copy-done.49, ...), custom_call_target="tpu_custom_call" | custom-call | bytes 9000 | tf_op jit(solution)/shard_map/pallas_call | solution.py:180
  85.4 13.2 %all-gather.3.refs_1_ = f32[4,6,1024]{2,1,0:T(8,128)} all-gather(f32[1,6,1024]{2,1,0:T(8,128)} %bitcast.60), channel_id=2, replica_groups=mesh['seg'=8,'stretch'=4] {'stretch'}, dimensions={0}, use_global_device_ids=true | all-gather | bytes 122880 | tf_op jit(solution)/shard_map/all_gather | solution.py:1227
  98.6 5.1 %collective-permute-done.18.refs_8_.refs_9_ = bf16[80,4096]{1,0:T(8,128)(2,1)} collective-permute-done((bf16[80,4096]{1,0:T(8,128)(2,1)}, bf16[80,4096]{1,0:T(8,128)(2,1)}, u32[]{:S(2)}, u32[]{:S(2)}) %collective-permute-start.18) | collective-permute-done | bytes 655392 | tf_op jit(solution)/shard_map/ppermute | solution.py:21
  104.6 1.9 collective-permute-start.21
  108.2 8.3 %shard_map.451 = (f32[6,1024]{1,0:T(8,128)}, f32[2,1,1024]{2,1,0:T(1,128)}, f32[2,1,1024]{2,1,0:T(1,128)}, f32[2,1024]{1,0:T(2,128)}, bf16[256,1024]{1,0:T(8,128...) custom-call(s32[3]{0:T(128)} %pad_add_fusion.refs_0_, ...), custom_call_target="tpu_custom_call" | custom-call | bytes 7000 | tf_op jit(solution)/shard_map/pallas_call | solution.py:180
  116.5 3.3 collective-permute-start.25
  119.9 1.6 collective-permute-done.25.refs_1_
  121.5 1.5 collective-permute-done.23.refs_11_.refs_12_
  123.8 1.0 collective-permute-start.26
  125.3 1.4 collective-permute-done.26.refs_17_.refs_18_
  126.8 2.8 collective-permute-done.27.refs_18_.refs_19_
  131.9 10.3 %shard_map.452 = (f32[2,1024]{1,0:T(2,128)}, bf16[2,256,1024]{2,1,0:T(8,128)(2,1)}, bf16[256,2048]{1,0:T(8,128)(2,1)}, bf16[256,2048]{1,0:T(8,128)(2,1)}, bf16[2...) custom-call(s32[3]{0:T(128)} %pad_add_fusion.refs_0_, f32[2,1024]{1,0:T(2,128)} %copy-done.48, f32[2,1,1024]{2,1,0:T(1,128)} %refs_2_.5, ...), custom_call_target="tpu_custom_call" | custom-call | bytes 11000 | tf_op jit(solution)/shard_map/pallas_call | solution.py:180
  143.8 9.0 %shard_map.453 = (bf16[256,1024]{1,0:T(8,128)(2,1)}, bf16[256,1024]{1,0:T(8,128)(2,1)}, bf16[256,1024]{1,0:T(8,128)(2,1)}) custom-call(s32[3]{0:T(128)} %pad_add_fusion.refs_0_, bf16[256,2048]{1,0:T(8,128)(2,1)} %get-tuple-element.933.refs_1_, bf16[256,2048]{1,0:T(8,128)(2,1)} %get-tuple-element.855.refs_2_, f32[256,1024]{1,0:T(8,128)} %get-tuple-element.856.refs_3_, ...), custom_call_target="tpu_custom_call" | custom-call | bytes 7000 | tf_op jit(solution)/shard_map/pallas_call | solution.py:180
  153.4 1.6 collective-permute-done.37.refs_4_
  155.9 7.2 %shard_map.454 = bf16[2048,1024]{1,0:T(8,128)(2,1)} custom-call(s32[3]{0:T(128)} %pad_add_fusion.refs_0_, bf16[256,2048]{1,0:T(8,128)(2,1)} %get-tuple-element.933.refs_1_, bf16[256,2048]{1,0:T(8,128)(2,1)} %collective-permute-done.33.refs_2_, bf16[256,1024]{1,0:T(8,128)(2,1)} %get-tuple-element.960.refs_3_.refs_1_, bf16[256,1024]{1,0:T(8,128)(2,1)} %copy-done.35), custom_call_target="tpu_custom_call" | custom-call | bytes 6000 | tf_op jit(solution)/shard_map/pallas_call | solution.py:180
  163.8 8.1 %shard_map.455.refs_4_.refs_3_ = bf16[256,4096]{1,0:T(8,128)(2,1)} custom-call(s32[3]{0:T(128)} %pad_add_fusion.refs_0_, bf16[256,1024]{1,0:T(8,128)(2,1)} %get-tuple-element.960.refs_3_.refs_1_, bf16[256,4096]{1,0:T(8,128)(2,1)} %get-tuple-element.961.refs_2_, bf16[512,1024]{1,0:T(8,128)(2,1)} %refs_3_.2, ...), custom_call_target="tpu_custom_call" | custom-call | bytes 7000 | tf_op jit(solution)/shard_map/pallas_call | solution.py:180
  172.3 11.7 %shard_map.456 = (f32[2,1024]{1,0:T(2,128)}, f32[2,1024]{1,0:T(2,128)}, f32[256,1024]{1,0:T(8,128)}, f32[256,1024]{1,0:T(8,128)}) custom-call(s32[3]{0:T(128)} %pad_add_fusion.refs_0_, f32[2,1024]{1,0:T(2,128)} %get-tuple-element.958.refs_1_, f32[16,1024]{1,0:T(8,128)} %get-tuple-element.1127.refs_5_.refs_3_.refs_2_.refs_8_, ...), custom_call_target="tpu_custom_call" | custom-call | bytes 10000 | tf_op jit(solution)/shard_map/pallas_call | solution.py:180
  184.1 2.1 collective-permute-start.38
  186.2 1.3 copy-done.24
  187.6 7.0 %shard_map.457 = (bf16[128,4096]{1,0:T(8,128)(2,1)}, bf16[128,4096]{1,0:T(8,128)(2,1)}, bf16[128,4096]{1,0:T(8,128)(2,1)}, bf16[128,4096]{1,0:T(8,128)(2,1)}) custom-call(s32[3]{0:T(128)} %pad_add_fusion.refs_0_, bf16[2,256,1024]{2,1,0:T(8,128)(2,1)} %get-tuple-element.1069.refs_1_.refs_13_, bf16[2,256,1024]{2,1,0:T(8,128)(2,1)} %collective-permute-done.32.refs_2_.refs_14_, ...), custom_call_target="tpu_custom_call" | custom-call | bytes 7000 | tf_op jit(solution)/shard_map/pallas_call | solution.py:180
  196.0 1.3 collective-permute-start.46
  197.4 8.3 %shard_map.458 = (f32[4,1024]{1,0:T(4,128)}, f32[2,1024]{1,0:T(2,128)}, f32[256,1024]{1,0:T(8,128)}, bf16[256,512]{1,0:T(8,128)(2,1)}, bf16[256,512]{1,0:T(8,128...) custom-call(s32[3]{0:T(128)} %pad_add_fusion.refs_0_, f32[2,1024]{1,0:T(2,128)} %copy-done.42, ...), custom_call_target="tpu_custom_call" | custom-call | bytes 9000 | tf_op jit(solution)/shard_map/pallas_call | solution.py:180
  205.6 1.3 collective-permute-start.40
  207.1 1.3 collective-permute-done.40.refs_3_
  210.6 14.6 %all-gather.1 = f32[32,1024]{1,0:T(8,128)} all-gather(f32[8,1024]{1,0:T(8,128)S(1)} %pad_maximum_fusion.1), channel_id=3, replica_groups=mesh['seg'=8,'stretch'=4] {'stretch'}, dimensions={0}, use_global_device_ids=true | all-gather | bytes 163840 | tf_op jit(solution)/shard_map/all_gather | solution.py:1294
  225.2 12.9 %shard_map.459 = (f32[2,1,1024]{2,1,0:T(1,128)}, f32[2,1,1024]{2,1,0:T(1,128)}, f32[2,1,1024]{2,1,0:T(1,128)}, f32[2,1,1024]{2,1,0:T(1,128)}, f32[2,1024]{1,0:T(...) custom-call(s32[3]{0:T(128)} %pad_add_fusion.refs_0_, ...), custom_call_target="tpu_custom_call" | custom-call | bytes 14000 | tf_op jit(solution)/shard_map/pallas_call | solution.py:180
  238.9 6.7 %shard_map.460 = (bf16[384,1024]{1,0:T(8,128)(2,1)}, bf16[384,1024]{1,0:T(8,128)(2,1)}, bf16[384,1024]{1,0:T(8,128)(2,1)}, bf16[384,1024]{1,0:T(8,128)(2,1)}) custom-call(s32[3]{0:T(128)} %pad_add_fusion.refs_0_, bf16[256,512]{1,0:T(8,128)(2,1)} %get-tuple-element.1062.refs_1_, bf16[256,512]{1,0:T(8,128)(2,1)} %get-tuple-element.1063.refs_2_, ...), custom_call_target="tpu_custom_call" | custom-call | bytes 6000 | tf_op jit(solution)/shard_map/pallas_call | solution.py:180
  245.6 1.0 copy-done.28
  246.6 4.1 %collective-permute-start.47 = (bf16[2,256,1024]{2,1,0:T(8,128)(2,1)S(1)}, bf16[2,256,1024]{2,1,0:T(8,128)(2,1)S(1)}, u32[]{:S(2)}, u32[]{:S(2)}) collective-permute-start(bf16[2,256,1024]{2,1,0:T(8,128)(2,1)S(1)} %copy-done.25), channel_id=1, source_target_pairs={{0,4},{4,0},{8,12},{12,8},{16,20},{20,16},{24,28},{28,24},{1,5},{5... | collective-permute-start | bytes 3145736 | tf_op jit(solution)/shard_map/ppermute | solution.py:21
  250.7 1.9 collective-permute-start.48
  252.6 4.4 %shard_map.461 = bf16[128,4096]{1,0:T(8,128)(2,1)} custom-call(s32[3]{0:T(128)} %pad_add_fusion.refs_0_, bf16[128,4096]{1,0:T(8,128)(2,1)} %get-tuple-element.1109.refs_1_, bf16[128,4096]{1,0:T(8,128)(2,1)} %copy-done.27, bf16[128,4096]{1,0:T(8,128)(2,1)} %copy-done.28, bf16[128,4096]{1,0:T(8,128)(2,1)} %collective-permute-done.46.refs_4_), custom_call_target="tpu_custom_call" | custom-call | bytes 3000 | tf_op jit(solution)/shard_map/pallas_call | solution.py:180
  257.3 1.2 collective-permute-start.49
  258.5 1.5 collective-permute-start.51
  260.0 5.6 %shard_map.462 = (f32[2,1024]{1,0:T(2,128)}, bf16[256,1024]{1,0:T(8,128)(2,1)}) custom-call(s32[3]{0:T(128)} %pad_add_fusion.refs_0_, f32[2,1024]{1,0:T(2,128)} %copy-done.41, f32[16,1024]{1,0:T(8,128)} %get-tuple-element.1127.refs_5_.refs_3_.refs_2_.refs_8_, f32[256,1024]{1,0:T(8,128)} %get-tuple-element.1128.refs_3_, ...), custom_call_target="tpu_custom_call" | custom-call | bytes 6000 | tf_op jit(solution)/shard_map/pallas_call | solution.py:180
  267.2 6.1 %shard_map.463 = (bf16[400,1024]{1,0:T(8,128)(2,1)}, bf16[400,1024]{1,0:T(8,128)(2,1)}, bf16[400,1024]{1,0:T(8,128)(2,1)}, bf16[400,1024]{1,0:T(8,128)(2,1)}) custom-call(s32[3]{0:T(128)} %pad_add_fusion.refs_0_, bf16[3,256,1024]{2,1,0:T(8,128)(2,1)} %get-tuple-element.1139.refs_15_.refs_1_, bf16[3,256,1024]{2,1,0:T(8,128)(2,1)} %collective-permute-done.35.refs_16_.refs_2_, ...), custom_call_target="tpu_custom_call" | custom-call | bytes 7000 | tf_op jit(solution)/shard_map/pallas_call | solution.py:180
  273.3 9.8 %all-gather.4 = f32[4,2,1024]{2,1,0:T(2,128)S(1)} all-gather(f32[1,2,1024]{2,1,0:T(2,128)S(1)} %bitcast.62), channel_id=4, replica_groups=mesh['seg'=8,'stretch'=4] {'stretch'}, dimensions={0}, use_global_device_ids=true | all-gather | bytes 40960 | tf_op jit(solution)/shard_map/all_gather | solution.py:1338
  283.2 11.2 %collective-permute-done.51.refs_4_ = bf16[384,1024]{1,0:T(8,128)(2,1)} collective-permute-done((bf16[384,1024]{1,0:T(8,128)(2,1)}, bf16[384,1024]{1,0:T(8,128)(2,1)}, u32[]{:S(2)}, u32[]{:S(2)}) %collective-permute-start.51) | collective-permute-done | bytes 786464 | tf_op jit(solution)/shard_map/ppermute | solution.py:21
  294.4 3.8 %shard_map.465 = bf16[384,1024]{1,0:T(8,128)(2,1)} custom-call(s32[3]{0:T(128)} %pad_add_fusion.refs_0_, bf16[384,1024]{1,0:T(8,128)(2,1)} %get-tuple-element.1187.refs_1_, bf16[384,1024]{1,0:T(8,128)(2,1)} %copy-done.32, bf16[384,1024]{1,0:T(8,128)(2,1)} %copy-done.33, bf16[384,1024]{1,0:T(8,128)(2,1)} %collective-permute-done.51.refs_4_), custom_call_target="tpu_custom_call" | custom-call | bytes 3000 | tf_op jit(solution)/shard_map/pallas_call | solution.py:180
  298.6 1.4 collective-permute-start.53
  300.0 1.0 collective-permute-start.54
  301.0 15.4 %collective-permute-done.52.refs_2_ = bf16[400,1024]{1,0:T(8,128)(2,1)S(1)} collective-permute-done((bf16[400,1024]{1,0:T(8,128)(2,1)}, bf16[400,1024]{1,0:T(8,128)(2,1)S(1)}, u32[]{:S(2)}, u32[]{:S(2)}) %collective-permute-start.52) | collective-permute-done | bytes 819232 | tf_op jit(solution)/shard_map/ppermute | solution.py:21
  316.4 18.4 %collective-permute-done.54.refs_4_ = bf16[400,1024]{1,0:T(8,128)(2,1)S(1)} collective-permute-done((bf16[400,1024]{1,0:T(8,128)(2,1)}, bf16[400,1024]{1,0:T(8,128)(2,1)S(1)}, u32[]{:S(2)}, u32[]{:S(2)}) %collective-permute-start.54) | collective-permute-done | bytes 819232 | tf_op jit(solution)/shard_map/ppermute | solution.py:21
  335.8 3.9 %shard_map.464 = (bf16[80,1024]{1,0:T(8,128)(2,1)}, bf16[80,1024]{1,0:T(8,128)(2,1)}, bf16[80,1024]{1,0:T(8,128)(2,1)}, bf16[80,1024]{1,0:T(8,128)(2,1)}, f32[128,1024]{1,0:T(8,128)}) custom-call(s32[3]{0:T(128)} %pad_add_fusion.refs_0_, bf16[400,1024]{1,0:T(8,128)(2,1)} %get-tuple-element.1177.refs_1_, bf16[400,1024]{1,0:T(8,128)(2,1)} %copy-done.29, ...), custom_call_target="tpu_custom_call" | custom-call | bytes 3000 | tf_op jit(solution)/shard_map/pallas_call | solution.py:180
  339.8 2.0 collective-permute-start.56
  343.9 1.7 slice_convert_fusion
  345.5 1.2 collective-permute-done.56
  346.8 9.9 %collective-permute-done.57 = bf16[80,1024]{1,0:T(8,128)(2,1)S(1)} collective-permute-done((bf16[80,1024]{1,0:T(8,128)(2,1)}, bf16[80,1024]{1,0:T(8,128)(2,1)S(1)}, u32[]{:S(2)}, u32[]{:S(2)}) %collective-permute-start.57) | collective-permute-done | bytes 163872 | tf_op jit(solution)/shard_map/ppermute | solution.py:32
  357.5 1.7 collective-permute-start.58
  359.2 1.0 convert_add_fusion
  (215 shorter events, 33.6 us)
Async XLA Ops:
  7.2 43.3 %all-gather.8.cloned.1.call-start = ((), (), s32[]{:S(2)}) async-start(), calls=%async_computation.3 | async-start | bytes 2359296 | tf_op jit(solution)/shard_map/all_gather | solution.py:1203
  12.7 118.6 %all-gather.10.cloned.1.call-start = ((), (), s32[]{:S(2)}) async-start(), calls=%async_computation.4 | async-start | bytes 3932160 | tf_op jit(solution)/shard_map/all_gather | solution.py:1212
  12.8 3.5 collective-permute-start.1
  13.5 3.0 collective-permute-start
  13.6 33.5 %collective-permute-start.3 = (bf16[272,1024]{1,0:T(8,128)(2,1)}, bf16[272,1024]{1,0:T(8,128)(2,1)S(1)}, u32[]{:S(2)}, u32[]{:S(2)}) collective-permute-start(bf16[272,1024]{1,0:T(8,128)(2,1)} %get-tuple-element.1037.refs_4_.refs_10_.refs_12_.refs_16_), channel_id=1, source_target_pairs={{0,8},{4,12},{8,0},{12,4},{16,24},{20,28},{24,16},{28,20},{1,9},{5... | collective-permute-start | bytes 1671176 | tf_op jit(solution)/shard_map/ppermute | solution.py:21
  14.8 32.3 %collective-permute-start.5 = (bf16[272,1024]{1,0:T(8,128)(2,1)}, bf16[272,1024]{1,0:T(8,128)(2,1)S(1)}, u32[]{:S(2)}, u32[]{:S(2)}) collective-permute-start(bf16[272,1024]{1,0:T(8,128)(2,1)} %get-tuple-element.1037.refs_4_.refs_10_.refs_12_.refs_16_), channel_id=1, source_target_pairs={{0,16},{4,20},{8,24},{12,28},{16,0},{20,4},{24,8},{28,12},{1,17},{... | collective-permute-start | bytes 1671176 | tf_op jit(solution)/shard_map/ppermute | solution.py:21
  16.1 29.2 %collective-permute-start.4 = (bf16[256,1024]{1,0:T(8,128)(2,1)}, bf16[256,1024]{1,0:T(8,128)(2,1)S(1)}, u32[]{:S(2)}, u32[]{:S(2)}) collective-permute-start(bf16[256,1024]{1,0:T(8,128)(2,1)} %get-tuple-element.1038.refs_5_.refs_11_.refs_13_.refs_17_), channel_id=1, source_target_pairs={{0,8},{4,12},{8,0},{12,4},{16,24},{20,28},{24,16},{28,20},{1,9},{5... | collective-permute-start | bytes 1572872 | tf_op jit(solution)/shard_map/ppermute | solution.py:21
  16.3 30.8 %collective-permute-start.6 = (bf16[256,1024]{1,0:T(8,128)(2,1)}, bf16[256,1024]{1,0:T(8,128)(2,1)S(1)}, u32[]{:S(2)}, u32[]{:S(2)}) collective-permute-start(bf16[256,1024]{1,0:T(8,128)(2,1)} %get-tuple-element.1038.refs_5_.refs_11_.refs_13_.refs_17_), channel_id=1, source_target_pairs={{0,16},{4,20},{8,24},{12,28},{16,0},{20,4},{24,8},{28,12},{1,17},{... | collective-permute-start | bytes 1572872 | tf_op jit(solution)/shard_map/ppermute | solution.py:21
  17.1 30.0 %collective-permute-start.2 = (bf16[2,1024]{1,0:T(2,128)(2,1)S(1)}, bf16[2,1024]{1,0:T(2,128)(2,1)S(1)}, u32[]{:S(2)}, u32[]{:S(2)}) collective-permute-start(bf16[2,1024]{1,0:T(2,128)(2,1)S(1)} %bitcast.63), channel_id=1, source_target_pairs={{0,1},{1,2},{2,3},{4,5},{5,6},{6,7},{8,9},{9,10},{10,11},{12,13},{... | collective-permute-start | bytes 12296 | tf_op jit(solution)/shard_map/ppermute | solution.py:27
  52.6 204.4 %reduce-scatter.4.cloned.1.call-start = ((), (), s32[]{:S(2)}) async-start(), calls=%async_computation.5 | async-start | bytes 5242880 | tf_op jit(solution)/shard_map/reduce_scatter | solution.py:1120
  52.7 2.1 collective-permute-start.12
  53.0 13.4 %collective-permute-start.14 = (bf16[256,1024]{1,0:T(8,128)(2,1)S(1)}, bf16[256,1024]{1,0:T(8,128)(2,1)S(1)}, u32[]{:S(2)}, u32[]{:S(2)}) collective-permute-start(bf16[256,1024]{1,0:T(8,128)(2,1)S(1)} %collective-permute-done.6.refs_9_.refs_15_.refs_17_.refs_21_), channel_id=1, source_target_pairs={{0,8},{4,12},{8,0},{12,4},{16,24},{20,28},{24,16},{28,20},{1,9},{5... | collective-permute-start | bytes 1572872 | tf_op jit(solution)/shard_map/ppermute | solution.py:21
  53.7 13.6 %collective-permute-start.10 = (bf16[256,1024]{1,0:T(8,128)(2,1)S(1)}, bf16[256,1024]{1,0:T(8,128)(2,1)S(1)}, u32[]{:S(2)}, u32[]{:S(2)}) collective-permute-start(bf16[256,1024]{1,0:T(8,128)(2,1)S(1)} %collective-permute-done.4.refs_7_.refs_13_.refs_15_.refs_19_), channel_id=1, source_target_pairs={{0,4},{4,0},{8,12},{12,8},{16,20},{20,16},{24,28},{28,24},{1,5},{5... | collective-permute-start | bytes 1572872 | tf_op jit(solution)/shard_map/ppermute | solution.py:21
  54.2 15.5 %collective-permute-start.7 = (bf16[80,4096]{1,0:T(8,128)(2,1)S(1)}, bf16[80,4096]{1,0:T(8,128)(2,1)S(1)}, u32[]{:S(2)}, u32[]{:S(2)}) collective-permute-start(bf16[80,4096]{1,0:T(8,128)(2,1)S(1)} %copy-done.15), channel_id=1, source_target_pairs={{0,4},{4,0},{8,12},{12,8},{16,20},{20,16},{24,28},{28,24},{1,5},{5... | collective-permute-start | bytes 1966088 | tf_op jit(solution)/shard_map/ppermute | solution.py:21
  54.2 15.5 %collective-permute-start.8 = (bf16[80,4096]{1,0:T(8,128)(2,1)}, bf16[80,4096]{1,0:T(8,128)(2,1)S(1)}, u32[]{:S(2)}, u32[]{:S(2)}) collective-permute-start(bf16[80,4096]{1,0:T(8,128)(2,1)} %get-tuple-element.968.refs_6_.refs_7_), channel_id=1, source_target_pairs={{0,4},{4,0},{8,12},{12,8},{16,20},{20,16},{24,28},{28,24},{1,5},{5... | collective-permute-start | bytes 1966088 | tf_op jit(solution)/shard_map/ppermute | solution.py:21
  54.7 14.2 %collective-permute-start.13 = (bf16[272,1024]{1,0:T(8,128)(2,1)S(1)}, bf16[272,1024]{1,0:T(8,128)(2,1)S(1)}, u32[]{:S(2)}, u32[]{:S(2)}) collective-permute-start(bf16[272,1024]{1,0:T(8,128)(2,1)S(1)} %collective-permute-done.3.refs_6_.refs_12_.refs_14_.refs_18_), channel_id=1, source_target_pairs={{0,16},{4,20},{8,24},{12,28},{16,0},{20,4},{24,8},{28,12},{1,17},{... | collective-permute-start | bytes 1671176 | tf_op jit(solution)/shard_map/ppermute | solution.py:21
  66.3 2.6 collective-permute-start.9
  67.3 2.4 collective-permute-start.11
  70.6 2.8 collective-permute-start.15
  71.0 2.3 collective-permute-start.16
  73.4 25.2 %collective-permute-start.17 = (bf16[80,4096]{1,0:T(8,128)(2,1)}, bf16[80,4096]{1,0:T(8,128)(2,1)}, u32[]{:S(2)}, u32[]{:S(2)}) collective-permute-start(bf16[80,4096]{1,0:T(8,128)(2,1)} %get-tuple-element.967.refs_5_.refs_6_), channel_id=1, source_target_pairs={{0,8},{4,12},{8,0},{12,4},{16,24},{20,28},{24,16},{28,20},{1,9},{5... | collective-permute-start | bytes 1966088 | tf_op jit(solution)/shard_map/ppermute | solution.py:21
  74.2 29.5 %collective-permute-start.18 = (bf16[80,4096]{1,0:T(8,128)(2,1)}, bf16[80,4096]{1,0:T(8,128)(2,1)}, u32[]{:S(2)}, u32[]{:S(2)}) collective-permute-start(bf16[80,4096]{1,0:T(8,128)(2,1)} %get-tuple-element.968.refs_6_.refs_7_), channel_id=1, source_target_pairs={{0,8},{4,12},{8,0},{12,4},{16,24},{20,28},{24,16},{28,20},{1,9},{5... | collective-permute-start | bytes 1966088 | tf_op jit(solution)/shard_map/ppermute | solution.py:21
  74.9 28.8 %collective-permute-start.19 = (bf16[80,4096]{1,0:T(8,128)(2,1)}, bf16[80,4096]{1,0:T(8,128)(2,1)}, u32[]{:S(2)}, u32[]{:S(2)}) collective-permute-start(bf16[80,4096]{1,0:T(8,128)(2,1)} %get-tuple-element.967.refs_5_.refs_6_), channel_id=1, source_target_pairs={{0,16},{4,20},{8,24},{12,28},{16,0},{20,4},{24,8},{28,12},{1,17},{... | collective-permute-start | bytes 1966088 | tf_op jit(solution)/shard_map/ppermute | solution.py:21
  75.7 28.9 %collective-permute-start.20 = (bf16[80,4096]{1,0:T(8,128)(2,1)}, bf16[80,4096]{1,0:T(8,128)(2,1)}, u32[]{:S(2)}, u32[]{:S(2)}) collective-permute-start(bf16[80,4096]{1,0:T(8,128)(2,1)} %get-tuple-element.968.refs_6_.refs_7_), channel_id=1, source_target_pairs={{0,16},{4,20},{8,24},{12,28},{16,0},{20,4},{24,8},{28,12},{1,17},{... | collective-permute-start | bytes 1966088 | tf_op jit(solution)/shard_map/ppermute | solution.py:21
  104.6 16.9 %collective-permute-start.21 = (bf16[80,4096]{1,0:T(8,128)(2,1)}, bf16[80,4096]{1,0:T(8,128)(2,1)}, u32[]{:S(2)}, u32[]{:S(2)}) collective-permute-start(bf16[80,4096]{1,0:T(8,128)(2,1)} %collective-permute-done.17.refs_7_.refs_8_), channel_id=1, source_target_pairs={{0,4},{4,0},{8,12},{12,8},{16,20},{20,16},{24,28},{28,24},{1,5},{5... | collective-permute-start | bytes 1966088 | tf_op jit(solution)/shard_map/ppermute | solution.py:21
  106.4 16.6 %collective-permute-start.23 = (bf16[80,4096]{1,0:T(8,128)(2,1)}, bf16[80,4096]{1,0:T(8,128)(2,1)S(1)}, u32[]{:S(2)}, u32[]{:S(2)}) collective-permute-start(bf16[80,4096]{1,0:T(8,128)(2,1)} %collective-permute-done.17.refs_7_.refs_8_), channel_id=1, source_target_pairs={{0,16},{4,20},{8,24},{12,28},{16,0},{20,4},{24,8},{28,12},{1,17},{... | collective-permute-start | bytes 1966088 | tf_op jit(solution)/shard_map/ppermute | solution.py:21
  107.2 14.3 %collective-permute-start.22 = (bf16[80,4096]{1,0:T(8,128)(2,1)}, bf16[80,4096]{1,0:T(8,128)(2,1)S(1)}, u32[]{:S(2)}, u32[]{:S(2)}) collective-permute-start(bf16[80,4096]{1,0:T(8,128)(2,1)} %collective-permute-done.18.refs_8_.refs_9_), channel_id=1, source_target_pairs={{0,4},{4,0},{8,12},{12,8},{16,20},{20,16},{24,28},{28,24},{1,5},{5... | collective-permute-start | bytes 1966088 | tf_op jit(solution)/shard_map/ppermute | solution.py:21
  107.5 16.3 %collective-permute-start.24 = (bf16[80,4096]{1,0:T(8,128)(2,1)}, bf16[80,4096]{1,0:T(8,128)(2,1)S(1)}, u32[]{:S(2)}, u32[]{:S(2)}) collective-permute-start(bf16[80,4096]{1,0:T(8,128)(2,1)} %collective-permute-done.20.refs_10_.refs_11_), channel_id=1, source_target_pairs={{0,8},{4,12},{8,0},{12,4},{16,24},{20,28},{24,16},{28,20},{1,9},{5... | collective-permute-start | bytes 1966088 | tf_op jit(solution)/shard_map/ppermute | solution.py:21
  116.5 4.9 %collective-permute-start.25 = (f32[2,1024]{1,0:T(2,128)}, f32[2,1024]{1,0:T(2,128)S(1)}, u32[]{:S(2)}, u32[]{:S(2)}) collective-permute-start(f32[2,1024]{1,0:T(2,128)} %get-tuple-element.719), channel_id=1, source_target_pairs={{0,1},{1,2},{2,3},{4,5},{5,6},{6,7},{8,9},{9,10},{10,11},{12,13},{... | collective-permute-start | bytes 24584 | tf_op jit(solution)/shard_map/ppermute | solution.py:27
  123.8 3.0 collective-permute-start.26
  124.8 4.7 %collective-permute-start.27 = (bf16[80,4096]{1,0:T(8,128)(2,1)}, bf16[80,4096]{1,0:T(8,128)(2,1)S(1)}, u32[]{:S(2)}, u32[]{:S(2)}) collective-permute-start(bf16[80,4096]{1,0:T(8,128)(2,1)} %collective-permute-done.20.refs_10_.refs_11_), channel_id=1, source_target_pairs={{0,4},{4,0},{8,12},{12,8},{16,20},{20,16},{24,28},{28,24},{1,5},{5... | collective-permute-start | bytes 1966088 | tf_op jit(solution)/shard_map/ppermute | solution.py:21
  124.8 4.7 %collective-permute-start.28 = (bf16[80,4096]{1,0:T(8,128)(2,1)S(1)}, bf16[80,4096]{1,0:T(8,128)(2,1)S(1)}, u32[]{:S(2)}, u32[]{:S(2)}) collective-permute-start(bf16[80,4096]{1,0:T(8,128)(2,1)S(1)} %collective-permute-done.23.refs_11_.refs_12_), channel_id=1, source_target_pairs={{0,4},{4,0},{8,12},{12,8},{16,20},{20,16},{24,28},{28,24},{1,5},{5... | collective-permute-start | bytes 1966088 | tf_op jit(solution)/shard_map/ppermute | solution.py:21
  125.3 5.9 %collective-permute-start.29 = (bf16[80,4096]{1,0:T(8,128)(2,1)S(1)}, bf16[80,4096]{1,0:T(8,128)(2,1)}, u32[]{:S(2)}, u32[]{:S(2)}) collective-permute-start(bf16[80,4096]{1,0:T(8,128)(2,1)S(1)} %collective-permute-done.24.refs_12_.refs_13_), channel_id=1, source_target_pairs={{0,4},{4,0},{8,12},{12,8},{16,20},{20,16},{24,28},{28,24},{1,5},{5... | collective-permute-start | bytes 1966088 | tf_op jit(solution)/shard_map/ppermute | solution.py:21
  131.3 10.9 %collective-permute-start.31 = (bf16[1536,1024]{1,0:T(8,128)(2,1)}, bf16[1536,1024]{1,0:T(8,128)(2,1)S(1)}, u32[]{:S(2)}, u32[]{:S(2)}) collective-permute-start(bf16[1536,1024]{1,0:T(8,128)(2,1)} %all-gather.10.cloned.1.call-done.refs_7_.refs_4_), channel_id=1, source_target_pairs={{0,4},{4,0},{8,12},{12,8},{16,20},{20,16},{24,28},{28,24},{1,5},{5... | collective-permute-start | bytes 9437192 | tf_op jit(solution)/shard_map/ppermute | solution.py:21
  131.8 10.4 %collective-permute-start.30 = (bf16[512,1024]{1,0:T(8,128)(2,1)}, bf16[512,1024]{1,0:T(8,128)(2,1)}, u32[]{:S(2)}, u32[]{:S(2)}) collective-permute-start(bf16[512,1024]{1,0:T(8,128)(2,1)} %refs_3_.2), channel_id=1, source_target_pairs={{0,4},{4,0},{8,12},{12,8},{16,20},{20,16},{24,28},{28,24},{1,5},{5... | collective-permute-start | bytes 3145736 | tf_op jit(solution)/shard_map/ppermute | solution.py:21
  142.2 10.6 %collective-permute-start.35 = (bf16[3,256,1024]{2,1,0:T(8,128)(2,1)}, bf16[3,256,1024]{2,1,0:T(8,128)(2,1)}, u32[]{:S(2)}, u32[]{:S(2)}) collective-permute-start(bf16[3,256,1024]{2,1,0:T(8,128)(2,1)} %get-tuple-element.1139.refs_15_.refs_1_), channel_id=1, source_target_pairs={{0,4},{4,0},{8,12},{12,8},{16,20},{20,16},{24,28},{28,24},{1,5},{5... | collective-permute-start | bytes 4718600 | tf_op jit(solution)/shard_map/ppermute | solution.py:21
  142.6 10.2 %collective-permute-start.32 = (bf16[2,256,1024]{2,1,0:T(8,128)(2,1)}, bf16[2,256,1024]{2,1,0:T(8,128)(2,1)}, u32[]{:S(2)}, u32[]{:S(2)}) collective-permute-start(bf16[2,256,1024]{2,1,0:T(8,128)(2,1)} %get-tuple-element.1069.refs_1_.refs_13_), channel_id=1, source_target_pairs={{0,4},{4,0},{8,12},{12,8},{16,20},{20,16},{24,28},{28,24},{1,5},{5... | collective-permute-start | bytes 3145736 | tf_op jit(solution)/shard_map/ppermute | solution.py:21
  142.8 10.0 %collective-permute-start.33 = (bf16[256,2048]{1,0:T(8,128)(2,1)}, bf16[256,2048]{1,0:T(8,128)(2,1)}, u32[]{:S(2)}, u32[]{:S(2)}) collective-permute-start(bf16[256,2048]{1,0:T(8,128)(2,1)} %get-tuple-element.855.refs_2_), channel_id=1, source_target_pairs={{0,4},{4,0},{8,12},{12,8},{16,20},{20,16},{24,28},{28,24},{1,5},{5... | collective-permute-start | bytes 3145736 | tf_op jit(solution)/shard_map/ppermute | solution.py:21
  143.2 9.7 %collective-permute-start.34 = (bf16[256,1024]{1,0:T(8,128)(2,1)}, bf16[256,1024]{1,0:T(8,128)(2,1)}, u32[]{:S(2)}, u32[]{:S(2)}) collective-permute-start(bf16[256,1024]{1,0:T(8,128)(2,1)} %get-tuple-element.1086.refs_11_), channel_id=1, source_target_pairs={{0,4},{4,0},{8,12},{12,8},{16,20},{20,16},{24,28},{28,24},{1,5},{5... | collective-permute-start | bytes 1572872 | tf_op jit(solution)/shard_map/ppermute | solution.py:21
  152.9 2.2 collective-permute-start.37
  153.3 9.7 %collective-permute-start.36 = (bf16[256,1024]{1,0:T(8,128)(2,1)}, bf16[256,1024]{1,0:T(8,128)(2,1)S(1)}, u32[]{:S(2)}, u32[]{:S(2)}) collective-permute-start(bf16[256,1024]{1,0:T(8,128)(2,1)} %get-tuple-element.1026.refs_3_.refs_9_), channel_id=1, source_target_pairs={{0,4},{4,0},{8,12},{12,8},{16,20},{20,16},{24,28},{28,24},{1,5},{5... | collective-permute-start | bytes 1572872 | tf_op jit(solution)/shard_map/ppermute | solution.py:21
  163.8 171.0 %reduce-scatter.6.cloned.1.call-start = ((), (), s32[]{:S(2)}) async-start(), calls=%async_computation.6 | async-start | bytes 1310720 | tf_op jit(solution)/shard_map/reduce_scatter | solution.py:1120
  171.9 14.3 %collective-permute-start.39 = (bf16[256,4096]{1,0:T(8,128)(2,1)}, bf16[256,4096]{1,0:T(8,128)(2,1)S(1)}, u32[]{:S(2)}, u32[]{:S(2)}) collective-permute-start(bf16[256,4096]{1,0:T(8,128)(2,1)} %shard_map.455.refs_4_.refs_3_), channel_id=1, source_target_pairs={{0,4},{4,0},{8,12},{12,8},{16,20},{20,16},{24,28},{28,24},{1,5},{5... | collective-permute-start | bytes 6291464 | tf_op jit(solution)/shard_map/ppermute | solution.py:21
  184.1 10.5 %collective-permute-start.38 = (f32[2,1024]{1,0:T(2,128)}, f32[2,1024]{1,0:T(2,128)S(1)}, u32[]{:S(2)}, u32[]{:S(2)}) collective-permute-start(f32[2,1024]{1,0:T(2,128)} %get-tuple-element.1054), channel_id=1, source_target_pairs={{1,0},{2,1},{3,2},{5,4},{6,5},{7,6},{9,8},{10,9},{11,10},{13,12},{... | collective-permute-start | bytes 24584 | tf_op jit(solution)/shard_map/ppermute | solution.py:27
  194.6 50.9 %collective-permute-start.44 = (bf16[128,4096]{1,0:T(8,128)(2,1)}, bf16[128,4096]{1,0:T(8,128)(2,1)S(1)}, u32[]{:S(2)}, u32[]{:S(2)}) collective-permute-start(bf16[128,4096]{1,0:T(8,128)(2,1)} %get-tuple-element.1073), channel_id=1, source_target_pairs={{0,8},{4,12},{8,0},{12,4},{16,24},{20,28},{24,16},{28,20},{1,9},{5... | collective-permute-start | bytes 3145736 | tf_op jit(solution)/shard_map/ppermute | solution.py:21
  195.4 50.2 %collective-permute-start.45 = (bf16[128,4096]{1,0:T(8,128)(2,1)}, bf16[128,4096]{1,0:T(8,128)(2,1)S(1)}, u32[]{:S(2)}, u32[]{:S(2)}) collective-permute-start(bf16[128,4096]{1,0:T(8,128)(2,1)} %get-tuple-element.1074), channel_id=1, source_target_pairs={{0,16},{4,20},{8,24},{12,28},{16,0},{20,4},{24,8},{28,12},{1,17},{... | collective-permute-start | bytes 3145736 | tf_op jit(solution)/shard_map/ppermute | solution.py:21
  196.0 49.6 %collective-permute-start.46 = (bf16[128,4096]{1,0:T(8,128)(2,1)}, bf16[128,4096]{1,0:T(8,128)(2,1)}, u32[]{:S(2)}, u32[]{:S(2)}) collective-permute-start(bf16[128,4096]{1,0:T(8,128)(2,1)} %get-tuple-element.1075), channel_id=1, source_target_pairs={{0,24},{4,28},{8,16},{12,20},{16,8},{20,12},{24,0},{28,4},{1,25},{... | collective-permute-start | bytes 3145736 | tf_op jit(solution)/shard_map/ppermute | solution.py:21
  205.6 2.7 collective-permute-start.40
  207.0 1.8 collective-permute-start.41
  208.4 29.8 %collective-permute-start.42 = (bf16[256,512]{1,0:T(8,128)(2,1)}, bf16[256,512]{1,0:T(8,128)(2,1)S(1)}, u32[]{:S(2)}, u32[]{:S(2)}) collective-permute-start(bf16[256,512]{1,0:T(8,128)(2,1)} %get-tuple-element.1059.refs_14_.refs_5_), channel_id=1, source_target_pairs={{0,4},{4,0},{8,12},{12,8},{16,20},{20,16},{24,28},{28,24},{1,5},{5... | collective-permute-start | bytes 786440 | tf_op jit(solution)/shard_map/ppermute | solution.py:21
  208.7 29.4 %collective-permute-start.43 = (bf16[256,512]{1,0:T(8,128)(2,1)}, bf16[256,512]{1,0:T(8,128)(2,1)}, u32[]{:S(2)}, u32[]{:S(2)}) collective-permute-start(bf16[256,512]{1,0:T(8,128)(2,1)} %get-tuple-element.1060.refs_15_.refs_6_), channel_id=1, source_target_pairs={{0,4},{4,0},{8,12},{12,8},{16,20},{20,16},{24,28},{28,24},{1,5},{5... | collective-permute-start | bytes 786440 | tf_op jit(solution)/shard_map/ppermute | solution.py:21
  246.6 10.4 %collective-permute-start.47 = (bf16[2,256,1024]{2,1,0:T(8,128)(2,1)S(1)}, bf16[2,256,1024]{2,1,0:T(8,128)(2,1)S(1)}, u32[]{:S(2)}, u32[]{:S(2)}) collective-permute-start(bf16[2,256,1024]{2,1,0:T(8,128)(2,1)S(1)} %copy-done.25), channel_id=1, source_target_pairs={{0,4},{4,0},{8,12},{12,8},{16,20},{20,16},{24,28},{28,24},{1,5},{5... | collective-permute-start | bytes 3145736 | tf_op jit(solution)/shard_map/ppermute | solution.py:21
  250.7 6.3 %collective-permute-start.48 = (f32[2,1024]{1,0:T(2,128)S(1)}, f32[2,1024]{1,0:T(2,128)S(1)}, u32[]{:S(2)}, u32[]{:S(2)}) collective-permute-start(f32[2,1024]{1,0:T(2,128)S(1)} %copy-done.46), channel_id=1, source_target_pairs={{1,0},{2,1},{3,2},{5,4},{6,5},{7,6},{9,8},{10,9},{11,10},{13,12},{... | collective-permute-start | bytes 24584 | tf_op jit(solution)/shard_map/ppermute | solution.py:27
  257.1 82.6 %reduce-scatter.8.cloned.1.call-start = ((), (), s32[]{:S(2)}) async-start(), calls=%async_computation.7 | async-start | bytes 983040 | tf_op jit(solution)/shard_map/reduce_scatter | solution.py:1120
  257.3 25.9 %collective-permute-start.49 = (bf16[384,1024]{1,0:T(8,128)(2,1)}, bf16[384,1024]{1,0:T(8,128)(2,1)S(1)}, u32[]{:S(2)}, u32[]{:S(2)}) collective-permute-start(bf16[384,1024]{1,0:T(8,128)(2,1)} %get-tuple-element.1123), channel_id=1, source_target_pairs={{0,8},{4,12},{8,0},{12,4},{16,24},{20,28},{24,16},{28,20},{1,9},{5... | collective-permute-start | bytes 2359304 | tf_op jit(solution)/shard_map/ppermute | solution.py:21
  258.5 24.7 %collective-permute-start.50 = (bf16[384,1024]{1,0:T(8,128)(2,1)}, bf16[384,1024]{1,0:T(8,128)(2,1)S(1)}, u32[]{:S(2)}, u32[]{:S(2)}) collective-permute-start(bf16[384,1024]{1,0:T(8,128)(2,1)} %get-tuple-element.1124), channel_id=1, source_target_pairs={{0,16},{4,20},{8,24},{12,28},{16,0},{20,4},{24,8},{28,12},{1,17},{... | collective-permute-start | bytes 2359304 | tf_op jit(solution)/shard_map/ppermute | solution.py:21
  258.5 35.9 %collective-permute-start.51 = (bf16[384,1024]{1,0:T(8,128)(2,1)}, bf16[384,1024]{1,0:T(8,128)(2,1)}, u32[]{:S(2)}, u32[]{:S(2)}) collective-permute-start(bf16[384,1024]{1,0:T(8,128)(2,1)} %get-tuple-element.1125), channel_id=1, source_target_pairs={{0,24},{4,28},{8,16},{12,20},{16,8},{20,12},{24,0},{28,4},{1,25},{... | collective-permute-start | bytes 2359304 | tf_op jit(solution)/shard_map/ppermute | solution.py:21
  298.3 18.1 %collective-permute-start.52 = (bf16[400,1024]{1,0:T(8,128)(2,1)}, bf16[400,1024]{1,0:T(8,128)(2,1)S(1)}, u32[]{:S(2)}, u32[]{:S(2)}) collective-permute-start(bf16[400,1024]{1,0:T(8,128)(2,1)} %get-tuple-element.1155), channel_id=1, source_target_pairs={{0,8},{4,12},{8,0},{12,4},{16,24},{20,28},{24,16},{28,20},{1,9},{5... | collective-permute-start | bytes 2457608 | tf_op jit(solution)/shard_map/ppermute | solution.py:21
  298.6 17.8 %collective-permute-start.53 = (bf16[400,1024]{1,0:T(8,128)(2,1)}, bf16[400,1024]{1,0:T(8,128)(2,1)S(1)}, u32[]{:S(2)}, u32[]{:S(2)}) collective-permute-start(bf16[400,1024]{1,0:T(8,128)(2,1)} %get-tuple-element.1156), channel_id=1, source_target_pairs={{0,16},{4,20},{8,24},{12,28},{16,0},{20,4},{24,8},{28,12},{1,17},{... | collective-permute-start | bytes 2457608 | tf_op jit(solution)/shard_map/ppermute | solution.py:21
  300.0 34.9 %collective-permute-start.54 = (bf16[400,1024]{1,0:T(8,128)(2,1)}, bf16[400,1024]{1,0:T(8,128)(2,1)S(1)}, u32[]{:S(2)}, u32[]{:S(2)}) collective-permute-start(bf16[400,1024]{1,0:T(8,128)(2,1)} %get-tuple-element.1157), channel_id=1, source_target_pairs={{0,24},{4,28},{8,16},{12,20},{16,8},{20,12},{24,0},{28,4},{1,25},{... | collective-permute-start | bytes 2457608 | tf_op jit(solution)/shard_map/ppermute | solution.py:21
  339.7 5.8 %collective-permute-start.55 = (bf16[80,1024]{1,0:T(8,128)(2,1)}, bf16[80,1024]{1,0:T(8,128)(2,1)S(1)}, u32[]{:S(2)}, u32[]{:S(2)}) collective-permute-start(bf16[80,1024]{1,0:T(8,128)(2,1)} %get-tuple-element.1194), channel_id=1, source_target_pairs={{0,1},{1,0},{2,3},{3,2},{4,5},{5,4},{6,7},{7,6},{8,9},{9,8},{10,11... | collective-permute-start | bytes 491528 | tf_op jit(solution)/shard_map/ppermute | solution.py:32
  339.8 6.9 %collective-permute-start.56 = (bf16[80,1024]{1,0:T(8,128)(2,1)}, bf16[80,1024]{1,0:T(8,128)(2,1)S(1)}, u32[]{:S(2)}, u32[]{:S(2)}) collective-permute-start(bf16[80,1024]{1,0:T(8,128)(2,1)} %get-tuple-element.1195), channel_id=1, source_target_pairs={{0,2},{1,3},{2,0},{3,1},{4,6},{5,7},{6,4},{7,5},{8,10},{9,11},{10,... | collective-permute-start | bytes 491528 | tf_op jit(solution)/shard_map/ppermute | solution.py:32
  341.8 14.9 %collective-permute-start.57 = (bf16[80,1024]{1,0:T(8,128)(2,1)}, bf16[80,1024]{1,0:T(8,128)(2,1)S(1)}, u32[]{:S(2)}, u32[]{:S(2)}) collective-permute-start(bf16[80,1024]{1,0:T(8,128)(2,1)} %get-tuple-element.1196), channel_id=1, source_target_pairs={{0,3},{1,2},{2,1},{3,0},{4,7},{5,6},{6,5},{7,4},{8,11},{9,10},{10,... | collective-permute-start | bytes 491528 | tf_op jit(solution)/shard_map/ppermute | solution.py:32
  357.5 3.4 collective-permute-start.58
  (50 other events, 515.3 us)
Sparse Core Ops, SparseCore 0:
  12.9 37.5 all-gather.7
  52.7 62.7 all-gather.9
  163.2 78.9 reduce-scatter.3
  257.2 24.2 reduce-scatter.5
  298.4 21.6 reduce-scatter.7

commit v4 on v3

--- a/solution.py
+++ b/solution.py
@@ -11,7 +11,7 @@
 ROWS = 64
 STEP = 512
 LANES = 512
-LIMIT = 60
+LIMIT = 63
 MIB = 2**20
 G1, B1, G2, B2, MK, MV, MR, DECAY, FIRST, CMK, CMR = range(11)
 
@@ -42,6 +42,13 @@
 
 def tie(value, *others):
     return lax.optimization_barrier((value, *others))[0]
+
+
+def exchange_two(value):
+    if lax.axis_size("stretch") != 4:
+        return lax.all_gather(value, "stretch")
+    near = across(value, 1)
+    return [value, near, across(jnp.concatenate([value, near], axis=0), 2)]
 
 
 class Live:
@@ -738,14 +745,16 @@
         len(steps_c) * (wide // width) + len(steps_k) * len(order), 10, 40)
 
 
-def mid_back(info, dxt, dxb, after, mid, cot, vec, kvr, wkv, rden, ent, pieces, spots, length, shard):
+def mid_back(info, dxt, dxb, after, head, mid, cot, vec, kvr, wkv, rden, ent, pieces, spots, length, shard):
     tokens, width = mid.shape
     batches = tokens // length
     steps = plan(pieces, spots["o"], shard)
 
     def body(info, small, get, raw, outs, big, put, scratch, loads):
-        after_ref, vec_ref, ent_ref = small
+        after_ref, head_ref, vec_ref, ent_ref = small
         dent_ref, total_ref = outs
+        dent_ref[2 * batches : 3 * batches, :] = ent_ref[2 * batches :, :]
+        dent_ref[3 * batches :, :] = head_ref[...]
         dmid_ref, low_ref, high_ref, rlow_ref, rhigh_ref, gn_ref = big
         w, sum_ref = scratch
         copies = loads.pieces(steps, raw, w, natural(info[0], shard))
@@ -796,8 +805,8 @@
 
     one, half = ((tokens, width), f32), ((tokens, width // 2), bf16)
     return call(
-        body, info, [after, vec, ent], [(a, None) for a in (dxt, dxb, mid, cot, kvr[0], kvr[2], wkv, rden)],
-        flat_pieces(pieces), [((2 * batches, width), f32), ((2, width), f32)], [one, half, half, half, half, one],
+        body, info, [after, head, vec, ent], [(a, None) for a in (dxt, dxb, mid, cot, kvr[0], kvr[2], wkv, rden)],
+        flat_pieces(pieces), [((4 * batches, width), f32), ((2, width), f32)], [one, half, half, half, half, one],
         [pltpu.VMEM((width, width), bf16), pltpu.VMEM((2, 8, width), f32)], len(steps), 9, 40)
 
 
@@ -805,8 +814,8 @@
               length, shard):
     tokens, width = stream.shape
     batches = tokens // length
-    stretches = len(back)
     relative = isinstance(back, list)
+    stretches = 4 if relative else len(back)
     if not relative:
         back = [back]
     plans = [plan(pieces, spots[k], shard) for k in "kvr"]
@@ -815,6 +824,9 @@
         back_ref = small[:-7]
         if not relative:
             back_ref = [back_ref[0].at[z] for z in range(stretches)]
+        else:
+            rows = 4 * batches
+            back_ref = [*back_ref[:2], *[back_ref[2].at[pl.ds(k * rows, rows)] for k in range(2)]]
         ent_ref, sums_ref, num_ref, den_ref, exp_ref, entry_ref, vec_ref = small[-7:]
         gnum_ref, gden_ref, gexp_ref, gffn_ref, head_ref, total_ref, extra_ref = outs
         d_ref, dxs_ref, dxa_ref = big
@@ -970,7 +982,7 @@
     groups = [g for g in groups if g]
     stretches = lax.axis_size("stretch")
     each_z = w // stretches
-    shapes = [(len(evens) * w, n_wide)] if stacked else [(len(items) * w, n_wide)] * len(evens)
+    shapes = [(len(evens) * len(items) * w, n_wide)] if stacked else [(len(items) * w, n_wide)] * len(evens)
     shares = [x.shape[0] // len(evens) for x in under]
     if under:
         shapes = [(len(items) * w + sum(shares), n_wide)] * len(evens)
@@ -1036,7 +1048,7 @@
                             big[evens.index(m)][k * w : (k + 1) * w, dst] = block[n * w : (n + 1) * w]
                             continue
                         for z in range(stretches):
-                            row = (z * len(evens) + evens.index(m)) * each_z
+                            row = ((z * len(evens) + evens.index(m)) * len(items) + k) * each_z
                             big[0][row : row + each_z, dst] = block[n * w + z * each_z : n * w + (z + 1) * each_z]
             if g == 0:
                 wait(copies_under)
@@ -1061,40 +1073,49 @@
     return out
 
 
-def grad_finish(info, sets):
+def grad_stack(info, key, recept):
     stretches = lax.axis_size("stretch")
-    n_wide = sets[0][0].shape[1]
-    rows = sum(own.shape[0] for own, _, _ in sets)
-    each = sets[0][0].shape[0] // sets[0][2] // stretches
+    own, width = recept[0].shape
+    each, blocks = own // stretches, key[0].shape[1] // width
+    rows = (blocks + 1) * each
     if each % 16:
-        parts = [total([own, *got]).astype(bf16).reshape(items, stretches, each, n_wide)
-                 for own, got, items in sets]
-        return jnp.swapaxes(jnp.concatenate(parts, axis=0), 0, 1).reshape(rows, n_wide)
-    flat = [(a, None) for own, got, _ in sets for a in (own, *got)]
+        wide = total(key).astype(bf16).reshape(stretches, each, blocks, width)
+        wide = jnp.swapaxes(wide, 1, 2).reshape(stretches, blocks * each, width)
+        narrow = total(recept).astype(bf16).reshape(stretches, each, width)
+        return jnp.concatenate([wide, narrow], axis=1).reshape(stretches * rows, width)
+    terms = len(key)
 
     def body(info, small, get, raw, outs, big, put, scratch, loads):
-        at, done = 0, 0
-        for own, got, items in sets:
-            refs = [get(at + k) for k in range(1 + len(got))]
-            at += len(refs)
-            for z in range(stretches):
-                for k in range(items):
-                    src = slice((k * stretches + z) * each, (k * stretches + z + 1) * each)
-                    first = z * (rows // stretches) + (done + k) * each
-                    big[0][first : first + each, :] = total([r[src, :] for r in refs]).astype(bf16)
-            done += items
-
-    return call(body, info, [], flat, [], [], [((rows, n_wide), bf16)], [], 0, 3, 24)[0]
-
-
-def grad_pieces(info, own, got, items, each, under):
+        keys, recepts = scratch
+        copies = []
+        for z in range(stretches):
+            src = pl.ds(z * each, each)
+            now = [loads.start(raw[j].at[src], keys.at[j, z]) for j in range(terms)]
+            copies.append(now + [loads.start(raw[terms + j].at[src], recepts.at[j, z]) for j in range(terms)])
+        for z in range(stretches):
+            wait(copies[z])
+            for q in range(blocks):
+                at = z * rows + q * each
+                big[0][at : at + each, :] = total(
+                    [keys[j, z, :, q * width : (q + 1) * width] for j in range(terms)]).astype(bf16)
+            at = z * rows + blocks * each
+            big[0][at : at + each, :] = total([recepts[j, z] for j in range(terms)]).astype(bf16)
+
+    return call(
+        body, info, [], [], [*key, *recept], [], [((stretches * rows, width), bf16)],
+        [pltpu.VMEM((terms, stretches, each, blocks * width), bf16),
+         pltpu.VMEM((terms, stretches, each, width), bf16)],
+        stretches * 2 * terms, 4, 24)[0]
+
+
+def grad_pieces(info, own, got, items, each):
     stretches = lax.axis_size("stretch")
     rows, n_wide = own.shape
     width = each * stretches
 
     def body(info, small, get, raw, outs, big, put, scratch, loads):
         refs = [get(k) for k in range(1 + len(got))]
-        first = items * width + under
+        first = items * width
         table = total([r[first : first + 16, :] for r in refs])
         half = n_wide // 2
         table = table[:, :half] + table[:, half:]
@@ -1108,12 +1129,10 @@
             big[j][items * each :, :half] = hi
             big[j][items * each :, half:] = lo
             put(j)
-        middle = slice(items * width, first)
-        big[stretches][...] = total([r[middle, :] for r in refs])
 
     return call(
         body, info, [], [(a, None) for a in (own, *got)], [], [],
-        [((items * each + 16, n_wide), bf16)] * stretches + [((under, n_wide), f32)], [], 0, 3, 24)
+        [((items * each + 16, n_wide), bf16)] * stretches, [], 0, 3, 24)
 
 
 def stretch_part(part):
@@ -1266,11 +1285,18 @@
     flat = tuple((j, None) for j in range(4))
     arrays = [v.near, v.far_sib, v.d_fval, hop(v.d_fval, 1)]
     v.stack_cv = weight_grad(info, arrays, [flat], "blocks", 6, stacked=True)[0]
-    v.dfrec_sib = hop(v.d_frec, 1)
+    dfrec_sib = hop(v.d_frec, 1)
+    if aligned:
+        v.parts_c = weight_grad(
+            info, [v.f_in, v.f_sib, v.d_frec, dfrec_sib], [((0, 1), (1, 1), (2, None), (3, None))], layout, 3)
+    else:
+        v.parts_c = weight_grad(
+            info, [*pairs((v.f_in[1], v.f_sib[1])), v.d_frec, dfrec_sib], [flat], layout, 3)
     v.drop("near", "far_sib")
     v.sync()
 
     z_cv = stretch_part(v.stack_cv)
+    v.got_c = grad_send(v.parts_c)
     v.dpre = hidden_back(info, v.act, v.d_fval, v.all_cv, fshard)
     dpre_sib = hop(v.dpre, 1)
     v.head_b, v.sums_c, v.dxt, v.dxb = chan_back(
@@ -1287,45 +1313,45 @@
     v.sync()
 
     v.got_ck = grad_send(v.parts_ck)
-    dent, v.sums_m, v.dmid, *lows, gn = mid_back(
-        info, v.dxt, v.dxb, v.next_b, v.mid, cot, v.vec, v.kvr, v.wkv, v.rden, v.ent, v.tm, spots,
+    backs, v.sums_m, v.dmid, *lows, gn = mid_back(
+        info, v.dxt, v.dxb, v.next_b, v.head_b, v.mid, cot, v.vec, v.kvr, v.wkv, v.rden, v.ent, v.tm, spots,
         length, shard)
     v.dbr, v.drec = lows[:2], lows[2:]
-    back = lax.all_gather(jnp.concatenate([dent, v.ent[2 * batches :], v.head_b], axis=0), "stretch")
+    back = exchange_two(backs)
     *v.grads, v.head_a, v.sums_t, v.extra, v.d_kv, v.dxs, v.dxa = time_back(
         info, gn, v.wkv, v.kvr, v.ent, back, v.sums, state, v.drec, stream, v.entry, v.vec,
         v.tm, spots, length, shard)
     v.dbr_sib = [hop(a, 1) for a in v.dbr]
     v.drec_sib = [hop(a, 1) for a in v.drec]
     dys = [([(at, None), (at + 1, None)], [(at + 2, None), (at + 3, None)]) for at in (0, 4)]
-    lows = [*v.dbr, *v.dbr_sib, *v.drec, *v.drec_sib, v.d_frec, v.dfrec_sib]
-    last = ((8, None), (9, None))
+    lows = [*v.dbr, *v.dbr_sib, *v.drec, *v.drec_sib]
+    gated = tie(v.gated, v.d_kv)
     if aligned:
-        v.parts_ocr = weight_grad(
-            info, [*lows, tie(v.gated, v.d_kv), v.g_sib, v.f_in, v.f_sib, v.kvr_in, v.kvr_sib],
-            [((10, None), (11, None), *dys[0]), ((12, 1), (13, 1), *last), ((14, 2), (15, 2), *dys[1])],
-            layout, 6)
+        v.parts_or = weight_grad(
+            info, [*lows, gated, v.g_sib, v.kvr_in, v.kvr_sib],
+            [((8, None), (9, None), *dys[0]), ((10, 2), (11, 2), *dys[1])], layout, 6, stacked=True)
     else:
-        xs = pairs((tie(v.gated, v.d_kv), v.g_sib), (v.f_in[1], v.f_sib[1]), (v.kvr_in[2], v.kvr_sib[2]))
-        v.parts_ocr = weight_grad(
-            info, [*lows, *xs],
-            [((10, None), (11, None), *dys[0]), ((12, None), (13, None), *last),
-             ((14, None), (15, None), *dys[1])], layout, 6)
+        xs = pairs((gated, v.g_sib), (v.kvr_in[2], v.kvr_sib[2]))
+        v.parts_or = weight_grad(
+            info, [*lows, *xs], [((8, None), (9, None), *dys[0]), ((10, None), (11, None), *dys[1])], layout, 6,
+            stacked=True)
     v.drop("wkv", "kvr", "ent", "sums", "entry", "tm", "dxt", "dxb", "mid", "rden", "next_b", "head_b")
     v.sync()
     v.dkv_sib = hop(v.d_kv, 1)
     v.next_a = along(v.head_a, -1)
-    v.part_ck = grad_finish(info, [(v.parts_ck[0], v.got_ck, 1)])
-    v.drop("gated", "g_sib", "dbr", "dbr_sib", "drec", "drec_sib", "f_in", "f_sib", "d_frec", "dfrec_sib",
-           "parts_ck", "got_ck")
+    z_or = stretch_part(v.parts_or[0])
+    v.stack = grad_stack(info, [v.parts_ck[0], *v.got_ck], [v.parts_c[0], *v.got_c])
+    v.drop("gated", "g_sib", "dbr", "dbr_sib", "drec", "drec_sib", "f_in", "f_sib", "d_frec",
+           "parts_ck", "got_ck", "parts_c", "got_c", "parts_or")
     v.z_cv = z_cv
     v.sync()
 
-    v.got_ocr = grad_send(v.parts_ocr)
-    z_ck = stretch_part(v.part_ck)
+    v.parts_cv = [v.z_cv[k * each : (k + 1) * each] for k in range(len(evens))]
+    z_rest = stretch_part(v.stack)
+    v.got_cv = grad_send(v.parts_cv)
     sums_i, v.grad_stream = in_back(info, v.dxs, v.dxa, v.next_a, v.dmid, stream, v.vec, length)
     table = jnp.concatenate([sums_i, v.sums_m, v.sums_t, v.extra, v.sums_c], axis=0)
-    under = [v.z_cv, vector_rows(table, width)]
+    under = [vector_rows(table, width)]
     if aligned:
         v.parts_kv = weight_grad(
             info, [v.kvr_in, v.kvr_sib, v.d_kv, v.dkv_sib],
@@ -1335,28 +1361,33 @@
         v.parts_kv = weight_grad(
             info, [*xs, v.d_kv, v.dkv_sib],
             [((2 * k, None), (2 * k + 1, None), (4, k), (5, k)) for k in range(2)], layout, 7, under=under)
+    v.drop("kvr_in", "kvr_sib", "d_kv", "dkv_sib", "dxs", "dxa", "dmid", "next_a", "stack",
+           "sums_m", "sums_t", "extra", "sums_c", "z_cv")
+    v.sync()
+
+    v.got_kv = grad_send(v.parts_kv)
     v.heads = lax.all_gather(v.head_a, "stretch")[0]
-    v.drop("kvr_in", "kvr_sib", "d_kv", "dkv_sib", "dxs", "dxa", "dmid", "next_a", "part_ck",
-           "sums_m", "sums_t", "extra", "sums_c", "z_cv")
-    v.sync()
-
-    v.got_kv = grad_send(v.parts_kv)
-    z_ocr = stretch_part(grad_finish(info, [(v.parts_ocr[0], v.got_ocr, 3)]))
-    v.z_ck = z_ck
-    v.drop("parts_ocr", "got_ocr")
+    v.out_cv = total([v.parts_cv[0], *v.got_cv])
+    v.drop("parts_cv", "got_cv")
+    v.z_or = z_or
     v.sync()
     rows = shard // stretches
     by_hops = stretches == 4 and rows % 16 == 0
     if by_hops:
-        *v.pieces, v.out_cv = grad_pieces(info, v.parts_kv[0], v.got_kv, 2, rows, each)
+        v.pieces = grad_pieces(info, v.parts_kv[0], v.got_kv, 2, rows)
     else:
         whole = total([v.parts_kv[0], *v.got_kv])
         first = 2 * shard
-        v.out_cv, v.table = whole[first : first + each], vector_read(whole[first + each :])
-        v.part_kv = grad_finish(info, [(v.parts_kv[0][:first], [g[:first] for g in v.got_kv], 2)])
-    v.z_ocr = z_ocr
-    v.drop("parts_kv", "got_kv")
-    v.sync()
+        v.table = vector_read(whole[first:])
+        v.part_kv = whole[:first].astype(bf16).reshape(2, stretches, rows, width)
+        v.part_kv = jnp.swapaxes(v.part_kv, 0, 1).reshape(first, width)
+    parts = [v.z_or[2 * k * rows : 2 * (k + 1) * rows] for k in range(len(evens))]
+    v.parts_or = [parts[0], *grad_send(parts)]
+    v.drop("parts_kv", "got_kv", "z_or")
+    v.sync()
+    blocks = wide // width
+    out_ck = jnp.concatenate([z_rest[q * rows : (q + 1) * rows] for q in range(blocks)], axis=1).astype(f32)
+    out_c = z_rest[blocks * rows : (blocks + 1) * rows].astype(f32)
     if by_hops:
         pieces = [v.pieces[0], *[across(v.pieces[j], j) for j in range(1, stretches)]]
         z_kv = total([p[: 2 * rows] for p in pieces])
@@ -1365,16 +1396,16 @@
     else:
         z_kv = stretch_part(v.part_kv)
         small = vector_finish(vector_own(v.table[:11], shard))
-    out_cv, out_ck = [v.out_cv], stretch_items(v.z_ck, 1)
-    out_o, out_c, out_r = stretch_items(v.z_ocr, 3)
     out_k, out_v = stretch_items(z_kv, 2)
+    out_o, out_r = stretch_items(total(v.parts_or), 2)
+    out_cv = v.out_cv
     grad_previous_mix = v.heads
     block_out, grad_stream = v.block_out, v.grad_stream
 
     shape = stream_in.shape
     return (
         block_out.reshape(shape), grad_stream.reshape(shape), *[small[i] for i in range(11)],
-        out_k, out_v, out_r, out_o, *out_ck, *out_cv, out_c,
+        out_k, out_v, out_r, out_o, out_ck, out_cv, out_c,
         *v.grads[:3], grad_previous_mix[:, None], v.grads[3], v.mean, v.log,
     )
 

time: 369 us -> 352 us (0.954)
  waiting for transfers between devices: 116 us -> 98.2 us
  starting transfers between devices: 48.6 us -> 62.9 us
  blocking collectives: 37.6 us -> 23.4 us
    ppermute x52 -> x58, waiting for transfers between devices: 100 us -> 67.4 us  [hop(): return lax.ppermute(value, 'seg', [(i, i ^ bit) for i in range(count)])]
    all_gather x1 -> x0, blocking collectives: 14.6 us -> none  [body(): lax.all_gather(jnp.concatenate([dent, v.ent[2 * batches:], v.head_b], axi...]
    ppermute x3 -> x5, waiting for transfers between devices: 11.2 us -> 25.7 us  [across(): return lax.ppermute(value, 'stretch', [(i, i ^ j) for i in range(count)])]
    ppermute x52 -> x58, starting transfers between devices: 35.2 us -> 44.9 us  [hop(): return lax.ppermute(value, 'seg', [(i, i ^ bit) for i in range(count)])]
    unnamed x102 -> x68, local copies, waits for them, and re-layouts: 9.91 us -> 5.01 us
  transfers between devices with their start and end apart: 64 -> 72, of which waited for: 21 -> 26; matrix products, arithmetic and copies ran while one was open for 2% -> 4% of each run, Pallas kernels for 34% -> 34%
where the time goes in v4:
time: 352 us; the launch traced here: 350 us
  Pallas kernels  125 us (36%)
  waiting for transfers between devices  98.2 us (28%)
  starting transfers between devices  62.9 us (18%)
  blocking collectives  23.4 us (7%)
  local copies, waits for them, and re-layouts  15.4 us (4%)
  between operations  14.7 us (4%)
  other arithmetic  10.3 us (3%)
    pallas_call x16, Pallas kernels, call(): pl.pallas_call(kernel, out_shape=[jax.ShapeDtypeStruct(s, d) for s, d in...  120 us
    ppermute x58, waiting for transfers between devices, hop(): return lax.ppermute(value, 'seg', [(i, i ^ bit) for i in range(count)])  67.4 us
    ppermute x58, starting transfers between devices, hop(): return lax.ppermute(value, 'seg', [(i, i ^ bit) for i in range(count)])  44.9 us
    ppermute x5, waiting for transfers between devices, across(): return lax.ppermute(value, 'stretch', [(i, i ^ j) for i in range(count)])  25.7 us
    all_gather x1, blocking collectives, body(): v.everyone = lax.all_gather(v.sums, 'stretch')  12.8 us
    ppermute x4, starting transfers between devices, along(): lax.ppermute(value, 'stretch', [(i, i + steps) for i in range(first, last)])  12.6 us
    all_gather x1, blocking collectives, body(): v.heads = lax.all_gather(v.head_a, 'stretch')[0]  10.6 us
  transfers between devices with their start and end apart: 72, of which 26 were waited for; matrix products, arithmetic and copies ran while one was open for 4% of the time, Pallas kernels for 34%

profile of v4, /device:TPU:9, one launch (start us, length us, event | category | flops | bytes accessed | tf_op | source)
XLA Modules:
  0.0 350.1 jit_solution(8357002718860362438)
XLA Ops:
  8.0 1.7 constant_dynamic-slice_fusion.3
  9.7 3.0 shard_map.448
  13.6 1.2 collective-permute-start.3
  14.8 1.2 collective-permute-start.5
  17.1 3.2 collective-permute-start.2
  20.3 2.4 shard_map.449
  22.8 22.5 %collective-permute-done.4.refs_7_.refs_13_.refs_16_.refs_21_ = bf16[256,1024]{1,0:T(8,128)(2,1)} collective-permute-done((bf16[256,1024]{1,0:T(8,128)(2,1)}, bf16[256,1024]{1,0:T(8,128)(2,1)}, u32[]{:S(2)}, u32[]{:S(2)}) %collective-permute-start.4) | collective-permute-done | bytes 524320 | tf_op jit(solution)/shard_map/ppermute | solution.py:21
  45.3 1.8 collective-permute-done.6.refs_9_.refs_15_.refs_18_.refs_23_
  47.1 3.4 all-gather.7.cloned.1.call-done
  50.5 1.2 constant_dynamic-slice_fusion.2
  55.6 10.9 %collective-permute-done.14.refs_11_.refs_17_.refs_20_.refs_25_ = bf16[256,1024]{1,0:T(8,128)(2,1)S(1)} collective-permute-done((bf16[256,1024]{1,0:T(8,128)(2,1)}, bf16[256,1024]{1,0:T(8,128)(2,1)S(1)}, u32[]{:S(2)}, u32[]{:S(2)}) %collective-permute-start.14) | collective-permute-done | bytes 524320 | tf_op jit(solution)/shard_map/ppermute | solution.py:21
  67.6 1.5 collective-permute-done.13.refs_10_.refs_16_.refs_19_.refs_24_
  72.5 2.2 collective-permute-done.16.refs_19_.refs_25_.refs_28_.refs_33_
  78.3 8.4 %shard_map.450 = (f32[6,1024]{1,0:T(8,128)}, f32[16,1024]{1,0:T(8,128)}, f32[2,1024]{1,0:T(2,128)}, bf16[3,256,1024]{2,1,0:T(8,128)(2,1)}, f32[256,1024]{1,0:T(8...) custom-call(s32[3]{0:T(128)} %pad_add_fusion.refs_0_, bf16[2,1024]{1,0:T(2,128)(2,1)} %copy-done.32, ...), custom_call_target="tpu_custom_call" | custom-call | bytes 9000 | tf_op jit(solution)/shard_map/pallas_call | solution.py:187
  86.8 12.8 %all-gather.2.refs_1_ = f32[4,6,1024]{2,1,0:T(8,128)} all-gather(f32[1,6,1024]{2,1,0:T(8,128)} %bitcast.58), channel_id=2, replica_groups=mesh['seg'=8,'stretch'=4] {'stretch'}, dimensions={0}, use_global_device_ids=true | all-gather | bytes 122880 | tf_op jit(solution)/shard_map/all_gather | solution.py:1246
  99.6 5.5 %collective-permute-done.18.refs_8_.refs_9_ = bf16[80,4096]{1,0:T(8,128)(2,1)} collective-permute-done((bf16[80,4096]{1,0:T(8,128)(2,1)}, bf16[80,4096]{1,0:T(8,128)(2,1)}, u32[]{:S(2)}, u32[]{:S(2)}) %collective-permute-start.18) | collective-permute-done | bytes 655392 | tf_op jit(solution)/shard_map/ppermute | solution.py:21
  105.9 1.9 collective-permute-start.21
  109.5 8.2 %shard_map.451 = (f32[6,1024]{1,0:T(8,128)}, f32[2,1,1024]{2,1,0:T(1,128)}, f32[2,1,1024]{2,1,0:T(1,128)}, f32[2,1024]{1,0:T(2,128)}, bf16[256,1024]{1,0:T(8,128...) custom-call(s32[3]{0:T(128)} %pad_add_fusion.refs_0_, ...), custom_call_target="tpu_custom_call" | custom-call | bytes 7000 | tf_op jit(solution)/shard_map/pallas_call | solution.py:187
  117.8 3.3 collective-permute-start.25
  121.1 1.7 collective-permute-done.25.refs_1_
  122.8 1.7 collective-permute-done.23.refs_11_.refs_12_
  125.2 1.0 collective-permute-start.26
  126.8 1.6 collective-permute-done.26.refs_17_.refs_18_
  131.7 10.3 %shard_map.452 = (f32[2,1024]{1,0:T(2,128)}, bf16[2,256,1024]{2,1,0:T(8,128)(2,1)}, bf16[256,2048]{1,0:T(8,128)(2,1)}, bf16[256,2048]{1,0:T(8,128)(2,1)}, bf16[2...) custom-call(s32[3]{0:T(128)} %pad_add_fusion.refs_0_, f32[2,1024]{1,0:T(2,128)} %copy-done.31, f32[2,1,1024]{2,1,0:T(1,128)} %refs_2_.5, ...), custom_call_target="tpu_custom_call" | custom-call | bytes 11000 | tf_op jit(solution)/shard_map/pallas_call | solution.py:187
  143.0 9.0 %shard_map.453 = (bf16[256,1024]{1,0:T(8,128)(2,1)}, bf16[256,1024]{1,0:T(8,128)(2,1)}, bf16[256,1024]{1,0:T(8,128)(2,1)}) custom-call(s32[3]{0:T(128)} %pad_add_fusion.refs_0_, bf16[256,2048]{1,0:T(8,128)(2,1)} %get-tuple-element.939.refs_1_, bf16[256,2048]{1,0:T(8,128)(2,1)} %get-tuple-element.857.refs_2_, f32[256,1024]{1,0:T(8,128)} %get-tuple-element.858.refs_3_, ...), custom_call_target="tpu_custom_call" | custom-call | bytes 7000 | tf_op jit(solution)/shard_map/pallas_call | solution.py:187
  152.7 1.7 collective-permute-done.37.refs_4_
  154.4 7.2 %shard_map.455 = bf16[2048,1024]{1,0:T(8,128)(2,1)} custom-call(s32[3]{0:T(128)} %pad_add_fusion.refs_0_, bf16[256,2048]{1,0:T(8,128)(2,1)} %get-tuple-element.939.refs_1_, bf16[256,2048]{1,0:T(8,128)(2,1)} %collective-permute-done.33.refs_2_, bf16[256,1024]{1,0:T(8,128)(2,1)} %get-tuple-element.965.refs_3_.refs_1_, ...), custom_call_target="tpu_custom_call" | custom-call | bytes 6000 | tf_op jit(solution)/shard_map/pallas_call | solution.py:187
  161.6 3.8 %shard_map.454 = (bf16[128,1024]{1,0:T(8,128)(2,1)}, bf16[128,1024]{1,0:T(8,128)(2,1)}, bf16[128,1024]{1,0:T(8,128)(2,1)}, bf16[128,1024]{1,0:T(8,128)(2,1)}) custom-call(s32[3]{0:T(128)} %pad_add_fusion.refs_0_, bf16[2,256,1024]{2,1,0:T(8,128)(2,1)} %get-tuple-element.992.refs_1_, bf16[2,256,1024]{2,1,0:T(8,128)(2,1)} %collective-permute-done.32.refs_2_, ...), custom_call_target="tpu_custom_call" | custom-call | bytes 3000 | tf_op jit(solution)/shard_map/pallas_call | solution.py:187
  165.6 8.1 %shard_map.456.refs_4_.refs_3_ = bf16[256,4096]{1,0:T(8,128)(2,1)} custom-call(s32[3]{0:T(128)} %pad_add_fusion.refs_0_, bf16[256,1024]{1,0:T(8,128)(2,1)} %get-tuple-element.965.refs_3_.refs_1_, bf16[256,4096]{1,0:T(8,128)(2,1)} %get-tuple-element.966.refs_2_, bf16[512,1024]{1,0:T(8,128)(2,1)} %refs_3_.2, ...), custom_call_target="tpu_custom_call" | custom-call | bytes 7000 | tf_op jit(solution)/shard_map/pallas_call | solution.py:187
  175.6 1.2 collective-permute-start.40
  176.8 11.8 %shard_map.457 = (f32[2,1024]{1,0:T(2,128)}, f32[2,1024]{1,0:T(2,128)}, f32[256,1024]{1,0:T(8,128)}, f32[256,1024]{1,0:T(8,128)}) custom-call(s32[3]{0:T(128)} %pad_add_fusion.refs_0_, f32[2,1024]{1,0:T(2,128)} %get-tuple-element.963.refs_1_, f32[16,1024]{1,0:T(8,128)} %get-tuple-element.1130.refs_5_.refs_3_.refs_2_.refs_10_, ...), custom_call_target="tpu_custom_call" | custom-call | bytes 10000 | tf_op jit(solution)/shard_map/pallas_call | solution.py:187
  188.6 2.3 collective-permute-start.41
  190.9 7.0 %shard_map.458 = (bf16[128,4096]{1,0:T(8,128)(2,1)}, bf16[128,4096]{1,0:T(8,128)(2,1)}, bf16[128,4096]{1,0:T(8,128)(2,1)}, bf16[128,4096]{1,0:T(8,128)(2,1)}) custom-call(s32[3]{0:T(128)} %pad_add_fusion.refs_0_, bf16[2,256,1024]{2,1,0:T(8,128)(2,1)} %get-tuple-element.992.refs_1_, bf16[2,256,1024]{2,1,0:T(8,128)(2,1)} %collective-permute-done.32.refs_2_, ...), custom_call_target="tpu_custom_call" | custom-call | bytes 7000 | tf_op jit(solution)/shard_map/pallas_call | solution.py:187
  199.5 1.2 collective-permute-start.51
  200.7 8.3 %shard_map.459 = (f32[8,1024]{1,0:T(8,128)}, f32[2,1024]{1,0:T(2,128)}, f32[256,1024]{1,0:T(8,128)}, bf16[256,512]{1,0:T(8,128)(2,1)}, bf16[256,512]{1,0:T(8,128...) custom-call(s32[3]{0:T(128)} %pad_add_fusion.refs_0_, f32[2,1024]{1,0:T(2,128)} %copy-done.26, ...), custom_call_target="tpu_custom_call" | custom-call | bytes 9000 | tf_op jit(solution)/shard_map/pallas_call | solution.py:187
  209.2 4.2 %collective-permute-done.43.refs_2_ = f32[8,1024]{1,0:T(8,128)S(1)} collective-permute-done((f32[8,1024]{1,0:T(8,128)}, f32[8,1024]{1,0:T(8,128)S(1)}, u32[]{:S(2)}, u32[]{:S(2)}) %collective-permute-start.43) | collective-permute-done | bytes 32800 | tf_op jit(solution)/shard_map/ppermute | solution.py:32
  214.2 2.3 collective-permute-start.44
  216.5 6.1 %collective-permute-start.45 = (bf16[256,512]{1,0:T(8,128)(2,1)}, bf16[256,512]{1,0:T(8,128)(2,1)S(1)}, u32[]{:S(2)}, u32[]{:S(2)}) collective-permute-start(bf16[256,512]{1,0:T(8,128)(2,1)} %get-tuple-element.1070.refs_1_), channel_id=1, source_target_pairs={{0,4},{4,0},{8,12},{12,8},{16,20},{20,16},{24,28},{28,24},{1,5},{5... | collective-permute-start | bytes 786440 | tf_op jit(solution)/shard_map/ppermute | solution.py:21
  222.5 4.5 %collective-permute-start.46 = (bf16[256,512]{1,0:T(8,128)(2,1)}, bf16[256,512]{1,0:T(8,128)(2,1)S(1)}, u32[]{:S(2)}, u32[]{:S(2)}) collective-permute-start(bf16[256,512]{1,0:T(8,128)(2,1)} %get-tuple-element.1071.refs_2_), channel_id=1, source_target_pairs={{0,4},{4,0},{8,12},{12,8},{16,20},{20,16},{24,28},{28,24},{1,5},{5... | collective-permute-start | bytes 786440 | tf_op jit(solution)/shard_map/ppermute | solution.py:21
  227.1 1.3 collective-permute-done.46.refs_4_
  228.8 12.8 %shard_map.460 = (f32[2,1,1024]{2,1,0:T(1,128)}, f32[2,1,1024]{2,1,0:T(1,128)}, f32[2,1,1024]{2,1,0:T(1,128)}, f32[2,1,1024]{2,1,0:T(1,128)}, f32[2,1024]{1,0:T(...) custom-call(s32[3]{0:T(128)} %pad_add_fusion.refs_0_, ...), custom_call_target="tpu_custom_call" | custom-call | bytes 14000 | tf_op jit(solution)/shard_map/pallas_call | solution.py:187
  242.3 5.6 %shard_map.461 = bf16[1024,1024]{1,0:T(8,128)(2,1)} custom-call(s32[3]{0:T(128)} %pad_add_fusion.refs_0_, bf16[256,512]{1,0:T(8,128)(2,1)} %get-tuple-element.1070.refs_1_, bf16[256,512]{1,0:T(8,128)(2,1)} %get-tuple-element.1071.refs_2_, bf16[256,512]{1,0:T(8,128)(2,1)} %copy-done.14, bf16[256,512]{1,0:T(8,128)(2,1)} %copy-done.15, ...), custom_call_target="tpu_custom_call" | custom-call | bytes 6000 | tf_op jit(solution)/shard_map/pallas_call | solution.py:187
  248.6 3.7 %collective-permute-start.53 = (f32[2,1024]{1,0:T(2,128)S(1)}, f32[2,1024]{1,0:T(2,128)S(1)}, u32[]{:S(2)}, u32[]{:S(2)}) collective-permute-start(f32[2,1024]{1,0:T(2,128)S(1)} %copy-done.30), channel_id=1, source_target_pairs={{1,0},{2,1},{3,2},{5,4},{6,5},{7,6},{9,8},{10,9},{11,10},{13,12},{... | collective-permute-start | bytes 24584 | tf_op jit(solution)/shard_map/ppermute | solution.py:27
  252.5 5.0 %shard_map.462 = bf16[640,1024]{1,0:T(8,128)(2,1)} custom-call(s32[3]{0:T(128)} %pad_add_fusion.refs_0_, bf16[128,4096]{1,0:T(8,128)(2,1)} %get-tuple-element.1114.refs_1_, bf16[128,4096]{1,0:T(8,128)(2,1)} %collective-permute-done.49.refs_2_, bf16[128,4096]{1,0:T(8,128)(2,1)} %collective-permute-done.50.refs_3_, ...), custom_call_target="tpu_custom_call" | custom-call | bytes 4000 | tf_op jit(solution)/shard_map/pallas_call | solution.py:187
  257.6 2.1 fusion.4
  260.1 2.3 collective-permute-start.56
  262.4 5.5 %shard_map.463 = (f32[2,1024]{1,0:T(2,128)}, bf16[256,1024]{1,0:T(8,128)(2,1)}) custom-call(s32[3]{0:T(128)} %pad_add_fusion.refs_0_, f32[2,1024]{1,0:T(2,128)} %copy-done.25, f32[16,1024]{1,0:T(8,128)} %get-tuple-element.1130.refs_5_.refs_3_.refs_2_.refs_10_, f32[256,1024]{1,0:T(8,128)} %get-tuple-element.1131.refs_3_, ...), custom_call_target="tpu_custom_call" | custom-call | bytes 6000 | tf_op jit(solution)/shard_map/pallas_call | solution.py:187
  269.6 5.6 %shard_map.464 = (bf16[272,1024]{1,0:T(8,128)(2,1)}, bf16[272,1024]{1,0:T(8,128)(2,1)}, bf16[272,1024]{1,0:T(8,128)(2,1)}, bf16[272,1024]{1,0:T(8,128)(2,1)}) custom-call(s32[3]{0:T(128)} %pad_add_fusion.refs_0_, bf16[3,256,1024]{2,1,0:T(8,128)(2,1)} %get-tuple-element.1142.refs_11_.refs_1_, bf16[3,256,1024]{2,1,0:T(8,128)(2,1)} %collective-permute-done.35.refs_12_.refs_2_, ...), custom_call_target="tpu_custom_call" | custom-call | bytes 7000 | tf_op jit(solution)/shard_map/pallas_call | solution.py:187
  276.4 2.3 collective-permute-start.59
  278.7 10.6 %all-gather.3 = f32[4,2,1024]{2,1,0:T(2,128)S(1)} all-gather(f32[1,2,1024]{2,1,0:T(2,128)S(1)} %bitcast.60), channel_id=3, replica_groups=mesh['seg'=8,'stretch'=4] {'stretch'}, dimensions={0}, use_global_device_ids=true | all-gather | bytes 40960 | tf_op jit(solution)/shard_map/all_gather | solution.py:1369
  289.3 2.1 convert_add_fusion
  291.4 9.8 %collective-permute-done.59.refs_4_ = bf16[272,1024]{1,0:T(8,128)(2,1)} collective-permute-done((bf16[272,1024]{1,0:T(8,128)(2,1)}, bf16[272,1024]{1,0:T(8,128)(2,1)}, u32[]{:S(2)}, u32[]{:S(2)}) %collective-permute-start.59) | collective-permute-done | bytes 557088 | tf_op jit(solution)/shard_map/ppermute | solution.py:21
  301.2 1.9 fusion.5
  303.3 1.4 collective-permute-start.61
  304.7 1.1 collective-permute-start.62
  305.7 3.2 shard_map.465
  309.0 1.2 collective-permute-done.62
  310.2 1.3 collective-permute-start.64
  311.5 1.3 collective-permute-start.65
  315.1 7.8 %collective-permute-done.63 = bf16[80,1024]{1,0:T(8,128)(2,1)S(1)} collective-permute-done((bf16[80,1024]{1,0:T(8,128)(2,1)}, bf16[80,1024]{1,0:T(8,128)(2,1)S(1)}, u32[]{:S(2)}, u32[]{:S(2)}) %collective-permute-start.63) | collective-permute-done | bytes 163872 | tf_op jit(solution)/shard_map/ppermute | solution.py:32
  322.9 3.1 collective-permute-done.64
  326.0 10.6 %collective-permute-done.65 = bf16[80,1024]{1,0:T(8,128)(2,1)S(1)} collective-permute-done((bf16[80,1024]{1,0:T(8,128)(2,1)}, bf16[80,1024]{1,0:T(8,128)(2,1)S(1)}, u32[]{:S(2)}, u32[]{:S(2)}) %collective-permute-start.65) | collective-permute-done | bytes 163872 | tf_op jit(solution)/shard_map/ppermute | solution.py:32
  337.4 1.4 collective-permute-start.66
  341.1 1.7 slice_convert_fusion
  (200 shorter events, 39.7 us)
Async XLA Ops:
  7.2 43.3 %all-gather.7.cloned.1.call-start = ((), (), s32[]{:S(2)}) async-start(), calls=%async_computation.3 | async-start | bytes 2359296 | tf_op jit(solution)/shard_map/all_gather | solution.py:1222
  12.7 118.4 %all-gather.9.cloned.1.call-start = ((), (), s32[]{:S(2)}) async-start(), calls=%async_computation.4 | async-start | bytes 3932160 | tf_op jit(solution)/shard_map/all_gather | solution.py:1231
  12.8 3.5 %collective-permute-start.1 = (bf16[256,1024]{1,0:T(8,128)(2,1)}, bf16[256,1024]{1,0:T(8,128)(2,1)S(1)}, u32[]{:S(2)}, u32[]{:S(2)}) collective-permute-start(bf16[256,1024]{1,0:T(8,128)(2,1)} %get-tuple-element.1047.refs_5_.refs_11_.refs_14_.refs_19_), channel_id=1, source_target_pairs={{0,4},{4,0},{8,12},{12,8},{16,20},{20,16},{24,28},{28,24},{1,5},{5... | collective-permute-start | bytes 1572872 | tf_op jit(solution)/shard_map/ppermute | solution.py:21
  13.6 33.5 %collective-permute-start.3 = (bf16[272,1024]{1,0:T(8,128)(2,1)}, bf16[272,1024]{1,0:T(8,128)(2,1)}, u32[]{:S(2)}, u32[]{:S(2)}) collective-permute-start(bf16[272,1024]{1,0:T(8,128)(2,1)} %get-tuple-element.1046.refs_4_.refs_10_.refs_13_.refs_18_), channel_id=1, source_target_pairs={{0,8},{4,12},{8,0},{12,4},{16,24},{20,28},{24,16},{28,20},{1,9},{5... | collective-permute-start | bytes 1671176 | tf_op jit(solution)/shard_map/ppermute | solution.py:21
  14.8 32.3 %collective-permute-start.5 = (bf16[272,1024]{1,0:T(8,128)(2,1)}, bf16[272,1024]{1,0:T(8,128)(2,1)}, u32[]{:S(2)}, u32[]{:S(2)}) collective-permute-start(bf16[272,1024]{1,0:T(8,128)(2,1)} %get-tuple-element.1046.refs_4_.refs_10_.refs_13_.refs_18_), channel_id=1, source_target_pairs={{0,16},{4,20},{8,24},{12,28},{16,0},{20,4},{24,8},{28,12},{1,17},{... | collective-permute-start | bytes 1671176 | tf_op jit(solution)/shard_map/ppermute | solution.py:21
  16.1 29.2 %collective-permute-start.4 = (bf16[256,1024]{1,0:T(8,128)(2,1)}, bf16[256,1024]{1,0:T(8,128)(2,1)}, u32[]{:S(2)}, u32[]{:S(2)}) collective-permute-start(bf16[256,1024]{1,0:T(8,128)(2,1)} %get-tuple-element.1047.refs_5_.refs_11_.refs_14_.refs_19_), channel_id=1, source_target_pairs={{0,8},{4,12},{8,0},{12,4},{16,24},{20,28},{24,16},{28,20},{1,9},{5... | collective-permute-start | bytes 1572872 | tf_op jit(solution)/shard_map/ppermute | solution.py:21
  16.3 30.8 %collective-permute-start.6 = (bf16[256,1024]{1,0:T(8,128)(2,1)}, bf16[256,1024]{1,0:T(8,128)(2,1)}, u32[]{:S(2)}, u32[]{:S(2)}) collective-permute-start(bf16[256,1024]{1,0:T(8,128)(2,1)} %get-tuple-element.1047.refs_5_.refs_11_.refs_14_.refs_19_), channel_id=1, source_target_pairs={{0,16},{4,20},{8,24},{12,28},{16,0},{20,4},{24,8},{28,12},{1,17},{... | collective-permute-start | bytes 1572872 | tf_op jit(solution)/shard_map/ppermute | solution.py:21
  17.1 30.0 %collective-permute-start.2 = (bf16[2,1024]{1,0:T(2,128)(2,1)S(1)}, bf16[2,1024]{1,0:T(2,128)(2,1)S(1)}, u32[]{:S(2)}, u32[]{:S(2)}) collective-permute-start(bf16[2,1024]{1,0:T(2,128)(2,1)S(1)} %bitcast.61), channel_id=1, source_target_pairs={{0,1},{1,2},{2,3},{4,5},{5,6},{6,7},{8,9},{9,10},{10,11},{12,13},{... | collective-permute-start | bytes 12296 | tf_op jit(solution)/shard_map/ppermute | solution.py:27
  52.6 205.0 %reduce-scatter.4.cloned.1.call-start = ((), (), s32[]{:S(2)}) async-start(), calls=%async_computation.5 | async-start | bytes 5242880 | tf_op jit(solution)/shard_map/reduce_scatter | solution.py:1139
  53.0 13.6 %collective-permute-start.14 = (bf16[256,1024]{1,0:T(8,128)(2,1)}, bf16[256,1024]{1,0:T(8,128)(2,1)S(1)}, u32[]{:S(2)}, u32[]{:S(2)}) collective-permute-start(bf16[256,1024]{1,0:T(8,128)(2,1)} %collective-permute-done.6.refs_9_.refs_15_.refs_18_.refs_23_), channel_id=1, source_target_pairs={{0,8},{4,12},{8,0},{12,4},{16,24},{20,28},{24,16},{28,20},{1,9},{5... | collective-permute-start | bytes 1572872 | tf_op jit(solution)/shard_map/ppermute | solution.py:21
  53.7 13.8 %collective-permute-start.10 = (bf16[256,1024]{1,0:T(8,128)(2,1)}, bf16[256,1024]{1,0:T(8,128)(2,1)}, u32[]{:S(2)}, u32[]{:S(2)}) collective-permute-start(bf16[256,1024]{1,0:T(8,128)(2,1)} %collective-permute-done.4.refs_7_.refs_13_.refs_16_.refs_21_), channel_id=1, source_target_pairs={{0,4},{4,0},{8,12},{12,8},{16,20},{20,16},{24,28},{28,24},{1,5},{5... | collective-permute-start | bytes 1572872 | tf_op jit(solution)/shard_map/ppermute | solution.py:21
  54.2 15.9 %collective-permute-start.7 = (bf16[80,4096]{1,0:T(8,128)(2,1)}, bf16[80,4096]{1,0:T(8,128)(2,1)S(1)}, u32[]{:S(2)}, u32[]{:S(2)}) collective-permute-start(bf16[80,4096]{1,0:T(8,128)(2,1)} %get-tuple-element.972.refs_5_.refs_6_), channel_id=1, source_target_pairs={{0,4},{4,0},{8,12},{12,8},{16,20},{20,16},{24,28},{28,24},{1,5},{5... | collective-permute-start | bytes 1966088 | tf_op jit(solution)/shard_map/ppermute | solution.py:21
  54.2 16.9 %collective-permute-start.8 = (bf16[80,4096]{1,0:T(8,128)(2,1)}, bf16[80,4096]{1,0:T(8,128)(2,1)S(1)}, u32[]{:S(2)}, u32[]{:S(2)}) collective-permute-start(bf16[80,4096]{1,0:T(8,128)(2,1)} %get-tuple-element.973.refs_6_.refs_7_), channel_id=1, source_target_pairs={{0,4},{4,0},{8,12},{12,8},{16,20},{20,16},{24,28},{28,24},{1,5},{5... | collective-permute-start | bytes 1966088 | tf_op jit(solution)/shard_map/ppermute | solution.py:21
  54.8 14.3 %collective-permute-start.13 = (bf16[272,1024]{1,0:T(8,128)(2,1)}, bf16[272,1024]{1,0:T(8,128)(2,1)S(1)}, u32[]{:S(2)}, u32[]{:S(2)}) collective-permute-start(bf16[272,1024]{1,0:T(8,128)(2,1)} %collective-permute-done.3.refs_6_.refs_12_.refs_15_.refs_20_), channel_id=1, source_target_pairs={{0,16},{4,20},{8,24},{12,28},{16,0},{20,4},{24,8},{28,12},{1,17},{... | collective-permute-start | bytes 1671176 | tf_op jit(solution)/shard_map/ppermute | solution.py:21
  74.7 24.8 %collective-permute-start.17 = (bf16[80,4096]{1,0:T(8,128)(2,1)}, bf16[80,4096]{1,0:T(8,128)(2,1)}, u32[]{:S(2)}, u32[]{:S(2)}) collective-permute-start(bf16[80,4096]{1,0:T(8,128)(2,1)} %get-tuple-element.972.refs_5_.refs_6_), channel_id=1, source_target_pairs={{0,8},{4,12},{8,0},{12,4},{16,24},{20,28},{24,16},{28,20},{1,9},{5... | collective-permute-start | bytes 1966088 | tf_op jit(solution)/shard_map/ppermute | solution.py:21
  75.5 29.6 %collective-permute-start.18 = (bf16[80,4096]{1,0:T(8,128)(2,1)}, bf16[80,4096]{1,0:T(8,128)(2,1)}, u32[]{:S(2)}, u32[]{:S(2)}) collective-permute-start(bf16[80,4096]{1,0:T(8,128)(2,1)} %get-tuple-element.973.refs_6_.refs_7_), channel_id=1, source_target_pairs={{0,8},{4,12},{8,0},{12,4},{16,24},{20,28},{24,16},{28,20},{1,9},{5... | collective-permute-start | bytes 1966088 | tf_op jit(solution)/shard_map/ppermute | solution.py:21
  76.3 28.8 %collective-permute-start.19 = (bf16[80,4096]{1,0:T(8,128)(2,1)}, bf16[80,4096]{1,0:T(8,128)(2,1)}, u32[]{:S(2)}, u32[]{:S(2)}) collective-permute-start(bf16[80,4096]{1,0:T(8,128)(2,1)} %get-tuple-element.972.refs_5_.refs_6_), channel_id=1, source_target_pairs={{0,16},{4,20},{8,24},{12,28},{16,0},{20,4},{24,8},{28,12},{1,17},{... | collective-permute-start | bytes 1966088 | tf_op jit(solution)/shard_map/ppermute | solution.py:21
  77.0 28.9 %collective-permute-start.20 = (bf16[80,4096]{1,0:T(8,128)(2,1)}, bf16[80,4096]{1,0:T(8,128)(2,1)}, u32[]{:S(2)}, u32[]{:S(2)}) collective-permute-start(bf16[80,4096]{1,0:T(8,128)(2,1)} %get-tuple-element.973.refs_6_.refs_7_), channel_id=1, source_target_pairs={{0,16},{4,20},{8,24},{12,28},{16,0},{20,4},{24,8},{28,12},{1,17},{... | collective-permute-start | bytes 1966088 | tf_op jit(solution)/shard_map/ppermute | solution.py:21
  105.9 16.8 %collective-permute-start.21 = (bf16[80,4096]{1,0:T(8,128)(2,1)}, bf16[80,4096]{1,0:T(8,128)(2,1)S(1)}, u32[]{:S(2)}, u32[]{:S(2)}) collective-permute-start(bf16[80,4096]{1,0:T(8,128)(2,1)} %collective-permute-done.17.refs_7_.refs_8_), channel_id=1, source_target_pairs={{0,4},{4,0},{8,12},{12,8},{16,20},{20,16},{24,28},{28,24},{1,5},{5... | collective-permute-start | bytes 1966088 | tf_op jit(solution)/shard_map/ppermute | solution.py:21
  107.8 16.7 %collective-permute-start.23 = (bf16[80,4096]{1,0:T(8,128)(2,1)}, bf16[80,4096]{1,0:T(8,128)(2,1)}, u32[]{:S(2)}, u32[]{:S(2)}) collective-permute-start(bf16[80,4096]{1,0:T(8,128)(2,1)} %collective-permute-done.17.refs_7_.refs_8_), channel_id=1, source_target_pairs={{0,16},{4,20},{8,24},{12,28},{16,0},{20,4},{24,8},{28,12},{1,17},{... | collective-permute-start | bytes 1966088 | tf_op jit(solution)/shard_map/ppermute | solution.py:21
  108.5 14.2 %collective-permute-start.22 = (bf16[80,4096]{1,0:T(8,128)(2,1)}, bf16[80,4096]{1,0:T(8,128)(2,1)}, u32[]{:S(2)}, u32[]{:S(2)}) collective-permute-start(bf16[80,4096]{1,0:T(8,128)(2,1)} %collective-permute-done.18.refs_8_.refs_9_), channel_id=1, source_target_pairs={{0,4},{4,0},{8,12},{12,8},{16,20},{20,16},{24,28},{28,24},{1,5},{5... | collective-permute-start | bytes 1966088 | tf_op jit(solution)/shard_map/ppermute | solution.py:21
  108.8 16.4 %collective-permute-start.24 = (bf16[80,4096]{1,0:T(8,128)(2,1)}, bf16[80,4096]{1,0:T(8,128)(2,1)}, u32[]{:S(2)}, u32[]{:S(2)}) collective-permute-start(bf16[80,4096]{1,0:T(8,128)(2,1)} %collective-permute-done.20.refs_10_.refs_11_), channel_id=1, source_target_pairs={{0,8},{4,12},{8,0},{12,4},{16,24},{20,28},{24,16},{28,20},{1,9},{5... | collective-permute-start | bytes 1966088 | tf_op jit(solution)/shard_map/ppermute | solution.py:21
  117.8 5.0 %collective-permute-start.25 = (f32[2,1024]{1,0:T(2,128)}, f32[2,1024]{1,0:T(2,128)S(1)}, u32[]{:S(2)}, u32[]{:S(2)}) collective-permute-start(f32[2,1024]{1,0:T(2,128)} %get-tuple-element.721), channel_id=1, source_target_pairs={{0,1},{1,2},{2,3},{4,5},{5,6},{6,7},{8,9},{9,10},{10,11},{12,13},{... | collective-permute-start | bytes 24584 | tf_op jit(solution)/shard_map/ppermute | solution.py:27
  125.2 3.1 collective-permute-start.26
  126.3 3.9 %collective-permute-start.28 = (bf16[80,4096]{1,0:T(8,128)(2,1)}, bf16[80,4096]{1,0:T(8,128)(2,1)}, u32[]{:S(2)}, u32[]{:S(2)}) collective-permute-start(bf16[80,4096]{1,0:T(8,128)(2,1)} %collective-permute-done.23.refs_11_.refs_12_), channel_id=1, source_target_pairs={{0,4},{4,0},{8,12},{12,8},{16,20},{20,16},{24,28},{28,24},{1,5},{5... | collective-permute-start | bytes 1966088 | tf_op jit(solution)/shard_map/ppermute | solution.py:21
  126.8 4.4 %collective-permute-start.29 = (bf16[80,4096]{1,0:T(8,128)(2,1)}, bf16[80,4096]{1,0:T(8,128)(2,1)}, u32[]{:S(2)}, u32[]{:S(2)}) collective-permute-start(bf16[80,4096]{1,0:T(8,128)(2,1)} %collective-permute-done.24.refs_12_.refs_13_), channel_id=1, source_target_pairs={{0,4},{4,0},{8,12},{12,8},{16,20},{20,16},{24,28},{28,24},{1,5},{5... | collective-permute-start | bytes 1966088 | tf_op jit(solution)/shard_map/ppermute | solution.py:21
  131.2 10.8 %collective-permute-start.31 = (bf16[1536,1024]{1,0:T(8,128)(2,1)}, bf16[1536,1024]{1,0:T(8,128)(2,1)}, u32[]{:S(2)}, u32[]{:S(2)}) collective-permute-start(bf16[1536,1024]{1,0:T(8,128)(2,1)} %all-gather.9.cloned.1.call-done.refs_7_.refs_4_), channel_id=1, source_target_pairs={{0,4},{4,0},{8,12},{12,8},{16,20},{20,16},{24,28},{28,24},{1,5},{5... | collective-permute-start | bytes 9437192 | tf_op jit(solution)/shard_map/ppermute | solution.py:21
  131.5 10.4 %collective-permute-start.30 = (bf16[512,1024]{1,0:T(8,128)(2,1)}, bf16[512,1024]{1,0:T(8,128)(2,1)}, u32[]{:S(2)}, u32[]{:S(2)}) collective-permute-start(bf16[512,1024]{1,0:T(8,128)(2,1)} %refs_3_.2), channel_id=1, source_target_pairs={{0,4},{4,0},{8,12},{12,8},{16,20},{20,16},{24,28},{28,24},{1,5},{5... | collective-permute-start | bytes 3145736 | tf_op jit(solution)/shard_map/ppermute | solution.py:21
  142.0 10.1 %collective-permute-start.35 = (bf16[3,256,1024]{2,1,0:T(8,128)(2,1)}, bf16[3,256,1024]{2,1,0:T(8,128)(2,1)}, u32[]{:S(2)}, u32[]{:S(2)}) collective-permute-start(bf16[3,256,1024]{2,1,0:T(8,128)(2,1)} %get-tuple-element.1142.refs_11_.refs_1_), channel_id=1, source_target_pairs={{0,4},{4,0},{8,12},{12,8},{16,20},{20,16},{24,28},{28,24},{1,5},{5... | collective-permute-start | bytes 4718600 | tf_op jit(solution)/shard_map/ppermute | solution.py:21
  142.4 9.7 %collective-permute-start.32 = (bf16[2,256,1024]{2,1,0:T(8,128)(2,1)}, bf16[2,256,1024]{2,1,0:T(8,128)(2,1)}, u32[]{:S(2)}, u32[]{:S(2)}) collective-permute-start(bf16[2,256,1024]{2,1,0:T(8,128)(2,1)} %get-tuple-element.992.refs_1_), channel_id=1, source_target_pairs={{0,4},{4,0},{8,12},{12,8},{16,20},{20,16},{24,28},{28,24},{1,5},{5... | collective-permute-start | bytes 3145736 | tf_op jit(solution)/shard_map/ppermute | solution.py:21
  142.5 9.5 %collective-permute-start.33 = (bf16[256,2048]{1,0:T(8,128)(2,1)}, bf16[256,2048]{1,0:T(8,128)(2,1)}, u32[]{:S(2)}, u32[]{:S(2)}) collective-permute-start(bf16[256,2048]{1,0:T(8,128)(2,1)} %get-tuple-element.857.refs_2_), channel_id=1, source_target_pairs={{0,4},{4,0},{8,12},{12,8},{16,20},{20,16},{24,28},{28,24},{1,5},{5... | collective-permute-start | bytes 3145736 | tf_op jit(solution)/shard_map/ppermute | solution.py:21
  142.9 9.1 %collective-permute-start.34 = (bf16[256,1024]{1,0:T(8,128)(2,1)}, bf16[256,1024]{1,0:T(8,128)(2,1)S(1)}, u32[]{:S(2)}, u32[]{:S(2)}) collective-permute-start(bf16[256,1024]{1,0:T(8,128)(2,1)} %get-tuple-element.1095.refs_9_), channel_id=1, source_target_pairs={{0,4},{4,0},{8,12},{12,8},{16,20},{20,16},{24,28},{28,24},{1,5},{5... | collective-permute-start | bytes 1572872 | tf_op jit(solution)/shard_map/ppermute | solution.py:21
  152.5 9.1 %collective-permute-start.36 = (bf16[256,1024]{1,0:T(8,128)(2,1)}, bf16[256,1024]{1,0:T(8,128)(2,1)}, u32[]{:S(2)}, u32[]{:S(2)}) collective-permute-start(bf16[256,1024]{1,0:T(8,128)(2,1)} %get-tuple-element.962.refs_3_), channel_id=1, source_target_pairs={{0,4},{4,0},{8,12},{12,8},{16,20},{20,16},{24,28},{28,24},{1,5},{5... | collective-permute-start | bytes 1572872 | tf_op jit(solution)/shard_map/ppermute | solution.py:21
  165.4 126.0 %reduce-scatter.6.cloned.1.call-start = ((), (), s32[]{:S(2)}) async-start(), calls=%async_computation.6 | async-start | bytes 2621440 | tf_op jit(solution)/shard_map/reduce_scatter | solution.py:1139
  173.7 17.2 %collective-permute-start.42 = (bf16[256,4096]{1,0:T(8,128)(2,1)}, bf16[256,4096]{1,0:T(8,128)(2,1)}, u32[]{:S(2)}, u32[]{:S(2)}) collective-permute-start(bf16[256,4096]{1,0:T(8,128)(2,1)} %shard_map.456.refs_4_.refs_3_), channel_id=1, source_target_pairs={{0,4},{4,0},{8,12},{12,8},{16,20},{20,16},{24,28},{28,24},{1,5},{5... | collective-permute-start | bytes 6291464 | tf_op jit(solution)/shard_map/ppermute | solution.py:21
  174.2 23.7 %collective-permute-start.38 = (bf16[128,1024]{1,0:T(8,128)(2,1)}, bf16[128,1024]{1,0:T(8,128)(2,1)S(1)}, u32[]{:S(2)}, u32[]{:S(2)}) collective-permute-start(bf16[128,1024]{1,0:T(8,128)(2,1)} %get-tuple-element.996), channel_id=1, source_target_pairs={{0,8},{4,12},{8,0},{12,4},{16,24},{20,28},{24,16},{28,20},{1,9},{5... | collective-permute-start | bytes 786440 | tf_op jit(solution)/shard_map/ppermute | solution.py:21
  174.9 23.0 %collective-permute-start.39 = (bf16[128,1024]{1,0:T(8,128)(2,1)}, bf16[128,1024]{1,0:T(8,128)(2,1)S(1)}, u32[]{:S(2)}, u32[]{:S(2)}) collective-permute-start(bf16[128,1024]{1,0:T(8,128)(2,1)} %get-tuple-element.997), channel_id=1, source_target_pairs={{0,16},{4,20},{8,24},{12,28},{16,0},{20,4},{24,8},{28,12},{1,17},{... | collective-permute-start | bytes 786440 | tf_op jit(solution)/shard_map/ppermute | solution.py:21
  175.6 22.4 %collective-permute-start.40 = (bf16[128,1024]{1,0:T(8,128)(2,1)}, bf16[128,1024]{1,0:T(8,128)(2,1)S(1)}, u32[]{:S(2)}, u32[]{:S(2)}) collective-permute-start(bf16[128,1024]{1,0:T(8,128)(2,1)} %get-tuple-element.998), channel_id=1, source_target_pairs={{0,24},{4,28},{8,16},{12,20},{16,8},{20,12},{24,0},{28,4},{1,25},{... | collective-permute-start | bytes 786440 | tf_op jit(solution)/shard_map/ppermute | solution.py:21
  188.6 9.3 %collective-permute-start.41 = (f32[2,1024]{1,0:T(2,128)}, f32[2,1024]{1,0:T(2,128)S(1)}, u32[]{:S(2)}, u32[]{:S(2)}) collective-permute-start(f32[2,1024]{1,0:T(2,128)} %get-tuple-element.1036.refs_2_), channel_id=1, source_target_pairs={{1,0},{2,1},{3,2},{5,4},{6,5},{7,6},{9,8},{10,9},{11,10},{13,12},{... | collective-permute-start | bytes 24584 | tf_op jit(solution)/shard_map/ppermute | solution.py:27
  198.0 50.0 %collective-permute-start.49 = (bf16[128,4096]{1,0:T(8,128)(2,1)}, bf16[128,4096]{1,0:T(8,128)(2,1)}, u32[]{:S(2)}, u32[]{:S(2)}) collective-permute-start(bf16[128,4096]{1,0:T(8,128)(2,1)} %get-tuple-element.1081), channel_id=1, source_target_pairs={{0,8},{4,12},{8,0},{12,4},{16,24},{20,28},{24,16},{28,20},{1,9},{5... | collective-permute-start | bytes 3145736 | tf_op jit(solution)/shard_map/ppermute | solution.py:21
  198.9 49.1 %collective-permute-start.50 = (bf16[128,4096]{1,0:T(8,128)(2,1)}, bf16[128,4096]{1,0:T(8,128)(2,1)}, u32[]{:S(2)}, u32[]{:S(2)}) collective-permute-start(bf16[128,4096]{1,0:T(8,128)(2,1)} %get-tuple-element.1082), channel_id=1, source_target_pairs={{0,16},{4,20},{8,24},{12,28},{16,0},{20,4},{24,8},{28,12},{1,17},{... | collective-permute-start | bytes 3145736 | tf_op jit(solution)/shard_map/ppermute | solution.py:21
  199.5 48.5 %collective-permute-start.51 = (bf16[128,4096]{1,0:T(8,128)(2,1)}, bf16[128,4096]{1,0:T(8,128)(2,1)}, u32[]{:S(2)}, u32[]{:S(2)}) collective-permute-start(bf16[128,4096]{1,0:T(8,128)(2,1)} %get-tuple-element.1083), channel_id=1, source_target_pairs={{0,24},{4,28},{8,16},{12,20},{16,8},{20,12},{24,0},{28,4},{1,25},{... | collective-permute-start | bytes 3145736 | tf_op jit(solution)/shard_map/ppermute | solution.py:21
  209.1 4.3 %collective-permute-start.43 = (f32[8,1024]{1,0:T(8,128)}, f32[8,1024]{1,0:T(8,128)S(1)}, u32[]{:S(2)}, u32[]{:S(2)}) collective-permute-start(f32[8,1024]{1,0:T(8,128)} %get-tuple-element.1062.refs_1_), channel_id=1, source_target_pairs={{0,1},{1,0},{2,3},{3,2},{4,5},{5,4},{6,7},{7,6},{8,9},{9,8},{10,11... | collective-permute-start | bytes 98312 | tf_op jit(solution)/shard_map/ppermute | solution.py:32
  214.2 8.4 %collective-permute-start.44 = (f32[16,1024]{1,0:T(8,128)S(1)}, f32[16,1024]{1,0:T(8,128)S(1)}, u32[]{:S(2)}, u32[]{:S(2)}) collective-permute-start(f32[16,1024]{1,0:T(8,128)S(1)} %pad_maximum_fusion.1), channel_id=1, source_target_pairs={{0,2},{1,3},{2,0},{3,1},{4,6},{5,7},{6,4},{7,5},{8,10},{9,11},{10,... | collective-permute-start | bytes 196616 | tf_op jit(solution)/shard_map/ppermute | solution.py:32
  216.5 10.6 %collective-permute-start.45 = (bf16[256,512]{1,0:T(8,128)(2,1)}, bf16[256,512]{1,0:T(8,128)(2,1)S(1)}, u32[]{:S(2)}, u32[]{:S(2)}) collective-permute-start(bf16[256,512]{1,0:T(8,128)(2,1)} %get-tuple-element.1070.refs_1_), channel_id=1, source_target_pairs={{0,4},{4,0},{8,12},{12,8},{16,20},{20,16},{24,28},{28,24},{1,5},{5... | collective-permute-start | bytes 786440 | tf_op jit(solution)/shard_map/ppermute | solution.py:21
  222.5 5.9 %collective-permute-start.46 = (bf16[256,512]{1,0:T(8,128)(2,1)}, bf16[256,512]{1,0:T(8,128)(2,1)S(1)}, u32[]{:S(2)}, u32[]{:S(2)}) collective-permute-start(bf16[256,512]{1,0:T(8,128)(2,1)} %get-tuple-element.1071.refs_2_), channel_id=1, source_target_pairs={{0,4},{4,0},{8,12},{12,8},{16,20},{20,16},{24,28},{28,24},{1,5},{5... | collective-permute-start | bytes 786440 | tf_op jit(solution)/shard_map/ppermute | solution.py:21
  227.1 14.6 %collective-permute-start.47 = (bf16[256,512]{1,0:T(8,128)(2,1)}, bf16[256,512]{1,0:T(8,128)(2,1)S(1)}, u32[]{:S(2)}, u32[]{:S(2)}) collective-permute-start(bf16[256,512]{1,0:T(8,128)(2,1)} %get-tuple-element.1067.refs_16_.refs_5_), channel_id=1, source_target_pairs={{0,4},{4,0},{8,12},{12,8},{16,20},{20,16},{24,28},{28,24},{1,5},{5... | collective-permute-start | bytes 786440 | tf_op jit(solution)/shard_map/ppermute | solution.py:21
  228.4 13.2 %collective-permute-start.48 = (bf16[256,512]{1,0:T(8,128)(2,1)}, bf16[256,512]{1,0:T(8,128)(2,1)}, u32[]{:S(2)}, u32[]{:S(2)}) collective-permute-start(bf16[256,512]{1,0:T(8,128)(2,1)} %get-tuple-element.1068.refs_17_.refs_6_), channel_id=1, source_target_pairs={{0,4},{4,0},{8,12},{12,8},{16,20},{20,16},{24,28},{28,24},{1,5},{5... | collective-permute-start | bytes 786440 | tf_op jit(solution)/shard_map/ppermute | solution.py:21
  248.0 93.1 %reduce-scatter.8.cloned.1.call-start = ((), (), s32[]{:S(2)}) async-start(), calls=%async_computation.7 | async-start | bytes 1638400 | tf_op jit(solution)/shard_map/reduce_scatter | solution.py:1139
  248.1 9.5 %collective-permute-start.52 = (bf16[2,256,1024]{2,1,0:T(8,128)(2,1)}, bf16[2,256,1024]{2,1,0:T(8,128)(2,1)}, u32[]{:S(2)}, u32[]{:S(2)}) collective-permute-start(bf16[2,256,1024]{2,1,0:T(8,128)(2,1)} %get-tuple-element.1144.refs_3_), channel_id=1, source_target_pairs={{0,4},{4,0},{8,12},{12,8},{16,20},{20,16},{24,28},{28,24},{1,5},{5... | collective-permute-start | bytes 3145736 | tf_op jit(solution)/shard_map/ppermute | solution.py:21
  248.6 8.9 %collective-permute-start.53 = (f32[2,1024]{1,0:T(2,128)S(1)}, f32[2,1024]{1,0:T(2,128)S(1)}, u32[]{:S(2)}, u32[]{:S(2)}) collective-permute-start(f32[2,1024]{1,0:T(2,128)S(1)} %copy-done.30), channel_id=1, source_target_pairs={{1,0},{2,1},{3,2},{5,4},{6,5},{7,6},{9,8},{10,9},{11,10},{13,12},{... | collective-permute-start | bytes 24584 | tf_op jit(solution)/shard_map/ppermute | solution.py:27
  259.7 15.6 %collective-permute-start.54 = (bf16[128,1024]{1,0:T(8,128)(2,1)}, bf16[128,1024]{1,0:T(8,128)(2,1)S(1)}, u32[]{:S(2)}, u32[]{:S(2)}) collective-permute-start(bf16[128,1024]{1,0:T(8,128)(2,1)} %get-tuple-element.1271), channel_id=1, source_target_pairs={{0,8},{4,12},{8,0},{12,4},{16,24},{20,28},{24,16},{28,20},{1,9},{5... | collective-permute-start | bytes 786440 | tf_op jit(solution)/shard_map/ppermute | solution.py:21
  259.8 15.5 %collective-permute-start.55 = (bf16[128,1024]{1,0:T(8,128)(2,1)}, bf16[128,1024]{1,0:T(8,128)(2,1)S(1)}, u32[]{:S(2)}, u32[]{:S(2)}) collective-permute-start(bf16[128,1024]{1,0:T(8,128)(2,1)} %get-tuple-element.1270), channel_id=1, source_target_pairs={{0,16},{4,20},{8,24},{12,28},{16,0},{20,4},{24,8},{28,12},{1,17},{... | collective-permute-start | bytes 786440 | tf_op jit(solution)/shard_map/ppermute | solution.py:21
  260.1 15.1 %collective-permute-start.56 = (bf16[128,1024]{1,0:T(8,128)(2,1)}, bf16[128,1024]{1,0:T(8,128)(2,1)}, u32[]{:S(2)}, u32[]{:S(2)}) collective-permute-start(bf16[128,1024]{1,0:T(8,128)(2,1)} %get-tuple-element.1269), channel_id=1, source_target_pairs={{0,24},{4,28},{8,16},{12,20},{16,8},{20,12},{24,0},{28,4},{1,25},{... | collective-permute-start | bytes 786440 | tf_op jit(solution)/shard_map/ppermute | solution.py:21
  276.0 15.4 %collective-permute-start.57 = (bf16[272,1024]{1,0:T(8,128)(2,1)}, bf16[272,1024]{1,0:T(8,128)(2,1)S(1)}, u32[]{:S(2)}, u32[]{:S(2)}) collective-permute-start(bf16[272,1024]{1,0:T(8,128)(2,1)} %get-tuple-element.1156), channel_id=1, source_target_pairs={{0,8},{4,12},{8,0},{12,4},{16,24},{20,28},{24,16},{28,20},{1,9},{5... | collective-permute-start | bytes 1671176 | tf_op jit(solution)/shard_map/ppermute | solution.py:21
  276.2 15.2 %collective-permute-start.58 = (bf16[272,1024]{1,0:T(8,128)(2,1)}, bf16[272,1024]{1,0:T(8,128)(2,1)}, u32[]{:S(2)}, u32[]{:S(2)}) collective-permute-start(bf16[272,1024]{1,0:T(8,128)(2,1)} %get-tuple-element.1157), channel_id=1, source_target_pairs={{0,16},{4,20},{8,24},{12,28},{16,0},{20,4},{24,8},{28,12},{1,17},{... | collective-permute-start | bytes 1671176 | tf_op jit(solution)/shard_map/ppermute | solution.py:21
  276.4 24.8 %collective-permute-start.59 = (bf16[272,1024]{1,0:T(8,128)(2,1)}, bf16[272,1024]{1,0:T(8,128)(2,1)}, u32[]{:S(2)}, u32[]{:S(2)}) collective-permute-start(bf16[272,1024]{1,0:T(8,128)(2,1)} %get-tuple-element.1158), channel_id=1, source_target_pairs={{0,24},{4,28},{8,16},{12,20},{16,8},{20,12},{24,0},{28,4},{1,25},{... | collective-permute-start | bytes 1671176 | tf_op jit(solution)/shard_map/ppermute | solution.py:21
  303.1 5.9 %collective-permute-start.60 = (bf16[64,1024]{1,0:T(8,128)(2,1)}, bf16[64,1024]{1,0:T(8,128)(2,1)S(1)}, u32[]{:S(2)}, u32[]{:S(2)}) collective-permute-start(bf16[64,1024]{1,0:T(8,128)(2,1)} %get-tuple-element.1274), channel_id=1, source_target_pairs={{0,8},{4,12},{8,0},{12,4},{16,24},{20,28},{24,16},{28,20},{1,9},{5... | collective-permute-start | bytes 393224 | tf_op jit(solution)/shard_map/ppermute | solution.py:21
  303.3 5.7 %collective-permute-start.61 = (bf16[64,1024]{1,0:T(8,128)(2,1)}, bf16[64,1024]{1,0:T(8,128)(2,1)S(1)}, u32[]{:S(2)}, u32[]{:S(2)}) collective-permute-start(bf16[64,1024]{1,0:T(8,128)(2,1)} %get-tuple-element.1273), channel_id=1, source_target_pairs={{0,16},{4,20},{8,24},{12,28},{16,0},{20,4},{24,8},{28,12},{1,17},{... | collective-permute-start | bytes 393224 | tf_op jit(solution)/shard_map/ppermute | solution.py:21
  304.7 5.5 %collective-permute-start.62 = (bf16[64,1024]{1,0:T(8,128)(2,1)}, bf16[64,1024]{1,0:T(8,128)(2,1)}, u32[]{:S(2)}, u32[]{:S(2)}) collective-permute-start(bf16[64,1024]{1,0:T(8,128)(2,1)} %get-tuple-element.1272), channel_id=1, source_target_pairs={{0,24},{4,28},{8,16},{12,20},{16,8},{20,12},{24,0},{28,4},{1,25},{... | collective-permute-start | bytes 393224 | tf_op jit(solution)/shard_map/ppermute | solution.py:21
  310.2 12.7 %collective-permute-start.63 = (bf16[80,1024]{1,0:T(8,128)(2,1)}, bf16[80,1024]{1,0:T(8,128)(2,1)S(1)}, u32[]{:S(2)}, u32[]{:S(2)}) collective-permute-start(bf16[80,1024]{1,0:T(8,128)(2,1)} %get-tuple-element.1195), channel_id=1, source_target_pairs={{0,1},{1,0},{2,3},{3,2},{4,5},{5,4},{6,7},{7,6},{8,9},{9,8},{10,11... | collective-permute-start | bytes 491528 | tf_op jit(solution)/shard_map/ppermute | solution.py:32
  310.2 15.8 %collective-permute-start.64 = (bf16[80,1024]{1,0:T(8,128)(2,1)}, bf16[80,1024]{1,0:T(8,128)(2,1)S(1)}, u32[]{:S(2)}, u32[]{:S(2)}) collective-permute-start(bf16[80,1024]{1,0:T(8,128)(2,1)} %get-tuple-element.1196), channel_id=1, source_target_pairs={{0,2},{1,3},{2,0},{3,1},{4,6},{5,7},{6,4},{7,5},{8,10},{9,11},{10,... | collective-permute-start | bytes 491528 | tf_op jit(solution)/shard_map/ppermute | solution.py:32
  311.5 25.1 %collective-permute-start.65 = (bf16[80,1024]{1,0:T(8,128)(2,1)}, bf16[80,1024]{1,0:T(8,128)(2,1)S(1)}, u32[]{:S(2)}, u32[]{:S(2)}) collective-permute-start(bf16[80,1024]{1,0:T(8,128)(2,1)} %get-tuple-element.1197), channel_id=1, source_target_pairs={{0,3},{1,2},{2,1},{3,0},{4,7},{5,6},{6,5},{7,4},{8,11},{9,10},{10,... | collective-permute-start | bytes 491528 | tf_op jit(solution)/shard_map/ppermute | solution.py:32
  337.4 3.1 collective-permute-start.66
  (41 other events, 293.5 us)
Sparse Core Ops, SparseCore 0:
  12.9 37.5 all-gather.6
  52.7 62.7 all-gather.8
  165.5 79.6 reduce-scatter.3
  248.1 42.0 reduce-scatter.5
  292.4 36.6 reduce-scatter.7

commit v5 on v4

--- a/solution.py
+++ b/solution.py
@@ -171,8 +171,11 @@
                 pending[k] = None
             return buffers[k]
 
-        def put(k):
-            stored[k] = loads.start(big_buffers[k], big_refs[k])
+        def put(k, part=None):
+            src, dst = big_buffers[k], big_refs[k]
+            if part is not None:
+                src, dst = src.at[part], dst.at[part]
+            stored.setdefault(k, []).append(loads.start(src, dst))
 
         body(info_ref, small_refs, get, raw_refs, out_refs, big_buffers, put, rest, loads)
         for k in range(n_large):
@@ -180,7 +183,7 @@
         for k in range(n_big):
             if k not in stored:
                 put(k)
-        wait(stored.values())
+        wait([c for copies in stored.values() for c in copies])
 
     hbm = pl.BlockSpec(memory_space=pltpu.HBM)
     vmem = pl.BlockSpec(memory_space=pltpu.VMEM)
@@ -403,7 +406,7 @@
             wait(copies[k])
             @columns(width, STEP)
             def _(n):
-                big[1 + k][:, n] = dot_nn(in_ref[k], w[k, :, n])
+                big[1 + k][:, n] = dot_nn(in_ref[k], w[k, :, n]).astype(big[1 + k].dtype)
             put(1 + k)
         project(0)
         project(1)
@@ -417,7 +420,8 @@
                 shifted = keys_ref[t, n] - at * rate
                 peak = jnp.max(shifted, axis=0, keepdims=True)
                 factor = jnp.exp(shifted - peak)
-                sum_ref[b : b + 1, n] = jnp.sum(factor * vals_ref[t, n], axis=0, keepdims=True)
+                sum_ref[b : b + 1, n] = jnp.sum(
+                    factor * vals_ref[t, n].astype(f32), axis=0, keepdims=True)
                 sum_ref[batches + b : batches + b + 1, n] = jnp.sum(factor, axis=0, keepdims=True)
                 sum_ref[2 * batches + b : 2 * batches + b + 1, n] = peak + (length - 1.0) * rate
         project(2)
@@ -426,7 +430,7 @@
     return call(
         body, info, [last, previous, *extra], [(stream, None)], flat_pieces(pieces),
         [((3 * batches, width), f32), ((16, width), f32), ((batches, width), f32)],
-        [((3, tokens, width), bf16)] + [((tokens, width), f32)] * 3,
+        [((3, tokens, width), bf16), ((tokens, width), f32)] + [((tokens, width), bf16)] * 2,
         [pltpu.VMEM((3, width, width), bf16), pltpu.VMEM((16 * len(order), width), bf16)],
         len(vplan) + sum(map(len, plans)), 9, 40)
 
@@ -497,16 +501,16 @@
             @columns(width, LANES)
             def _(n):
                 _, factor, p, o, e = wkv_terms(kvr_ref, ent_ref, vec_ref, b, t, n, batches, length)
-                vals = kvr_ref[1][t, n]
+                vals = kvr_ref[1][t, n].astype(f32)
                 num = (two_part(lower, factor * vals) * p
                        + ent_ref[b : b + 1, n] * o + vals * e)
                 den = (two_part(lower, factor) * p
                        + ent_ref[batches + b : batches + b + 1, n] * o + e)
                 rden = 1.0 / den
                 wkv = num * rden
-                wkv_ref[t, n] = wkv
-                rden_ref[t, n] = rden
-                gated_ref[t, n] = (jax.nn.sigmoid(kvr_ref[2][t, n]) * wkv).astype(bf16)
+                wkv_ref[t, n] = wkv.astype(bf16)
+                rden_ref[t, n] = rden.astype(bf16)
+                gated_ref[t, n] = (jax.nn.sigmoid(kvr_ref[2][t, n].astype(f32)) * wkv).astype(bf16)
         put(0)
         put(1)
         put(2)
@@ -520,17 +524,17 @@
         def _(i):
             r = row_chunk(0, i, 0)
             nb, _ = norm(mid_ref[r, :])
-            xb_ref[r, :] = nb * vec_ref[G2 : G2 + 1] + vec_ref[B2 : B2 + 1]
+            xb_ref[r, :] = (nb * vec_ref[G2 : G2 + 1] + vec_ref[B2 : B2 + 1]).astype(bf16)
         for b in range(batches):
-            last = (b + 1) * length - 1
-            edge_ref[b : b + 1, :] = xb_ref[last : last + 1, :]
-
-    one = ((tokens, width), f32)
+            last = (b + 1) * length
+            edge_ref[b : b + 1, :] = xb_ref[last - 16 : last, :].astype(f32)[15:]
+
+    one, low = ((tokens, width), f32), ((tokens, width), bf16)
     return call(
         body, info, [*everyone, *state, vec], [(a, None) for a in (*kvr, stream)], flat_pieces(pieces),
         [((3 * batches, width), f32), ((batches, 1, width), f32), ((batches, 1, width), f32),
          ((batches, width), f32)],
-        [((tokens, width), bf16), one, one, one, one],
+        [low, low, low, one, low],
         [pltpu.VMEM((width, width), bf16)], len(steps), 7, 40)
 
 
@@ -596,7 +600,7 @@
         for b in range(batches):
             def step(i, before):
                 r = row_chunk(b, i, length)
-                x = xb_ref[r, :]
+                x = xb_ref[r, :].astype(f32)
                 xt = down_one(x, before)
                 for k, row in enumerate((CMK, CMR)):
                     mix = vec_ref[row : row + 1]
@@ -618,13 +622,13 @@
         wait(copies_c)
         @columns(width, STEP)
         def _(n):
-            frec_ref[:, n] = dot_nn(in_ref[1], wc[:, n])
+            frec_ref[:, n] = dot_nn(in_ref[1], wc[:, n]).astype(bf16)
 
     return call(
         body, info, [edge, previous, vec], [(xb, None)], flat_pieces(pieces_ck),
         [((batches, width), f32)],
         [((2, tokens, width), bf16), ((tokens, wide // 2), bf16), ((tokens, wide // 2), bf16),
-         ((tokens, wide), bf16), ((tokens, width), f32)],
+         ((tokens, wide), bf16), ((tokens, width), bf16)],
         [pltpu.VMEM((width, wide), bf16), pltpu.VMEM((width, width), bf16)],
         len(steps_c) * (wide // width) + len(steps_k) * len(order), 11, 40)
 
@@ -652,7 +656,7 @@
         @pl.loop(0, tokens // ROWS)
         def _(i):
             r = row_chunk(0, i, 0)
-            sig = jax.nn.sigmoid(frec_ref[r, :])
+            sig = jax.nn.sigmoid(frec_ref[r, :].astype(f32))
             cots, value = cot_ref[r, :].astype(f32), fval[r, :]
             df_ref[r, :] = (cots * sig).astype(bf16)
             out_ref[r, :] = (mid_ref[r, :] + sig * value).astype(bf16)
@@ -681,10 +685,11 @@
             block = slice(at * fshard, (at + 1) * fshard)
             d = dot_nt(dfval_ref[...], wv[block, :]) * (2.0 * act_ref[:, block].astype(f32))
             dpre_ref[:, block] = d.astype(bf16)
+            put(0, (slice(None), pl.ds(at * fshard, fshard)))
 
     return call(
         body, info, [], [(dfval, None), (act, None)], cv, [], [((tokens, wide), bf16)],
-        [pltpu.VMEM((wide, width), bf16)], value_copies(stretches), 7, 40)[0]
+        [pltpu.VMEM((wide, width), bf16)], value_copies(stretches) + len(order), 7, 40)[0]
 
 
 def chan_back(info, dpre, dfrec, xb, entry, vec, pieces_ck, length, shard, fshard):
@@ -722,23 +727,23 @@
         for b in range(batches):
             def step(i, before):
                 r = row_chunk(b, i, length)
-                x = xb_ref[r, :]
+                x = xb_ref[r, :].astype(f32)
                 gap = x - down_one(x, before)
                 a, c = df[r, :], dr[r, :]
                 ck, cr = vec_ref[CMK : CMK + 1], vec_ref[CMR : CMR + 1]
-                dxt_ref[r, :] = a * (1.0 - ck) + c * (1.0 - cr)
-                dxb_ref[r, :] = a * ck + c * cr
+                dxt_ref[r, :] = (a * (1.0 - ck) + c * (1.0 - cr)).astype(bf16)
+                dxb_ref[r, :] = (a * ck + c * cr).astype(bf16)
                 sum_ref[0] += fold(a * gap)
                 sum_ref[1] += fold(c * gap)
                 return x[ROWS - 1 :]
             lax.fori_loop(0, length // ROWS, step, entry_ref[b : b + 1])
-            head_ref[b : b + 1, :] = dxt_ref[b * length : b * length + 1, :]
+            head_ref[b : b + 1, :] = dxt_ref[b * length : b * length + 16, :].astype(f32)[:1]
         column_sums(total_ref, sum_ref)
 
-    one = ((tokens, width), f32)
+    low = ((tokens, width), bf16)
     return call(
         body, info, [entry, vec], [(a, None) for a in (dfrec, dpre, xb)], flat_pieces(pieces_ck),
-        [((batches, width), f32), ((2, width), f32)], [one, one],
+        [((batches, width), f32), ((2, width), f32)], [low, low],
         [pltpu.VMEM((width, wide), bf16), pltpu.VMEM((width, width), bf16),
          pltpu.VMEM((tokens, width), f32), pltpu.VMEM((tokens, width), f32),
          pltpu.VMEM((2, 8, width), f32)],
@@ -756,7 +761,7 @@
         dent_ref[2 * batches : 3 * batches, :] = ent_ref[2 * batches :, :]
         dent_ref[3 * batches :, :] = head_ref[...]
         dmid_ref, low_ref, high_ref, rlow_ref, rhigh_ref, gn_ref = big
-        w, sum_ref = scratch
+        w, sum_ref, dgate = scratch
         copies = loads.pieces(steps, raw, w, natural(info[0], shard))
         sum_ref[...] = jnp.zeros_like(sum_ref)
         dxt_ref, dxb_ref, mid_ref, cot_ref = get(0), get(1), get(2), get(3)
@@ -764,10 +769,10 @@
             def step(k, after_row):
                 r = row_chunk(b, length // ROWS - 1 - k, length)
                 nb, inverse = norm(mid_ref[r, :])
-                dx = dxt_ref[r, :]
-                d = dxb_ref[r, :] + up_one(dx, after_row)
+                dx = dxt_ref[r, :].astype(f32)
+                d = dxb_ref[r, :].astype(f32) + up_one(dx, after_row)
                 back = cot_ref[r, :].astype(f32) + norm_back(d, nb, inverse, vec_ref[G2 : G2 + 1])
-                dmid_ref[r, :] = back
+                dmid_ref[r, :] = back.astype(bf16)
                 low_ref[r, :] = back[:, : width // 2].astype(bf16)
                 high_ref[r, :] = back[:, width // 2 :].astype(bf16)
                 sum_ref[0] += fold(d * nb)
@@ -781,8 +786,8 @@
         wait(copies)
         @columns(width, STEP)
         def _(n):
-            gn_ref[:, n] = (dot_nt(low_ref[...], w[n, : width // 2])
-                            + dot_nt(high_ref[...], w[n, width // 2 :]))
+            dgate[:, n] = (dot_nt(low_ref[...], w[n, : width // 2])
+                           + dot_nt(high_ref[...], w[n, width // 2 :]))
         kvr_ref = [get(4), None, get(5)]
         wkv_ref, rden_ref = get(6), get(7)
         lanes = min(LANES, width // 2)
@@ -793,21 +798,22 @@
             part, at_half = (rlow_ref, rhigh_ref)[half], slice(q * lanes, (q + 1) * lanes)
             if True:
                 _, _, _, o, _ = wkv_terms(kvr_ref, ent_ref, vec_ref, b, t, n, batches, length)
-                sig = jax.nn.sigmoid(kvr_ref[2][t, n])
-                d = gn_ref[t, n] * sig
-                wkvs = wkv_ref[t, n]
+                sig = jax.nn.sigmoid(kvr_ref[2][t, n].astype(f32))
+                d = dgate[t, n] * sig
+                wkvs = wkv_ref[t, n].astype(f32)
                 part[t, at_half] = (d * wkvs * (1.0 - sig)).astype(bf16)
-                gn = d * rden_ref[t, n]
-                gn_ref[t, n] = gn
+                gn = d * rden_ref[t, n].astype(f32)
+                gn_ref[t, n] = gn.astype(bf16)
                 go = gn * o
                 dent_ref[b : b + 1, n] = jnp.sum(go, axis=0, keepdims=True)
                 dent_ref[batches + b : batches + b + 1, n] = -jnp.sum(go * wkvs, axis=0, keepdims=True)
 
-    one, half = ((tokens, width), f32), ((tokens, width // 2), bf16)
+    low, half = ((tokens, width), bf16), ((tokens, width // 2), bf16)
     return call(
         body, info, [after, head, vec, ent], [(a, None) for a in (dxt, dxb, mid, cot, kvr[0], kvr[2], wkv, rden)],
-        flat_pieces(pieces), [((4 * batches, width), f32), ((2, width), f32)], [one, half, half, half, half, one],
-        [pltpu.VMEM((width, width), bf16), pltpu.VMEM((2, 8, width), f32)], len(steps), 9, 40)
+        flat_pieces(pieces), [((4 * batches, width), f32), ((2, width), f32)], [low, half, half, half, half, low],
+        [pltpu.VMEM((width, width), bf16), pltpu.VMEM((2, 8, width), f32), pltpu.VMEM((tokens, width), f32)],
+        len(steps), 9, 40)
 
 
 def time_back(info, gn, wkv, kvr, ent, back, sums, state, drec, stream, entry, vec, pieces, spots,
@@ -875,8 +881,8 @@
             @columns(width, LANES)
             def _(n):
                 at, factor, p, o, e = wkv_terms(kvr_ref, ent_ref, vec_ref, b, t, n, batches, length)
-                vals, g = kvr_ref[1][t, n], gn_ref[t, n]
-                gd = -g * wkv_ref[t, n]
+                vals, g = kvr_ref[1][t, n].astype(f32), gn_ref[t, n].astype(f32)
+                gd = -g * wkv_ref[t, n].astype(f32)
                 direct = e * (g * vals + gd)
                 opened = o * (g * ent_ref[b : b + 1, n] + gd * ent_ref[batches + b : batches + b + 1, n])
                 rn = two_part(upper, g * p) + later_ref[b : b + 1, n]
@@ -918,20 +924,20 @@
                     dxs = dxs + d * (1.0 - mix)
                     dxa = dxa + d * mix
                     sum_ref[k] += fold(d * gap)
-                dxs_ref[r, :] = dxs
-                dxa_ref[r, :] = dxa
+                dxs_ref[r, :] = dxs.astype(bf16)
+                dxa_ref[r, :] = dxa.astype(bf16)
                 return xa[ROWS - 1 :]
             lax.fori_loop(0, length // ROWS, step, entry_ref[b : b + 1])
-            head_ref[b : b + 1, :] = dxs_ref[b * length : b * length + 1, :]
+            head_ref[b : b + 1, :] = dxs_ref[b * length : b * length + 16, :].astype(f32)[:1]
         column_sums(total_ref, sum_ref)
 
-    one = ((tokens, width), f32)
+    low = ((tokens, width), bf16)
     return call(
         body, info, [*back, ent, sums, *state, entry, vec],
         [(a, None) for a in (gn, wkv, kvr[0], kvr[1], stream, *drec)], flat_pieces(pieces),
         [((batches, 1, width), f32)] * 4
         + [((batches, width), f32), ((3, width), f32), ((2, width), f32)],
-        [((2, tokens, width), bf16), one, one],
+        [((2, tokens, width), bf16), low, low],
         [pltpu.VMEM((3, width, width), bf16), pltpu.VMEM((3, tokens, width), f32),
          pltpu.VMEM((3, 8, width), f32), pltpu.VMEM((2 * batches, width), f32),
          pltpu.VMEM((2 * batches, width), f32)],
@@ -952,10 +958,10 @@
             def step(k, after_row):
                 r = row_chunk(b, length // ROWS - 1 - k, length)
                 na, inverse = norm(stream_ref[r, :].astype(f32))
-                dx = dxs_ref[r, :]
-                d = dxa_ref[r, :] + up_one(dx, after_row)
+                dx = dxs_ref[r, :].astype(f32)
+                d = dxa_ref[r, :].astype(f32) + up_one(dx, after_row)
                 back = norm_back(d, na, inverse, vec_ref[G1 : G1 + 1])
-                out_ref[r, :] = (dmid_ref[r, :] + back).astype(bf16)
+                out_ref[r, :] = (dmid_ref[r, :].astype(f32) + back).astype(bf16)
                 sum_ref[0] += fold(d * na)
                 sum_ref[1] += fold(d)
                 return dx[:1]
@@ -1005,42 +1011,43 @@
                 return ref.at[:, pl.ds(natural(info[0], w)(m), w)]
             return ref.at[:, pl.ds(evens.index(m) * w, w)]
 
-        copies = []
+        x_loads, dy_loads = {}, {}
         for k, (x, x_sib, dy, dy_sib) in enumerate(items):
-            now = []
             for at, part in ((0, dy), (tokens, dy_sib)):
                 if relative:
                     each = n_wide // count
                     for n, m in enumerate(relative_order()):
                         cols = natural(info[0], each)(m if at == 0 else m ^ 1)
-                        now.append(loads.start(
+                        dy_loads.setdefault(k, []).append(loads.start(
                             view(part).at[:, pl.ds(n * each, each)],
                             dy_all.at[k, pl.ds(at, tokens), pl.ds(cols, each)]))
                     continue
                 pieces = part if isinstance(part, list) else [part]
                 each = n_wide // len(pieces)
                 for n, piece in enumerate(pieces):
-                    now.append(loads.start(
+                    dy_loads.setdefault(k, []).append(loads.start(
                         view(piece), dy_all.at[k, pl.ds(at, tokens), pl.ds(n * each, each)]))
-            for at, part in ((0, x), (tokens, x_sib)):
-                ref, rows = view(part), pl.ds(at, tokens)
-                if layout == "joined":
-                    for g, ms in enumerate(groups):
+            for g, ms in enumerate(groups):
+                for at, part in ((0, x), (tokens, x_sib)):
+                    ref, rows = view(part), pl.ds(at, tokens)
+                    if layout == "joined":
                         cols = pl.ds(g * pair * w, len(ms) * w)
-                        now.append(loads.start(
+                        x_loads.setdefault((k, g), []).append(loads.start(
                             ref.at[:, cols], x_all.at[k, g, rows, pl.ds(0, len(ms) * w)]))
-                    continue
-                for g, ms in enumerate(groups):
+                        continue
                     for n, m in enumerate(ms):
-                        now.append(loads.start(
+                        x_loads.setdefault((k, g), []).append(loads.start(
                             columns_of(ref, m), x_all.at[k, g, rows, pl.ds(n * w, w)]))
-            copies.append(now)
+
+        def need(table, key):
+            wait(table.pop(key, ()))
+
         step = min(512, n_wide)
-        for k in range(len(items)):
-            wait(copies[k])
         for g, ms in enumerate(groups):
             for k in range(len(items)):
+                need(x_loads, (k, g))
                 for q in range(n_wide // step):
+                    need(dy_loads, k)
                     dst = slice(q * step, (q + 1) * step)
                     block = dot_tn(x_all[k, g, :, : len(ms) * w], dy_all[k, :, dst]).astype(bf16)
                     for n, m in enumerate(ms):
@@ -1052,14 +1059,20 @@
                             big[0][row : row + each_z, dst] = block[n * w + z * each_z : n * w + (z + 1) * each_z]
             if g == 0:
                 wait(copies_under)
-            for m in ms if not stacked else []:
-                put(evens.index(m))
+            for m in ms:
+                if not stacked:
+                    put(evens.index(m))
+                    continue
+                rows = len(items) * each_z
+                if rows % 16 == 0:
+                    for z in range(stretches):
+                        put(0, pl.ds((z * len(evens) + evens.index(m)) * rows, rows))
 
     return call(
         body, info, [], [], [*arrays, *under], [], [(shape, bf16) for shape in shapes],
         [pltpu.VMEM((len(items), len(groups), 2 * tokens, pair * w), bf16),
          pltpu.VMEM((len(items), 2 * tokens, n_wide), bf16)],
-        len(items) * (4 + 2 * len(evens) + 2 * count) + len(under) * len(evens), us, 40)
+        len(items) * (4 + 2 * len(evens) + 2 * count) + len(evens) * (len(under) + stretches), us, 40)
 
 
 def grad_send(parts):
@@ -1285,19 +1298,20 @@
     flat = tuple((j, None) for j in range(4))
     arrays = [v.near, v.far_sib, v.d_fval, hop(v.d_fval, 1)]
     v.stack_cv = weight_grad(info, arrays, [flat], "blocks", 6, stacked=True)[0]
-    dfrec_sib = hop(v.d_frec, 1)
+    v.dfrec_sib = hop(v.d_frec, 1)
+    v.drop("near", "far_sib")
+    v.sync()
+
+    z_cv = stretch_part(v.stack_cv)
+    v.dpre = hidden_back(info, v.act, v.d_fval, v.all_cv, fshard)
+    d_frec = tie(v.d_frec, v.dpre)
     if aligned:
         v.parts_c = weight_grad(
-            info, [v.f_in, v.f_sib, v.d_frec, dfrec_sib], [((0, 1), (1, 1), (2, None), (3, None))], layout, 3)
+            info, [v.f_in, v.f_sib, d_frec, v.dfrec_sib], [((0, 1), (1, 1), (2, None), (3, None))], layout, 3)
     else:
         v.parts_c = weight_grad(
-            info, [*pairs((v.f_in[1], v.f_sib[1])), v.d_frec, dfrec_sib], [flat], layout, 3)
-    v.drop("near", "far_sib")
-    v.sync()
-
-    z_cv = stretch_part(v.stack_cv)
+            info, [*pairs((v.f_in[1], v.f_sib[1])), d_frec, v.dfrec_sib], [flat], layout, 3)
     v.got_c = grad_send(v.parts_c)
-    v.dpre = hidden_back(info, v.act, v.d_fval, v.all_cv, fshard)
     dpre_sib = hop(v.dpre, 1)
     v.head_b, v.sums_c, v.dxt, v.dxb = chan_back(
         info, v.dpre, v.d_frec, v.xb, v.entry_b, v.vec, v.all_ck, length, shard, fshard)

time: 352 us -> 354 us (level); the launches traced: 350 us -> 348 us
  waiting for transfers between devices: 98.2 us -> 103 us
  Pallas kernels: 125 us -> 121 us
    ppermute x58, starting transfers between devices: 44.9 us -> 38 us  [hop(): return lax.ppermute(value, 'seg', [(i, i ^ bit) for i in range(count)])]
    ppermute x5, waiting for transfers between devices: 25.7 us -> 30.2 us  [across(): return lax.ppermute(value, 'stretch', [(i, i ^ j) for i in range(count)])]
    pallas_call x16, Pallas kernels: 120 us -> 116 us  [call(): pl.pallas_call(kernel, out_shape=[jax.ShapeDtypeStruct(s, d) for s, d in...]
  transfers between devices with their start and end apart: 72 -> 72, of which waited for: 26 -> 27; matrix products, arithmetic and copies ran while one was open for 4% -> 4% of each run, Pallas kernels for 34% -> 34%
where the time goes in v5:
time: 354 us; the launch traced here: 348 us
  Pallas kernels  121 us (34%)
  waiting for transfers between devices  103 us (29%)
  starting transfers between devices  60.2 us (17%)
  blocking collectives  23.2 us (7%)
  local copies, waits for them, and re-layouts  15 us (4%)
  between operations  15 us (4%)
  other arithmetic  10.3 us (3%)
    pallas_call x16, Pallas kernels, call(): pl.pallas_call(kernel, out_shape=[jax.ShapeDtypeStruct(s, d) for s, d in...  116 us
    ppermute x58, waiting for transfers between devices, hop(): return lax.ppermute(value, 'seg', [(i, i ^ bit) for i in range(count)])  67.9 us
    ppermute x58, starting transfers between devices, hop(): return lax.ppermute(value, 'seg', [(i, i ^ bit) for i in range(count)])  38 us
    ppermute x5, waiting for transfers between devices, across(): return lax.ppermute(value, 'stretch', [(i, i ^ j) for i in range(count)])  30.2 us
    ppermute x4, starting transfers between devices, along(): lax.ppermute(value, 'stretch', [(i, i + steps) for i in range(first, last)])  13.7 us
    all_gather x1, blocking collectives, body(): v.everyone = lax.all_gather(v.sums, 'stretch')  12.8 us
    all_gather x1, blocking collectives, body(): v.heads = lax.all_gather(v.head_a, 'stretch')[0]  10.4 us
    ppermute x5, starting transfers between devices, across(): return lax.ppermute(value, 'stretch', [(i, i ^ j) for i in range(count)])  8.1 us
  transfers between devices with their start and end apart: 72, of which 27 were waited for; matrix products, arithmetic and copies ran while one was open for 4% of the time, Pallas kernels for 34%

profile of v5, /device:TPU:9, one launch (start us, length us, event | category | flops | bytes accessed | tf_op | source)
XLA Modules:
  0.0 347.6 jit_solution(7387105914569351287)
XLA Ops:
  8.0 1.7 constant_dynamic-slice_fusion.3
  9.7 3.0 shard_map.448
  13.6 1.2 collective-permute-start.3
  14.8 1.2 collective-permute-start.5
  17.1 3.2 collective-permute-start.2
  20.3 2.4 shard_map.449
  22.8 22.5 %collective-permute-done.4.refs_7_.refs_13_.refs_16_.refs_21_ = bf16[256,1024]{1,0:T(8,128)(2,1)} collective-permute-done((bf16[256,1024]{1,0:T(8,128)(2,1)}, bf16[256,1024]{1,0:T(8,128)(2,1)}, u32[]{:S(2)}, u32[]{:S(2)}) %collective-permute-start.4) | collective-permute-done | bytes 524320 | tf_op jit(solution)/shard_map/ppermute | solution.py:21
  45.3 1.8 collective-permute-done.6.refs_9_.refs_15_.refs_18_.refs_23_
  47.1 3.4 all-gather.7.cloned.1.call-done
  50.5 1.2 constant_dynamic-slice_fusion.2
  55.7 10.9 %collective-permute-done.14.refs_11_.refs_17_.refs_20_.refs_25_ = bf16[256,1024]{1,0:T(8,128)(2,1)S(1)} collective-permute-done((bf16[256,1024]{1,0:T(8,128)(2,1)}, bf16[256,1024]{1,0:T(8,128)(2,1)S(1)}, u32[]{:S(2)}, u32[]{:S(2)}) %collective-permute-start.14) | collective-permute-done | bytes 524320 | tf_op jit(solution)/shard_map/ppermute | solution.py:21
  66.6 1.0 collective-permute-start.9
  67.6 1.5 collective-permute-done.13.refs_10_.refs_16_.refs_19_.refs_24_
  70.1 1.0 copy-done.9
  72.5 2.2 collective-permute-done.16.refs_19_.refs_25_.refs_28_.refs_33_
  78.3 8.3 %shard_map.450 = (f32[6,1024]{1,0:T(8,128)}, f32[16,1024]{1,0:T(8,128)}, f32[2,1024]{1,0:T(2,128)}, bf16[3,256,1024]{2,1,0:T(8,128)(2,1)}, f32[256,1024]{1,0:T(8...) custom-call(s32[3]{0:T(128)} %pad_add_fusion.refs_0_, bf16[2,1024]{1,0:T(2,128)(2,1)} %copy-done.32, ...), custom_call_target="tpu_custom_call" | custom-call | bytes 9000 | tf_op jit(solution)/shard_map/pallas_call | solution.py:190
  86.6 12.8 %all-gather.2.refs_1_ = f32[4,6,1024]{2,1,0:T(8,128)} all-gather(f32[1,6,1024]{2,1,0:T(8,128)} %bitcast.58), channel_id=2, replica_groups=mesh['seg'=8,'stretch'=4] {'stretch'}, dimensions={0}, use_global_device_ids=true | all-gather | bytes 122880 | tf_op jit(solution)/shard_map/all_gather | solution.py:1259
  99.4 5.7 %collective-permute-done.18.refs_8_.refs_9_ = bf16[80,4096]{1,0:T(8,128)(2,1)} collective-permute-done((bf16[80,4096]{1,0:T(8,128)(2,1)}, bf16[80,4096]{1,0:T(8,128)(2,1)}, u32[]{:S(2)}, u32[]{:S(2)}) %collective-permute-start.18) | collective-permute-done | bytes 655392 | tf_op jit(solution)/shard_map/ppermute | solution.py:21
  105.9 1.8 collective-permute-start.21
  109.5 7.8 %shard_map.451 = (f32[6,1024]{1,0:T(8,128)}, f32[2,1,1024]{2,1,0:T(1,128)}, f32[2,1,1024]{2,1,0:T(1,128)}, f32[2,1024]{1,0:T(2,128)}, bf16[256,1024]{1,0:T(8,128...) custom-call(s32[3]{0:T(128)} %pad_add_fusion.refs_0_, ...), custom_call_target="tpu_custom_call" | custom-call | bytes 7000 | tf_op jit(solution)/shard_map/pallas_call | solution.py:190
  117.3 3.7 %collective-permute-start.25 = (f32[2,1024]{1,0:T(2,128)}, f32[2,1024]{1,0:T(2,128)S(1)}, u32[]{:S(2)}, u32[]{:S(2)}) collective-permute-start(f32[2,1024]{1,0:T(2,128)} %get-tuple-element.719), channel_id=1, source_target_pairs={{0,1},{1,2},{2,3},{4,5},{5,6},{6,7},{8,9},{9,10},{10,11},{12,13},{... | collective-permute-start | bytes 24584 | tf_op jit(solution)/shard_map/ppermute | solution.py:27
  121.0 1.3 collective-permute-done.25.refs_1_
  122.3 2.1 collective-permute-done.23.refs_11_.refs_12_
  125.2 1.0 collective-permute-start.26
  126.8 1.6 collective-permute-done.26.refs_17_.refs_18_
  131.7 10.0 %shard_map.452 = (f32[2,1024]{1,0:T(2,128)}, bf16[2,256,1024]{2,1,0:T(8,128)(2,1)}, bf16[256,2048]{1,0:T(8,128)(2,1)}, bf16[256,2048]{1,0:T(8,128)(2,1)}, bf16[2...) custom-call(s32[3]{0:T(128)} %pad_add_fusion.refs_0_, f32[2,1024]{1,0:T(2,128)} %copy-done.30, f32[2,1,1024]{2,1,0:T(1,128)} %refs_2_.5, ...), custom_call_target="tpu_custom_call" | custom-call | bytes 11000 | tf_op jit(solution)/shard_map/pallas_call | solution.py:190
  142.7 8.8 %shard_map.453 = (bf16[256,1024]{1,0:T(8,128)(2,1)}, bf16[256,1024]{1,0:T(8,128)(2,1)}, bf16[256,1024]{1,0:T(8,128)(2,1)}) custom-call(s32[3]{0:T(128)} %pad_add_fusion.refs_0_, bf16[256,2048]{1,0:T(8,128)(2,1)} %get-tuple-element.933.refs_1_, bf16[256,2048]{1,0:T(8,128)(2,1)} %get-tuple-element.855.refs_2_, bf16[256,1024]{1,0:T(8,128)(2,1)} %get-tuple-element.856.refs_3_, ...), custom_call_target="tpu_custom_call" | custom-call | bytes 7000 | tf_op jit(solution)/shard_map/pallas_call | solution.py:190
  152.2 1.7 collective-permute-done.37.refs_4_
  154.0 6.3 %shard_map.454 = bf16[2048,1024]{1,0:T(8,128)(2,1)} custom-call(s32[3]{0:T(128)} %pad_add_fusion.refs_0_, bf16[256,2048]{1,0:T(8,128)(2,1)} %get-tuple-element.933.refs_1_, bf16[256,2048]{1,0:T(8,128)(2,1)} %collective-permute-done.33.refs_2_, bf16[256,1024]{1,0:T(8,128)(2,1)} %get-tuple-element.960.refs_3_.refs_1_, ...), custom_call_target="tpu_custom_call" | custom-call | bytes 6000 | tf_op jit(solution)/shard_map/pallas_call | solution.py:190
  160.6 7.6 %shard_map.455.refs_4_.refs_3_ = bf16[256,4096]{1,0:T(8,128)(2,1)} custom-call(s32[3]{0:T(128)} %pad_add_fusion.refs_0_, bf16[256,1024]{1,0:T(8,128)(2,1)} %get-tuple-element.960.refs_3_.refs_1_, bf16[256,4096]{1,0:T(8,128)(2,1)} %get-tuple-element.961.refs_2_, bf16[512,1024]{1,0:T(8,128)(2,1)} %refs_3_.2, ...), custom_call_target="tpu_custom_call" | custom-call | bytes 7000 | tf_op jit(solution)/shard_map/pallas_call | solution.py:190
  168.6 4.0 %shard_map.457 = (bf16[128,1024]{1,0:T(8,128)(2,1)}, bf16[128,1024]{1,0:T(8,128)(2,1)}, bf16[128,1024]{1,0:T(8,128)(2,1)}, bf16[128,1024]{1,0:T(8,128)(2,1)}) custom-call(s32[3]{0:T(128)} %pad_add_fusion.refs_0_, bf16[2,256,1024]{2,1,0:T(8,128)(2,1)} %get-tuple-element.987.refs_1_, bf16[2,256,1024]{2,1,0:T(8,128)(2,1)} %collective-permute-done.32.refs_2_, ...), custom_call_target="tpu_custom_call" | custom-call | bytes 3000 | tf_op jit(solution)/shard_map/pallas_call | solution.py:190
  174.1 1.2 collective-permute-start.40
  175.3 11.3 %shard_map.456 = (f32[2,1024]{1,0:T(2,128)}, f32[2,1024]{1,0:T(2,128)}, bf16[256,1024]{1,0:T(8,128)(2,1)}, bf16[256,1024]{1,0:T(8,128)(2,1)}) custom-call(s32[3]{0:T(128)} %pad_add_fusion.refs_0_, f32[2,1024]{1,0:T(2,128)} %get-tuple-element.958.refs_1_, f32[16,1024]{1,0:T(8,128)} %get-tuple-element.1126.refs_5_.refs_3_.refs_2_.refs_10_, ...), custom_call_target="tpu_custom_call" | custom-call | bytes 10000 | tf_op jit(solution)/shard_map/pallas_call | solution.py:190
  186.6 2.2 collective-permute-start.41
  188.9 7.2 %shard_map.458 = (bf16[128,4096]{1,0:T(8,128)(2,1)}, bf16[128,4096]{1,0:T(8,128)(2,1)}, bf16[128,4096]{1,0:T(8,128)(2,1)}, bf16[128,4096]{1,0:T(8,128)(2,1)}) custom-call(s32[3]{0:T(128)} %pad_add_fusion.refs_0_, bf16[2,256,1024]{2,1,0:T(8,128)(2,1)} %get-tuple-element.987.refs_1_, bf16[2,256,1024]{2,1,0:T(8,128)(2,1)} %collective-permute-done.32.refs_2_, ...), custom_call_target="tpu_custom_call" | custom-call | bytes 7000 | tf_op jit(solution)/shard_map/pallas_call | solution.py:190
  197.7 1.2 collective-permute-start.51
  198.9 7.6 %shard_map.459 = (f32[8,1024]{1,0:T(8,128)}, f32[2,1024]{1,0:T(2,128)}, bf16[256,1024]{1,0:T(8,128)(2,1)}, bf16[256,512]{1,0:T(8,128)(2,1)}, bf16[256,512]{1,0:T...) custom-call(s32[3]{0:T(128)} %pad_add_fusion.refs_0_, ...), custom_call_target="tpu_custom_call" | custom-call | bytes 9000 | tf_op jit(solution)/shard_map/pallas_call | solution.py:190
  206.6 4.2 %collective-permute-done.43.refs_2_ = f32[8,1024]{1,0:T(8,128)S(1)} collective-permute-done((f32[8,1024]{1,0:T(8,128)}, f32[8,1024]{1,0:T(8,128)S(1)}, u32[]{:S(2)}, u32[]{:S(2)}) %collective-permute-start.43) | collective-permute-done | bytes 32800 | tf_op jit(solution)/shard_map/ppermute | solution.py:32
  211.6 5.4 %collective-permute-start.44 = (f32[16,1024]{1,0:T(8,128)S(1)}, f32[16,1024]{1,0:T(8,128)S(1)}, u32[]{:S(2)}, u32[]{:S(2)}) collective-permute-start(f32[16,1024]{1,0:T(8,128)S(1)} %pad_maximum_fusion.1), channel_id=1, source_target_pairs={{0,2},{1,3},{2,0},{3,1},{4,6},{5,7},{6,4},{7,5},{8,10},{9,11},{10,... | collective-permute-start | bytes 196616 | tf_op jit(solution)/shard_map/ppermute | solution.py:32
  217.9 4.5 %collective-permute-done.44.refs_3_ = f32[16,1024]{1,0:T(8,128)S(1)} collective-permute-done((f32[16,1024]{1,0:T(8,128)S(1)}, f32[16,1024]{1,0:T(8,128)S(1)}, u32[]{:S(2)}, u32[]{:S(2)}) %collective-permute-start.44) | collective-permute-done | bytes 65568 | tf_op jit(solution)/shard_map/ppermute | solution.py:32
  223.0 1.3 collective-permute-done.46.refs_4_
  224.7 12.1 %shard_map.460 = (f32[2,1,1024]{2,1,0:T(1,128)}, f32[2,1,1024]{2,1,0:T(1,128)}, f32[2,1,1024]{2,1,0:T(1,128)}, f32[2,1,1024]{2,1,0:T(1,128)}, f32[2,1024]{1,0:T(...) custom-call(s32[3]{0:T(128)} %pad_add_fusion.refs_0_, ...), custom_call_target="tpu_custom_call" | custom-call | bytes 14000 | tf_op jit(solution)/shard_map/pallas_call | solution.py:190
  237.6 5.5 %shard_map.461 = bf16[1024,1024]{1,0:T(8,128)(2,1)} custom-call(s32[3]{0:T(128)} %pad_add_fusion.refs_0_, bf16[256,512]{1,0:T(8,128)(2,1)} %get-tuple-element.1066.refs_1_, bf16[256,512]{1,0:T(8,128)(2,1)} %get-tuple-element.1067.refs_2_, bf16[256,512]{1,0:T(8,128)(2,1)} %copy-done.14, bf16[256,512]{1,0:T(8,128)(2,1)} %copy-done.15, ...), custom_call_target="tpu_custom_call" | custom-call | bytes 6000 | tf_op jit(solution)/shard_map/pallas_call | solution.py:190
  243.2 2.5 collective-permute-start.52
  245.6 4.6 %collective-permute-start.53 = (f32[2,1024]{1,0:T(2,128)S(1)}, f32[2,1024]{1,0:T(2,128)S(1)}, u32[]{:S(2)}, u32[]{:S(2)}) collective-permute-start(f32[2,1024]{1,0:T(2,128)S(1)} %copy-done.29), channel_id=1, source_target_pairs={{1,0},{2,1},{3,2},{5,4},{6,5},{7,6},{9,8},{10,9},{11,10},{13,12},{... | collective-permute-start | bytes 24584 | tf_op jit(solution)/shard_map/ppermute | solution.py:27
  250.3 5.1 %shard_map.462 = bf16[640,1024]{1,0:T(8,128)(2,1)} custom-call(s32[3]{0:T(128)} %pad_add_fusion.refs_0_, bf16[128,4096]{1,0:T(8,128)(2,1)} %get-tuple-element.1110.refs_1_, bf16[128,4096]{1,0:T(8,128)(2,1)} %collective-permute-done.49.refs_2_, bf16[128,4096]{1,0:T(8,128)(2,1)} %collective-permute-done.50.refs_3_, ...), custom_call_target="tpu_custom_call" | custom-call | bytes 4000 | tf_op jit(solution)/shard_map/pallas_call | solution.py:190
  255.5 2.1 fusion.4
  257.6 2.6 collective-permute-start.56
  260.2 5.2 %shard_map.463 = (f32[2,1024]{1,0:T(2,128)}, bf16[256,1024]{1,0:T(8,128)(2,1)}) custom-call(s32[3]{0:T(128)} %pad_add_fusion.refs_0_, f32[2,1024]{1,0:T(2,128)} %copy-done.25, f32[16,1024]{1,0:T(8,128)} %get-tuple-element.1126.refs_5_.refs_3_.refs_2_.refs_10_, bf16[256,1024]{1,0:T(8,128)(2,1)} %get-tuple-element.1127.refs_3_, ...), custom_call_target="tpu_custom_call" | custom-call | bytes 6000 | tf_op jit(solution)/shard_map/pallas_call | solution.py:190
  267.0 5.6 %shard_map.464 = (bf16[272,1024]{1,0:T(8,128)(2,1)}, bf16[272,1024]{1,0:T(8,128)(2,1)}, bf16[272,1024]{1,0:T(8,128)(2,1)}, bf16[272,1024]{1,0:T(8,128)(2,1)}) custom-call(s32[3]{0:T(128)} %pad_add_fusion.refs_0_, bf16[3,256,1024]{2,1,0:T(8,128)(2,1)} %get-tuple-element.1138.refs_11_.refs_1_, bf16[3,256,1024]{2,1,0:T(8,128)(2,1)} %collective-permute-done.35.refs_12_.refs_2_, ...), custom_call_target="tpu_custom_call" | custom-call | bytes 7000 | tf_op jit(solution)/shard_map/pallas_call | solution.py:190
  273.7 2.3 collective-permute-start.59
  276.1 10.4 %all-gather.3 = f32[4,2,1024]{2,1,0:T(2,128)S(1)} all-gather(f32[1,2,1024]{2,1,0:T(2,128)S(1)} %bitcast.60), channel_id=3, replica_groups=mesh['seg'=8,'stretch'=4] {'stretch'}, dimensions={0}, use_global_device_ids=true | all-gather | bytes 40960 | tf_op jit(solution)/shard_map/all_gather | solution.py:1383
  286.5 2.1 convert_add_fusion
  288.6 10.0 %collective-permute-done.59.refs_4_ = bf16[272,1024]{1,0:T(8,128)(2,1)} collective-permute-done((bf16[272,1024]{1,0:T(8,128)(2,1)}, bf16[272,1024]{1,0:T(8,128)(2,1)}, u32[]{:S(2)}, u32[]{:S(2)}) %collective-permute-start.59) | collective-permute-done | bytes 557088 | tf_op jit(solution)/shard_map/ppermute | solution.py:21
  298.6 1.8 fusion.5
  300.7 1.2 collective-permute-start.61
  302.0 1.1 collective-permute-start.62
  303.1 3.2 shard_map.465
  308.1 1.9 collective-permute-start.65
  312.3 7.4 %collective-permute-done.63 = bf16[80,1024]{1,0:T(8,128)(2,1)S(1)} collective-permute-done((bf16[80,1024]{1,0:T(8,128)(2,1)}, bf16[80,1024]{1,0:T(8,128)(2,1)S(1)}, u32[]{:S(2)}, u32[]{:S(2)}) %collective-permute-start.63) | collective-permute-done | bytes 163872 | tf_op jit(solution)/shard_map/ppermute | solution.py:32
  319.7 2.8 collective-permute-done.64
  322.5 11.3 %collective-permute-done.65 = bf16[80,1024]{1,0:T(8,128)(2,1)S(1)} collective-permute-done((bf16[80,1024]{1,0:T(8,128)(2,1)}, bf16[80,1024]{1,0:T(8,128)(2,1)S(1)}, u32[]{:S(2)}, u32[]{:S(2)}) %collective-permute-start.65) | collective-permute-done | bytes 163872 | tf_op jit(solution)/shard_map/ppermute | solution.py:32
  334.5 1.4 collective-permute-start.66
  338.3 1.7 slice_convert_fusion
  (200 shorter events, 39.7 us)
Async XLA Ops:
  7.2 43.3 %all-gather.7.cloned.1.call-start = ((), (), s32[]{:S(2)}) async-start(), calls=%async_computation.3 | async-start | bytes 2359296 | tf_op jit(solution)/shard_map/all_gather | solution.py:1235
  12.7 118.4 %all-gather.9.cloned.1.call-start = ((), (), s32[]{:S(2)}) async-start(), calls=%async_computation.4 | async-start | bytes 3932160 | tf_op jit(solution)/shard_map/all_gather | solution.py:1244
  12.8 3.5 %collective-permute-start.1 = (bf16[256,1024]{1,0:T(8,128)(2,1)}, bf16[256,1024]{1,0:T(8,128)(2,1)S(1)}, u32[]{:S(2)}, u32[]{:S(2)}) collective-permute-start(bf16[256,1024]{1,0:T(8,128)(2,1)} %get-tuple-element.1043.refs_5_.refs_11_.refs_14_.refs_19_), channel_id=1, source_target_pairs={{0,4},{4,0},{8,12},{12,8},{16,20},{20,16},{24,28},{28,24},{1,5},{5... | collective-permute-start | bytes 1572872 | tf_op jit(solution)/shard_map/ppermute | solution.py:21
  13.5 3.0 collective-permute-start
  13.6 33.5 %collective-permute-start.3 = (bf16[272,1024]{1,0:T(8,128)(2,1)}, bf16[272,1024]{1,0:T(8,128)(2,1)}, u32[]{:S(2)}, u32[]{:S(2)}) collective-permute-start(bf16[272,1024]{1,0:T(8,128)(2,1)} %get-tuple-element.1042.refs_4_.refs_10_.refs_13_.refs_18_), channel_id=1, source_target_pairs={{0,8},{4,12},{8,0},{12,4},{16,24},{20,28},{24,16},{28,20},{1,9},{5... | collective-permute-start | bytes 1671176 | tf_op jit(solution)/shard_map/ppermute | solution.py:21
  14.8 32.3 %collective-permute-start.5 = (bf16[272,1024]{1,0:T(8,128)(2,1)}, bf16[272,1024]{1,0:T(8,128)(2,1)}, u32[]{:S(2)}, u32[]{:S(2)}) collective-permute-start(bf16[272,1024]{1,0:T(8,128)(2,1)} %get-tuple-element.1042.refs_4_.refs_10_.refs_13_.refs_18_), channel_id=1, source_target_pairs={{0,16},{4,20},{8,24},{12,28},{16,0},{20,4},{24,8},{28,12},{1,17},{... | collective-permute-start | bytes 1671176 | tf_op jit(solution)/shard_map/ppermute | solution.py:21
  16.1 29.2 %collective-permute-start.4 = (bf16[256,1024]{1,0:T(8,128)(2,1)}, bf16[256,1024]{1,0:T(8,128)(2,1)}, u32[]{:S(2)}, u32[]{:S(2)}) collective-permute-start(bf16[256,1024]{1,0:T(8,128)(2,1)} %get-tuple-element.1043.refs_5_.refs_11_.refs_14_.refs_19_), channel_id=1, source_target_pairs={{0,8},{4,12},{8,0},{12,4},{16,24},{20,28},{24,16},{28,20},{1,9},{5... | collective-permute-start | bytes 1572872 | tf_op jit(solution)/shard_map/ppermute | solution.py:21
  16.3 30.8 %collective-permute-start.6 = (bf16[256,1024]{1,0:T(8,128)(2,1)}, bf16[256,1024]{1,0:T(8,128)(2,1)}, u32[]{:S(2)}, u32[]{:S(2)}) collective-permute-start(bf16[256,1024]{1,0:T(8,128)(2,1)} %get-tuple-element.1043.refs_5_.refs_11_.refs_14_.refs_19_), channel_id=1, source_target_pairs={{0,16},{4,20},{8,24},{12,28},{16,0},{20,4},{24,8},{28,12},{1,17},{... | collective-permute-start | bytes 1572872 | tf_op jit(solution)/shard_map/ppermute | solution.py:21
  17.1 30.0 %collective-permute-start.2 = (bf16[2,1024]{1,0:T(2,128)(2,1)S(1)}, bf16[2,1024]{1,0:T(2,128)(2,1)S(1)}, u32[]{:S(2)}, u32[]{:S(2)}) collective-permute-start(bf16[2,1024]{1,0:T(2,128)(2,1)S(1)} %bitcast.61), channel_id=1, source_target_pairs={{0,1},{1,2},{2,3},{4,5},{5,6},{6,7},{8,9},{9,10},{10,11},{12,13},{... | collective-permute-start | bytes 12296 | tf_op jit(solution)/shard_map/ppermute | solution.py:27
  52.6 202.9 %reduce-scatter.4.cloned.1.call-start = ((), (), s32[]{:S(2)}) async-start(), calls=%async_computation.5 | async-start | bytes 5242880 | tf_op jit(solution)/shard_map/reduce_scatter | solution.py:1152
  53.0 13.6 %collective-permute-start.14 = (bf16[256,1024]{1,0:T(8,128)(2,1)}, bf16[256,1024]{1,0:T(8,128)(2,1)S(1)}, u32[]{:S(2)}, u32[]{:S(2)}) collective-permute-start(bf16[256,1024]{1,0:T(8,128)(2,1)} %collective-permute-done.6.refs_9_.refs_15_.refs_18_.refs_23_), channel_id=1, source_target_pairs={{0,8},{4,12},{8,0},{12,4},{16,24},{20,28},{24,16},{28,20},{1,9},{5... | collective-permute-start | bytes 1572872 | tf_op jit(solution)/shard_map/ppermute | solution.py:21
  53.7 13.8 %collective-permute-start.10 = (bf16[256,1024]{1,0:T(8,128)(2,1)}, bf16[256,1024]{1,0:T(8,128)(2,1)}, u32[]{:S(2)}, u32[]{:S(2)}) collective-permute-start(bf16[256,1024]{1,0:T(8,128)(2,1)} %collective-permute-done.4.refs_7_.refs_13_.refs_16_.refs_21_), channel_id=1, source_target_pairs={{0,4},{4,0},{8,12},{12,8},{16,20},{20,16},{24,28},{28,24},{1,5},{5... | collective-permute-start | bytes 1572872 | tf_op jit(solution)/shard_map/ppermute | solution.py:21
  54.2 15.9 %collective-permute-start.7 = (bf16[80,4096]{1,0:T(8,128)(2,1)}, bf16[80,4096]{1,0:T(8,128)(2,1)S(1)}, u32[]{:S(2)}, u32[]{:S(2)}) collective-permute-start(bf16[80,4096]{1,0:T(8,128)(2,1)} %get-tuple-element.967.refs_5_.refs_6_), channel_id=1, source_target_pairs={{0,4},{4,0},{8,12},{12,8},{16,20},{20,16},{24,28},{28,24},{1,5},{5... | collective-permute-start | bytes 1966088 | tf_op jit(solution)/shard_map/ppermute | solution.py:21
  54.2 16.9 %collective-permute-start.8 = (bf16[80,4096]{1,0:T(8,128)(2,1)}, bf16[80,4096]{1,0:T(8,128)(2,1)S(1)}, u32[]{:S(2)}, u32[]{:S(2)}) collective-permute-start(bf16[80,4096]{1,0:T(8,128)(2,1)} %get-tuple-element.968.refs_6_.refs_7_), channel_id=1, source_target_pairs={{0,4},{4,0},{8,12},{12,8},{16,20},{20,16},{24,28},{28,24},{1,5},{5... | collective-permute-start | bytes 1966088 | tf_op jit(solution)/shard_map/ppermute | solution.py:21
  54.9 14.3 %collective-permute-start.13 = (bf16[272,1024]{1,0:T(8,128)(2,1)}, bf16[272,1024]{1,0:T(8,128)(2,1)S(1)}, u32[]{:S(2)}, u32[]{:S(2)}) collective-permute-start(bf16[272,1024]{1,0:T(8,128)(2,1)} %collective-permute-done.3.refs_6_.refs_12_.refs_15_.refs_20_), channel_id=1, source_target_pairs={{0,16},{4,20},{8,24},{12,28},{16,0},{20,4},{24,8},{28,12},{1,17},{... | collective-permute-start | bytes 1671176 | tf_op jit(solution)/shard_map/ppermute | solution.py:21
  74.7 24.7 %collective-permute-start.17 = (bf16[80,4096]{1,0:T(8,128)(2,1)}, bf16[80,4096]{1,0:T(8,128)(2,1)}, u32[]{:S(2)}, u32[]{:S(2)}) collective-permute-start(bf16[80,4096]{1,0:T(8,128)(2,1)} %get-tuple-element.967.refs_5_.refs_6_), channel_id=1, source_target_pairs={{0,8},{4,12},{8,0},{12,4},{16,24},{20,28},{24,16},{28,20},{1,9},{5... | collective-permute-start | bytes 1966088 | tf_op jit(solution)/shard_map/ppermute | solution.py:21
  75.5 29.6 %collective-permute-start.18 = (bf16[80,4096]{1,0:T(8,128)(2,1)}, bf16[80,4096]{1,0:T(8,128)(2,1)}, u32[]{:S(2)}, u32[]{:S(2)}) collective-permute-start(bf16[80,4096]{1,0:T(8,128)(2,1)} %get-tuple-element.968.refs_6_.refs_7_), channel_id=1, source_target_pairs={{0,8},{4,12},{8,0},{12,4},{16,24},{20,28},{24,16},{28,20},{1,9},{5... | collective-permute-start | bytes 1966088 | tf_op jit(solution)/shard_map/ppermute | solution.py:21
  76.2 28.8 %collective-permute-start.19 = (bf16[80,4096]{1,0:T(8,128)(2,1)}, bf16[80,4096]{1,0:T(8,128)(2,1)}, u32[]{:S(2)}, u32[]{:S(2)}) collective-permute-start(bf16[80,4096]{1,0:T(8,128)(2,1)} %get-tuple-element.967.refs_5_.refs_6_), channel_id=1, source_target_pairs={{0,16},{4,20},{8,24},{12,28},{16,0},{20,4},{24,8},{28,12},{1,17},{... | collective-permute-start | bytes 1966088 | tf_op jit(solution)/shard_map/ppermute | solution.py:21
  77.0 28.9 %collective-permute-start.20 = (bf16[80,4096]{1,0:T(8,128)(2,1)}, bf16[80,4096]{1,0:T(8,128)(2,1)}, u32[]{:S(2)}, u32[]{:S(2)}) collective-permute-start(bf16[80,4096]{1,0:T(8,128)(2,1)} %get-tuple-element.968.refs_6_.refs_7_), channel_id=1, source_target_pairs={{0,16},{4,20},{8,24},{12,28},{16,0},{20,4},{24,8},{28,12},{1,17},{... | collective-permute-start | bytes 1966088 | tf_op jit(solution)/shard_map/ppermute | solution.py:21
  105.9 16.4 %collective-permute-start.21 = (bf16[80,4096]{1,0:T(8,128)(2,1)}, bf16[80,4096]{1,0:T(8,128)(2,1)S(1)}, u32[]{:S(2)}, u32[]{:S(2)}) collective-permute-start(bf16[80,4096]{1,0:T(8,128)(2,1)} %collective-permute-done.17.refs_7_.refs_8_), channel_id=1, source_target_pairs={{0,4},{4,0},{8,12},{12,8},{16,20},{20,16},{24,28},{28,24},{1,5},{5... | collective-permute-start | bytes 1966088 | tf_op jit(solution)/shard_map/ppermute | solution.py:21
  107.8 16.7 %collective-permute-start.23 = (bf16[80,4096]{1,0:T(8,128)(2,1)}, bf16[80,4096]{1,0:T(8,128)(2,1)}, u32[]{:S(2)}, u32[]{:S(2)}) collective-permute-start(bf16[80,4096]{1,0:T(8,128)(2,1)} %collective-permute-done.17.refs_7_.refs_8_), channel_id=1, source_target_pairs={{0,16},{4,20},{8,24},{12,28},{16,0},{20,4},{24,8},{28,12},{1,17},{... | collective-permute-start | bytes 1966088 | tf_op jit(solution)/shard_map/ppermute | solution.py:21
  108.5 13.8 %collective-permute-start.22 = (bf16[80,4096]{1,0:T(8,128)(2,1)}, bf16[80,4096]{1,0:T(8,128)(2,1)}, u32[]{:S(2)}, u32[]{:S(2)}) collective-permute-start(bf16[80,4096]{1,0:T(8,128)(2,1)} %collective-permute-done.18.refs_8_.refs_9_), channel_id=1, source_target_pairs={{0,4},{4,0},{8,12},{12,8},{16,20},{20,16},{24,28},{28,24},{1,5},{5... | collective-permute-start | bytes 1966088 | tf_op jit(solution)/shard_map/ppermute | solution.py:21
  108.8 16.4 %collective-permute-start.24 = (bf16[80,4096]{1,0:T(8,128)(2,1)}, bf16[80,4096]{1,0:T(8,128)(2,1)}, u32[]{:S(2)}, u32[]{:S(2)}) collective-permute-start(bf16[80,4096]{1,0:T(8,128)(2,1)} %collective-permute-done.20.refs_10_.refs_11_), channel_id=1, source_target_pairs={{0,8},{4,12},{8,0},{12,4},{16,24},{20,28},{24,16},{28,20},{1,9},{5... | collective-permute-start | bytes 1966088 | tf_op jit(solution)/shard_map/ppermute | solution.py:21
  117.3 5.0 %collective-permute-start.25 = (f32[2,1024]{1,0:T(2,128)}, f32[2,1024]{1,0:T(2,128)S(1)}, u32[]{:S(2)}, u32[]{:S(2)}) collective-permute-start(f32[2,1024]{1,0:T(2,128)} %get-tuple-element.719), channel_id=1, source_target_pairs={{0,1},{1,2},{2,3},{4,5},{5,6},{6,7},{8,9},{9,10},{10,11},{12,13},{... | collective-permute-start | bytes 24584 | tf_op jit(solution)/shard_map/ppermute | solution.py:27
  125.2 3.1 collective-permute-start.26
  126.3 3.9 %collective-permute-start.28 = (bf16[80,4096]{1,0:T(8,128)(2,1)}, bf16[80,4096]{1,0:T(8,128)(2,1)}, u32[]{:S(2)}, u32[]{:S(2)}) collective-permute-start(bf16[80,4096]{1,0:T(8,128)(2,1)} %collective-permute-done.23.refs_11_.refs_12_), channel_id=1, source_target_pairs={{0,4},{4,0},{8,12},{12,8},{16,20},{20,16},{24,28},{28,24},{1,5},{5... | collective-permute-start | bytes 1966088 | tf_op jit(solution)/shard_map/ppermute | solution.py:21
  126.8 4.4 %collective-permute-start.29 = (bf16[80,4096]{1,0:T(8,128)(2,1)}, bf16[80,4096]{1,0:T(8,128)(2,1)}, u32[]{:S(2)}, u32[]{:S(2)}) collective-permute-start(bf16[80,4096]{1,0:T(8,128)(2,1)} %collective-permute-done.24.refs_12_.refs_13_), channel_id=1, source_target_pairs={{0,4},{4,0},{8,12},{12,8},{16,20},{20,16},{24,28},{28,24},{1,5},{5... | collective-permute-start | bytes 1966088 | tf_op jit(solution)/shard_map/ppermute | solution.py:21
  131.1 10.5 %collective-permute-start.31 = (bf16[1536,1024]{1,0:T(8,128)(2,1)}, bf16[1536,1024]{1,0:T(8,128)(2,1)}, u32[]{:S(2)}, u32[]{:S(2)}) collective-permute-start(bf16[1536,1024]{1,0:T(8,128)(2,1)} %all-gather.9.cloned.1.call-done.refs_7_.refs_4_), channel_id=1, source_target_pairs={{0,4},{4,0},{8,12},{12,8},{16,20},{20,16},{24,28},{28,24},{1,5},{5... | collective-permute-start | bytes 9437192 | tf_op jit(solution)/shard_map/ppermute | solution.py:21
  131.5 10.1 %collective-permute-start.30 = (bf16[512,1024]{1,0:T(8,128)(2,1)}, bf16[512,1024]{1,0:T(8,128)(2,1)}, u32[]{:S(2)}, u32[]{:S(2)}) collective-permute-start(bf16[512,1024]{1,0:T(8,128)(2,1)} %refs_3_.2), channel_id=1, source_target_pairs={{0,4},{4,0},{8,12},{12,8},{16,20},{20,16},{24,28},{28,24},{1,5},{5... | collective-permute-start | bytes 3145736 | tf_op jit(solution)/shard_map/ppermute | solution.py:21
  141.7 10.0 %collective-permute-start.35 = (bf16[3,256,1024]{2,1,0:T(8,128)(2,1)}, bf16[3,256,1024]{2,1,0:T(8,128)(2,1)}, u32[]{:S(2)}, u32[]{:S(2)}) collective-permute-start(bf16[3,256,1024]{2,1,0:T(8,128)(2,1)} %get-tuple-element.1138.refs_11_.refs_1_), channel_id=1, source_target_pairs={{0,4},{4,0},{8,12},{12,8},{16,20},{20,16},{24,28},{28,24},{1,5},{5... | collective-permute-start | bytes 4718600 | tf_op jit(solution)/shard_map/ppermute | solution.py:21
  142.1 9.5 %collective-permute-start.32 = (bf16[2,256,1024]{2,1,0:T(8,128)(2,1)}, bf16[2,256,1024]{2,1,0:T(8,128)(2,1)}, u32[]{:S(2)}, u32[]{:S(2)}) collective-permute-start(bf16[2,256,1024]{2,1,0:T(8,128)(2,1)} %get-tuple-element.987.refs_1_), channel_id=1, source_target_pairs={{0,4},{4,0},{8,12},{12,8},{16,20},{20,16},{24,28},{28,24},{1,5},{5... | collective-permute-start | bytes 3145736 | tf_op jit(solution)/shard_map/ppermute | solution.py:21
  142.2 9.4 %collective-permute-start.33 = (bf16[256,2048]{1,0:T(8,128)(2,1)}, bf16[256,2048]{1,0:T(8,128)(2,1)}, u32[]{:S(2)}, u32[]{:S(2)}) collective-permute-start(bf16[256,2048]{1,0:T(8,128)(2,1)} %get-tuple-element.855.refs_2_), channel_id=1, source_target_pairs={{0,4},{4,0},{8,12},{12,8},{16,20},{20,16},{24,28},{28,24},{1,5},{5... | collective-permute-start | bytes 3145736 | tf_op jit(solution)/shard_map/ppermute | solution.py:21
  142.6 9.0 %collective-permute-start.34 = (bf16[256,1024]{1,0:T(8,128)(2,1)}, bf16[256,1024]{1,0:T(8,128)(2,1)S(1)}, u32[]{:S(2)}, u32[]{:S(2)}) collective-permute-start(bf16[256,1024]{1,0:T(8,128)(2,1)} %get-tuple-element.1091.refs_9_), channel_id=1, source_target_pairs={{0,4},{4,0},{8,12},{12,8},{16,20},{20,16},{24,28},{28,24},{1,5},{5... | collective-permute-start | bytes 1572872 | tf_op jit(solution)/shard_map/ppermute | solution.py:21
  152.1 8.2 %collective-permute-start.36 = (bf16[256,1024]{1,0:T(8,128)(2,1)}, bf16[256,1024]{1,0:T(8,128)(2,1)}, u32[]{:S(2)}, u32[]{:S(2)}) collective-permute-start(bf16[256,1024]{1,0:T(8,128)(2,1)} %get-tuple-element.991.refs_3_), channel_id=1, source_target_pairs={{0,4},{4,0},{8,12},{12,8},{16,20},{20,16},{24,28},{28,24},{1,5},{5... | collective-permute-start | bytes 1572872 | tf_op jit(solution)/shard_map/ppermute | solution.py:21
  160.4 128.2 %reduce-scatter.6.cloned.1.call-start = ((), (), s32[]{:S(2)}) async-start(), calls=%async_computation.6 | async-start | bytes 2621440 | tf_op jit(solution)/shard_map/reduce_scatter | solution.py:1152
  168.2 20.7 %collective-permute-start.42 = (bf16[256,4096]{1,0:T(8,128)(2,1)}, bf16[256,4096]{1,0:T(8,128)(2,1)}, u32[]{:S(2)}, u32[]{:S(2)}) collective-permute-start(bf16[256,4096]{1,0:T(8,128)(2,1)} %shard_map.455.refs_4_.refs_3_), channel_id=1, source_target_pairs={{0,4},{4,0},{8,12},{12,8},{16,20},{20,16},{24,28},{28,24},{1,5},{5... | collective-permute-start | bytes 6291464 | tf_op jit(solution)/shard_map/ppermute | solution.py:21
  172.6 23.5 %collective-permute-start.38 = (bf16[128,1024]{1,0:T(8,128)(2,1)}, bf16[128,1024]{1,0:T(8,128)(2,1)S(1)}, u32[]{:S(2)}, u32[]{:S(2)}) collective-permute-start(bf16[128,1024]{1,0:T(8,128)(2,1)} %get-tuple-element.992), channel_id=1, source_target_pairs={{0,8},{4,12},{8,0},{12,4},{16,24},{20,28},{24,16},{28,20},{1,9},{5... | collective-permute-start | bytes 786440 | tf_op jit(solution)/shard_map/ppermute | solution.py:21
  173.4 22.8 %collective-permute-start.39 = (bf16[128,1024]{1,0:T(8,128)(2,1)}, bf16[128,1024]{1,0:T(8,128)(2,1)S(1)}, u32[]{:S(2)}, u32[]{:S(2)}) collective-permute-start(bf16[128,1024]{1,0:T(8,128)(2,1)} %get-tuple-element.993), channel_id=1, source_target_pairs={{0,16},{4,20},{8,24},{12,28},{16,0},{20,4},{24,8},{28,12},{1,17},{... | collective-permute-start | bytes 786440 | tf_op jit(solution)/shard_map/ppermute | solution.py:21
  174.1 22.1 %collective-permute-start.40 = (bf16[128,1024]{1,0:T(8,128)(2,1)}, bf16[128,1024]{1,0:T(8,128)(2,1)S(1)}, u32[]{:S(2)}, u32[]{:S(2)}) collective-permute-start(bf16[128,1024]{1,0:T(8,128)(2,1)} %get-tuple-element.994), channel_id=1, source_target_pairs={{0,24},{4,28},{8,16},{12,20},{16,8},{20,12},{24,0},{28,4},{1,25},{... | collective-permute-start | bytes 786440 | tf_op jit(solution)/shard_map/ppermute | solution.py:21
  186.6 9.5 %collective-permute-start.41 = (f32[2,1024]{1,0:T(2,128)}, f32[2,1024]{1,0:T(2,128)S(1)}, u32[]{:S(2)}, u32[]{:S(2)}) collective-permute-start(f32[2,1024]{1,0:T(2,128)} %get-tuple-element.1032.refs_2_), channel_id=1, source_target_pairs={{1,0},{2,1},{3,2},{5,4},{6,5},{7,6},{9,8},{10,9},{11,10},{13,12},{... | collective-permute-start | bytes 24584 | tf_op jit(solution)/shard_map/ppermute | solution.py:27
  196.2 46.9 %collective-permute-start.49 = (bf16[128,4096]{1,0:T(8,128)(2,1)}, bf16[128,4096]{1,0:T(8,128)(2,1)}, u32[]{:S(2)}, u32[]{:S(2)}) collective-permute-start(bf16[128,4096]{1,0:T(8,128)(2,1)} %get-tuple-element.1077), channel_id=1, source_target_pairs={{0,8},{4,12},{8,0},{12,4},{16,24},{20,28},{24,16},{28,20},{1,9},{5... | collective-permute-start | bytes 3145736 | tf_op jit(solution)/shard_map/ppermute | solution.py:21
  197.1 46.0 %collective-permute-start.50 = (bf16[128,4096]{1,0:T(8,128)(2,1)}, bf16[128,4096]{1,0:T(8,128)(2,1)}, u32[]{:S(2)}, u32[]{:S(2)}) collective-permute-start(bf16[128,4096]{1,0:T(8,128)(2,1)} %get-tuple-element.1078), channel_id=1, source_target_pairs={{0,16},{4,20},{8,24},{12,28},{16,0},{20,4},{24,8},{28,12},{1,17},{... | collective-permute-start | bytes 3145736 | tf_op jit(solution)/shard_map/ppermute | solution.py:21
  197.7 45.3 %collective-permute-start.51 = (bf16[128,4096]{1,0:T(8,128)(2,1)}, bf16[128,4096]{1,0:T(8,128)(2,1)}, u32[]{:S(2)}, u32[]{:S(2)}) collective-permute-start(bf16[128,4096]{1,0:T(8,128)(2,1)} %get-tuple-element.1079), channel_id=1, source_target_pairs={{0,24},{4,28},{8,16},{12,20},{16,8},{20,12},{24,0},{28,4},{1,25},{... | collective-permute-start | bytes 3145736 | tf_op jit(solution)/shard_map/ppermute | solution.py:21
  206.5 4.3 %collective-permute-start.43 = (f32[8,1024]{1,0:T(8,128)}, f32[8,1024]{1,0:T(8,128)S(1)}, u32[]{:S(2)}, u32[]{:S(2)}) collective-permute-start(f32[8,1024]{1,0:T(8,128)} %get-tuple-element.1058.refs_1_), channel_id=1, source_target_pairs={{0,1},{1,0},{2,3},{3,2},{4,5},{5,4},{6,7},{7,6},{8,9},{9,8},{10,11... | collective-permute-start | bytes 98312 | tf_op jit(solution)/shard_map/ppermute | solution.py:32
  211.6 10.8 %collective-permute-start.44 = (f32[16,1024]{1,0:T(8,128)S(1)}, f32[16,1024]{1,0:T(8,128)S(1)}, u32[]{:S(2)}, u32[]{:S(2)}) collective-permute-start(f32[16,1024]{1,0:T(8,128)S(1)} %pad_maximum_fusion.1), channel_id=1, source_target_pairs={{0,2},{1,3},{2,0},{3,1},{4,6},{5,7},{6,4},{7,5},{8,10},{9,11},{10,... | collective-permute-start | bytes 196616 | tf_op jit(solution)/shard_map/ppermute | solution.py:32
  217.0 5.9 %collective-permute-start.45 = (bf16[256,512]{1,0:T(8,128)(2,1)}, bf16[256,512]{1,0:T(8,128)(2,1)S(1)}, u32[]{:S(2)}, u32[]{:S(2)}) collective-permute-start(bf16[256,512]{1,0:T(8,128)(2,1)} %get-tuple-element.1066.refs_1_), channel_id=1, source_target_pairs={{0,4},{4,0},{8,12},{12,8},{16,20},{20,16},{24,28},{28,24},{1,5},{5... | collective-permute-start | bytes 786440 | tf_op jit(solution)/shard_map/ppermute | solution.py:21
  222.9 13.9 %collective-permute-start.47 = (bf16[256,512]{1,0:T(8,128)(2,1)}, bf16[256,512]{1,0:T(8,128)(2,1)S(1)}, u32[]{:S(2)}, u32[]{:S(2)}) collective-permute-start(bf16[256,512]{1,0:T(8,128)(2,1)} %get-tuple-element.1063.refs_16_.refs_5_), channel_id=1, source_target_pairs={{0,4},{4,0},{8,12},{12,8},{16,20},{20,16},{24,28},{28,24},{1,5},{5... | collective-permute-start | bytes 786440 | tf_op jit(solution)/shard_map/ppermute | solution.py:21
  224.3 12.6 %collective-permute-start.48 = (bf16[256,512]{1,0:T(8,128)(2,1)}, bf16[256,512]{1,0:T(8,128)(2,1)}, u32[]{:S(2)}, u32[]{:S(2)}) collective-permute-start(bf16[256,512]{1,0:T(8,128)(2,1)} %get-tuple-element.1064.refs_17_.refs_6_), channel_id=1, source_target_pairs={{0,4},{4,0},{8,12},{12,8},{16,20},{20,16},{24,28},{28,24},{1,5},{5... | collective-permute-start | bytes 786440 | tf_op jit(solution)/shard_map/ppermute | solution.py:21
  243.1 95.2 %reduce-scatter.8.cloned.1.call-start = ((), (), s32[]{:S(2)}) async-start(), calls=%async_computation.7 | async-start | bytes 1638400 | tf_op jit(solution)/shard_map/reduce_scatter | solution.py:1152
  243.2 12.3 %collective-permute-start.52 = (bf16[2,256,1024]{2,1,0:T(8,128)(2,1)}, bf16[2,256,1024]{2,1,0:T(8,128)(2,1)}, u32[]{:S(2)}, u32[]{:S(2)}) collective-permute-start(bf16[2,256,1024]{2,1,0:T(8,128)(2,1)} %get-tuple-element.1140.refs_3_), channel_id=1, source_target_pairs={{0,4},{4,0},{8,12},{12,8},{16,20},{20,16},{24,28},{28,24},{1,5},{5... | collective-permute-start | bytes 3145736 | tf_op jit(solution)/shard_map/ppermute | solution.py:21
  245.6 9.8 %collective-permute-start.53 = (f32[2,1024]{1,0:T(2,128)S(1)}, f32[2,1024]{1,0:T(2,128)S(1)}, u32[]{:S(2)}, u32[]{:S(2)}) collective-permute-start(f32[2,1024]{1,0:T(2,128)S(1)} %copy-done.29), channel_id=1, source_target_pairs={{1,0},{2,1},{3,2},{5,4},{6,5},{7,6},{9,8},{10,9},{11,10},{13,12},{... | collective-permute-start | bytes 24584 | tf_op jit(solution)/shard_map/ppermute | solution.py:27
  257.6 15.0 %collective-permute-start.54 = (bf16[128,1024]{1,0:T(8,128)(2,1)}, bf16[128,1024]{1,0:T(8,128)(2,1)S(1)}, u32[]{:S(2)}, u32[]{:S(2)}) collective-permute-start(bf16[128,1024]{1,0:T(8,128)(2,1)} %get-tuple-element.1267), channel_id=1, source_target_pairs={{0,8},{4,12},{8,0},{12,4},{16,24},{20,28},{24,16},{28,20},{1,9},{5... | collective-permute-start | bytes 786440 | tf_op jit(solution)/shard_map/ppermute | solution.py:21
  257.6 15.1 %collective-permute-start.55 = (bf16[128,1024]{1,0:T(8,128)(2,1)}, bf16[128,1024]{1,0:T(8,128)(2,1)S(1)}, u32[]{:S(2)}, u32[]{:S(2)}) collective-permute-start(bf16[128,1024]{1,0:T(8,128)(2,1)} %get-tuple-element.1266), channel_id=1, source_target_pairs={{0,16},{4,20},{8,24},{12,28},{16,0},{20,4},{24,8},{28,12},{1,17},{... | collective-permute-start | bytes 786440 | tf_op jit(solution)/shard_map/ppermute | solution.py:21
  257.6 15.1 %collective-permute-start.56 = (bf16[128,1024]{1,0:T(8,128)(2,1)}, bf16[128,1024]{1,0:T(8,128)(2,1)}, u32[]{:S(2)}, u32[]{:S(2)}) collective-permute-start(bf16[128,1024]{1,0:T(8,128)(2,1)} %get-tuple-element.1265), channel_id=1, source_target_pairs={{0,24},{4,28},{8,16},{12,20},{16,8},{20,12},{24,0},{28,4},{1,25},{... | collective-permute-start | bytes 786440 | tf_op jit(solution)/shard_map/ppermute | solution.py:21
  273.4 15.2 %collective-permute-start.57 = (bf16[272,1024]{1,0:T(8,128)(2,1)}, bf16[272,1024]{1,0:T(8,128)(2,1)S(1)}, u32[]{:S(2)}, u32[]{:S(2)}) collective-permute-start(bf16[272,1024]{1,0:T(8,128)(2,1)} %get-tuple-element.1152), channel_id=1, source_target_pairs={{0,8},{4,12},{8,0},{12,4},{16,24},{20,28},{24,16},{28,20},{1,9},{5... | collective-permute-start | bytes 1671176 | tf_op jit(solution)/shard_map/ppermute | solution.py:21
  273.5 15.1 %collective-permute-start.58 = (bf16[272,1024]{1,0:T(8,128)(2,1)}, bf16[272,1024]{1,0:T(8,128)(2,1)}, u32[]{:S(2)}, u32[]{:S(2)}) collective-permute-start(bf16[272,1024]{1,0:T(8,128)(2,1)} %get-tuple-element.1153), channel_id=1, source_target_pairs={{0,16},{4,20},{8,24},{12,28},{16,0},{20,4},{24,8},{28,12},{1,17},{... | collective-permute-start | bytes 1671176 | tf_op jit(solution)/shard_map/ppermute | solution.py:21
  273.7 24.9 %collective-permute-start.59 = (bf16[272,1024]{1,0:T(8,128)(2,1)}, bf16[272,1024]{1,0:T(8,128)(2,1)}, u32[]{:S(2)}, u32[]{:S(2)}) collective-permute-start(bf16[272,1024]{1,0:T(8,128)(2,1)} %get-tuple-element.1154), channel_id=1, source_target_pairs={{0,24},{4,28},{8,16},{12,20},{16,8},{20,12},{24,0},{28,4},{1,25},{... | collective-permute-start | bytes 1671176 | tf_op jit(solution)/shard_map/ppermute | solution.py:21
  300.5 5.9 %collective-permute-start.60 = (bf16[64,1024]{1,0:T(8,128)(2,1)}, bf16[64,1024]{1,0:T(8,128)(2,1)S(1)}, u32[]{:S(2)}, u32[]{:S(2)}) collective-permute-start(bf16[64,1024]{1,0:T(8,128)(2,1)} %get-tuple-element.1270), channel_id=1, source_target_pairs={{0,8},{4,12},{8,0},{12,4},{16,24},{20,28},{24,16},{28,20},{1,9},{5... | collective-permute-start | bytes 393224 | tf_op jit(solution)/shard_map/ppermute | solution.py:21
  300.7 5.7 %collective-permute-start.61 = (bf16[64,1024]{1,0:T(8,128)(2,1)}, bf16[64,1024]{1,0:T(8,128)(2,1)S(1)}, u32[]{:S(2)}, u32[]{:S(2)}) collective-permute-start(bf16[64,1024]{1,0:T(8,128)(2,1)} %get-tuple-element.1269), channel_id=1, source_target_pairs={{0,16},{4,20},{8,24},{12,28},{16,0},{20,4},{24,8},{28,12},{1,17},{... | collective-permute-start | bytes 393224 | tf_op jit(solution)/shard_map/ppermute | solution.py:21
  302.0 5.4 %collective-permute-start.62 = (bf16[64,1024]{1,0:T(8,128)(2,1)}, bf16[64,1024]{1,0:T(8,128)(2,1)}, u32[]{:S(2)}, u32[]{:S(2)}) collective-permute-start(bf16[64,1024]{1,0:T(8,128)(2,1)} %get-tuple-element.1268), channel_id=1, source_target_pairs={{0,24},{4,28},{8,16},{12,20},{16,8},{20,12},{24,0},{28,4},{1,25},{... | collective-permute-start | bytes 393224 | tf_op jit(solution)/shard_map/ppermute | solution.py:21
  307.3 12.4 %collective-permute-start.63 = (bf16[80,1024]{1,0:T(8,128)(2,1)}, bf16[80,1024]{1,0:T(8,128)(2,1)S(1)}, u32[]{:S(2)}, u32[]{:S(2)}) collective-permute-start(bf16[80,1024]{1,0:T(8,128)(2,1)} %get-tuple-element.1191), channel_id=1, source_target_pairs={{0,1},{1,0},{2,3},{3,2},{4,5},{5,4},{6,7},{7,6},{8,9},{9,8},{10,11... | collective-permute-start | bytes 491528 | tf_op jit(solution)/shard_map/ppermute | solution.py:32
  307.3 15.1 %collective-permute-start.64 = (bf16[80,1024]{1,0:T(8,128)(2,1)}, bf16[80,1024]{1,0:T(8,128)(2,1)S(1)}, u32[]{:S(2)}, u32[]{:S(2)}) collective-permute-start(bf16[80,1024]{1,0:T(8,128)(2,1)} %get-tuple-element.1192), channel_id=1, source_target_pairs={{0,2},{1,3},{2,0},{3,1},{4,6},{5,7},{6,4},{7,5},{8,10},{9,11},{10,... | collective-permute-start | bytes 491528 | tf_op jit(solution)/shard_map/ppermute | solution.py:32
  308.1 25.7 %collective-permute-start.65 = (bf16[80,1024]{1,0:T(8,128)(2,1)}, bf16[80,1024]{1,0:T(8,128)(2,1)S(1)}, u32[]{:S(2)}, u32[]{:S(2)}) collective-permute-start(bf16[80,1024]{1,0:T(8,128)(2,1)} %get-tuple-element.1193), channel_id=1, source_target_pairs={{0,3},{1,2},{2,1},{3,0},{4,7},{5,6},{6,5},{7,4},{8,11},{9,10},{10,... | collective-permute-start | bytes 491528 | tf_op jit(solution)/shard_map/ppermute | solution.py:32
  334.5 3.1 collective-permute-start.66
  (41 other events, 291.9 us)
Sparse Core Ops, SparseCore 0:
  12.9 37.5 all-gather.6
  52.7 62.7 all-gather.8
  160.5 79.5 reduce-scatter.3
  243.2 44.2 reduce-scatter.5
  289.7 36.5 reduce-scatter.7

commit v6 on v5

--- a/solution.py
+++ b/solution.py
@@ -355,12 +355,17 @@
 def recept_blocks(loads, steps, raw, w, info, shard, width, wide):
     each = shard * width // wide
     place = natural(info[0], shard)
-    return [
-        loads.start(raw[piece].at[pl.ds(row, count), pl.ds(q * width, width)],
-                    w.at[pl.ds(place(m) + q * each + within, count)])
-        for piece, row, count, m, within in steps
-        for q in range(wide // width)
-    ]
+    sem = loads.sems.at[loads.used]
+    loads.used += 1
+
+    @pl.loop(0, wide // width)
+    def _(q):
+        for piece, row, rows, m, within in steps:
+            pltpu.make_async_copy(
+                raw[piece].at[pl.ds(row, rows), pl.ds(pl.multiple_of(q * width, width), width)],
+                w.at[pl.ds(pl.multiple_of(place(m) + q * each, each) + within, rows)], sem).start()
+
+    return lambda: pltpu.make_async_copy(w, w, sem).wait()
 
 
 def time_in(info, stream, last, previous, given, pieces, spots, length, shard):
@@ -538,18 +543,29 @@
         [pltpu.VMEM((width, width), bf16)], len(steps), 7, 40)
 
 
-def key_blocks(loads, steps, raw, w, info, shard, fshard, wanted):
-    order = relative_order()
+def key_blocks(loads, steps, raw, w, info, shard, fshard, start=0):
+    count = lax.axis_size("seg")
+    half = count // 2
     place = natural(info[0], shard)
-    out = {}
-    for m in wanted:
+    first = loads.used
+    loads.used += count
+
+    @pl.loop(0, count)
+    def _(turn):
+        at = lax.rem(turn + start, count)
+        m = lax.rem(at, half) * 2 + lax.div(at, half)
         cols = pl.ds(natural(info[0], fshard)(m), fshard)
-        out[m] = [
-            loads.start(raw[piece].at[pl.ds(row, count), cols],
-                        w.at[pl.ds(place(m2) + within, count), pl.ds(order.index(m) * fshard, fshard)])
-            for piece, row, count, m2, within in steps
-        ]
-    return out
+        dst = pl.ds(pl.multiple_of(at * fshard, fshard), fshard)
+        for piece, row, rows, m2, within in steps:
+            pltpu.make_async_copy(
+                raw[piece].at[pl.ds(row, rows), cols], w.at[pl.ds(place(m2) + within, rows), dst],
+                loads.sems.at[first + at]).start()
+
+    def arrive(at):
+        block = w.at[:, pl.ds(at * fshard, fshard)]
+        pltpu.make_async_copy(block, block, loads.sems.at[first + at]).wait()
+
+    return arrive
 
 
 def value_blocks(loads, raw, w, fshard, stretches):
@@ -592,8 +608,8 @@
         wk, wc = scratch
         half = len(order) // 2
         turn = order[half:] + order[:half]
-        blocks = key_blocks(loads, steps_k, raw, wk, info, shard, fshard, turn)
-        copies_c = recept_blocks(loads, steps_c, raw, wc, info, shard, width, wide)
+        arrive = key_blocks(loads, steps_k, raw, wk, info, shard, fshard, half)
+        arrive_c = recept_blocks(loads, steps_c, raw, wc, info, shard, width, wide)
         for b in range(batches):
             entry_ref[b : b + 1, :] = jnp.where(info[1] == 1, prev_ref[b], edge_ref[b : b + 1, :])
         xb_ref = get(0)
@@ -609,8 +625,8 @@
             lax.fori_loop(0, length // ROWS, step, entry_ref[b : b + 1])
         put(0)
         for m in turn:
-            wait(blocks[m])
             at = order.index(m)
+            arrive(at)
             hid_ref, lo = (near_ref, at * fshard) if at < half else (far_ref, (at - half) * fshard)
             act = jnp.maximum(dot_nn(in_ref[0], wk[:, at * fshard : (at + 1) * fshard]), 0.0)
             act_ref[:, at * fshard : (at + 1) * fshard] = act.astype(bf16)
@@ -619,7 +635,7 @@
                 put(2)
         put(1)
         put(3)
-        wait(copies_c)
+        arrive_c()
         @columns(width, STEP)
         def _(n):
             frec_ref[:, n] = dot_nn(in_ref[1], wc[:, n]).astype(bf16)
@@ -630,7 +646,7 @@
         [((2, tokens, width), bf16), ((tokens, wide // 2), bf16), ((tokens, wide // 2), bf16),
          ((tokens, wide), bf16), ((tokens, width), bf16)],
         [pltpu.VMEM((width, wide), bf16), pltpu.VMEM((width, width), bf16)],
-        len(steps_c) * (wide // width) + len(steps_k) * len(order), 11, 40)
+        1 + len(order), 11, 40)
 
 
 def chan_out(info, near, far, frec, mid, cot, cv, fshard):
@@ -705,18 +721,18 @@
         head_ref, total_ref = outs
         dxt_ref, dxb_ref = big
         wk, wc, df, dr, sum_ref = scratch
-        copies_c = recept_blocks(loads, steps_c, raw, wc, info, shard, width, wide)
-        keys = key_blocks(loads, steps_k, raw, wk, info, shard, fshard, order)
+        arrive_c = recept_blocks(loads, steps_c, raw, wc, info, shard, width, wide)
+        arrive = key_blocks(loads, steps_k, raw, wk, info, shard, fshard)
         dfrec_ref = get(0)
-        wait(copies_c)
+        arrive_c()
         @columns(width, STEP)
         def _(n):
             dr[:, n] = dot_nt(dfrec_ref[...], wc[n, :])
         dpre_ref = get(1)
         half = len(order) // 2
         for k in range(2):
-            for m in order[k * half : (k + 1) * half]:
-                wait(keys[m])
+            for at in range(k * half, (k + 1) * half):
+                arrive(at)
             part_of = slice(k * wide // 2, (k + 1) * wide // 2)
             @columns(width, STEP)
             def _(n):
@@ -747,7 +763,7 @@
         [pltpu.VMEM((width, wide), bf16), pltpu.VMEM((width, width), bf16),
          pltpu.VMEM((tokens, width), f32), pltpu.VMEM((tokens, width), f32),
          pltpu.VMEM((2, 8, width), f32)],
-        len(steps_c) * (wide // width) + len(steps_k) * len(order), 10, 40)
+        1 + len(order), 10, 40)
 
 
 def mid_back(info, dxt, dxb, after, head, mid, cot, vec, kvr, wkv, rden, ent, pieces, spots, length, shard):

time: 354 us -> 346 us (0.977); the launches traced: 348 us -> 344 us
    ppermute x58, starting transfers between devices: 38 us -> 45.6 us  [hop(): return lax.ppermute(value, 'seg', [(i, i ^ bit) for i in range(count)])]
    ppermute x5, waiting for transfers between devices: 30.2 us -> 26.6 us  [across(): return lax.ppermute(value, 'stretch', [(i, i ^ j) for i in range(count)])]
  transfers between devices with their start and end apart: 72 -> 72, of which waited for: 27 -> 27; matrix products, arithmetic and copies ran while one was open for 4% -> 4% of each run, Pallas kernels for 34% -> 33%
where the time goes in v6:
time: 346 us; the launch traced here: 344 us
  Pallas kernels  118 us (34%)
  waiting for transfers between devices  99.8 us (29%)
  starting transfers between devices  62.3 us (18%)
  blocking collectives  24.4 us (7%)
  local copies, waits for them, and re-layouts  15.1 us (4%)
  between operations  14.7 us (4%)
  other arithmetic  10.3 us (3%)
    pallas_call x16, Pallas kernels, call(): pl.pallas_call(kernel, out_shape=[jax.ShapeDtypeStruct(s, d) for s, d in...  112 us
    ppermute x58, waiting for transfers between devices, hop(): return lax.ppermute(value, 'seg', [(i, i ^ bit) for i in range(count)])  68 us
    ppermute x58, starting transfers between devices, hop(): return lax.ppermute(value, 'seg', [(i, i ^ bit) for i in range(count)])  45.6 us
    ppermute x5, waiting for transfers between devices, across(): return lax.ppermute(value, 'stretch', [(i, i ^ j) for i in range(count)])  26.6 us
    all_gather x1, blocking collectives, body(): v.everyone = lax.all_gather(v.sums, 'stretch')  12.8 us
    all_gather x1, blocking collectives, body(): v.heads = lax.all_gather(v.head_a, 'stretch')[0]  11.7 us
    ppermute x4, starting transfers between devices, along(): lax.ppermute(value, 'stretch', [(i, i + steps) for i in range(first, last)])  11.2 us
  transfers between devices with their start and end apart: 72, of which 27 were waited for; matrix products, arithmetic and copies ran while one was open for 4% of the time, Pallas kernels for 33%

profile of v6, /device:TPU:9, one launch (start us, length us, event | category | flops | bytes accessed | tf_op | source)
XLA Modules:
  0.0 344.3 jit_solution(63891965406916819)
XLA Ops:
  8.0 1.7 constant_dynamic-slice_fusion.3
  9.7 3.0 shard_map.448
  13.6 1.2 collective-permute-start.3
  14.8 1.2 collective-permute-start.5
  17.1 3.2 collective-permute-start.2
  20.3 2.4 shard_map.449
  22.8 22.5 %collective-permute-done.4.refs_7_.refs_13_.refs_16_.refs_21_ = bf16[256,1024]{1,0:T(8,128)(2,1)} collective-permute-done((bf16[256,1024]{1,0:T(8,128)(2,1)}, bf16[256,1024]{1,0:T(8,128)(2,1)}, u32[]{:S(2)}, u32[]{:S(2)}) %collective-permute-start.4) | collective-permute-done | bytes 524320 | tf_op jit(solution)/shard_map/ppermute | solution.py:21
  45.3 1.8 collective-permute-done.6.refs_9_.refs_15_.refs_18_.refs_23_
  47.1 3.4 all-gather.7.cloned.1.call-done
  55.7 10.9 %collective-permute-done.14.refs_11_.refs_17_.refs_20_.refs_25_ = bf16[256,1024]{1,0:T(8,128)(2,1)S(1)} collective-permute-done((bf16[256,1024]{1,0:T(8,128)(2,1)}, bf16[256,1024]{1,0:T(8,128)(2,1)S(1)}, u32[]{:S(2)}, u32[]{:S(2)}) %collective-permute-start.14) | collective-permute-done | bytes 524320 | tf_op jit(solution)/shard_map/ppermute | solution.py:21
  67.6 1.5 collective-permute-done.13.refs_10_.refs_16_.refs_19_.refs_24_
  72.5 2.2 collective-permute-done.16.refs_19_.refs_25_.refs_28_.refs_33_
  78.3 8.3 %shard_map.450 = (f32[6,1024]{1,0:T(8,128)}, f32[16,1024]{1,0:T(8,128)}, f32[2,1024]{1,0:T(2,128)}, bf16[3,256,1024]{2,1,0:T(8,128)(2,1)}, f32[256,1024]{1,0:T(8...) custom-call(s32[3]{0:T(128)} %pad_add_fusion.refs_0_, bf16[2,1024]{1,0:T(2,128)(2,1)} %copy-done.32, ...), custom_call_target="tpu_custom_call" | custom-call | bytes 9000 | tf_op jit(solution)/shard_map/pallas_call | solution.py:190
  86.6 12.8 %all-gather.2.refs_1_ = f32[4,6,1024]{2,1,0:T(8,128)} all-gather(f32[1,6,1024]{2,1,0:T(8,128)} %bitcast.58), channel_id=2, replica_groups=mesh['seg'=8,'stretch'=4] {'stretch'}, dimensions={0}, use_global_device_ids=true | all-gather | bytes 122880 | tf_op jit(solution)/shard_map/all_gather | solution.py:1275
  99.4 5.7 %collective-permute-done.18.refs_8_.refs_9_ = bf16[80,4096]{1,0:T(8,128)(2,1)} collective-permute-done((bf16[80,4096]{1,0:T(8,128)(2,1)}, bf16[80,4096]{1,0:T(8,128)(2,1)}, u32[]{:S(2)}, u32[]{:S(2)}) %collective-permute-start.18) | collective-permute-done | bytes 655392 | tf_op jit(solution)/shard_map/ppermute | solution.py:21
  105.9 1.8 collective-permute-start.21
  109.5 7.8 %shard_map.451 = (f32[6,1024]{1,0:T(8,128)}, f32[2,1,1024]{2,1,0:T(1,128)}, f32[2,1,1024]{2,1,0:T(1,128)}, f32[2,1024]{1,0:T(2,128)}, bf16[256,1024]{1,0:T(8,128...) custom-call(s32[3]{0:T(128)} %pad_add_fusion.refs_0_, ...), custom_call_target="tpu_custom_call" | custom-call | bytes 7000 | tf_op jit(solution)/shard_map/pallas_call | solution.py:190
  117.3 3.4 collective-permute-start.25
  120.7 1.6 collective-permute-done.25.refs_1_
  122.3 2.1 collective-permute-done.23.refs_11_.refs_12_
  126.8 1.6 collective-permute-done.26.refs_17_.refs_18_
  131.7 8.4 %shard_map.452 = (f32[2,1024]{1,0:T(2,128)}, bf16[2,256,1024]{2,1,0:T(8,128)(2,1)}, bf16[256,2048]{1,0:T(8,128)(2,1)}, bf16[256,2048]{1,0:T(8,128)(2,1)}, bf16[2...) custom-call(s32[3]{0:T(128)} %pad_add_fusion.refs_0_, f32[2,1024]{1,0:T(2,128)} %copy-done.30, f32[2,1,1024]{2,1,0:T(1,128)} %refs_2_.5, ...), custom_call_target="tpu_custom_call" | custom-call | bytes 11000 | tf_op jit(solution)/shard_map/pallas_call | solution.py:190
  141.2 8.8 %shard_map.453 = (bf16[256,1024]{1,0:T(8,128)(2,1)}, bf16[256,1024]{1,0:T(8,128)(2,1)}, bf16[256,1024]{1,0:T(8,128)(2,1)}) custom-call(s32[3]{0:T(128)} %pad_add_fusion.refs_0_, bf16[256,2048]{1,0:T(8,128)(2,1)} %get-tuple-element.933.refs_1_, bf16[256,2048]{1,0:T(8,128)(2,1)} %get-tuple-element.855.refs_2_, bf16[256,1024]{1,0:T(8,128)(2,1)} %get-tuple-element.856.refs_3_, ...), custom_call_target="tpu_custom_call" | custom-call | bytes 7000 | tf_op jit(solution)/shard_map/pallas_call | solution.py:190
  150.7 1.7 collective-permute-done.37.refs_4_
  152.4 6.4 %shard_map.454 = bf16[2048,1024]{1,0:T(8,128)(2,1)} custom-call(s32[3]{0:T(128)} %pad_add_fusion.refs_0_, bf16[256,2048]{1,0:T(8,128)(2,1)} %get-tuple-element.933.refs_1_, bf16[256,2048]{1,0:T(8,128)(2,1)} %collective-permute-done.33.refs_2_, bf16[256,1024]{1,0:T(8,128)(2,1)} %get-tuple-element.960.refs_3_.refs_1_, ...), custom_call_target="tpu_custom_call" | custom-call | bytes 6000 | tf_op jit(solution)/shard_map/pallas_call | solution.py:190
  159.1 7.6 %shard_map.455.refs_4_.refs_3_ = bf16[256,4096]{1,0:T(8,128)(2,1)} custom-call(s32[3]{0:T(128)} %pad_add_fusion.refs_0_, bf16[256,1024]{1,0:T(8,128)(2,1)} %get-tuple-element.960.refs_3_.refs_1_, bf16[256,4096]{1,0:T(8,128)(2,1)} %get-tuple-element.961.refs_2_, bf16[512,1024]{1,0:T(8,128)(2,1)} %refs_3_.2, ...), custom_call_target="tpu_custom_call" | custom-call | bytes 7000 | tf_op jit(solution)/shard_map/pallas_call | solution.py:190
  167.1 4.0 %shard_map.457 = (bf16[128,1024]{1,0:T(8,128)(2,1)}, bf16[128,1024]{1,0:T(8,128)(2,1)}, bf16[128,1024]{1,0:T(8,128)(2,1)}, bf16[128,1024]{1,0:T(8,128)(2,1)}) custom-call(s32[3]{0:T(128)} %pad_add_fusion.refs_0_, bf16[2,256,1024]{2,1,0:T(8,128)(2,1)} %get-tuple-element.987.refs_1_, bf16[2,256,1024]{2,1,0:T(8,128)(2,1)} %collective-permute-done.32.refs_2_, ...), custom_call_target="tpu_custom_call" | custom-call | bytes 3000 | tf_op jit(solution)/shard_map/pallas_call | solution.py:190
  172.6 1.2 collective-permute-start.40
  173.8 9.9 %shard_map.456 = (f32[2,1024]{1,0:T(2,128)}, f32[2,1024]{1,0:T(2,128)}, bf16[256,1024]{1,0:T(8,128)(2,1)}, bf16[256,1024]{1,0:T(8,128)(2,1)}) custom-call(s32[3]{0:T(128)} %pad_add_fusion.refs_0_, f32[2,1024]{1,0:T(2,128)} %get-tuple-element.958.refs_1_, f32[16,1024]{1,0:T(8,128)} %get-tuple-element.1126.refs_5_.refs_3_.refs_2_.refs_10_, ...), custom_call_target="tpu_custom_call" | custom-call | bytes 10000 | tf_op jit(solution)/shard_map/pallas_call | solution.py:190
  183.7 2.3 collective-permute-start.41
  186.0 7.2 %shard_map.458 = (bf16[128,4096]{1,0:T(8,128)(2,1)}, bf16[128,4096]{1,0:T(8,128)(2,1)}, bf16[128,4096]{1,0:T(8,128)(2,1)}, bf16[128,4096]{1,0:T(8,128)(2,1)}) custom-call(s32[3]{0:T(128)} %pad_add_fusion.refs_0_, bf16[2,256,1024]{2,1,0:T(8,128)(2,1)} %get-tuple-element.987.refs_1_, bf16[2,256,1024]{2,1,0:T(8,128)(2,1)} %collective-permute-done.32.refs_2_, ...), custom_call_target="tpu_custom_call" | custom-call | bytes 7000 | tf_op jit(solution)/shard_map/pallas_call | solution.py:190
  196.0 7.6 %shard_map.459 = (f32[8,1024]{1,0:T(8,128)}, f32[2,1024]{1,0:T(2,128)}, bf16[256,1024]{1,0:T(8,128)(2,1)}, bf16[256,512]{1,0:T(8,128)(2,1)}, bf16[256,512]{1,0:T...) custom-call(s32[3]{0:T(128)} %pad_add_fusion.refs_0_, ...), custom_call_target="tpu_custom_call" | custom-call | bytes 9000 | tf_op jit(solution)/shard_map/pallas_call | solution.py:190
  203.7 4.2 %collective-permute-done.43.refs_2_ = f32[8,1024]{1,0:T(8,128)S(1)} collective-permute-done((f32[8,1024]{1,0:T(8,128)}, f32[8,1024]{1,0:T(8,128)S(1)}, u32[]{:S(2)}, u32[]{:S(2)}) %collective-permute-start.43) | collective-permute-done | bytes 32800 | tf_op jit(solution)/shard_map/ppermute | solution.py:32
  208.7 2.3 collective-permute-start.44
  211.1 5.3 %collective-permute-start.45 = (bf16[256,512]{1,0:T(8,128)(2,1)}, bf16[256,512]{1,0:T(8,128)(2,1)S(1)}, u32[]{:S(2)}, u32[]{:S(2)}) collective-permute-start(bf16[256,512]{1,0:T(8,128)(2,1)} %get-tuple-element.1066.refs_1_), channel_id=1, source_target_pairs={{0,4},{4,0},{8,12},{12,8},{16,20},{20,16},{24,28},{28,24},{1,5},{5... | collective-permute-start | bytes 786440 | tf_op jit(solution)/shard_map/ppermute | solution.py:21
  216.3 4.2 %collective-permute-start.46 = (bf16[256,512]{1,0:T(8,128)(2,1)}, bf16[256,512]{1,0:T(8,128)(2,1)S(1)}, u32[]{:S(2)}, u32[]{:S(2)}) collective-permute-start(bf16[256,512]{1,0:T(8,128)(2,1)} %get-tuple-element.1067.refs_2_), channel_id=1, source_target_pairs={{0,4},{4,0},{8,12},{12,8},{16,20},{20,16},{24,28},{28,24},{1,5},{5... | collective-permute-start | bytes 786440 | tf_op jit(solution)/shard_map/ppermute | solution.py:21
  220.6 1.3 collective-permute-done.46.refs_4_
  222.3 12.2 %shard_map.460 = (f32[2,1,1024]{2,1,0:T(1,128)}, f32[2,1,1024]{2,1,0:T(1,128)}, f32[2,1,1024]{2,1,0:T(1,128)}, f32[2,1,1024]{2,1,0:T(1,128)}, f32[2,1024]{1,0:T(...) custom-call(s32[3]{0:T(128)} %pad_add_fusion.refs_0_, ...), custom_call_target="tpu_custom_call" | custom-call | bytes 14000 | tf_op jit(solution)/shard_map/pallas_call | solution.py:190
  235.2 5.5 %shard_map.461 = bf16[1024,1024]{1,0:T(8,128)(2,1)} custom-call(s32[3]{0:T(128)} %pad_add_fusion.refs_0_, bf16[256,512]{1,0:T(8,128)(2,1)} %get-tuple-element.1066.refs_1_, bf16[256,512]{1,0:T(8,128)(2,1)} %get-tuple-element.1067.refs_2_, bf16[256,512]{1,0:T(8,128)(2,1)} %copy-done.14, bf16[256,512]{1,0:T(8,128)(2,1)} %copy-done.15, ...), custom_call_target="tpu_custom_call" | custom-call | bytes 6000 | tf_op jit(solution)/shard_map/pallas_call | solution.py:190
  240.8 1.9 collective-permute-start.52
  242.8 2.4 collective-permute-start.53
  245.3 4.7 %shard_map.462 = bf16[640,1024]{1,0:T(8,128)(2,1)} custom-call(s32[3]{0:T(128)} %pad_add_fusion.refs_0_, bf16[128,4096]{1,0:T(8,128)(2,1)} %get-tuple-element.1110.refs_1_, bf16[128,4096]{1,0:T(8,128)(2,1)} %collective-permute-done.49.refs_2_, bf16[128,4096]{1,0:T(8,128)(2,1)} %collective-permute-done.50.refs_3_, ...), custom_call_target="tpu_custom_call" | custom-call | bytes 4000 | tf_op jit(solution)/shard_map/pallas_call | solution.py:190
  250.0 2.1 fusion.4
  252.1 1.3 collective-permute-start.54
  253.6 1.2 collective-permute-start.56
  254.8 5.2 %shard_map.463 = (f32[2,1024]{1,0:T(2,128)}, bf16[256,1024]{1,0:T(8,128)(2,1)}) custom-call(s32[3]{0:T(128)} %pad_add_fusion.refs_0_, f32[2,1024]{1,0:T(2,128)} %copy-done.25, f32[16,1024]{1,0:T(8,128)} %get-tuple-element.1126.refs_5_.refs_3_.refs_2_.refs_10_, bf16[256,1024]{1,0:T(8,128)(2,1)} %get-tuple-element.1127.refs_3_, ...), custom_call_target="tpu_custom_call" | custom-call | bytes 6000 | tf_op jit(solution)/shard_map/pallas_call | solution.py:190
  261.6 5.6 %shard_map.464 = (bf16[272,1024]{1,0:T(8,128)(2,1)}, bf16[272,1024]{1,0:T(8,128)(2,1)}, bf16[272,1024]{1,0:T(8,128)(2,1)}, bf16[272,1024]{1,0:T(8,128)(2,1)}) custom-call(s32[3]{0:T(128)} %pad_add_fusion.refs_0_, bf16[3,256,1024]{2,1,0:T(8,128)(2,1)} %get-tuple-element.1138.refs_11_.refs_1_, bf16[3,256,1024]{2,1,0:T(8,128)(2,1)} %collective-permute-done.35.refs_12_.refs_2_, ...), custom_call_target="tpu_custom_call" | custom-call | bytes 7000 | tf_op jit(solution)/shard_map/pallas_call | solution.py:190
  268.0 1.3 collective-permute-start.57
  269.4 1.2 collective-permute-start.59
  270.7 11.7 %all-gather.3 = f32[4,2,1024]{2,1,0:T(2,128)S(1)} all-gather(f32[1,2,1024]{2,1,0:T(2,128)S(1)} %bitcast.60), channel_id=3, replica_groups=mesh['seg'=8,'stretch'=4] {'stretch'}, dimensions={0}, use_global_device_ids=true | all-gather | bytes 40960 | tf_op jit(solution)/shard_map/all_gather | solution.py:1399
  282.3 2.1 convert_add_fusion
  284.5 9.6 %collective-permute-done.59.refs_4_ = bf16[272,1024]{1,0:T(8,128)(2,1)} collective-permute-done((bf16[272,1024]{1,0:T(8,128)(2,1)}, bf16[272,1024]{1,0:T(8,128)(2,1)}, u32[]{:S(2)}, u32[]{:S(2)}) %collective-permute-start.59) | collective-permute-done | bytes 557088 | tf_op jit(solution)/shard_map/ppermute | solution.py:21
  294.1 1.9 fusion.5
  296.2 1.2 collective-permute-start.61
  297.4 1.3 collective-permute-start.62
  298.7 3.2 shard_map.465
  302.0 1.5 collective-permute-done.62
  303.5 1.4 collective-permute-start.64
  304.9 1.2 collective-permute-start.65
  308.4 7.7 %collective-permute-done.63 = bf16[80,1024]{1,0:T(8,128)(2,1)S(1)} collective-permute-done((bf16[80,1024]{1,0:T(8,128)(2,1)}, bf16[80,1024]{1,0:T(8,128)(2,1)S(1)}, u32[]{:S(2)}, u32[]{:S(2)}) %collective-permute-start.63) | collective-permute-done | bytes 163872 | tf_op jit(solution)/shard_map/ppermute | solution.py:32
  316.2 3.0 collective-permute-done.64
  319.2 11.6 %collective-permute-done.65 = bf16[80,1024]{1,0:T(8,128)(2,1)S(1)} collective-permute-done((bf16[80,1024]{1,0:T(8,128)(2,1)}, bf16[80,1024]{1,0:T(8,128)(2,1)S(1)}, u32[]{:S(2)}, u32[]{:S(2)}) %collective-permute-start.65) | collective-permute-done | bytes 163872 | tf_op jit(solution)/shard_map/ppermute | solution.py:32
  331.5 1.4 collective-permute-start.66
  335.3 1.7 slice_convert_fusion
  (200 shorter events, 42.2 us)
Async XLA Ops:
  7.2 43.3 %all-gather.7.cloned.1.call-start = ((), (), s32[]{:S(2)}) async-start(), calls=%async_computation.3 | async-start | bytes 2359296 | tf_op jit(solution)/shard_map/all_gather | solution.py:1251
  12.7 118.4 %all-gather.9.cloned.1.call-start = ((), (), s32[]{:S(2)}) async-start(), calls=%async_computation.4 | async-start | bytes 3932160 | tf_op jit(solution)/shard_map/all_gather | solution.py:1260
  12.8 3.5 %collective-permute-start.1 = (bf16[256,1024]{1,0:T(8,128)(2,1)}, bf16[256,1024]{1,0:T(8,128)(2,1)S(1)}, u32[]{:S(2)}, u32[]{:S(2)}) collective-permute-start(bf16[256,1024]{1,0:T(8,128)(2,1)} %get-tuple-element.1043.refs_5_.refs_11_.refs_14_.refs_19_), channel_id=1, source_target_pairs={{0,4},{4,0},{8,12},{12,8},{16,20},{20,16},{24,28},{28,24},{1,5},{5... | collective-permute-start | bytes 1572872 | tf_op jit(solution)/shard_map/ppermute | solution.py:21
  13.6 33.5 %collective-permute-start.3 = (bf16[272,1024]{1,0:T(8,128)(2,1)}, bf16[272,1024]{1,0:T(8,128)(2,1)}, u32[]{:S(2)}, u32[]{:S(2)}) collective-permute-start(bf16[272,1024]{1,0:T(8,128)(2,1)} %get-tuple-element.1042.refs_4_.refs_10_.refs_13_.refs_18_), channel_id=1, source_target_pairs={{0,8},{4,12},{8,0},{12,4},{16,24},{20,28},{24,16},{28,20},{1,9},{5... | collective-permute-start | bytes 1671176 | tf_op jit(solution)/shard_map/ppermute | solution.py:21
  14.8 32.3 %collective-permute-start.5 = (bf16[272,1024]{1,0:T(8,128)(2,1)}, bf16[272,1024]{1,0:T(8,128)(2,1)}, u32[]{:S(2)}, u32[]{:S(2)}) collective-permute-start(bf16[272,1024]{1,0:T(8,128)(2,1)} %get-tuple-element.1042.refs_4_.refs_10_.refs_13_.refs_18_), channel_id=1, source_target_pairs={{0,16},{4,20},{8,24},{12,28},{16,0},{20,4},{24,8},{28,12},{1,17},{... | collective-permute-start | bytes 1671176 | tf_op jit(solution)/shard_map/ppermute | solution.py:21
  16.1 29.2 %collective-permute-start.4 = (bf16[256,1024]{1,0:T(8,128)(2,1)}, bf16[256,1024]{1,0:T(8,128)(2,1)}, u32[]{:S(2)}, u32[]{:S(2)}) collective-permute-start(bf16[256,1024]{1,0:T(8,128)(2,1)} %get-tuple-element.1043.refs_5_.refs_11_.refs_14_.refs_19_), channel_id=1, source_target_pairs={{0,8},{4,12},{8,0},{12,4},{16,24},{20,28},{24,16},{28,20},{1,9},{5... | collective-permute-start | bytes 1572872 | tf_op jit(solution)/shard_map/ppermute | solution.py:21
  16.3 30.8 %collective-permute-start.6 = (bf16[256,1024]{1,0:T(8,128)(2,1)}, bf16[256,1024]{1,0:T(8,128)(2,1)}, u32[]{:S(2)}, u32[]{:S(2)}) collective-permute-start(bf16[256,1024]{1,0:T(8,128)(2,1)} %get-tuple-element.1043.refs_5_.refs_11_.refs_14_.refs_19_), channel_id=1, source_target_pairs={{0,16},{4,20},{8,24},{12,28},{16,0},{20,4},{24,8},{28,12},{1,17},{... | collective-permute-start | bytes 1572872 | tf_op jit(solution)/shard_map/ppermute | solution.py:21
  17.1 30.0 %collective-permute-start.2 = (bf16[2,1024]{1,0:T(2,128)(2,1)S(1)}, bf16[2,1024]{1,0:T(2,128)(2,1)S(1)}, u32[]{:S(2)}, u32[]{:S(2)}) collective-permute-start(bf16[2,1024]{1,0:T(2,128)(2,1)S(1)} %bitcast.61), channel_id=1, source_target_pairs={{0,1},{1,2},{2,3},{4,5},{5,6},{6,7},{8,9},{9,10},{10,11},{12,13},{... | collective-permute-start | bytes 12296 | tf_op jit(solution)/shard_map/ppermute | solution.py:27
  52.6 197.4 %reduce-scatter.4.cloned.1.call-start = ((), (), s32[]{:S(2)}) async-start(), calls=%async_computation.5 | async-start | bytes 5242880 | tf_op jit(solution)/shard_map/reduce_scatter | solution.py:1168
  53.0 13.6 %collective-permute-start.14 = (bf16[256,1024]{1,0:T(8,128)(2,1)}, bf16[256,1024]{1,0:T(8,128)(2,1)S(1)}, u32[]{:S(2)}, u32[]{:S(2)}) collective-permute-start(bf16[256,1024]{1,0:T(8,128)(2,1)} %collective-permute-done.6.refs_9_.refs_15_.refs_18_.refs_23_), channel_id=1, source_target_pairs={{0,8},{4,12},{8,0},{12,4},{16,24},{20,28},{24,16},{28,20},{1,9},{5... | collective-permute-start | bytes 1572872 | tf_op jit(solution)/shard_map/ppermute | solution.py:21
  53.7 13.8 %collective-permute-start.10 = (bf16[256,1024]{1,0:T(8,128)(2,1)}, bf16[256,1024]{1,0:T(8,128)(2,1)}, u32[]{:S(2)}, u32[]{:S(2)}) collective-permute-start(bf16[256,1024]{1,0:T(8,128)(2,1)} %collective-permute-done.4.refs_7_.refs_13_.refs_16_.refs_21_), channel_id=1, source_target_pairs={{0,4},{4,0},{8,12},{12,8},{16,20},{20,16},{24,28},{28,24},{1,5},{5... | collective-permute-start | bytes 1572872 | tf_op jit(solution)/shard_map/ppermute | solution.py:21
  54.2 15.9 %collective-permute-start.7 = (bf16[80,4096]{1,0:T(8,128)(2,1)}, bf16[80,4096]{1,0:T(8,128)(2,1)S(1)}, u32[]{:S(2)}, u32[]{:S(2)}) collective-permute-start(bf16[80,4096]{1,0:T(8,128)(2,1)} %get-tuple-element.967.refs_5_.refs_6_), channel_id=1, source_target_pairs={{0,4},{4,0},{8,12},{12,8},{16,20},{20,16},{24,28},{28,24},{1,5},{5... | collective-permute-start | bytes 1966088 | tf_op jit(solution)/shard_map/ppermute | solution.py:21
  54.2 16.9 %collective-permute-start.8 = (bf16[80,4096]{1,0:T(8,128)(2,1)}, bf16[80,4096]{1,0:T(8,128)(2,1)S(1)}, u32[]{:S(2)}, u32[]{:S(2)}) collective-permute-start(bf16[80,4096]{1,0:T(8,128)(2,1)} %get-tuple-element.968.refs_6_.refs_7_), channel_id=1, source_target_pairs={{0,4},{4,0},{8,12},{12,8},{16,20},{20,16},{24,28},{28,24},{1,5},{5... | collective-permute-start | bytes 1966088 | tf_op jit(solution)/shard_map/ppermute | solution.py:21
  54.9 14.3 %collective-permute-start.13 = (bf16[272,1024]{1,0:T(8,128)(2,1)}, bf16[272,1024]{1,0:T(8,128)(2,1)S(1)}, u32[]{:S(2)}, u32[]{:S(2)}) collective-permute-start(bf16[272,1024]{1,0:T(8,128)(2,1)} %collective-permute-done.3.refs_6_.refs_12_.refs_15_.refs_20_), channel_id=1, source_target_pairs={{0,16},{4,20},{8,24},{12,28},{16,0},{20,4},{24,8},{28,12},{1,17},{... | collective-permute-start | bytes 1671176 | tf_op jit(solution)/shard_map/ppermute | solution.py:21
  74.7 24.7 %collective-permute-start.17 = (bf16[80,4096]{1,0:T(8,128)(2,1)}, bf16[80,4096]{1,0:T(8,128)(2,1)}, u32[]{:S(2)}, u32[]{:S(2)}) collective-permute-start(bf16[80,4096]{1,0:T(8,128)(2,1)} %get-tuple-element.967.refs_5_.refs_6_), channel_id=1, source_target_pairs={{0,8},{4,12},{8,0},{12,4},{16,24},{20,28},{24,16},{28,20},{1,9},{5... | collective-permute-start | bytes 1966088 | tf_op jit(solution)/shard_map/ppermute | solution.py:21
  75.5 29.6 %collective-permute-start.18 = (bf16[80,4096]{1,0:T(8,128)(2,1)}, bf16[80,4096]{1,0:T(8,128)(2,1)}, u32[]{:S(2)}, u32[]{:S(2)}) collective-permute-start(bf16[80,4096]{1,0:T(8,128)(2,1)} %get-tuple-element.968.refs_6_.refs_7_), channel_id=1, source_target_pairs={{0,8},{4,12},{8,0},{12,4},{16,24},{20,28},{24,16},{28,20},{1,9},{5... | collective-permute-start | bytes 1966088 | tf_op jit(solution)/shard_map/ppermute | solution.py:21
  76.2 28.8 %collective-permute-start.19 = (bf16[80,4096]{1,0:T(8,128)(2,1)}, bf16[80,4096]{1,0:T(8,128)(2,1)}, u32[]{:S(2)}, u32[]{:S(2)}) collective-permute-start(bf16[80,4096]{1,0:T(8,128)(2,1)} %get-tuple-element.967.refs_5_.refs_6_), channel_id=1, source_target_pairs={{0,16},{4,20},{8,24},{12,28},{16,0},{20,4},{24,8},{28,12},{1,17},{... | collective-permute-start | bytes 1966088 | tf_op jit(solution)/shard_map/ppermute | solution.py:21
  77.0 28.9 %collective-permute-start.20 = (bf16[80,4096]{1,0:T(8,128)(2,1)}, bf16[80,4096]{1,0:T(8,128)(2,1)}, u32[]{:S(2)}, u32[]{:S(2)}) collective-permute-start(bf16[80,4096]{1,0:T(8,128)(2,1)} %get-tuple-element.968.refs_6_.refs_7_), channel_id=1, source_target_pairs={{0,16},{4,20},{8,24},{12,28},{16,0},{20,4},{24,8},{28,12},{1,17},{... | collective-permute-start | bytes 1966088 | tf_op jit(solution)/shard_map/ppermute | solution.py:21
  105.9 16.4 %collective-permute-start.21 = (bf16[80,4096]{1,0:T(8,128)(2,1)}, bf16[80,4096]{1,0:T(8,128)(2,1)S(1)}, u32[]{:S(2)}, u32[]{:S(2)}) collective-permute-start(bf16[80,4096]{1,0:T(8,128)(2,1)} %collective-permute-done.17.refs_7_.refs_8_), channel_id=1, source_target_pairs={{0,4},{4,0},{8,12},{12,8},{16,20},{20,16},{24,28},{28,24},{1,5},{5... | collective-permute-start | bytes 1966088 | tf_op jit(solution)/shard_map/ppermute | solution.py:21
  107.8 16.7 %collective-permute-start.23 = (bf16[80,4096]{1,0:T(8,128)(2,1)}, bf16[80,4096]{1,0:T(8,128)(2,1)}, u32[]{:S(2)}, u32[]{:S(2)}) collective-permute-start(bf16[80,4096]{1,0:T(8,128)(2,1)} %collective-permute-done.17.refs_7_.refs_8_), channel_id=1, source_target_pairs={{0,16},{4,20},{8,24},{12,28},{16,0},{20,4},{24,8},{28,12},{1,17},{... | collective-permute-start | bytes 1966088 | tf_op jit(solution)/shard_map/ppermute | solution.py:21
  108.5 13.8 %collective-permute-start.22 = (bf16[80,4096]{1,0:T(8,128)(2,1)}, bf16[80,4096]{1,0:T(8,128)(2,1)}, u32[]{:S(2)}, u32[]{:S(2)}) collective-permute-start(bf16[80,4096]{1,0:T(8,128)(2,1)} %collective-permute-done.18.refs_8_.refs_9_), channel_id=1, source_target_pairs={{0,4},{4,0},{8,12},{12,8},{16,20},{20,16},{24,28},{28,24},{1,5},{5... | collective-permute-start | bytes 1966088 | tf_op jit(solution)/shard_map/ppermute | solution.py:21
  108.8 16.4 %collective-permute-start.24 = (bf16[80,4096]{1,0:T(8,128)(2,1)}, bf16[80,4096]{1,0:T(8,128)(2,1)}, u32[]{:S(2)}, u32[]{:S(2)}) collective-permute-start(bf16[80,4096]{1,0:T(8,128)(2,1)} %collective-permute-done.20.refs_10_.refs_11_), channel_id=1, source_target_pairs={{0,8},{4,12},{8,0},{12,4},{16,24},{20,28},{24,16},{28,20},{1,9},{5... | collective-permute-start | bytes 1966088 | tf_op jit(solution)/shard_map/ppermute | solution.py:21
  117.3 5.0 %collective-permute-start.25 = (f32[2,1024]{1,0:T(2,128)}, f32[2,1024]{1,0:T(2,128)S(1)}, u32[]{:S(2)}, u32[]{:S(2)}) collective-permute-start(f32[2,1024]{1,0:T(2,128)} %get-tuple-element.719), channel_id=1, source_target_pairs={{0,1},{1,2},{2,3},{4,5},{5,6},{6,7},{8,9},{9,10},{10,11},{12,13},{... | collective-permute-start | bytes 24584 | tf_op jit(solution)/shard_map/ppermute | solution.py:27
  125.2 3.1 collective-permute-start.26
  126.3 3.9 %collective-permute-start.28 = (bf16[80,4096]{1,0:T(8,128)(2,1)}, bf16[80,4096]{1,0:T(8,128)(2,1)}, u32[]{:S(2)}, u32[]{:S(2)}) collective-permute-start(bf16[80,4096]{1,0:T(8,128)(2,1)} %collective-permute-done.23.refs_11_.refs_12_), channel_id=1, source_target_pairs={{0,4},{4,0},{8,12},{12,8},{16,20},{20,16},{24,28},{28,24},{1,5},{5... | collective-permute-start | bytes 1966088 | tf_op jit(solution)/shard_map/ppermute | solution.py:21
  126.8 4.4 %collective-permute-start.29 = (bf16[80,4096]{1,0:T(8,128)(2,1)}, bf16[80,4096]{1,0:T(8,128)(2,1)}, u32[]{:S(2)}, u32[]{:S(2)}) collective-permute-start(bf16[80,4096]{1,0:T(8,128)(2,1)} %collective-permute-done.24.refs_12_.refs_13_), channel_id=1, source_target_pairs={{0,4},{4,0},{8,12},{12,8},{16,20},{20,16},{24,28},{28,24},{1,5},{5... | collective-permute-start | bytes 1966088 | tf_op jit(solution)/shard_map/ppermute | solution.py:21
  131.1 9.0 %collective-permute-start.31 = (bf16[1536,1024]{1,0:T(8,128)(2,1)}, bf16[1536,1024]{1,0:T(8,128)(2,1)}, u32[]{:S(2)}, u32[]{:S(2)}) collective-permute-start(bf16[1536,1024]{1,0:T(8,128)(2,1)} %all-gather.9.cloned.1.call-done.refs_7_.refs_4_), channel_id=1, source_target_pairs={{0,4},{4,0},{8,12},{12,8},{16,20},{20,16},{24,28},{28,24},{1,5},{5... | collective-permute-start | bytes 9437192 | tf_op jit(solution)/shard_map/ppermute | solution.py:21
  131.5 8.6 %collective-permute-start.30 = (bf16[512,1024]{1,0:T(8,128)(2,1)}, bf16[512,1024]{1,0:T(8,128)(2,1)}, u32[]{:S(2)}, u32[]{:S(2)}) collective-permute-start(bf16[512,1024]{1,0:T(8,128)(2,1)} %refs_3_.2), channel_id=1, source_target_pairs={{0,4},{4,0},{8,12},{12,8},{16,20},{20,16},{24,28},{28,24},{1,5},{5... | collective-permute-start | bytes 3145736 | tf_op jit(solution)/shard_map/ppermute | solution.py:21
  140.1 10.0 %collective-permute-start.35 = (bf16[3,256,1024]{2,1,0:T(8,128)(2,1)}, bf16[3,256,1024]{2,1,0:T(8,128)(2,1)}, u32[]{:S(2)}, u32[]{:S(2)}) collective-permute-start(bf16[3,256,1024]{2,1,0:T(8,128)(2,1)} %get-tuple-element.1138.refs_11_.refs_1_), channel_id=1, source_target_pairs={{0,4},{4,0},{8,12},{12,8},{16,20},{20,16},{24,28},{28,24},{1,5},{5... | collective-permute-start | bytes 4718600 | tf_op jit(solution)/shard_map/ppermute | solution.py:21
  140.6 9.5 %collective-permute-start.32 = (bf16[2,256,1024]{2,1,0:T(8,128)(2,1)}, bf16[2,256,1024]{2,1,0:T(8,128)(2,1)}, u32[]{:S(2)}, u32[]{:S(2)}) collective-permute-start(bf16[2,256,1024]{2,1,0:T(8,128)(2,1)} %get-tuple-element.987.refs_1_), channel_id=1, source_target_pairs={{0,4},{4,0},{8,12},{12,8},{16,20},{20,16},{24,28},{28,24},{1,5},{5... | collective-permute-start | bytes 3145736 | tf_op jit(solution)/shard_map/ppermute | solution.py:21
  140.7 9.4 %collective-permute-start.33 = (bf16[256,2048]{1,0:T(8,128)(2,1)}, bf16[256,2048]{1,0:T(8,128)(2,1)}, u32[]{:S(2)}, u32[]{:S(2)}) collective-permute-start(bf16[256,2048]{1,0:T(8,128)(2,1)} %get-tuple-element.855.refs_2_), channel_id=1, source_target_pairs={{0,4},{4,0},{8,12},{12,8},{16,20},{20,16},{24,28},{28,24},{1,5},{5... | collective-permute-start | bytes 3145736 | tf_op jit(solution)/shard_map/ppermute | solution.py:21
  141.1 9.0 %collective-permute-start.34 = (bf16[256,1024]{1,0:T(8,128)(2,1)}, bf16[256,1024]{1,0:T(8,128)(2,1)S(1)}, u32[]{:S(2)}, u32[]{:S(2)}) collective-permute-start(bf16[256,1024]{1,0:T(8,128)(2,1)} %get-tuple-element.1091.refs_9_), channel_id=1, source_target_pairs={{0,4},{4,0},{8,12},{12,8},{16,20},{20,16},{24,28},{28,24},{1,5},{5... | collective-permute-start | bytes 1572872 | tf_op jit(solution)/shard_map/ppermute | solution.py:21
  150.5 8.3 %collective-permute-start.36 = (bf16[256,1024]{1,0:T(8,128)(2,1)}, bf16[256,1024]{1,0:T(8,128)(2,1)}, u32[]{:S(2)}, u32[]{:S(2)}) collective-permute-start(bf16[256,1024]{1,0:T(8,128)(2,1)} %get-tuple-element.991.refs_3_), channel_id=1, source_target_pairs={{0,4},{4,0},{8,12},{12,8},{16,20},{20,16},{24,28},{28,24},{1,5},{5... | collective-permute-start | bytes 1572872 | tf_op jit(solution)/shard_map/ppermute | solution.py:21
  158.8 125.7 %reduce-scatter.6.cloned.1.call-start = ((), (), s32[]{:S(2)}) async-start(), calls=%async_computation.6 | async-start | bytes 2621440 | tf_op jit(solution)/shard_map/reduce_scatter | solution.py:1168
  166.7 19.3 %collective-permute-start.42 = (bf16[256,4096]{1,0:T(8,128)(2,1)}, bf16[256,4096]{1,0:T(8,128)(2,1)}, u32[]{:S(2)}, u32[]{:S(2)}) collective-permute-start(bf16[256,4096]{1,0:T(8,128)(2,1)} %shard_map.455.refs_4_.refs_3_), channel_id=1, source_target_pairs={{0,4},{4,0},{8,12},{12,8},{16,20},{20,16},{24,28},{28,24},{1,5},{5... | collective-permute-start | bytes 6291464 | tf_op jit(solution)/shard_map/ppermute | solution.py:21
  171.1 22.1 %collective-permute-start.38 = (bf16[128,1024]{1,0:T(8,128)(2,1)}, bf16[128,1024]{1,0:T(8,128)(2,1)S(1)}, u32[]{:S(2)}, u32[]{:S(2)}) collective-permute-start(bf16[128,1024]{1,0:T(8,128)(2,1)} %get-tuple-element.992), channel_id=1, source_target_pairs={{0,8},{4,12},{8,0},{12,4},{16,24},{20,28},{24,16},{28,20},{1,9},{5... | collective-permute-start | bytes 786440 | tf_op jit(solution)/shard_map/ppermute | solution.py:21
  171.9 21.4 %collective-permute-start.39 = (bf16[128,1024]{1,0:T(8,128)(2,1)}, bf16[128,1024]{1,0:T(8,128)(2,1)S(1)}, u32[]{:S(2)}, u32[]{:S(2)}) collective-permute-start(bf16[128,1024]{1,0:T(8,128)(2,1)} %get-tuple-element.993), channel_id=1, source_target_pairs={{0,16},{4,20},{8,24},{12,28},{16,0},{20,4},{24,8},{28,12},{1,17},{... | collective-permute-start | bytes 786440 | tf_op jit(solution)/shard_map/ppermute | solution.py:21
  172.6 20.7 %collective-permute-start.40 = (bf16[128,1024]{1,0:T(8,128)(2,1)}, bf16[128,1024]{1,0:T(8,128)(2,1)S(1)}, u32[]{:S(2)}, u32[]{:S(2)}) collective-permute-start(bf16[128,1024]{1,0:T(8,128)(2,1)} %get-tuple-element.994), channel_id=1, source_target_pairs={{0,24},{4,28},{8,16},{12,20},{16,8},{20,12},{24,0},{28,4},{1,25},{... | collective-permute-start | bytes 786440 | tf_op jit(solution)/shard_map/ppermute | solution.py:21
  183.7 9.5 %collective-permute-start.41 = (f32[2,1024]{1,0:T(2,128)}, f32[2,1024]{1,0:T(2,128)S(1)}, u32[]{:S(2)}, u32[]{:S(2)}) collective-permute-start(f32[2,1024]{1,0:T(2,128)} %get-tuple-element.1032.refs_2_), channel_id=1, source_target_pairs={{1,0},{2,1},{3,2},{5,4},{6,5},{7,6},{9,8},{10,9},{11,10},{13,12},{... | collective-permute-start | bytes 24584 | tf_op jit(solution)/shard_map/ppermute | solution.py:27
  193.3 47.4 %collective-permute-start.49 = (bf16[128,4096]{1,0:T(8,128)(2,1)}, bf16[128,4096]{1,0:T(8,128)(2,1)}, u32[]{:S(2)}, u32[]{:S(2)}) collective-permute-start(bf16[128,4096]{1,0:T(8,128)(2,1)} %get-tuple-element.1077), channel_id=1, source_target_pairs={{0,8},{4,12},{8,0},{12,4},{16,24},{20,28},{24,16},{28,20},{1,9},{5... | collective-permute-start | bytes 3145736 | tf_op jit(solution)/shard_map/ppermute | solution.py:21
  194.2 46.5 %collective-permute-start.50 = (bf16[128,4096]{1,0:T(8,128)(2,1)}, bf16[128,4096]{1,0:T(8,128)(2,1)}, u32[]{:S(2)}, u32[]{:S(2)}) collective-permute-start(bf16[128,4096]{1,0:T(8,128)(2,1)} %get-tuple-element.1078), channel_id=1, source_target_pairs={{0,16},{4,20},{8,24},{12,28},{16,0},{20,4},{24,8},{28,12},{1,17},{... | collective-permute-start | bytes 3145736 | tf_op jit(solution)/shard_map/ppermute | solution.py:21
  194.9 45.9 %collective-permute-start.51 = (bf16[128,4096]{1,0:T(8,128)(2,1)}, bf16[128,4096]{1,0:T(8,128)(2,1)}, u32[]{:S(2)}, u32[]{:S(2)}) collective-permute-start(bf16[128,4096]{1,0:T(8,128)(2,1)} %get-tuple-element.1079), channel_id=1, source_target_pairs={{0,24},{4,28},{8,16},{12,20},{16,8},{20,12},{24,0},{28,4},{1,25},{... | collective-permute-start | bytes 3145736 | tf_op jit(solution)/shard_map/ppermute | solution.py:21
  203.7 4.3 %collective-permute-start.43 = (f32[8,1024]{1,0:T(8,128)}, f32[8,1024]{1,0:T(8,128)S(1)}, u32[]{:S(2)}, u32[]{:S(2)}) collective-permute-start(f32[8,1024]{1,0:T(8,128)} %get-tuple-element.1058.refs_1_), channel_id=1, source_target_pairs={{0,1},{1,0},{2,3},{3,2},{4,5},{5,4},{6,7},{7,6},{8,9},{9,8},{10,11... | collective-permute-start | bytes 98312 | tf_op jit(solution)/shard_map/ppermute | solution.py:32
  208.7 7.6 %collective-permute-start.44 = (f32[16,1024]{1,0:T(8,128)S(1)}, f32[16,1024]{1,0:T(8,128)S(1)}, u32[]{:S(2)}, u32[]{:S(2)}) collective-permute-start(f32[16,1024]{1,0:T(8,128)S(1)} %pad_maximum_fusion.1), channel_id=1, source_target_pairs={{0,2},{1,3},{2,0},{3,1},{4,6},{5,7},{6,4},{7,5},{8,10},{9,11},{10,... | collective-permute-start | bytes 196616 | tf_op jit(solution)/shard_map/ppermute | solution.py:32
  211.1 9.5 %collective-permute-start.45 = (bf16[256,512]{1,0:T(8,128)(2,1)}, bf16[256,512]{1,0:T(8,128)(2,1)S(1)}, u32[]{:S(2)}, u32[]{:S(2)}) collective-permute-start(bf16[256,512]{1,0:T(8,128)(2,1)} %get-tuple-element.1066.refs_1_), channel_id=1, source_target_pairs={{0,4},{4,0},{8,12},{12,8},{16,20},{20,16},{24,28},{28,24},{1,5},{5... | collective-permute-start | bytes 786440 | tf_op jit(solution)/shard_map/ppermute | solution.py:21
  216.3 5.6 %collective-permute-start.46 = (bf16[256,512]{1,0:T(8,128)(2,1)}, bf16[256,512]{1,0:T(8,128)(2,1)S(1)}, u32[]{:S(2)}, u32[]{:S(2)}) collective-permute-start(bf16[256,512]{1,0:T(8,128)(2,1)} %get-tuple-element.1067.refs_2_), channel_id=1, source_target_pairs={{0,4},{4,0},{8,12},{12,8},{16,20},{20,16},{24,28},{28,24},{1,5},{5... | collective-permute-start | bytes 786440 | tf_op jit(solution)/shard_map/ppermute | solution.py:21
  220.6 13.9 %collective-permute-start.47 = (bf16[256,512]{1,0:T(8,128)(2,1)}, bf16[256,512]{1,0:T(8,128)(2,1)S(1)}, u32[]{:S(2)}, u32[]{:S(2)}) collective-permute-start(bf16[256,512]{1,0:T(8,128)(2,1)} %get-tuple-element.1063.refs_16_.refs_5_), channel_id=1, source_target_pairs={{0,4},{4,0},{8,12},{12,8},{16,20},{20,16},{24,28},{28,24},{1,5},{5... | collective-permute-start | bytes 786440 | tf_op jit(solution)/shard_map/ppermute | solution.py:21
  221.9 12.6 %collective-permute-start.48 = (bf16[256,512]{1,0:T(8,128)(2,1)}, bf16[256,512]{1,0:T(8,128)(2,1)}, u32[]{:S(2)}, u32[]{:S(2)}) collective-permute-start(bf16[256,512]{1,0:T(8,128)(2,1)} %get-tuple-element.1064.refs_17_.refs_6_), channel_id=1, source_target_pairs={{0,4},{4,0},{8,12},{12,8},{16,20},{20,16},{24,28},{28,24},{1,5},{5... | collective-permute-start | bytes 786440 | tf_op jit(solution)/shard_map/ppermute | solution.py:21
  240.8 94.5 %reduce-scatter.8.cloned.1.call-start = ((), (), s32[]{:S(2)}) async-start(), calls=%async_computation.7 | async-start | bytes 1638400 | tf_op jit(solution)/shard_map/reduce_scatter | solution.py:1168
  240.8 9.2 %collective-permute-start.52 = (bf16[2,256,1024]{2,1,0:T(8,128)(2,1)}, bf16[2,256,1024]{2,1,0:T(8,128)(2,1)}, u32[]{:S(2)}, u32[]{:S(2)}) collective-permute-start(bf16[2,256,1024]{2,1,0:T(8,128)(2,1)} %get-tuple-element.1140.refs_3_), channel_id=1, source_target_pairs={{0,4},{4,0},{8,12},{12,8},{16,20},{20,16},{24,28},{28,24},{1,5},{5... | collective-permute-start | bytes 3145736 | tf_op jit(solution)/shard_map/ppermute | solution.py:21
  242.8 7.2 %collective-permute-start.53 = (f32[2,1024]{1,0:T(2,128)S(1)}, f32[2,1024]{1,0:T(2,128)S(1)}, u32[]{:S(2)}, u32[]{:S(2)}) collective-permute-start(f32[2,1024]{1,0:T(2,128)S(1)} %copy-done.29), channel_id=1, source_target_pairs={{1,0},{2,1},{3,2},{5,4},{6,5},{7,6},{9,8},{10,9},{11,10},{13,12},{... | collective-permute-start | bytes 24584 | tf_op jit(solution)/shard_map/ppermute | solution.py:27
  252.1 15.1 %collective-permute-start.54 = (bf16[128,1024]{1,0:T(8,128)(2,1)}, bf16[128,1024]{1,0:T(8,128)(2,1)S(1)}, u32[]{:S(2)}, u32[]{:S(2)}) collective-permute-start(bf16[128,1024]{1,0:T(8,128)(2,1)} %get-tuple-element.1267), channel_id=1, source_target_pairs={{0,8},{4,12},{8,0},{12,4},{16,24},{20,28},{24,16},{28,20},{1,9},{5... | collective-permute-start | bytes 786440 | tf_op jit(solution)/shard_map/ppermute | solution.py:21
  253.4 13.8 %collective-permute-start.55 = (bf16[128,1024]{1,0:T(8,128)(2,1)}, bf16[128,1024]{1,0:T(8,128)(2,1)S(1)}, u32[]{:S(2)}, u32[]{:S(2)}) collective-permute-start(bf16[128,1024]{1,0:T(8,128)(2,1)} %get-tuple-element.1266), channel_id=1, source_target_pairs={{0,16},{4,20},{8,24},{12,28},{16,0},{20,4},{24,8},{28,12},{1,17},{... | collective-permute-start | bytes 786440 | tf_op jit(solution)/shard_map/ppermute | solution.py:21
  253.6 13.7 %collective-permute-start.56 = (bf16[128,1024]{1,0:T(8,128)(2,1)}, bf16[128,1024]{1,0:T(8,128)(2,1)}, u32[]{:S(2)}, u32[]{:S(2)}) collective-permute-start(bf16[128,1024]{1,0:T(8,128)(2,1)} %get-tuple-element.1265), channel_id=1, source_target_pairs={{0,24},{4,28},{8,16},{12,20},{16,8},{20,12},{24,0},{28,4},{1,25},{... | collective-permute-start | bytes 786440 | tf_op jit(solution)/shard_map/ppermute | solution.py:21
  268.0 16.6 %collective-permute-start.57 = (bf16[272,1024]{1,0:T(8,128)(2,1)}, bf16[272,1024]{1,0:T(8,128)(2,1)S(1)}, u32[]{:S(2)}, u32[]{:S(2)}) collective-permute-start(bf16[272,1024]{1,0:T(8,128)(2,1)} %get-tuple-element.1152), channel_id=1, source_target_pairs={{0,8},{4,12},{8,0},{12,4},{16,24},{20,28},{24,16},{28,20},{1,9},{5... | collective-permute-start | bytes 1671176 | tf_op jit(solution)/shard_map/ppermute | solution.py:21
  269.2 15.3 %collective-permute-start.58 = (bf16[272,1024]{1,0:T(8,128)(2,1)}, bf16[272,1024]{1,0:T(8,128)(2,1)}, u32[]{:S(2)}, u32[]{:S(2)}) collective-permute-start(bf16[272,1024]{1,0:T(8,128)(2,1)} %get-tuple-element.1153), channel_id=1, source_target_pairs={{0,16},{4,20},{8,24},{12,28},{16,0},{20,4},{24,8},{28,12},{1,17},{... | collective-permute-start | bytes 1671176 | tf_op jit(solution)/shard_map/ppermute | solution.py:21
  269.4 24.7 %collective-permute-start.59 = (bf16[272,1024]{1,0:T(8,128)(2,1)}, bf16[272,1024]{1,0:T(8,128)(2,1)}, u32[]{:S(2)}, u32[]{:S(2)}) collective-permute-start(bf16[272,1024]{1,0:T(8,128)(2,1)} %get-tuple-element.1154), channel_id=1, source_target_pairs={{0,24},{4,28},{8,16},{12,20},{16,8},{20,12},{24,0},{28,4},{1,25},{... | collective-permute-start | bytes 1671176 | tf_op jit(solution)/shard_map/ppermute | solution.py:21
  296.0 5.9 %collective-permute-start.60 = (bf16[64,1024]{1,0:T(8,128)(2,1)}, bf16[64,1024]{1,0:T(8,128)(2,1)S(1)}, u32[]{:S(2)}, u32[]{:S(2)}) collective-permute-start(bf16[64,1024]{1,0:T(8,128)(2,1)} %get-tuple-element.1270), channel_id=1, source_target_pairs={{0,8},{4,12},{8,0},{12,4},{16,24},{20,28},{24,16},{28,20},{1,9},{5... | collective-permute-start | bytes 393224 | tf_op jit(solution)/shard_map/ppermute | solution.py:21
  296.2 5.8 %collective-permute-start.61 = (bf16[64,1024]{1,0:T(8,128)(2,1)}, bf16[64,1024]{1,0:T(8,128)(2,1)S(1)}, u32[]{:S(2)}, u32[]{:S(2)}) collective-permute-start(bf16[64,1024]{1,0:T(8,128)(2,1)} %get-tuple-element.1269), channel_id=1, source_target_pairs={{0,16},{4,20},{8,24},{12,28},{16,0},{20,4},{24,8},{28,12},{1,17},{... | collective-permute-start | bytes 393224 | tf_op jit(solution)/shard_map/ppermute | solution.py:21
  297.4 6.1 %collective-permute-start.62 = (bf16[64,1024]{1,0:T(8,128)(2,1)}, bf16[64,1024]{1,0:T(8,128)(2,1)}, u32[]{:S(2)}, u32[]{:S(2)}) collective-permute-start(bf16[64,1024]{1,0:T(8,128)(2,1)} %get-tuple-element.1268), channel_id=1, source_target_pairs={{0,24},{4,28},{8,16},{12,20},{16,8},{20,12},{24,0},{28,4},{1,25},{... | collective-permute-start | bytes 393224 | tf_op jit(solution)/shard_map/ppermute | solution.py:21
  303.5 12.7 %collective-permute-start.63 = (bf16[80,1024]{1,0:T(8,128)(2,1)}, bf16[80,1024]{1,0:T(8,128)(2,1)S(1)}, u32[]{:S(2)}, u32[]{:S(2)}) collective-permute-start(bf16[80,1024]{1,0:T(8,128)(2,1)} %get-tuple-element.1191), channel_id=1, source_target_pairs={{0,1},{1,0},{2,3},{3,2},{4,5},{5,4},{6,7},{7,6},{8,9},{9,8},{10,11... | collective-permute-start | bytes 491528 | tf_op jit(solution)/shard_map/ppermute | solution.py:32
  303.5 15.7 %collective-permute-start.64 = (bf16[80,1024]{1,0:T(8,128)(2,1)}, bf16[80,1024]{1,0:T(8,128)(2,1)S(1)}, u32[]{:S(2)}, u32[]{:S(2)}) collective-permute-start(bf16[80,1024]{1,0:T(8,128)(2,1)} %get-tuple-element.1192), channel_id=1, source_target_pairs={{0,2},{1,3},{2,0},{3,1},{4,6},{5,7},{6,4},{7,5},{8,10},{9,11},{10,... | collective-permute-start | bytes 491528 | tf_op jit(solution)/shard_map/ppermute | solution.py:32
  304.9 25.9 %collective-permute-start.65 = (bf16[80,1024]{1,0:T(8,128)(2,1)}, bf16[80,1024]{1,0:T(8,128)(2,1)S(1)}, u32[]{:S(2)}, u32[]{:S(2)}) collective-permute-start(bf16[80,1024]{1,0:T(8,128)(2,1)} %get-tuple-element.1193), channel_id=1, source_target_pairs={{0,3},{1,2},{2,1},{3,0},{4,7},{5,6},{6,5},{7,4},{8,11},{9,10},{10,... | collective-permute-start | bytes 491528 | tf_op jit(solution)/shard_map/ppermute | solution.py:32
  331.5 3.1 collective-permute-start.66
  (41 other events, 296.4 us)
Sparse Core Ops, SparseCore 0:
  12.9 37.5 all-gather.6
  52.7 62.7 all-gather.8
  159.0 79.5 reduce-scatter.3
  240.9 43.6 reduce-scatter.5
  286.7 39.2 reduce-scatter.7

commit v7 on v6

--- a/solution.py
+++ b/solution.py
@@ -435,7 +435,7 @@
     return call(
         body, info, [last, previous, *extra], [(stream, None)], flat_pieces(pieces),
         [((3 * batches, width), f32), ((16, width), f32), ((batches, width), f32)],
-        [((3, tokens, width), bf16), ((tokens, width), f32)] + [((tokens, width), bf16)] * 2,
+        [((3, tokens, width), bf16)] + [((tokens, width), f32)] * 3,
         [pltpu.VMEM((3, width, width), bf16), pltpu.VMEM((16 * len(order), width), bf16)],
         len(vplan) + sum(map(len, plans)), 9, 40)
 
@@ -513,7 +513,7 @@
                        + ent_ref[batches + b : batches + b + 1, n] * o + e)
                 rden = 1.0 / den
                 wkv = num * rden
-                wkv_ref[t, n] = wkv.astype(bf16)
+                wkv_ref[t, n] = wkv
                 rden_ref[t, n] = rden.astype(bf16)
                 gated_ref[t, n] = (jax.nn.sigmoid(kvr_ref[2][t, n].astype(f32)) * wkv).astype(bf16)
         put(0)
@@ -529,17 +529,17 @@
         def _(i):
             r = row_chunk(0, i, 0)
             nb, _ = norm(mid_ref[r, :])
-            xb_ref[r, :] = (nb * vec_ref[G2 : G2 + 1] + vec_ref[B2 : B2 + 1]).astype(bf16)
+            xb_ref[r, :] = nb * vec_ref[G2 : G2 + 1] + vec_ref[B2 : B2 + 1]
         for b in range(batches):
             last = (b + 1) * length
-            edge_ref[b : b + 1, :] = xb_ref[last - 16 : last, :].astype(f32)[15:]
+            edge_ref[b : b + 1, :] = xb_ref[last - 1 : last, :]
 
     one, low = ((tokens, width), f32), ((tokens, width), bf16)
     return call(
         body, info, [*everyone, *state, vec], [(a, None) for a in (*kvr, stream)], flat_pieces(pieces),
         [((3 * batches, width), f32), ((batches, 1, width), f32), ((batches, 1, width), f32),
          ((batches, width), f32)],
-        [low, low, low, one, low],
+        [low, one, low, one, one],
         [pltpu.VMEM((width, width), bf16)], len(steps), 7, 40)
 
 
@@ -638,13 +638,13 @@
         arrive_c()
         @columns(width, STEP)
         def _(n):
-            frec_ref[:, n] = dot_nn(in_ref[1], wc[:, n]).astype(bf16)
+            frec_ref[:, n] = dot_nn(in_ref[1], wc[:, n])
 
     return call(
         body, info, [edge, previous, vec], [(xb, None)], flat_pieces(pieces_ck),
         [((batches, width), f32)],
         [((2, tokens, width), bf16), ((tokens, wide // 2), bf16), ((tokens, wide // 2), bf16),
-         ((tokens, wide), bf16), ((tokens, width), bf16)],
+         ((tokens, wide), bf16), ((tokens, width), f32)],
         [pltpu.VMEM((width, wide), bf16), pltpu.VMEM((width, width), bf16)],
         1 + len(order), 11, 40)
 

time: 346 us -> 347 us (level)
  transfers between devices with their start and end apart: 72 -> 72, of which waited for: 27 -> 28; matrix products, arithmetic and copies ran while one was open for 4% -> 4% of each run, Pallas kernels for 33% -> 34%
where the time goes in v7:
time: 347 us; the launch traced here: 345 us
  Pallas kernels  119 us (34%)
  waiting for transfers between devices  101 us (29%)
  starting transfers between devices  60 us (17%)
  blocking collectives  24.5 us (7%)
  local copies, waits for them, and re-layouts  15.2 us (4%)
  between operations  14.7 us (4%)
  other arithmetic  10.3 us (3%)
    pallas_call x16, Pallas kernels, call(): pl.pallas_call(kernel, out_shape=[jax.ShapeDtypeStruct(s, d) for s, d in...  114 us
    ppermute x58, waiting for transfers between devices, hop(): return lax.ppermute(value, 'seg', [(i, i ^ bit) for i in range(count)])  67 us
    ppermute x58, starting transfers between devices, hop(): return lax.ppermute(value, 'seg', [(i, i ^ bit) for i in range(count)])  43.3 us
    ppermute x5, waiting for transfers between devices, across(): return lax.ppermute(value, 'stretch', [(i, i ^ j) for i in range(count)])  28.8 us
    all_gather x1, blocking collectives, body(): v.everyone = lax.all_gather(v.sums, 'stretch')  12.8 us
    all_gather x1, blocking collectives, body(): v.heads = lax.all_gather(v.head_a, 'stretch')[0]  11.8 us
    ppermute x4, starting transfers between devices, along(): lax.ppermute(value, 'stretch', [(i, i + steps) for i in range(first, last)])  11.3 us
  transfers between devices with their start and end apart: 72, of which 28 were waited for; matrix products, arithmetic and copies ran while one was open for 4% of the time, Pallas kernels for 34%

profile of v7, /device:TPU:9, one launch (start us, length us, event | category | flops | bytes accessed | tf_op | source)
XLA Modules:
  0.0 345.2 jit_solution(13790104879694234501)
XLA Ops:
  8.0 1.7 constant_dynamic-slice_fusion.3
  9.7 3.0 shard_map.448
  13.6 1.2 collective-permute-start.3
  14.8 1.2 collective-permute-start.5
  17.1 3.2 collective-permute-start.2
  20.3 2.4 shard_map.449
  22.8 22.5 %collective-permute-done.4.refs_7_.refs_13_.refs_16_.refs_21_ = bf16[256,1024]{1,0:T(8,128)(2,1)} collective-permute-done((bf16[256,1024]{1,0:T(8,128)(2,1)}, bf16[256,1024]{1,0:T(8,128)(2,1)}, u32[]{:S(2)}, u32[]{:S(2)}) %collective-permute-start.4) | collective-permute-done | bytes 524320 | tf_op jit(solution)/shard_map/ppermute | solution.py:21
  45.3 1.8 collective-permute-done.6.refs_9_.refs_15_.refs_18_.refs_23_
  47.1 3.4 all-gather.7.cloned.1.call-done
  55.7 10.9 %collective-permute-done.14.refs_11_.refs_17_.refs_20_.refs_25_ = bf16[256,1024]{1,0:T(8,128)(2,1)S(1)} collective-permute-done((bf16[256,1024]{1,0:T(8,128)(2,1)}, bf16[256,1024]{1,0:T(8,128)(2,1)S(1)}, u32[]{:S(2)}, u32[]{:S(2)}) %collective-permute-start.14) | collective-permute-done | bytes 524320 | tf_op jit(solution)/shard_map/ppermute | solution.py:21
  67.6 1.5 collective-permute-done.13.refs_10_.refs_16_.refs_19_.refs_24_
  72.6 2.2 collective-permute-done.16.refs_19_.refs_25_.refs_28_.refs_33_
  78.4 8.4 %shard_map.450 = (f32[6,1024]{1,0:T(8,128)}, f32[16,1024]{1,0:T(8,128)}, f32[2,1024]{1,0:T(2,128)}, bf16[3,256,1024]{2,1,0:T(8,128)(2,1)}, f32[256,1024]{1,0:T(8...) custom-call(s32[3]{0:T(128)} %pad_add_fusion.refs_0_, bf16[2,1024]{1,0:T(2,128)(2,1)} %copy-done.32, ...), custom_call_target="tpu_custom_call" | custom-call | bytes 9000 | tf_op jit(solution)/shard_map/pallas_call | solution.py:190
  86.9 12.8 %all-gather.2.refs_1_ = f32[4,6,1024]{2,1,0:T(8,128)} all-gather(f32[1,6,1024]{2,1,0:T(8,128)} %bitcast.58), channel_id=2, replica_groups=mesh['seg'=8,'stretch'=4] {'stretch'}, dimensions={0}, use_global_device_ids=true | all-gather | bytes 122880 | tf_op jit(solution)/shard_map/all_gather | solution.py:1275
  99.6 5.5 %collective-permute-done.18.refs_8_.refs_9_ = bf16[80,4096]{1,0:T(8,128)(2,1)} collective-permute-done((bf16[80,4096]{1,0:T(8,128)(2,1)}, bf16[80,4096]{1,0:T(8,128)(2,1)}, u32[]{:S(2)}, u32[]{:S(2)}) %collective-permute-start.18) | collective-permute-done | bytes 655392 | tf_op jit(solution)/shard_map/ppermute | solution.py:21
  106.0 1.8 collective-permute-start.21
  109.6 8.2 %shard_map.451 = (f32[6,1024]{1,0:T(8,128)}, f32[2,1,1024]{2,1,0:T(1,128)}, f32[2,1,1024]{2,1,0:T(1,128)}, f32[2,1024]{1,0:T(2,128)}, bf16[256,1024]{1,0:T(8,128...) custom-call(s32[3]{0:T(128)} %pad_add_fusion.refs_0_, ...), custom_call_target="tpu_custom_call" | custom-call | bytes 7000 | tf_op jit(solution)/shard_map/pallas_call | solution.py:190
  117.8 3.3 collective-permute-start.25
  121.2 1.7 collective-permute-done.25.refs_1_
  122.9 1.7 collective-permute-done.23.refs_11_.refs_12_
  126.9 1.6 collective-permute-done.26.refs_17_.refs_18_
  131.8 8.7 %shard_map.452 = (f32[2,1024]{1,0:T(2,128)}, bf16[2,256,1024]{2,1,0:T(8,128)(2,1)}, bf16[256,2048]{1,0:T(8,128)(2,1)}, bf16[256,2048]{1,0:T(8,128)(2,1)}, bf16[2...) custom-call(s32[3]{0:T(128)} %pad_add_fusion.refs_0_, f32[2,1024]{1,0:T(2,128)} %copy-done.31, f32[2,1,1024]{2,1,0:T(1,128)} %refs_2_.5, ...), custom_call_target="tpu_custom_call" | custom-call | bytes 11000 | tf_op jit(solution)/shard_map/pallas_call | solution.py:190
  141.6 9.0 %shard_map.453 = (bf16[256,1024]{1,0:T(8,128)(2,1)}, bf16[256,1024]{1,0:T(8,128)(2,1)}, bf16[256,1024]{1,0:T(8,128)(2,1)}) custom-call(s32[3]{0:T(128)} %pad_add_fusion.refs_0_, bf16[256,2048]{1,0:T(8,128)(2,1)} %get-tuple-element.933.refs_1_, bf16[256,2048]{1,0:T(8,128)(2,1)} %get-tuple-element.855.refs_2_, f32[256,1024]{1,0:T(8,128)} %get-tuple-element.856.refs_3_, ...), custom_call_target="tpu_custom_call" | custom-call | bytes 7000 | tf_op jit(solution)/shard_map/pallas_call | solution.py:190
  151.2 1.7 collective-permute-done.37.refs_4_
  152.9 6.3 %shard_map.454 = bf16[2048,1024]{1,0:T(8,128)(2,1)} custom-call(s32[3]{0:T(128)} %pad_add_fusion.refs_0_, bf16[256,2048]{1,0:T(8,128)(2,1)} %get-tuple-element.933.refs_1_, bf16[256,2048]{1,0:T(8,128)(2,1)} %collective-permute-done.33.refs_2_, bf16[256,1024]{1,0:T(8,128)(2,1)} %get-tuple-element.960.refs_3_.refs_1_, ...), custom_call_target="tpu_custom_call" | custom-call | bytes 6000 | tf_op jit(solution)/shard_map/pallas_call | solution.py:190
  159.6 7.6 %shard_map.455.refs_4_.refs_3_ = bf16[256,4096]{1,0:T(8,128)(2,1)} custom-call(s32[3]{0:T(128)} %pad_add_fusion.refs_0_, bf16[256,1024]{1,0:T(8,128)(2,1)} %get-tuple-element.960.refs_3_.refs_1_, bf16[256,4096]{1,0:T(8,128)(2,1)} %get-tuple-element.961.refs_2_, bf16[512,1024]{1,0:T(8,128)(2,1)} %refs_3_.2, ...), custom_call_target="tpu_custom_call" | custom-call | bytes 7000 | tf_op jit(solution)/shard_map/pallas_call | solution.py:190
  167.6 4.0 %shard_map.457 = (bf16[128,1024]{1,0:T(8,128)(2,1)}, bf16[128,1024]{1,0:T(8,128)(2,1)}, bf16[128,1024]{1,0:T(8,128)(2,1)}, bf16[128,1024]{1,0:T(8,128)(2,1)}) custom-call(s32[3]{0:T(128)} %pad_add_fusion.refs_0_, bf16[2,256,1024]{2,1,0:T(8,128)(2,1)} %get-tuple-element.987.refs_1_, bf16[2,256,1024]{2,1,0:T(8,128)(2,1)} %collective-permute-done.32.refs_2_, ...), custom_call_target="tpu_custom_call" | custom-call | bytes 3000 | tf_op jit(solution)/shard_map/pallas_call | solution.py:190
  173.1 1.2 collective-permute-start.40
  174.4 10.0 %shard_map.456 = (f32[2,1024]{1,0:T(2,128)}, f32[2,1024]{1,0:T(2,128)}, bf16[256,1024]{1,0:T(8,128)(2,1)}, bf16[256,1024]{1,0:T(8,128)(2,1)}) custom-call(s32[3]{0:T(128)} %pad_add_fusion.refs_0_, f32[2,1024]{1,0:T(2,128)} %get-tuple-element.958.refs_1_, f32[16,1024]{1,0:T(8,128)} %get-tuple-element.1126.refs_5_.refs_3_.refs_2_.refs_10_, ...), custom_call_target="tpu_custom_call" | custom-call | bytes 10000 | tf_op jit(solution)/shard_map/pallas_call | solution.py:190
  184.3 2.3 collective-permute-start.41
  186.6 7.2 %shard_map.458 = (bf16[128,4096]{1,0:T(8,128)(2,1)}, bf16[128,4096]{1,0:T(8,128)(2,1)}, bf16[128,4096]{1,0:T(8,128)(2,1)}, bf16[128,4096]{1,0:T(8,128)(2,1)}) custom-call(s32[3]{0:T(128)} %pad_add_fusion.refs_0_, bf16[2,256,1024]{2,1,0:T(8,128)(2,1)} %get-tuple-element.987.refs_1_, bf16[2,256,1024]{2,1,0:T(8,128)(2,1)} %collective-permute-done.32.refs_2_, ...), custom_call_target="tpu_custom_call" | custom-call | bytes 7000 | tf_op jit(solution)/shard_map/pallas_call | solution.py:190
  195.5 1.2 collective-permute-start.51
  196.7 7.9 %shard_map.459 = (f32[8,1024]{1,0:T(8,128)}, f32[2,1024]{1,0:T(2,128)}, bf16[256,1024]{1,0:T(8,128)(2,1)}, bf16[256,512]{1,0:T(8,128)(2,1)}, bf16[256,512]{1,0:T...) custom-call(s32[3]{0:T(128)} %pad_add_fusion.refs_0_, ...), custom_call_target="tpu_custom_call" | custom-call | bytes 9000 | tf_op jit(solution)/shard_map/pallas_call | solution.py:190
  204.6 4.2 %collective-permute-done.43.refs_2_ = f32[8,1024]{1,0:T(8,128)S(1)} collective-permute-done((f32[8,1024]{1,0:T(8,128)}, f32[8,1024]{1,0:T(8,128)S(1)}, u32[]{:S(2)}, u32[]{:S(2)}) %collective-permute-start.43) | collective-permute-done | bytes 32800 | tf_op jit(solution)/shard_map/ppermute | solution.py:32
  209.6 2.3 collective-permute-start.44
  212.0 4.8 %collective-permute-start.45 = (bf16[256,512]{1,0:T(8,128)(2,1)}, bf16[256,512]{1,0:T(8,128)(2,1)S(1)}, u32[]{:S(2)}, u32[]{:S(2)}) collective-permute-start(bf16[256,512]{1,0:T(8,128)(2,1)} %get-tuple-element.1066.refs_1_), channel_id=1, source_target_pairs={{0,4},{4,0},{8,12},{12,8},{16,20},{20,16},{24,28},{28,24},{1,5},{5... | collective-permute-start | bytes 786440 | tf_op jit(solution)/shard_map/ppermute | solution.py:21
  216.8 1.8 collective-permute-done.44.refs_3_
  218.6 2.6 collective-permute-start.46
  221.3 1.3 collective-permute-done.46.refs_4_
  223.0 12.5 %shard_map.460 = (f32[2,1,1024]{2,1,0:T(1,128)}, f32[2,1,1024]{2,1,0:T(1,128)}, f32[2,1,1024]{2,1,0:T(1,128)}, f32[2,1,1024]{2,1,0:T(1,128)}, f32[2,1024]{1,0:T(...) custom-call(s32[3]{0:T(128)} %pad_add_fusion.refs_0_, ...), custom_call_target="tpu_custom_call" | custom-call | bytes 14000 | tf_op jit(solution)/shard_map/pallas_call | solution.py:190
  236.2 5.5 %shard_map.461 = bf16[1024,1024]{1,0:T(8,128)(2,1)} custom-call(s32[3]{0:T(128)} %pad_add_fusion.refs_0_, bf16[256,512]{1,0:T(8,128)(2,1)} %get-tuple-element.1066.refs_1_, bf16[256,512]{1,0:T(8,128)(2,1)} %get-tuple-element.1067.refs_2_, bf16[256,512]{1,0:T(8,128)(2,1)} %copy-done.14, bf16[256,512]{1,0:T(8,128)(2,1)} %copy-done.15, ...), custom_call_target="tpu_custom_call" | custom-call | bytes 6000 | tf_op jit(solution)/shard_map/pallas_call | solution.py:190
  241.7 1.6 collective-permute-start.52
  243.4 2.5 collective-permute-start.53
  246.0 4.7 %shard_map.462 = bf16[640,1024]{1,0:T(8,128)(2,1)} custom-call(s32[3]{0:T(128)} %pad_add_fusion.refs_0_, bf16[128,4096]{1,0:T(8,128)(2,1)} %get-tuple-element.1110.refs_1_, bf16[128,4096]{1,0:T(8,128)(2,1)} %collective-permute-done.49.refs_2_, bf16[128,4096]{1,0:T(8,128)(2,1)} %collective-permute-done.50.refs_3_, ...), custom_call_target="tpu_custom_call" | custom-call | bytes 4000 | tf_op jit(solution)/shard_map/pallas_call | solution.py:190
  250.7 2.1 fusion.4
  252.8 1.3 collective-permute-start.54
  254.1 1.3 collective-permute-start.55
  255.5 5.2 %shard_map.463 = (f32[2,1024]{1,0:T(2,128)}, bf16[256,1024]{1,0:T(8,128)(2,1)}) custom-call(s32[3]{0:T(128)} %pad_add_fusion.refs_0_, f32[2,1024]{1,0:T(2,128)} %copy-done.25, f32[16,1024]{1,0:T(8,128)} %get-tuple-element.1126.refs_5_.refs_3_.refs_2_.refs_10_, bf16[256,1024]{1,0:T(8,128)(2,1)} %get-tuple-element.1127.refs_3_, ...), custom_call_target="tpu_custom_call" | custom-call | bytes 6000 | tf_op jit(solution)/shard_map/pallas_call | solution.py:190
  262.3 5.6 %shard_map.464 = (bf16[272,1024]{1,0:T(8,128)(2,1)}, bf16[272,1024]{1,0:T(8,128)(2,1)}, bf16[272,1024]{1,0:T(8,128)(2,1)}, bf16[272,1024]{1,0:T(8,128)(2,1)}) custom-call(s32[3]{0:T(128)} %pad_add_fusion.refs_0_, bf16[3,256,1024]{2,1,0:T(8,128)(2,1)} %get-tuple-element.1138.refs_11_.refs_1_, bf16[3,256,1024]{2,1,0:T(8,128)(2,1)} %collective-permute-done.35.refs_12_.refs_2_, ...), custom_call_target="tpu_custom_call" | custom-call | bytes 7000 | tf_op jit(solution)/shard_map/pallas_call | solution.py:190
  268.7 1.3 collective-permute-start.57
  270.0 1.3 collective-permute-start.58
  271.4 11.8 %all-gather.3 = f32[4,2,1024]{2,1,0:T(2,128)S(1)} all-gather(f32[1,2,1024]{2,1,0:T(2,128)S(1)} %bitcast.60), channel_id=3, replica_groups=mesh['seg'=8,'stretch'=4] {'stretch'}, dimensions={0}, use_global_device_ids=true | all-gather | bytes 40960 | tf_op jit(solution)/shard_map/all_gather | solution.py:1399
  283.1 2.1 convert_add_fusion
  285.4 9.5 %collective-permute-done.59.refs_4_ = bf16[272,1024]{1,0:T(8,128)(2,1)} collective-permute-done((bf16[272,1024]{1,0:T(8,128)(2,1)}, bf16[272,1024]{1,0:T(8,128)(2,1)}, u32[]{:S(2)}, u32[]{:S(2)}) %collective-permute-start.59) | collective-permute-done | bytes 557088 | tf_op jit(solution)/shard_map/ppermute | solution.py:21
  294.9 1.9 fusion.5
  296.8 1.2 collective-permute-start.60
  298.2 1.2 collective-permute-start.62
  299.4 3.2 shard_map.465
  303.8 1.7 collective-permute-start.64
  308.8 8.2 %collective-permute-done.63 = bf16[80,1024]{1,0:T(8,128)(2,1)S(1)} collective-permute-done((bf16[80,1024]{1,0:T(8,128)(2,1)}, bf16[80,1024]{1,0:T(8,128)(2,1)S(1)}, u32[]{:S(2)}, u32[]{:S(2)}) %collective-permute-start.63) | collective-permute-done | bytes 163872 | tf_op jit(solution)/shard_map/ppermute | solution.py:32
  317.0 2.9 collective-permute-done.64
  319.9 11.7 %collective-permute-done.65 = bf16[80,1024]{1,0:T(8,128)(2,1)S(1)} collective-permute-done((bf16[80,1024]{1,0:T(8,128)(2,1)}, bf16[80,1024]{1,0:T(8,128)(2,1)S(1)}, u32[]{:S(2)}, u32[]{:S(2)}) %collective-permute-start.65) | collective-permute-done | bytes 163872 | tf_op jit(solution)/shard_map/ppermute | solution.py:32
  332.3 1.5 collective-permute-start.66
  336.2 1.7 slice_convert_fusion
  (200 shorter events, 43.0 us)
Async XLA Ops:
  7.2 43.3 %all-gather.7.cloned.1.call-start = ((), (), s32[]{:S(2)}) async-start(), calls=%async_computation.3 | async-start | bytes 2359296 | tf_op jit(solution)/shard_map/all_gather | solution.py:1251
  12.7 118.5 %all-gather.9.cloned.1.call-start = ((), (), s32[]{:S(2)}) async-start(), calls=%async_computation.4 | async-start | bytes 3932160 | tf_op jit(solution)/shard_map/all_gather | solution.py:1260
  12.8 3.5 %collective-permute-start.1 = (bf16[256,1024]{1,0:T(8,128)(2,1)}, bf16[256,1024]{1,0:T(8,128)(2,1)S(1)}, u32[]{:S(2)}, u32[]{:S(2)}) collective-permute-start(bf16[256,1024]{1,0:T(8,128)(2,1)} %get-tuple-element.1043.refs_5_.refs_11_.refs_14_.refs_19_), channel_id=1, source_target_pairs={{0,4},{4,0},{8,12},{12,8},{16,20},{20,16},{24,28},{28,24},{1,5},{5... | collective-permute-start | bytes 1572872 | tf_op jit(solution)/shard_map/ppermute | solution.py:21
  13.6 33.5 %collective-permute-start.3 = (bf16[272,1024]{1,0:T(8,128)(2,1)}, bf16[272,1024]{1,0:T(8,128)(2,1)}, u32[]{:S(2)}, u32[]{:S(2)}) collective-permute-start(bf16[272,1024]{1,0:T(8,128)(2,1)} %get-tuple-element.1042.refs_4_.refs_10_.refs_13_.refs_18_), channel_id=1, source_target_pairs={{0,8},{4,12},{8,0},{12,4},{16,24},{20,28},{24,16},{28,20},{1,9},{5... | collective-permute-start | bytes 1671176 | tf_op jit(solution)/shard_map/ppermute | solution.py:21
  14.8 32.3 %collective-permute-start.5 = (bf16[272,1024]{1,0:T(8,128)(2,1)}, bf16[272,1024]{1,0:T(8,128)(2,1)}, u32[]{:S(2)}, u32[]{:S(2)}) collective-permute-start(bf16[272,1024]{1,0:T(8,128)(2,1)} %get-tuple-element.1042.refs_4_.refs_10_.refs_13_.refs_18_), channel_id=1, source_target_pairs={{0,16},{4,20},{8,24},{12,28},{16,0},{20,4},{24,8},{28,12},{1,17},{... | collective-permute-start | bytes 1671176 | tf_op jit(solution)/shard_map/ppermute | solution.py:21
  16.1 29.2 %collective-permute-start.4 = (bf16[256,1024]{1,0:T(8,128)(2,1)}, bf16[256,1024]{1,0:T(8,128)(2,1)}, u32[]{:S(2)}, u32[]{:S(2)}) collective-permute-start(bf16[256,1024]{1,0:T(8,128)(2,1)} %get-tuple-element.1043.refs_5_.refs_11_.refs_14_.refs_19_), channel_id=1, source_target_pairs={{0,8},{4,12},{8,0},{12,4},{16,24},{20,28},{24,16},{28,20},{1,9},{5... | collective-permute-start | bytes 1572872 | tf_op jit(solution)/shard_map/ppermute | solution.py:21
  16.3 30.8 %collective-permute-start.6 = (bf16[256,1024]{1,0:T(8,128)(2,1)}, bf16[256,1024]{1,0:T(8,128)(2,1)}, u32[]{:S(2)}, u32[]{:S(2)}) collective-permute-start(bf16[256,1024]{1,0:T(8,128)(2,1)} %get-tuple-element.1043.refs_5_.refs_11_.refs_14_.refs_19_), channel_id=1, source_target_pairs={{0,16},{4,20},{8,24},{12,28},{16,0},{20,4},{24,8},{28,12},{1,17},{... | collective-permute-start | bytes 1572872 | tf_op jit(solution)/shard_map/ppermute | solution.py:21
  17.1 30.0 %collective-permute-start.2 = (bf16[2,1024]{1,0:T(2,128)(2,1)S(1)}, bf16[2,1024]{1,0:T(2,128)(2,1)S(1)}, u32[]{:S(2)}, u32[]{:S(2)}) collective-permute-start(bf16[2,1024]{1,0:T(2,128)(2,1)S(1)} %bitcast.61), channel_id=1, source_target_pairs={{0,1},{1,2},{2,3},{4,5},{5,6},{6,7},{8,9},{9,10},{10,11},{12,13},{... | collective-permute-start | bytes 12296 | tf_op jit(solution)/shard_map/ppermute | solution.py:27
  52.6 198.1 %reduce-scatter.4.cloned.1.call-start = ((), (), s32[]{:S(2)}) async-start(), calls=%async_computation.5 | async-start | bytes 5242880 | tf_op jit(solution)/shard_map/reduce_scatter | solution.py:1168
  53.0 13.6 %collective-permute-start.14 = (bf16[256,1024]{1,0:T(8,128)(2,1)}, bf16[256,1024]{1,0:T(8,128)(2,1)S(1)}, u32[]{:S(2)}, u32[]{:S(2)}) collective-permute-start(bf16[256,1024]{1,0:T(8,128)(2,1)} %collective-permute-done.6.refs_9_.refs_15_.refs_18_.refs_23_), channel_id=1, source_target_pairs={{0,8},{4,12},{8,0},{12,4},{16,24},{20,28},{24,16},{28,20},{1,9},{5... | collective-permute-start | bytes 1572872 | tf_op jit(solution)/shard_map/ppermute | solution.py:21
  53.7 13.8 %collective-permute-start.10 = (bf16[256,1024]{1,0:T(8,128)(2,1)}, bf16[256,1024]{1,0:T(8,128)(2,1)}, u32[]{:S(2)}, u32[]{:S(2)}) collective-permute-start(bf16[256,1024]{1,0:T(8,128)(2,1)} %collective-permute-done.4.refs_7_.refs_13_.refs_16_.refs_21_), channel_id=1, source_target_pairs={{0,4},{4,0},{8,12},{12,8},{16,20},{20,16},{24,28},{28,24},{1,5},{5... | collective-permute-start | bytes 1572872 | tf_op jit(solution)/shard_map/ppermute | solution.py:21
  54.3 15.9 %collective-permute-start.7 = (bf16[80,4096]{1,0:T(8,128)(2,1)}, bf16[80,4096]{1,0:T(8,128)(2,1)S(1)}, u32[]{:S(2)}, u32[]{:S(2)}) collective-permute-start(bf16[80,4096]{1,0:T(8,128)(2,1)} %get-tuple-element.967.refs_5_.refs_6_), channel_id=1, source_target_pairs={{0,4},{4,0},{8,12},{12,8},{16,20},{20,16},{24,28},{28,24},{1,5},{5... | collective-permute-start | bytes 1966088 | tf_op jit(solution)/shard_map/ppermute | solution.py:21
  54.3 17.0 %collective-permute-start.8 = (bf16[80,4096]{1,0:T(8,128)(2,1)}, bf16[80,4096]{1,0:T(8,128)(2,1)S(1)}, u32[]{:S(2)}, u32[]{:S(2)}) collective-permute-start(bf16[80,4096]{1,0:T(8,128)(2,1)} %get-tuple-element.968.refs_6_.refs_7_), channel_id=1, source_target_pairs={{0,4},{4,0},{8,12},{12,8},{16,20},{20,16},{24,28},{28,24},{1,5},{5... | collective-permute-start | bytes 1966088 | tf_op jit(solution)/shard_map/ppermute | solution.py:21
  54.9 14.3 %collective-permute-start.13 = (bf16[272,1024]{1,0:T(8,128)(2,1)}, bf16[272,1024]{1,0:T(8,128)(2,1)S(1)}, u32[]{:S(2)}, u32[]{:S(2)}) collective-permute-start(bf16[272,1024]{1,0:T(8,128)(2,1)} %collective-permute-done.3.refs_6_.refs_12_.refs_15_.refs_20_), channel_id=1, source_target_pairs={{0,16},{4,20},{8,24},{12,28},{16,0},{20,4},{24,8},{28,12},{1,17},{... | collective-permute-start | bytes 1671176 | tf_op jit(solution)/shard_map/ppermute | solution.py:21
  74.8 24.8 %collective-permute-start.17 = (bf16[80,4096]{1,0:T(8,128)(2,1)}, bf16[80,4096]{1,0:T(8,128)(2,1)}, u32[]{:S(2)}, u32[]{:S(2)}) collective-permute-start(bf16[80,4096]{1,0:T(8,128)(2,1)} %get-tuple-element.967.refs_5_.refs_6_), channel_id=1, source_target_pairs={{0,8},{4,12},{8,0},{12,4},{16,24},{20,28},{24,16},{28,20},{1,9},{5... | collective-permute-start | bytes 1966088 | tf_op jit(solution)/shard_map/ppermute | solution.py:21
  75.6 29.6 %collective-permute-start.18 = (bf16[80,4096]{1,0:T(8,128)(2,1)}, bf16[80,4096]{1,0:T(8,128)(2,1)}, u32[]{:S(2)}, u32[]{:S(2)}) collective-permute-start(bf16[80,4096]{1,0:T(8,128)(2,1)} %get-tuple-element.968.refs_6_.refs_7_), channel_id=1, source_target_pairs={{0,8},{4,12},{8,0},{12,4},{16,24},{20,28},{24,16},{28,20},{1,9},{5... | collective-permute-start | bytes 1966088 | tf_op jit(solution)/shard_map/ppermute | solution.py:21
  76.3 28.8 %collective-permute-start.19 = (bf16[80,4096]{1,0:T(8,128)(2,1)}, bf16[80,4096]{1,0:T(8,128)(2,1)}, u32[]{:S(2)}, u32[]{:S(2)}) collective-permute-start(bf16[80,4096]{1,0:T(8,128)(2,1)} %get-tuple-element.967.refs_5_.refs_6_), channel_id=1, source_target_pairs={{0,16},{4,20},{8,24},{12,28},{16,0},{20,4},{24,8},{28,12},{1,17},{... | collective-permute-start | bytes 1966088 | tf_op jit(solution)/shard_map/ppermute | solution.py:21
  77.1 28.9 %collective-permute-start.20 = (bf16[80,4096]{1,0:T(8,128)(2,1)}, bf16[80,4096]{1,0:T(8,128)(2,1)}, u32[]{:S(2)}, u32[]{:S(2)}) collective-permute-start(bf16[80,4096]{1,0:T(8,128)(2,1)} %get-tuple-element.968.refs_6_.refs_7_), channel_id=1, source_target_pairs={{0,16},{4,20},{8,24},{12,28},{16,0},{20,4},{24,8},{28,12},{1,17},{... | collective-permute-start | bytes 1966088 | tf_op jit(solution)/shard_map/ppermute | solution.py:21
  106.0 16.8 %collective-permute-start.21 = (bf16[80,4096]{1,0:T(8,128)(2,1)}, bf16[80,4096]{1,0:T(8,128)(2,1)S(1)}, u32[]{:S(2)}, u32[]{:S(2)}) collective-permute-start(bf16[80,4096]{1,0:T(8,128)(2,1)} %collective-permute-done.17.refs_7_.refs_8_), channel_id=1, source_target_pairs={{0,4},{4,0},{8,12},{12,8},{16,20},{20,16},{24,28},{28,24},{1,5},{5... | collective-permute-start | bytes 1966088 | tf_op jit(solution)/shard_map/ppermute | solution.py:21
  107.9 16.7 %collective-permute-start.23 = (bf16[80,4096]{1,0:T(8,128)(2,1)}, bf16[80,4096]{1,0:T(8,128)(2,1)}, u32[]{:S(2)}, u32[]{:S(2)}) collective-permute-start(bf16[80,4096]{1,0:T(8,128)(2,1)} %collective-permute-done.17.refs_7_.refs_8_), channel_id=1, source_target_pairs={{0,16},{4,20},{8,24},{12,28},{16,0},{20,4},{24,8},{28,12},{1,17},{... | collective-permute-start | bytes 1966088 | tf_op jit(solution)/shard_map/ppermute | solution.py:21
  108.6 14.2 %collective-permute-start.22 = (bf16[80,4096]{1,0:T(8,128)(2,1)}, bf16[80,4096]{1,0:T(8,128)(2,1)}, u32[]{:S(2)}, u32[]{:S(2)}) collective-permute-start(bf16[80,4096]{1,0:T(8,128)(2,1)} %collective-permute-done.18.refs_8_.refs_9_), channel_id=1, source_target_pairs={{0,4},{4,0},{8,12},{12,8},{16,20},{20,16},{24,28},{28,24},{1,5},{5... | collective-permute-start | bytes 1966088 | tf_op jit(solution)/shard_map/ppermute | solution.py:21
  108.9 16.4 %collective-permute-start.24 = (bf16[80,4096]{1,0:T(8,128)(2,1)}, bf16[80,4096]{1,0:T(8,128)(2,1)}, u32[]{:S(2)}, u32[]{:S(2)}) collective-permute-start(bf16[80,4096]{1,0:T(8,128)(2,1)} %collective-permute-done.20.refs_10_.refs_11_), channel_id=1, source_target_pairs={{0,8},{4,12},{8,0},{12,4},{16,24},{20,28},{24,16},{28,20},{1,9},{5... | collective-permute-start | bytes 1966088 | tf_op jit(solution)/shard_map/ppermute | solution.py:21
  117.8 5.0 %collective-permute-start.25 = (f32[2,1024]{1,0:T(2,128)}, f32[2,1024]{1,0:T(2,128)S(1)}, u32[]{:S(2)}, u32[]{:S(2)}) collective-permute-start(f32[2,1024]{1,0:T(2,128)} %get-tuple-element.719), channel_id=1, source_target_pairs={{0,1},{1,2},{2,3},{4,5},{5,6},{6,7},{8,9},{9,10},{10,11},{12,13},{... | collective-permute-start | bytes 24584 | tf_op jit(solution)/shard_map/ppermute | solution.py:27
  125.3 3.1 collective-permute-start.26
  126.4 3.9 %collective-permute-start.28 = (bf16[80,4096]{1,0:T(8,128)(2,1)}, bf16[80,4096]{1,0:T(8,128)(2,1)}, u32[]{:S(2)}, u32[]{:S(2)}) collective-permute-start(bf16[80,4096]{1,0:T(8,128)(2,1)} %collective-permute-done.23.refs_11_.refs_12_), channel_id=1, source_target_pairs={{0,4},{4,0},{8,12},{12,8},{16,20},{20,16},{24,28},{28,24},{1,5},{5... | collective-permute-start | bytes 1966088 | tf_op jit(solution)/shard_map/ppermute | solution.py:21
  126.9 4.4 %collective-permute-start.29 = (bf16[80,4096]{1,0:T(8,128)(2,1)}, bf16[80,4096]{1,0:T(8,128)(2,1)}, u32[]{:S(2)}, u32[]{:S(2)}) collective-permute-start(bf16[80,4096]{1,0:T(8,128)(2,1)} %collective-permute-done.24.refs_12_.refs_13_), channel_id=1, source_target_pairs={{0,4},{4,0},{8,12},{12,8},{16,20},{20,16},{24,28},{28,24},{1,5},{5... | collective-permute-start | bytes 1966088 | tf_op jit(solution)/shard_map/ppermute | solution.py:21
  131.2 9.3 %collective-permute-start.31 = (bf16[1536,1024]{1,0:T(8,128)(2,1)}, bf16[1536,1024]{1,0:T(8,128)(2,1)}, u32[]{:S(2)}, u32[]{:S(2)}) collective-permute-start(bf16[1536,1024]{1,0:T(8,128)(2,1)} %all-gather.9.cloned.1.call-done.refs_7_.refs_4_), channel_id=1, source_target_pairs={{0,4},{4,0},{8,12},{12,8},{16,20},{20,16},{24,28},{28,24},{1,5},{5... | collective-permute-start | bytes 9437192 | tf_op jit(solution)/shard_map/ppermute | solution.py:21
  131.6 8.9 %collective-permute-start.30 = (bf16[512,1024]{1,0:T(8,128)(2,1)}, bf16[512,1024]{1,0:T(8,128)(2,1)}, u32[]{:S(2)}, u32[]{:S(2)}) collective-permute-start(bf16[512,1024]{1,0:T(8,128)(2,1)} %refs_3_.2), channel_id=1, source_target_pairs={{0,4},{4,0},{8,12},{12,8},{16,20},{20,16},{24,28},{28,24},{1,5},{5... | collective-permute-start | bytes 3145736 | tf_op jit(solution)/shard_map/ppermute | solution.py:21
  140.5 10.1 %collective-permute-start.35 = (bf16[3,256,1024]{2,1,0:T(8,128)(2,1)}, bf16[3,256,1024]{2,1,0:T(8,128)(2,1)}, u32[]{:S(2)}, u32[]{:S(2)}) collective-permute-start(bf16[3,256,1024]{2,1,0:T(8,128)(2,1)} %get-tuple-element.1138.refs_11_.refs_1_), channel_id=1, source_target_pairs={{0,4},{4,0},{8,12},{12,8},{16,20},{20,16},{24,28},{28,24},{1,5},{5... | collective-permute-start | bytes 4718600 | tf_op jit(solution)/shard_map/ppermute | solution.py:21
  140.9 9.6 %collective-permute-start.32 = (bf16[2,256,1024]{2,1,0:T(8,128)(2,1)}, bf16[2,256,1024]{2,1,0:T(8,128)(2,1)}, u32[]{:S(2)}, u32[]{:S(2)}) collective-permute-start(bf16[2,256,1024]{2,1,0:T(8,128)(2,1)} %get-tuple-element.987.refs_1_), channel_id=1, source_target_pairs={{0,4},{4,0},{8,12},{12,8},{16,20},{20,16},{24,28},{28,24},{1,5},{5... | collective-permute-start | bytes 3145736 | tf_op jit(solution)/shard_map/ppermute | solution.py:21
  141.1 9.5 %collective-permute-start.33 = (bf16[256,2048]{1,0:T(8,128)(2,1)}, bf16[256,2048]{1,0:T(8,128)(2,1)}, u32[]{:S(2)}, u32[]{:S(2)}) collective-permute-start(bf16[256,2048]{1,0:T(8,128)(2,1)} %get-tuple-element.855.refs_2_), channel_id=1, source_target_pairs={{0,4},{4,0},{8,12},{12,8},{16,20},{20,16},{24,28},{28,24},{1,5},{5... | collective-permute-start | bytes 3145736 | tf_op jit(solution)/shard_map/ppermute | solution.py:21
  141.4 9.1 %collective-permute-start.34 = (bf16[256,1024]{1,0:T(8,128)(2,1)}, bf16[256,1024]{1,0:T(8,128)(2,1)S(1)}, u32[]{:S(2)}, u32[]{:S(2)}) collective-permute-start(bf16[256,1024]{1,0:T(8,128)(2,1)} %get-tuple-element.1091.refs_9_), channel_id=1, source_target_pairs={{0,4},{4,0},{8,12},{12,8},{16,20},{20,16},{24,28},{28,24},{1,5},{5... | collective-permute-start | bytes 1572872 | tf_op jit(solution)/shard_map/ppermute | solution.py:21
  151.0 8.3 %collective-permute-start.36 = (bf16[256,1024]{1,0:T(8,128)(2,1)}, bf16[256,1024]{1,0:T(8,128)(2,1)}, u32[]{:S(2)}, u32[]{:S(2)}) collective-permute-start(bf16[256,1024]{1,0:T(8,128)(2,1)} %get-tuple-element.991.refs_3_), channel_id=1, source_target_pairs={{0,4},{4,0},{8,12},{12,8},{16,20},{20,16},{24,28},{28,24},{1,5},{5... | collective-permute-start | bytes 1572872 | tf_op jit(solution)/shard_map/ppermute | solution.py:21
  159.3 126.1 %reduce-scatter.6.cloned.1.call-start = ((), (), s32[]{:S(2)}) async-start(), calls=%async_computation.6 | async-start | bytes 2621440 | tf_op jit(solution)/shard_map/reduce_scatter | solution.py:1168
  167.2 19.4 %collective-permute-start.42 = (bf16[256,4096]{1,0:T(8,128)(2,1)}, bf16[256,4096]{1,0:T(8,128)(2,1)}, u32[]{:S(2)}, u32[]{:S(2)}) collective-permute-start(bf16[256,4096]{1,0:T(8,128)(2,1)} %shard_map.455.refs_4_.refs_3_), channel_id=1, source_target_pairs={{0,4},{4,0},{8,12},{12,8},{16,20},{20,16},{24,28},{28,24},{1,5},{5... | collective-permute-start | bytes 6291464 | tf_op jit(solution)/shard_map/ppermute | solution.py:21
  171.7 22.2 %collective-permute-start.38 = (bf16[128,1024]{1,0:T(8,128)(2,1)}, bf16[128,1024]{1,0:T(8,128)(2,1)S(1)}, u32[]{:S(2)}, u32[]{:S(2)}) collective-permute-start(bf16[128,1024]{1,0:T(8,128)(2,1)} %get-tuple-element.992), channel_id=1, source_target_pairs={{0,8},{4,12},{8,0},{12,4},{16,24},{20,28},{24,16},{28,20},{1,9},{5... | collective-permute-start | bytes 786440 | tf_op jit(solution)/shard_map/ppermute | solution.py:21
  172.4 21.5 %collective-permute-start.39 = (bf16[128,1024]{1,0:T(8,128)(2,1)}, bf16[128,1024]{1,0:T(8,128)(2,1)S(1)}, u32[]{:S(2)}, u32[]{:S(2)}) collective-permute-start(bf16[128,1024]{1,0:T(8,128)(2,1)} %get-tuple-element.993), channel_id=1, source_target_pairs={{0,16},{4,20},{8,24},{12,28},{16,0},{20,4},{24,8},{28,12},{1,17},{... | collective-permute-start | bytes 786440 | tf_op jit(solution)/shard_map/ppermute | solution.py:21
  173.1 20.8 %collective-permute-start.40 = (bf16[128,1024]{1,0:T(8,128)(2,1)}, bf16[128,1024]{1,0:T(8,128)(2,1)S(1)}, u32[]{:S(2)}, u32[]{:S(2)}) collective-permute-start(bf16[128,1024]{1,0:T(8,128)(2,1)} %get-tuple-element.994), channel_id=1, source_target_pairs={{0,24},{4,28},{8,16},{12,20},{16,8},{20,12},{24,0},{28,4},{1,25},{... | collective-permute-start | bytes 786440 | tf_op jit(solution)/shard_map/ppermute | solution.py:21
  184.3 9.5 %collective-permute-start.41 = (f32[2,1024]{1,0:T(2,128)}, f32[2,1024]{1,0:T(2,128)S(1)}, u32[]{:S(2)}, u32[]{:S(2)}) collective-permute-start(f32[2,1024]{1,0:T(2,128)} %get-tuple-element.1032.refs_2_), channel_id=1, source_target_pairs={{1,0},{2,1},{3,2},{5,4},{6,5},{7,6},{9,8},{10,9},{11,10},{13,12},{... | collective-permute-start | bytes 24584 | tf_op jit(solution)/shard_map/ppermute | solution.py:27
  193.9 47.7 %collective-permute-start.49 = (bf16[128,4096]{1,0:T(8,128)(2,1)}, bf16[128,4096]{1,0:T(8,128)(2,1)}, u32[]{:S(2)}, u32[]{:S(2)}) collective-permute-start(bf16[128,4096]{1,0:T(8,128)(2,1)} %get-tuple-element.1077), channel_id=1, source_target_pairs={{0,8},{4,12},{8,0},{12,4},{16,24},{20,28},{24,16},{28,20},{1,9},{5... | collective-permute-start | bytes 3145736 | tf_op jit(solution)/shard_map/ppermute | solution.py:21
  194.8 46.8 %collective-permute-start.50 = (bf16[128,4096]{1,0:T(8,128)(2,1)}, bf16[128,4096]{1,0:T(8,128)(2,1)}, u32[]{:S(2)}, u32[]{:S(2)}) collective-permute-start(bf16[128,4096]{1,0:T(8,128)(2,1)} %get-tuple-element.1078), channel_id=1, source_target_pairs={{0,16},{4,20},{8,24},{12,28},{16,0},{20,4},{24,8},{28,12},{1,17},{... | collective-permute-start | bytes 3145736 | tf_op jit(solution)/shard_map/ppermute | solution.py:21
  195.5 46.2 %collective-permute-start.51 = (bf16[128,4096]{1,0:T(8,128)(2,1)}, bf16[128,4096]{1,0:T(8,128)(2,1)}, u32[]{:S(2)}, u32[]{:S(2)}) collective-permute-start(bf16[128,4096]{1,0:T(8,128)(2,1)} %get-tuple-element.1079), channel_id=1, source_target_pairs={{0,24},{4,28},{8,16},{12,20},{16,8},{20,12},{24,0},{28,4},{1,25},{... | collective-permute-start | bytes 3145736 | tf_op jit(solution)/shard_map/ppermute | solution.py:21
  204.6 4.3 %collective-permute-start.43 = (f32[8,1024]{1,0:T(8,128)}, f32[8,1024]{1,0:T(8,128)S(1)}, u32[]{:S(2)}, u32[]{:S(2)}) collective-permute-start(f32[8,1024]{1,0:T(8,128)} %get-tuple-element.1058.refs_1_), channel_id=1, source_target_pairs={{0,1},{1,0},{2,3},{3,2},{4,5},{5,4},{6,7},{7,6},{8,9},{9,8},{10,11... | collective-permute-start | bytes 98312 | tf_op jit(solution)/shard_map/ppermute | solution.py:32
  209.6 9.0 %collective-permute-start.44 = (f32[16,1024]{1,0:T(8,128)S(1)}, f32[16,1024]{1,0:T(8,128)S(1)}, u32[]{:S(2)}, u32[]{:S(2)}) collective-permute-start(f32[16,1024]{1,0:T(8,128)S(1)} %pad_maximum_fusion.1), channel_id=1, source_target_pairs={{0,2},{1,3},{2,0},{3,1},{4,6},{5,7},{6,4},{7,5},{8,10},{9,11},{10,... | collective-permute-start | bytes 196616 | tf_op jit(solution)/shard_map/ppermute | solution.py:32
  212.0 9.2 %collective-permute-start.45 = (bf16[256,512]{1,0:T(8,128)(2,1)}, bf16[256,512]{1,0:T(8,128)(2,1)S(1)}, u32[]{:S(2)}, u32[]{:S(2)}) collective-permute-start(bf16[256,512]{1,0:T(8,128)(2,1)} %get-tuple-element.1066.refs_1_), channel_id=1, source_target_pairs={{0,4},{4,0},{8,12},{12,8},{16,20},{20,16},{24,28},{28,24},{1,5},{5... | collective-permute-start | bytes 786440 | tf_op jit(solution)/shard_map/ppermute | solution.py:21
  218.6 4.0 %collective-permute-start.46 = (bf16[256,512]{1,0:T(8,128)(2,1)}, bf16[256,512]{1,0:T(8,128)(2,1)S(1)}, u32[]{:S(2)}, u32[]{:S(2)}) collective-permute-start(bf16[256,512]{1,0:T(8,128)(2,1)} %get-tuple-element.1067.refs_2_), channel_id=1, source_target_pairs={{0,4},{4,0},{8,12},{12,8},{16,20},{20,16},{24,28},{28,24},{1,5},{5... | collective-permute-start | bytes 786440 | tf_op jit(solution)/shard_map/ppermute | solution.py:21
  221.2 14.2 %collective-permute-start.47 = (bf16[256,512]{1,0:T(8,128)(2,1)}, bf16[256,512]{1,0:T(8,128)(2,1)S(1)}, u32[]{:S(2)}, u32[]{:S(2)}) collective-permute-start(bf16[256,512]{1,0:T(8,128)(2,1)} %get-tuple-element.1063.refs_16_.refs_5_), channel_id=1, source_target_pairs={{0,4},{4,0},{8,12},{12,8},{16,20},{20,16},{24,28},{28,24},{1,5},{5... | collective-permute-start | bytes 786440 | tf_op jit(solution)/shard_map/ppermute | solution.py:21
  222.6 12.9 %collective-permute-start.48 = (bf16[256,512]{1,0:T(8,128)(2,1)}, bf16[256,512]{1,0:T(8,128)(2,1)}, u32[]{:S(2)}, u32[]{:S(2)}) collective-permute-start(bf16[256,512]{1,0:T(8,128)(2,1)} %get-tuple-element.1064.refs_17_.refs_6_), channel_id=1, source_target_pairs={{0,4},{4,0},{8,12},{12,8},{16,20},{20,16},{24,28},{28,24},{1,5},{5... | collective-permute-start | bytes 786440 | tf_op jit(solution)/shard_map/ppermute | solution.py:21
  241.7 94.5 %reduce-scatter.8.cloned.1.call-start = ((), (), s32[]{:S(2)}) async-start(), calls=%async_computation.7 | async-start | bytes 1638400 | tf_op jit(solution)/shard_map/reduce_scatter | solution.py:1168
  241.7 9.0 %collective-permute-start.52 = (bf16[2,256,1024]{2,1,0:T(8,128)(2,1)}, bf16[2,256,1024]{2,1,0:T(8,128)(2,1)}, u32[]{:S(2)}, u32[]{:S(2)}) collective-permute-start(bf16[2,256,1024]{2,1,0:T(8,128)(2,1)} %get-tuple-element.1140.refs_3_), channel_id=1, source_target_pairs={{0,4},{4,0},{8,12},{12,8},{16,20},{20,16},{24,28},{28,24},{1,5},{5... | collective-permute-start | bytes 3145736 | tf_op jit(solution)/shard_map/ppermute | solution.py:21
  243.4 7.3 %collective-permute-start.53 = (f32[2,1024]{1,0:T(2,128)S(1)}, f32[2,1024]{1,0:T(2,128)S(1)}, u32[]{:S(2)}, u32[]{:S(2)}) collective-permute-start(f32[2,1024]{1,0:T(2,128)S(1)} %copy-done.30), channel_id=1, source_target_pairs={{1,0},{2,1},{3,2},{5,4},{6,5},{7,6},{9,8},{10,9},{11,10},{13,12},{... | collective-permute-start | bytes 24584 | tf_op jit(solution)/shard_map/ppermute | solution.py:27
  252.8 15.1 %collective-permute-start.54 = (bf16[128,1024]{1,0:T(8,128)(2,1)}, bf16[128,1024]{1,0:T(8,128)(2,1)S(1)}, u32[]{:S(2)}, u32[]{:S(2)}) collective-permute-start(bf16[128,1024]{1,0:T(8,128)(2,1)} %get-tuple-element.1267), channel_id=1, source_target_pairs={{0,8},{4,12},{8,0},{12,4},{16,24},{20,28},{24,16},{28,20},{1,9},{5... | collective-permute-start | bytes 786440 | tf_op jit(solution)/shard_map/ppermute | solution.py:21
  254.1 13.8 %collective-permute-start.55 = (bf16[128,1024]{1,0:T(8,128)(2,1)}, bf16[128,1024]{1,0:T(8,128)(2,1)S(1)}, u32[]{:S(2)}, u32[]{:S(2)}) collective-permute-start(bf16[128,1024]{1,0:T(8,128)(2,1)} %get-tuple-element.1266), channel_id=1, source_target_pairs={{0,16},{4,20},{8,24},{12,28},{16,0},{20,4},{24,8},{28,12},{1,17},{... | collective-permute-start | bytes 786440 | tf_op jit(solution)/shard_map/ppermute | solution.py:21
  255.4 12.5 %collective-permute-start.56 = (bf16[128,1024]{1,0:T(8,128)(2,1)}, bf16[128,1024]{1,0:T(8,128)(2,1)}, u32[]{:S(2)}, u32[]{:S(2)}) collective-permute-start(bf16[128,1024]{1,0:T(8,128)(2,1)} %get-tuple-element.1265), channel_id=1, source_target_pairs={{0,24},{4,28},{8,16},{12,20},{16,8},{20,12},{24,0},{28,4},{1,25},{... | collective-permute-start | bytes 786440 | tf_op jit(solution)/shard_map/ppermute | solution.py:21
  268.7 16.7 %collective-permute-start.57 = (bf16[272,1024]{1,0:T(8,128)(2,1)}, bf16[272,1024]{1,0:T(8,128)(2,1)S(1)}, u32[]{:S(2)}, u32[]{:S(2)}) collective-permute-start(bf16[272,1024]{1,0:T(8,128)(2,1)} %get-tuple-element.1152), channel_id=1, source_target_pairs={{0,8},{4,12},{8,0},{12,4},{16,24},{20,28},{24,16},{28,20},{1,9},{5... | collective-permute-start | bytes 1671176 | tf_op jit(solution)/shard_map/ppermute | solution.py:21
  270.0 15.4 %collective-permute-start.58 = (bf16[272,1024]{1,0:T(8,128)(2,1)}, bf16[272,1024]{1,0:T(8,128)(2,1)}, u32[]{:S(2)}, u32[]{:S(2)}) collective-permute-start(bf16[272,1024]{1,0:T(8,128)(2,1)} %get-tuple-element.1153), channel_id=1, source_target_pairs={{0,16},{4,20},{8,24},{12,28},{16,0},{20,4},{24,8},{28,12},{1,17},{... | collective-permute-start | bytes 1671176 | tf_op jit(solution)/shard_map/ppermute | solution.py:21
  271.3 23.6 %collective-permute-start.59 = (bf16[272,1024]{1,0:T(8,128)(2,1)}, bf16[272,1024]{1,0:T(8,128)(2,1)}, u32[]{:S(2)}, u32[]{:S(2)}) collective-permute-start(bf16[272,1024]{1,0:T(8,128)(2,1)} %get-tuple-element.1154), channel_id=1, source_target_pairs={{0,24},{4,28},{8,16},{12,20},{16,8},{20,12},{24,0},{28,4},{1,25},{... | collective-permute-start | bytes 1671176 | tf_op jit(solution)/shard_map/ppermute | solution.py:21
  296.8 5.9 %collective-permute-start.60 = (bf16[64,1024]{1,0:T(8,128)(2,1)}, bf16[64,1024]{1,0:T(8,128)(2,1)S(1)}, u32[]{:S(2)}, u32[]{:S(2)}) collective-permute-start(bf16[64,1024]{1,0:T(8,128)(2,1)} %get-tuple-element.1270), channel_id=1, source_target_pairs={{0,8},{4,12},{8,0},{12,4},{16,24},{20,28},{24,16},{28,20},{1,9},{5... | collective-permute-start | bytes 393224 | tf_op jit(solution)/shard_map/ppermute | solution.py:21
  298.0 5.8 %collective-permute-start.61 = (bf16[64,1024]{1,0:T(8,128)(2,1)}, bf16[64,1024]{1,0:T(8,128)(2,1)S(1)}, u32[]{:S(2)}, u32[]{:S(2)}) collective-permute-start(bf16[64,1024]{1,0:T(8,128)(2,1)} %get-tuple-element.1269), channel_id=1, source_target_pairs={{0,16},{4,20},{8,24},{12,28},{16,0},{20,4},{24,8},{28,12},{1,17},{... | collective-permute-start | bytes 393224 | tf_op jit(solution)/shard_map/ppermute | solution.py:21
  298.2 5.7 %collective-permute-start.62 = (bf16[64,1024]{1,0:T(8,128)(2,1)}, bf16[64,1024]{1,0:T(8,128)(2,1)}, u32[]{:S(2)}, u32[]{:S(2)}) collective-permute-start(bf16[64,1024]{1,0:T(8,128)(2,1)} %get-tuple-element.1268), channel_id=1, source_target_pairs={{0,24},{4,28},{8,16},{12,20},{16,8},{20,12},{24,0},{28,4},{1,25},{... | collective-permute-start | bytes 393224 | tf_op jit(solution)/shard_map/ppermute | solution.py:21
  303.8 13.2 %collective-permute-start.63 = (bf16[80,1024]{1,0:T(8,128)(2,1)}, bf16[80,1024]{1,0:T(8,128)(2,1)S(1)}, u32[]{:S(2)}, u32[]{:S(2)}) collective-permute-start(bf16[80,1024]{1,0:T(8,128)(2,1)} %get-tuple-element.1191), channel_id=1, source_target_pairs={{0,1},{1,0},{2,3},{3,2},{4,5},{5,4},{6,7},{7,6},{8,9},{9,8},{10,11... | collective-permute-start | bytes 491528 | tf_op jit(solution)/shard_map/ppermute | solution.py:32
  303.8 16.0 %collective-permute-start.64 = (bf16[80,1024]{1,0:T(8,128)(2,1)}, bf16[80,1024]{1,0:T(8,128)(2,1)S(1)}, u32[]{:S(2)}, u32[]{:S(2)}) collective-permute-start(bf16[80,1024]{1,0:T(8,128)(2,1)} %get-tuple-element.1192), channel_id=1, source_target_pairs={{0,2},{1,3},{2,0},{3,1},{4,6},{5,7},{6,4},{7,5},{8,10},{9,11},{10,... | collective-permute-start | bytes 491528 | tf_op jit(solution)/shard_map/ppermute | solution.py:32
  305.6 26.0 %collective-permute-start.65 = (bf16[80,1024]{1,0:T(8,128)(2,1)}, bf16[80,1024]{1,0:T(8,128)(2,1)S(1)}, u32[]{:S(2)}, u32[]{:S(2)}) collective-permute-start(bf16[80,1024]{1,0:T(8,128)(2,1)} %get-tuple-element.1193), channel_id=1, source_target_pairs={{0,3},{1,2},{2,1},{3,0},{4,7},{5,6},{6,5},{7,4},{8,11},{9,10},{10,... | collective-permute-start | bytes 491528 | tf_op jit(solution)/shard_map/ppermute | solution.py:32
  332.3 3.2 collective-permute-start.66
  (41 other events, 295.3 us)
Sparse Core Ops, SparseCore 0:
  12.9 37.5 all-gather.6
  52.8 62.6 all-gather.8
  159.4 79.5 reduce-scatter.3
  241.8 43.5 reduce-scatter.5
  287.5 39.8 reduce-scatter.7

commit v8 on v7

--- a/solution.py
+++ b/solution.py
@@ -140,7 +140,7 @@
         c.wait()
 
 
-def call(body, info, small, large, raw, outs, big_outs, scratch, copies, us, limit):
+def call(body, info, small, large, raw, outs, big_outs, scratch, copies, us, limit, late=()):
     n_small, n_large, n_raw = len(small), len(large), len(raw)
     n_out, n_big = len(outs), len(big_outs)
 
@@ -161,8 +161,15 @@
         rest = take(len(refs) - at)
         loads = Loads(sems)
         pending = []
-        for (array, index), ref, buf in zip(large, large_refs, buffers):
-            pending.append(loads.start(ref if index is None else ref.at[index], buf))
+        for k, ((array, index), ref, buf) in enumerate(zip(large, large_refs, buffers)):
+            src = ref if index is None else ref.at[index]
+            pending.append((src, buf) if k in late else loads.start(src, buf))
+
+        def start_late():
+            for k in late:
+                pending[k] = loads.start(*pending[k])
+
+        loads.start_late = start_late
         stored = {}
 
         def get(k):
@@ -568,7 +575,7 @@
     return arrive
 
 
-def value_blocks(loads, raw, w, fshard, stretches):
+def value_blocks(loads, raw, w, fshard, stretches, after_first=None):
     order = relative_order()
     others = [m for m in order if m % 2 == 0 and m]
     each = fshard // stretches
@@ -578,6 +585,8 @@
         base = m - m % 2
         if base == 0:
             out[m] = [loads.start(own, w.at[pl.ds(at * fshard, fshard)])]
+            if at == 0 and after_first is not None:
+                after_first()
             continue
         out[m] = [
             loads.start(
@@ -659,6 +668,7 @@
         out_ref, df_ref, dr_ref = big
         w, fval = scratch
         blocks = value_blocks(loads, raw, w, fshard, stretches)
+        loads.start_late()
         half = len(order) // 2
         for k in range(2):
             hid_ref = get(k)
@@ -682,7 +692,7 @@
     return call(
         body, info, [], [(a, None) for a in (near, far, frec, mid, cot)], cv, [], [low, low, low],
         [pltpu.VMEM((wide, width), bf16), pltpu.VMEM((tokens, width), f32)],
-        value_copies(stretches), 7, 40)
+        value_copies(stretches), 7, 40, late=(2, 3, 4))
 
 
 def hidden_back(info, act, dfval, cv, fshard):
@@ -694,7 +704,7 @@
     def body(info, small, get, raw, outs, big, put, scratch, loads):
         (dpre_ref,) = big
         (wv,) = scratch
-        values = value_blocks(loads, raw, wv, fshard, stretches)
+        values = value_blocks(loads, raw, wv, fshard, stretches, loads.start_late)
         dfval_ref, act_ref = get(0), get(1)
         for at, m in enumerate(order):
             wait(values[m])
@@ -705,7 +715,7 @@
 
     return call(
         body, info, [], [(dfval, None), (act, None)], cv, [], [((tokens, wide), bf16)],
-        [pltpu.VMEM((wide, width), bf16)], value_copies(stretches) + len(order), 7, 40)[0]
+        [pltpu.VMEM((wide, width), bf16)], value_copies(stretches) + len(order), 7, 40, late=(1,))[0]
 
 
 def chan_back(info, dpre, dfrec, xb, entry, vec, pieces_ck, length, shard, fshard):
@@ -723,6 +733,7 @@
         wk, wc, df, dr, sum_ref = scratch
         arrive_c = recept_blocks(loads, steps_c, raw, wc, info, shard, width, wide)
         arrive = key_blocks(loads, steps_k, raw, wk, info, shard, fshard)
+        loads.start_late()
         dfrec_ref = get(0)
         arrive_c()
         @columns(width, STEP)
@@ -763,7 +774,7 @@
         [pltpu.VMEM((width, wide), bf16), pltpu.VMEM((width, width), bf16),
          pltpu.VMEM((tokens, width), f32), pltpu.VMEM((tokens, width), f32),
          pltpu.VMEM((2, 8, width), f32)],
-        1 + len(order), 10, 40)
+        1 + len(order), 10, 40, late=(2,))
 
 
 def mid_back(info, dxt, dxb, after, head, mid, cot, vec, kvr, wkv, rden, ent, pieces, spots, length, shard):

time: 347 us -> 346 us (level)
  transfers between devices with their start and end apart: 72 -> 72, of which waited for: 28 -> 27; matrix products, arithmetic and copies ran while one was open for 4% -> 4% of each run, Pallas kernels for 34% -> 33%
where the time goes in v8:
time: 346 us; the launch traced here: 344 us
  Pallas kernels  118 us (34%)
  waiting for transfers between devices  99.2 us (29%)
  starting transfers between devices  62.2 us (18%)
  blocking collectives  24.5 us (7%)
  local copies, waits for them, and re-layouts  15.2 us (4%)
  between operations  14.7 us (4%)
  other arithmetic  10.3 us (3%)
    pallas_call x16, Pallas kernels, call(): pl.pallas_call(kernel, out_shape=[jax.ShapeDtypeStruct(s, d) for s, d in...  113 us
    ppermute x58, waiting for transfers between devices, hop(): return lax.ppermute(value, 'seg', [(i, i ^ bit) for i in range(count)])  66.9 us
    ppermute x58, starting transfers between devices, hop(): return lax.ppermute(value, 'seg', [(i, i ^ bit) for i in range(count)])  45.1 us
    ppermute x5, waiting for transfers between devices, across(): return lax.ppermute(value, 'stretch', [(i, i ^ j) for i in range(count)])  27 us
    all_gather x1, blocking collectives, body(): v.everyone = lax.all_gather(v.sums, 'stretch')  12.8 us
    all_gather x1, blocking collectives, body(): v.heads = lax.all_gather(v.head_a, 'stretch')[0]  11.7 us
    ppermute x4, starting transfers between devices, along(): lax.ppermute(value, 'stretch', [(i, i + steps) for i in range(first, last)])  11.6 us
  transfers between devices with their start and end apart: 72, of which 27 were waited for; matrix products, arithmetic and copies ran while one was open for 4% of the time, Pallas kernels for 33%

profile of v8, /device:TPU:9, one launch (start us, length us, event | category | flops | bytes accessed | tf_op | source)
XLA Modules:
  0.0 344.4 jit_solution(18289591265034285722)
XLA Ops:
  8.0 1.7 constant_dynamic-slice_fusion.3
  9.7 3.0 shard_map.448
  13.6 1.2 collective-permute-start.3
  14.8 1.2 collective-permute-start.5
  17.1 3.2 collective-permute-start.2
  20.3 2.4 shard_map.449
  22.8 22.5 %collective-permute-done.4.refs_7_.refs_13_.refs_16_.refs_21_ = bf16[256,1024]{1,0:T(8,128)(2,1)} collective-permute-done((bf16[256,1024]{1,0:T(8,128)(2,1)}, bf16[256,1024]{1,0:T(8,128)(2,1)}, u32[]{:S(2)}, u32[]{:S(2)}) %collective-permute-start.4) | collective-permute-done | bytes 524320 | tf_op jit(solution)/shard_map/ppermute | solution.py:21
  45.3 1.8 collective-permute-done.6.refs_9_.refs_15_.refs_18_.refs_23_
  47.1 3.4 all-gather.7.cloned.1.call-done
  50.5 1.2 constant_dynamic-slice_fusion.2
  55.7 10.9 %collective-permute-done.14.refs_11_.refs_17_.refs_20_.refs_25_ = bf16[256,1024]{1,0:T(8,128)(2,1)S(1)} collective-permute-done((bf16[256,1024]{1,0:T(8,128)(2,1)}, bf16[256,1024]{1,0:T(8,128)(2,1)S(1)}, u32[]{:S(2)}, u32[]{:S(2)}) %collective-permute-start.14) | collective-permute-done | bytes 524320 | tf_op jit(solution)/shard_map/ppermute | solution.py:21
  67.6 1.5 collective-permute-done.13.refs_10_.refs_16_.refs_19_.refs_24_
  72.6 2.2 collective-permute-done.16.refs_19_.refs_25_.refs_28_.refs_33_
  78.4 8.4 %shard_map.450 = (f32[6,1024]{1,0:T(8,128)}, f32[16,1024]{1,0:T(8,128)}, f32[2,1024]{1,0:T(2,128)}, bf16[3,256,1024]{2,1,0:T(8,128)(2,1)}, f32[256,1024]{1,0:T(8...) custom-call(s32[3]{0:T(128)} %pad_add_fusion.refs_0_, bf16[2,1024]{1,0:T(2,128)(2,1)} %copy-done.32, ...), custom_call_target="tpu_custom_call" | custom-call | bytes 9000 | tf_op jit(solution)/shard_map/pallas_call | solution.py:197
  86.9 12.8 %all-gather.2.refs_1_ = f32[4,6,1024]{2,1,0:T(8,128)} all-gather(f32[1,6,1024]{2,1,0:T(8,128)} %bitcast.58), channel_id=2, replica_groups=mesh['seg'=8,'stretch'=4] {'stretch'}, dimensions={0}, use_global_device_ids=true | all-gather | bytes 122880 | tf_op jit(solution)/shard_map/all_gather | solution.py:1286
  99.6 5.5 %collective-permute-done.18.refs_8_.refs_9_ = bf16[80,4096]{1,0:T(8,128)(2,1)} collective-permute-done((bf16[80,4096]{1,0:T(8,128)(2,1)}, bf16[80,4096]{1,0:T(8,128)(2,1)}, u32[]{:S(2)}, u32[]{:S(2)}) %collective-permute-start.18) | collective-permute-done | bytes 655392 | tf_op jit(solution)/shard_map/ppermute | solution.py:21
  106.0 1.8 collective-permute-start.21
  109.6 8.2 %shard_map.451 = (f32[6,1024]{1,0:T(8,128)}, f32[2,1,1024]{2,1,0:T(1,128)}, f32[2,1,1024]{2,1,0:T(1,128)}, f32[2,1024]{1,0:T(2,128)}, bf16[256,1024]{1,0:T(8,128...) custom-call(s32[3]{0:T(128)} %pad_add_fusion.refs_0_, ...), custom_call_target="tpu_custom_call" | custom-call | bytes 7000 | tf_op jit(solution)/shard_map/pallas_call | solution.py:197
  117.8 3.3 collective-permute-start.25
  121.2 1.7 collective-permute-done.25.refs_1_
  122.9 1.7 collective-permute-done.23.refs_11_.refs_12_
  126.9 1.6 collective-permute-done.26.refs_17_.refs_18_
  131.8 8.7 %shard_map.452 = (f32[2,1024]{1,0:T(2,128)}, bf16[2,256,1024]{2,1,0:T(8,128)(2,1)}, bf16[256,2048]{1,0:T(8,128)(2,1)}, bf16[256,2048]{1,0:T(8,128)(2,1)}, bf16[2...) custom-call(s32[3]{0:T(128)} %pad_add_fusion.refs_0_, f32[2,1024]{1,0:T(2,128)} %copy-done.31, f32[2,1,1024]{2,1,0:T(1,128)} %refs_2_.5, ...), custom_call_target="tpu_custom_call" | custom-call | bytes 11000 | tf_op jit(solution)/shard_map/pallas_call | solution.py:197
  141.6 8.2 %shard_map.453 = (bf16[256,1024]{1,0:T(8,128)(2,1)}, bf16[256,1024]{1,0:T(8,128)(2,1)}, bf16[256,1024]{1,0:T(8,128)(2,1)}) custom-call(s32[3]{0:T(128)} %pad_add_fusion.refs_0_, bf16[256,2048]{1,0:T(8,128)(2,1)} %get-tuple-element.933.refs_1_, bf16[256,2048]{1,0:T(8,128)(2,1)} %get-tuple-element.855.refs_2_, f32[256,1024]{1,0:T(8,128)} %get-tuple-element.856.refs_3_, ...), custom_call_target="tpu_custom_call" | custom-call | bytes 7000 | tf_op jit(solution)/shard_map/pallas_call | solution.py:197
  150.4 1.7 collective-permute-done.37.refs_4_
  152.2 6.4 %shard_map.454 = bf16[2048,1024]{1,0:T(8,128)(2,1)} custom-call(s32[3]{0:T(128)} %pad_add_fusion.refs_0_, bf16[256,2048]{1,0:T(8,128)(2,1)} %get-tuple-element.933.refs_1_, bf16[256,2048]{1,0:T(8,128)(2,1)} %collective-permute-done.33.refs_2_, bf16[256,1024]{1,0:T(8,128)(2,1)} %get-tuple-element.960.refs_3_.refs_1_, ...), custom_call_target="tpu_custom_call" | custom-call | bytes 6000 | tf_op jit(solution)/shard_map/pallas_call | solution.py:197
  158.8 7.6 %shard_map.455.refs_4_.refs_3_ = bf16[256,4096]{1,0:T(8,128)(2,1)} custom-call(s32[3]{0:T(128)} %pad_add_fusion.refs_0_, bf16[256,1024]{1,0:T(8,128)(2,1)} %get-tuple-element.960.refs_3_.refs_1_, bf16[256,4096]{1,0:T(8,128)(2,1)} %get-tuple-element.961.refs_2_, bf16[512,1024]{1,0:T(8,128)(2,1)} %refs_3_.2, ...), custom_call_target="tpu_custom_call" | custom-call | bytes 7000 | tf_op jit(solution)/shard_map/pallas_call | solution.py:197
  166.9 4.0 %shard_map.457 = (bf16[128,1024]{1,0:T(8,128)(2,1)}, bf16[128,1024]{1,0:T(8,128)(2,1)}, bf16[128,1024]{1,0:T(8,128)(2,1)}, bf16[128,1024]{1,0:T(8,128)(2,1)}) custom-call(s32[3]{0:T(128)} %pad_add_fusion.refs_0_, bf16[2,256,1024]{2,1,0:T(8,128)(2,1)} %get-tuple-element.987.refs_1_, bf16[2,256,1024]{2,1,0:T(8,128)(2,1)} %collective-permute-done.32.refs_2_, ...), custom_call_target="tpu_custom_call" | custom-call | bytes 3000 | tf_op jit(solution)/shard_map/pallas_call | solution.py:197
  172.5 1.2 collective-permute-start.40
  173.7 9.7 %shard_map.456 = (f32[2,1024]{1,0:T(2,128)}, f32[2,1024]{1,0:T(2,128)}, bf16[256,1024]{1,0:T(8,128)(2,1)}, bf16[256,1024]{1,0:T(8,128)(2,1)}) custom-call(s32[3]{0:T(128)} %pad_add_fusion.refs_0_, f32[2,1024]{1,0:T(2,128)} %get-tuple-element.958.refs_1_, f32[16,1024]{1,0:T(8,128)} %get-tuple-element.1126.refs_5_.refs_3_.refs_2_.refs_10_, ...), custom_call_target="tpu_custom_call" | custom-call | bytes 10000 | tf_op jit(solution)/shard_map/pallas_call | solution.py:197
  183.4 2.3 collective-permute-start.41
  185.6 7.2 %shard_map.458 = (bf16[128,4096]{1,0:T(8,128)(2,1)}, bf16[128,4096]{1,0:T(8,128)(2,1)}, bf16[128,4096]{1,0:T(8,128)(2,1)}, bf16[128,4096]{1,0:T(8,128)(2,1)}) custom-call(s32[3]{0:T(128)} %pad_add_fusion.refs_0_, bf16[2,256,1024]{2,1,0:T(8,128)(2,1)} %get-tuple-element.987.refs_1_, bf16[2,256,1024]{2,1,0:T(8,128)(2,1)} %collective-permute-done.32.refs_2_, ...), custom_call_target="tpu_custom_call" | custom-call | bytes 7000 | tf_op jit(solution)/shard_map/pallas_call | solution.py:197
  194.5 1.2 collective-permute-start.51
  195.7 7.8 %shard_map.459 = (f32[8,1024]{1,0:T(8,128)}, f32[2,1024]{1,0:T(2,128)}, bf16[256,1024]{1,0:T(8,128)(2,1)}, bf16[256,512]{1,0:T(8,128)(2,1)}, bf16[256,512]{1,0:T...) custom-call(s32[3]{0:T(128)} %pad_add_fusion.refs_0_, ...), custom_call_target="tpu_custom_call" | custom-call | bytes 9000 | tf_op jit(solution)/shard_map/pallas_call | solution.py:197
  203.6 4.2 %collective-permute-done.43.refs_2_ = f32[8,1024]{1,0:T(8,128)S(1)} collective-permute-done((f32[8,1024]{1,0:T(8,128)}, f32[8,1024]{1,0:T(8,128)S(1)}, u32[]{:S(2)}, u32[]{:S(2)}) %collective-permute-start.43) | collective-permute-done | bytes 32800 | tf_op jit(solution)/shard_map/ppermute | solution.py:32
  208.6 2.3 collective-permute-start.44
  211.0 5.1 %collective-permute-start.45 = (bf16[256,512]{1,0:T(8,128)(2,1)}, bf16[256,512]{1,0:T(8,128)(2,1)S(1)}, u32[]{:S(2)}, u32[]{:S(2)}) collective-permute-start(bf16[256,512]{1,0:T(8,128)(2,1)} %get-tuple-element.1066.refs_1_), channel_id=1, source_target_pairs={{0,4},{4,0},{8,12},{12,8},{16,20},{20,16},{24,28},{28,24},{1,5},{5... | collective-permute-start | bytes 786440 | tf_op jit(solution)/shard_map/ppermute | solution.py:21
  216.1 4.3 %collective-permute-start.46 = (bf16[256,512]{1,0:T(8,128)(2,1)}, bf16[256,512]{1,0:T(8,128)(2,1)S(1)}, u32[]{:S(2)}, u32[]{:S(2)}) collective-permute-start(bf16[256,512]{1,0:T(8,128)(2,1)} %get-tuple-element.1067.refs_2_), channel_id=1, source_target_pairs={{0,4},{4,0},{8,12},{12,8},{16,20},{20,16},{24,28},{28,24},{1,5},{5... | collective-permute-start | bytes 786440 | tf_op jit(solution)/shard_map/ppermute | solution.py:21
  220.4 1.3 collective-permute-done.46.refs_4_
  222.1 12.5 %shard_map.460 = (f32[2,1,1024]{2,1,0:T(1,128)}, f32[2,1,1024]{2,1,0:T(1,128)}, f32[2,1,1024]{2,1,0:T(1,128)}, f32[2,1,1024]{2,1,0:T(1,128)}, f32[2,1024]{1,0:T(...) custom-call(s32[3]{0:T(128)} %pad_add_fusion.refs_0_, ...), custom_call_target="tpu_custom_call" | custom-call | bytes 14000 | tf_op jit(solution)/shard_map/pallas_call | solution.py:197
  235.3 5.5 %shard_map.461 = bf16[1024,1024]{1,0:T(8,128)(2,1)} custom-call(s32[3]{0:T(128)} %pad_add_fusion.refs_0_, bf16[256,512]{1,0:T(8,128)(2,1)} %get-tuple-element.1066.refs_1_, bf16[256,512]{1,0:T(8,128)(2,1)} %get-tuple-element.1067.refs_2_, bf16[256,512]{1,0:T(8,128)(2,1)} %copy-done.14, bf16[256,512]{1,0:T(8,128)(2,1)} %copy-done.15, ...), custom_call_target="tpu_custom_call" | custom-call | bytes 6000 | tf_op jit(solution)/shard_map/pallas_call | solution.py:197
  240.9 1.5 collective-permute-start.52
  242.4 2.8 collective-permute-start.53
  245.3 4.7 %shard_map.462 = bf16[640,1024]{1,0:T(8,128)(2,1)} custom-call(s32[3]{0:T(128)} %pad_add_fusion.refs_0_, bf16[128,4096]{1,0:T(8,128)(2,1)} %get-tuple-element.1110.refs_1_, bf16[128,4096]{1,0:T(8,128)(2,1)} %collective-permute-done.49.refs_2_, bf16[128,4096]{1,0:T(8,128)(2,1)} %collective-permute-done.50.refs_3_, ...), custom_call_target="tpu_custom_call" | custom-call | bytes 4000 | tf_op jit(solution)/shard_map/pallas_call | solution.py:197
  250.1 2.1 fusion.4
  252.2 1.3 collective-permute-start.54
  253.5 1.1 collective-permute-start.55
  254.8 5.2 %shard_map.463 = (f32[2,1024]{1,0:T(2,128)}, bf16[256,1024]{1,0:T(8,128)(2,1)}) custom-call(s32[3]{0:T(128)} %pad_add_fusion.refs_0_, f32[2,1024]{1,0:T(2,128)} %copy-done.25, f32[16,1024]{1,0:T(8,128)} %get-tuple-element.1126.refs_5_.refs_3_.refs_2_.refs_10_, bf16[256,1024]{1,0:T(8,128)(2,1)} %get-tuple-element.1127.refs_3_, ...), custom_call_target="tpu_custom_call" | custom-call | bytes 6000 | tf_op jit(solution)/shard_map/pallas_call | solution.py:197
  261.6 5.6 %shard_map.464 = (bf16[272,1024]{1,0:T(8,128)(2,1)}, bf16[272,1024]{1,0:T(8,128)(2,1)}, bf16[272,1024]{1,0:T(8,128)(2,1)}, bf16[272,1024]{1,0:T(8,128)(2,1)}) custom-call(s32[3]{0:T(128)} %pad_add_fusion.refs_0_, bf16[3,256,1024]{2,1,0:T(8,128)(2,1)} %get-tuple-element.1138.refs_11_.refs_1_, bf16[3,256,1024]{2,1,0:T(8,128)(2,1)} %collective-permute-done.35.refs_12_.refs_2_, ...), custom_call_target="tpu_custom_call" | custom-call | bytes 7000 | tf_op jit(solution)/shard_map/pallas_call | solution.py:197
  268.0 1.3 collective-permute-start.57
  269.3 1.1 collective-permute-start.58
  270.7 11.7 %all-gather.3 = f32[4,2,1024]{2,1,0:T(2,128)S(1)} all-gather(f32[1,2,1024]{2,1,0:T(2,128)S(1)} %bitcast.60), channel_id=3, replica_groups=mesh['seg'=8,'stretch'=4] {'stretch'}, dimensions={0}, use_global_device_ids=true | all-gather | bytes 40960 | tf_op jit(solution)/shard_map/all_gather | solution.py:1410
  282.4 2.1 convert_add_fusion
  284.6 9.6 %collective-permute-done.59.refs_4_ = bf16[272,1024]{1,0:T(8,128)(2,1)} collective-permute-done((bf16[272,1024]{1,0:T(8,128)(2,1)}, bf16[272,1024]{1,0:T(8,128)(2,1)}, u32[]{:S(2)}, u32[]{:S(2)}) %collective-permute-start.59) | collective-permute-done | bytes 557088 | tf_op jit(solution)/shard_map/ppermute | solution.py:21
  294.2 2.0 fusion.5
  297.5 1.3 collective-permute-start.62
  298.8 3.2 shard_map.465
  303.0 1.4 collective-permute-start.64
  304.4 1.2 collective-permute-start.65
  308.0 7.6 %collective-permute-done.63 = bf16[80,1024]{1,0:T(8,128)(2,1)S(1)} collective-permute-done((bf16[80,1024]{1,0:T(8,128)(2,1)}, bf16[80,1024]{1,0:T(8,128)(2,1)S(1)}, u32[]{:S(2)}, u32[]{:S(2)}) %collective-permute-start.63) | collective-permute-done | bytes 163872 | tf_op jit(solution)/shard_map/ppermute | solution.py:32
  315.6 3.1 collective-permute-done.64
  318.7 12.1 %collective-permute-done.65 = bf16[80,1024]{1,0:T(8,128)(2,1)S(1)} collective-permute-done((bf16[80,1024]{1,0:T(8,128)(2,1)}, bf16[80,1024]{1,0:T(8,128)(2,1)S(1)}, u32[]{:S(2)}, u32[]{:S(2)}) %collective-permute-start.65) | collective-permute-done | bytes 163872 | tf_op jit(solution)/shard_map/ppermute | solution.py:32
  331.5 1.5 collective-permute-start.66
  335.4 1.7 slice_convert_fusion
  (200 shorter events, 42.1 us)
Async XLA Ops:
  7.2 43.3 %all-gather.7.cloned.1.call-start = ((), (), s32[]{:S(2)}) async-start(), calls=%async_computation.3 | async-start | bytes 2359296 | tf_op jit(solution)/shard_map/all_gather | solution.py:1262
  12.7 118.5 %all-gather.9.cloned.1.call-start = ((), (), s32[]{:S(2)}) async-start(), calls=%async_computation.4 | async-start | bytes 3932160 | tf_op jit(solution)/shard_map/all_gather | solution.py:1271
  12.8 3.5 %collective-permute-start.1 = (bf16[256,1024]{1,0:T(8,128)(2,1)}, bf16[256,1024]{1,0:T(8,128)(2,1)S(1)}, u32[]{:S(2)}, u32[]{:S(2)}) collective-permute-start(bf16[256,1024]{1,0:T(8,128)(2,1)} %get-tuple-element.1043.refs_5_.refs_11_.refs_14_.refs_19_), channel_id=1, source_target_pairs={{0,4},{4,0},{8,12},{12,8},{16,20},{20,16},{24,28},{28,24},{1,5},{5... | collective-permute-start | bytes 1572872 | tf_op jit(solution)/shard_map/ppermute | solution.py:21
  13.6 33.5 %collective-permute-start.3 = (bf16[272,1024]{1,0:T(8,128)(2,1)}, bf16[272,1024]{1,0:T(8,128)(2,1)}, u32[]{:S(2)}, u32[]{:S(2)}) collective-permute-start(bf16[272,1024]{1,0:T(8,128)(2,1)} %get-tuple-element.1042.refs_4_.refs_10_.refs_13_.refs_18_), channel_id=1, source_target_pairs={{0,8},{4,12},{8,0},{12,4},{16,24},{20,28},{24,16},{28,20},{1,9},{5... | collective-permute-start | bytes 1671176 | tf_op jit(solution)/shard_map/ppermute | solution.py:21
  14.8 32.3 %collective-permute-start.5 = (bf16[272,1024]{1,0:T(8,128)(2,1)}, bf16[272,1024]{1,0:T(8,128)(2,1)}, u32[]{:S(2)}, u32[]{:S(2)}) collective-permute-start(bf16[272,1024]{1,0:T(8,128)(2,1)} %get-tuple-element.1042.refs_4_.refs_10_.refs_13_.refs_18_), channel_id=1, source_target_pairs={{0,16},{4,20},{8,24},{12,28},{16,0},{20,4},{24,8},{28,12},{1,17},{... | collective-permute-start | bytes 1671176 | tf_op jit(solution)/shard_map/ppermute | solution.py:21
  16.1 29.2 %collective-permute-start.4 = (bf16[256,1024]{1,0:T(8,128)(2,1)}, bf16[256,1024]{1,0:T(8,128)(2,1)}, u32[]{:S(2)}, u32[]{:S(2)}) collective-permute-start(bf16[256,1024]{1,0:T(8,128)(2,1)} %get-tuple-element.1043.refs_5_.refs_11_.refs_14_.refs_19_), channel_id=1, source_target_pairs={{0,8},{4,12},{8,0},{12,4},{16,24},{20,28},{24,16},{28,20},{1,9},{5... | collective-permute-start | bytes 1572872 | tf_op jit(solution)/shard_map/ppermute | solution.py:21
  16.3 30.8 %collective-permute-start.6 = (bf16[256,1024]{1,0:T(8,128)(2,1)}, bf16[256,1024]{1,0:T(8,128)(2,1)}, u32[]{:S(2)}, u32[]{:S(2)}) collective-permute-start(bf16[256,1024]{1,0:T(8,128)(2,1)} %get-tuple-element.1043.refs_5_.refs_11_.refs_14_.refs_19_), channel_id=1, source_target_pairs={{0,16},{4,20},{8,24},{12,28},{16,0},{20,4},{24,8},{28,12},{1,17},{... | collective-permute-start | bytes 1572872 | tf_op jit(solution)/shard_map/ppermute | solution.py:21
  17.1 30.0 %collective-permute-start.2 = (bf16[2,1024]{1,0:T(2,128)(2,1)S(1)}, bf16[2,1024]{1,0:T(2,128)(2,1)S(1)}, u32[]{:S(2)}, u32[]{:S(2)}) collective-permute-start(bf16[2,1024]{1,0:T(2,128)(2,1)S(1)} %bitcast.61), channel_id=1, source_target_pairs={{0,1},{1,2},{2,3},{4,5},{5,6},{6,7},{8,9},{9,10},{10,11},{12,13},{... | collective-permute-start | bytes 12296 | tf_op jit(solution)/shard_map/ppermute | solution.py:27
  52.6 197.4 %reduce-scatter.4.cloned.1.call-start = ((), (), s32[]{:S(2)}) async-start(), calls=%async_computation.5 | async-start | bytes 5242880 | tf_op jit(solution)/shard_map/reduce_scatter | solution.py:1179
  53.0 13.6 %collective-permute-start.14 = (bf16[256,1024]{1,0:T(8,128)(2,1)}, bf16[256,1024]{1,0:T(8,128)(2,1)S(1)}, u32[]{:S(2)}, u32[]{:S(2)}) collective-permute-start(bf16[256,1024]{1,0:T(8,128)(2,1)} %collective-permute-done.6.refs_9_.refs_15_.refs_18_.refs_23_), channel_id=1, source_target_pairs={{0,8},{4,12},{8,0},{12,4},{16,24},{20,28},{24,16},{28,20},{1,9},{5... | collective-permute-start | bytes 1572872 | tf_op jit(solution)/shard_map/ppermute | solution.py:21
  53.7 13.8 %collective-permute-start.10 = (bf16[256,1024]{1,0:T(8,128)(2,1)}, bf16[256,1024]{1,0:T(8,128)(2,1)}, u32[]{:S(2)}, u32[]{:S(2)}) collective-permute-start(bf16[256,1024]{1,0:T(8,128)(2,1)} %collective-permute-done.4.refs_7_.refs_13_.refs_16_.refs_21_), channel_id=1, source_target_pairs={{0,4},{4,0},{8,12},{12,8},{16,20},{20,16},{24,28},{28,24},{1,5},{5... | collective-permute-start | bytes 1572872 | tf_op jit(solution)/shard_map/ppermute | solution.py:21
  54.3 15.9 %collective-permute-start.7 = (bf16[80,4096]{1,0:T(8,128)(2,1)}, bf16[80,4096]{1,0:T(8,128)(2,1)S(1)}, u32[]{:S(2)}, u32[]{:S(2)}) collective-permute-start(bf16[80,4096]{1,0:T(8,128)(2,1)} %get-tuple-element.967.refs_5_.refs_6_), channel_id=1, source_target_pairs={{0,4},{4,0},{8,12},{12,8},{16,20},{20,16},{24,28},{28,24},{1,5},{5... | collective-permute-start | bytes 1966088 | tf_op jit(solution)/shard_map/ppermute | solution.py:21
  54.3 17.0 %collective-permute-start.8 = (bf16[80,4096]{1,0:T(8,128)(2,1)}, bf16[80,4096]{1,0:T(8,128)(2,1)S(1)}, u32[]{:S(2)}, u32[]{:S(2)}) collective-permute-start(bf16[80,4096]{1,0:T(8,128)(2,1)} %get-tuple-element.968.refs_6_.refs_7_), channel_id=1, source_target_pairs={{0,4},{4,0},{8,12},{12,8},{16,20},{20,16},{24,28},{28,24},{1,5},{5... | collective-permute-start | bytes 1966088 | tf_op jit(solution)/shard_map/ppermute | solution.py:21
  54.9 14.3 %collective-permute-start.13 = (bf16[272,1024]{1,0:T(8,128)(2,1)}, bf16[272,1024]{1,0:T(8,128)(2,1)S(1)}, u32[]{:S(2)}, u32[]{:S(2)}) collective-permute-start(bf16[272,1024]{1,0:T(8,128)(2,1)} %collective-permute-done.3.refs_6_.refs_12_.refs_15_.refs_20_), channel_id=1, source_target_pairs={{0,16},{4,20},{8,24},{12,28},{16,0},{20,4},{24,8},{28,12},{1,17},{... | collective-permute-start | bytes 1671176 | tf_op jit(solution)/shard_map/ppermute | solution.py:21
  74.8 24.8 %collective-permute-start.17 = (bf16[80,4096]{1,0:T(8,128)(2,1)}, bf16[80,4096]{1,0:T(8,128)(2,1)}, u32[]{:S(2)}, u32[]{:S(2)}) collective-permute-start(bf16[80,4096]{1,0:T(8,128)(2,1)} %get-tuple-element.967.refs_5_.refs_6_), channel_id=1, source_target_pairs={{0,8},{4,12},{8,0},{12,4},{16,24},{20,28},{24,16},{28,20},{1,9},{5... | collective-permute-start | bytes 1966088 | tf_op jit(solution)/shard_map/ppermute | solution.py:21
  75.6 29.6 %collective-permute-start.18 = (bf16[80,4096]{1,0:T(8,128)(2,1)}, bf16[80,4096]{1,0:T(8,128)(2,1)}, u32[]{:S(2)}, u32[]{:S(2)}) collective-permute-start(bf16[80,4096]{1,0:T(8,128)(2,1)} %get-tuple-element.968.refs_6_.refs_7_), channel_id=1, source_target_pairs={{0,8},{4,12},{8,0},{12,4},{16,24},{20,28},{24,16},{28,20},{1,9},{5... | collective-permute-start | bytes 1966088 | tf_op jit(solution)/shard_map/ppermute | solution.py:21
  76.3 28.8 %collective-permute-start.19 = (bf16[80,4096]{1,0:T(8,128)(2,1)}, bf16[80,4096]{1,0:T(8,128)(2,1)}, u32[]{:S(2)}, u32[]{:S(2)}) collective-permute-start(bf16[80,4096]{1,0:T(8,128)(2,1)} %get-tuple-element.967.refs_5_.refs_6_), channel_id=1, source_target_pairs={{0,16},{4,20},{8,24},{12,28},{16,0},{20,4},{24,8},{28,12},{1,17},{... | collective-permute-start | bytes 1966088 | tf_op jit(solution)/shard_map/ppermute | solution.py:21
  77.1 28.9 %collective-permute-start.20 = (bf16[80,4096]{1,0:T(8,128)(2,1)}, bf16[80,4096]{1,0:T(8,128)(2,1)}, u32[]{:S(2)}, u32[]{:S(2)}) collective-permute-start(bf16[80,4096]{1,0:T(8,128)(2,1)} %get-tuple-element.968.refs_6_.refs_7_), channel_id=1, source_target_pairs={{0,16},{4,20},{8,24},{12,28},{16,0},{20,4},{24,8},{28,12},{1,17},{... | collective-permute-start | bytes 1966088 | tf_op jit(solution)/shard_map/ppermute | solution.py:21
  106.0 16.8 %collective-permute-start.21 = (bf16[80,4096]{1,0:T(8,128)(2,1)}, bf16[80,4096]{1,0:T(8,128)(2,1)S(1)}, u32[]{:S(2)}, u32[]{:S(2)}) collective-permute-start(bf16[80,4096]{1,0:T(8,128)(2,1)} %collective-permute-done.17.refs_7_.refs_8_), channel_id=1, source_target_pairs={{0,4},{4,0},{8,12},{12,8},{16,20},{20,16},{24,28},{28,24},{1,5},{5... | collective-permute-start | bytes 1966088 | tf_op jit(solution)/shard_map/ppermute | solution.py:21
  107.9 16.7 %collective-permute-start.23 = (bf16[80,4096]{1,0:T(8,128)(2,1)}, bf16[80,4096]{1,0:T(8,128)(2,1)}, u32[]{:S(2)}, u32[]{:S(2)}) collective-permute-start(bf16[80,4096]{1,0:T(8,128)(2,1)} %collective-permute-done.17.refs_7_.refs_8_), channel_id=1, source_target_pairs={{0,16},{4,20},{8,24},{12,28},{16,0},{20,4},{24,8},{28,12},{1,17},{... | collective-permute-start | bytes 1966088 | tf_op jit(solution)/shard_map/ppermute | solution.py:21
  108.6 14.2 %collective-permute-start.22 = (bf16[80,4096]{1,0:T(8,128)(2,1)}, bf16[80,4096]{1,0:T(8,128)(2,1)}, u32[]{:S(2)}, u32[]{:S(2)}) collective-permute-start(bf16[80,4096]{1,0:T(8,128)(2,1)} %collective-permute-done.18.refs_8_.refs_9_), channel_id=1, source_target_pairs={{0,4},{4,0},{8,12},{12,8},{16,20},{20,16},{24,28},{28,24},{1,5},{5... | collective-permute-start | bytes 1966088 | tf_op jit(solution)/shard_map/ppermute | solution.py:21
  108.9 16.4 %collective-permute-start.24 = (bf16[80,4096]{1,0:T(8,128)(2,1)}, bf16[80,4096]{1,0:T(8,128)(2,1)}, u32[]{:S(2)}, u32[]{:S(2)}) collective-permute-start(bf16[80,4096]{1,0:T(8,128)(2,1)} %collective-permute-done.20.refs_10_.refs_11_), channel_id=1, source_target_pairs={{0,8},{4,12},{8,0},{12,4},{16,24},{20,28},{24,16},{28,20},{1,9},{5... | collective-permute-start | bytes 1966088 | tf_op jit(solution)/shard_map/ppermute | solution.py:21
  117.8 5.0 %collective-permute-start.25 = (f32[2,1024]{1,0:T(2,128)}, f32[2,1024]{1,0:T(2,128)S(1)}, u32[]{:S(2)}, u32[]{:S(2)}) collective-permute-start(f32[2,1024]{1,0:T(2,128)} %get-tuple-element.719), channel_id=1, source_target_pairs={{0,1},{1,2},{2,3},{4,5},{5,6},{6,7},{8,9},{9,10},{10,11},{12,13},{... | collective-permute-start | bytes 24584 | tf_op jit(solution)/shard_map/ppermute | solution.py:27
  125.3 3.1 collective-permute-start.26
  126.4 3.9 %collective-permute-start.28 = (bf16[80,4096]{1,0:T(8,128)(2,1)}, bf16[80,4096]{1,0:T(8,128)(2,1)}, u32[]{:S(2)}, u32[]{:S(2)}) collective-permute-start(bf16[80,4096]{1,0:T(8,128)(2,1)} %collective-permute-done.23.refs_11_.refs_12_), channel_id=1, source_target_pairs={{0,4},{4,0},{8,12},{12,8},{16,20},{20,16},{24,28},{28,24},{1,5},{5... | collective-permute-start | bytes 1966088 | tf_op jit(solution)/shard_map/ppermute | solution.py:21
  126.9 4.4 %collective-permute-start.29 = (bf16[80,4096]{1,0:T(8,128)(2,1)}, bf16[80,4096]{1,0:T(8,128)(2,1)}, u32[]{:S(2)}, u32[]{:S(2)}) collective-permute-start(bf16[80,4096]{1,0:T(8,128)(2,1)} %collective-permute-done.24.refs_12_.refs_13_), channel_id=1, source_target_pairs={{0,4},{4,0},{8,12},{12,8},{16,20},{20,16},{24,28},{28,24},{1,5},{5... | collective-permute-start | bytes 1966088 | tf_op jit(solution)/shard_map/ppermute | solution.py:21
  131.2 9.3 %collective-permute-start.31 = (bf16[1536,1024]{1,0:T(8,128)(2,1)}, bf16[1536,1024]{1,0:T(8,128)(2,1)}, u32[]{:S(2)}, u32[]{:S(2)}) collective-permute-start(bf16[1536,1024]{1,0:T(8,128)(2,1)} %all-gather.9.cloned.1.call-done.refs_7_.refs_4_), channel_id=1, source_target_pairs={{0,4},{4,0},{8,12},{12,8},{16,20},{20,16},{24,28},{28,24},{1,5},{5... | collective-permute-start | bytes 9437192 | tf_op jit(solution)/shard_map/ppermute | solution.py:21
  131.6 8.9 %collective-permute-start.30 = (bf16[512,1024]{1,0:T(8,128)(2,1)}, bf16[512,1024]{1,0:T(8,128)(2,1)}, u32[]{:S(2)}, u32[]{:S(2)}) collective-permute-start(bf16[512,1024]{1,0:T(8,128)(2,1)} %refs_3_.2), channel_id=1, source_target_pairs={{0,4},{4,0},{8,12},{12,8},{16,20},{20,16},{24,28},{28,24},{1,5},{5... | collective-permute-start | bytes 3145736 | tf_op jit(solution)/shard_map/ppermute | solution.py:21
  140.5 9.3 %collective-permute-start.35 = (bf16[3,256,1024]{2,1,0:T(8,128)(2,1)}, bf16[3,256,1024]{2,1,0:T(8,128)(2,1)}, u32[]{:S(2)}, u32[]{:S(2)}) collective-permute-start(bf16[3,256,1024]{2,1,0:T(8,128)(2,1)} %get-tuple-element.1138.refs_11_.refs_1_), channel_id=1, source_target_pairs={{0,4},{4,0},{8,12},{12,8},{16,20},{20,16},{24,28},{28,24},{1,5},{5... | collective-permute-start | bytes 4718600 | tf_op jit(solution)/shard_map/ppermute | solution.py:21
  140.9 8.9 %collective-permute-start.32 = (bf16[2,256,1024]{2,1,0:T(8,128)(2,1)}, bf16[2,256,1024]{2,1,0:T(8,128)(2,1)}, u32[]{:S(2)}, u32[]{:S(2)}) collective-permute-start(bf16[2,256,1024]{2,1,0:T(8,128)(2,1)} %get-tuple-element.987.refs_1_), channel_id=1, source_target_pairs={{0,4},{4,0},{8,12},{12,8},{16,20},{20,16},{24,28},{28,24},{1,5},{5... | collective-permute-start | bytes 3145736 | tf_op jit(solution)/shard_map/ppermute | solution.py:21
  141.1 8.8 %collective-permute-start.33 = (bf16[256,2048]{1,0:T(8,128)(2,1)}, bf16[256,2048]{1,0:T(8,128)(2,1)}, u32[]{:S(2)}, u32[]{:S(2)}) collective-permute-start(bf16[256,2048]{1,0:T(8,128)(2,1)} %get-tuple-element.855.refs_2_), channel_id=1, source_target_pairs={{0,4},{4,0},{8,12},{12,8},{16,20},{20,16},{24,28},{28,24},{1,5},{5... | collective-permute-start | bytes 3145736 | tf_op jit(solution)/shard_map/ppermute | solution.py:21
  141.4 8.4 %collective-permute-start.34 = (bf16[256,1024]{1,0:T(8,128)(2,1)}, bf16[256,1024]{1,0:T(8,128)(2,1)S(1)}, u32[]{:S(2)}, u32[]{:S(2)}) collective-permute-start(bf16[256,1024]{1,0:T(8,128)(2,1)} %get-tuple-element.1091.refs_9_), channel_id=1, source_target_pairs={{0,4},{4,0},{8,12},{12,8},{16,20},{20,16},{24,28},{28,24},{1,5},{5... | collective-permute-start | bytes 1572872 | tf_op jit(solution)/shard_map/ppermute | solution.py:21
  150.3 8.3 %collective-permute-start.36 = (bf16[256,1024]{1,0:T(8,128)(2,1)}, bf16[256,1024]{1,0:T(8,128)(2,1)}, u32[]{:S(2)}, u32[]{:S(2)}) collective-permute-start(bf16[256,1024]{1,0:T(8,128)(2,1)} %get-tuple-element.991.refs_3_), channel_id=1, source_target_pairs={{0,4},{4,0},{8,12},{12,8},{16,20},{20,16},{24,28},{28,24},{1,5},{5... | collective-permute-start | bytes 1572872 | tf_op jit(solution)/shard_map/ppermute | solution.py:21
  158.6 126.0 %reduce-scatter.6.cloned.1.call-start = ((), (), s32[]{:S(2)}) async-start(), calls=%async_computation.6 | async-start | bytes 2621440 | tf_op jit(solution)/shard_map/reduce_scatter | solution.py:1179
  166.5 19.1 %collective-permute-start.42 = (bf16[256,4096]{1,0:T(8,128)(2,1)}, bf16[256,4096]{1,0:T(8,128)(2,1)}, u32[]{:S(2)}, u32[]{:S(2)}) collective-permute-start(bf16[256,4096]{1,0:T(8,128)(2,1)} %shard_map.455.refs_4_.refs_3_), channel_id=1, source_target_pairs={{0,4},{4,0},{8,12},{12,8},{16,20},{20,16},{24,28},{28,24},{1,5},{5... | collective-permute-start | bytes 6291464 | tf_op jit(solution)/shard_map/ppermute | solution.py:21
  171.0 21.9 %collective-permute-start.38 = (bf16[128,1024]{1,0:T(8,128)(2,1)}, bf16[128,1024]{1,0:T(8,128)(2,1)S(1)}, u32[]{:S(2)}, u32[]{:S(2)}) collective-permute-start(bf16[128,1024]{1,0:T(8,128)(2,1)} %get-tuple-element.992), channel_id=1, source_target_pairs={{0,8},{4,12},{8,0},{12,4},{16,24},{20,28},{24,16},{28,20},{1,9},{5... | collective-permute-start | bytes 786440 | tf_op jit(solution)/shard_map/ppermute | solution.py:21
  171.8 21.2 %collective-permute-start.39 = (bf16[128,1024]{1,0:T(8,128)(2,1)}, bf16[128,1024]{1,0:T(8,128)(2,1)S(1)}, u32[]{:S(2)}, u32[]{:S(2)}) collective-permute-start(bf16[128,1024]{1,0:T(8,128)(2,1)} %get-tuple-element.993), channel_id=1, source_target_pairs={{0,16},{4,20},{8,24},{12,28},{16,0},{20,4},{24,8},{28,12},{1,17},{... | collective-permute-start | bytes 786440 | tf_op jit(solution)/shard_map/ppermute | solution.py:21
  172.5 20.5 %collective-permute-start.40 = (bf16[128,1024]{1,0:T(8,128)(2,1)}, bf16[128,1024]{1,0:T(8,128)(2,1)S(1)}, u32[]{:S(2)}, u32[]{:S(2)}) collective-permute-start(bf16[128,1024]{1,0:T(8,128)(2,1)} %get-tuple-element.994), channel_id=1, source_target_pairs={{0,24},{4,28},{8,16},{12,20},{16,8},{20,12},{24,0},{28,4},{1,25},{... | collective-permute-start | bytes 786440 | tf_op jit(solution)/shard_map/ppermute | solution.py:21
  183.4 9.5 %collective-permute-start.41 = (f32[2,1024]{1,0:T(2,128)}, f32[2,1024]{1,0:T(2,128)S(1)}, u32[]{:S(2)}, u32[]{:S(2)}) collective-permute-start(f32[2,1024]{1,0:T(2,128)} %get-tuple-element.1032.refs_2_), channel_id=1, source_target_pairs={{1,0},{2,1},{3,2},{5,4},{6,5},{7,6},{9,8},{10,9},{11,10},{13,12},{... | collective-permute-start | bytes 24584 | tf_op jit(solution)/shard_map/ppermute | solution.py:27
  193.0 47.8 %collective-permute-start.49 = (bf16[128,4096]{1,0:T(8,128)(2,1)}, bf16[128,4096]{1,0:T(8,128)(2,1)}, u32[]{:S(2)}, u32[]{:S(2)}) collective-permute-start(bf16[128,4096]{1,0:T(8,128)(2,1)} %get-tuple-element.1077), channel_id=1, source_target_pairs={{0,8},{4,12},{8,0},{12,4},{16,24},{20,28},{24,16},{28,20},{1,9},{5... | collective-permute-start | bytes 3145736 | tf_op jit(solution)/shard_map/ppermute | solution.py:21
  193.9 46.9 %collective-permute-start.50 = (bf16[128,4096]{1,0:T(8,128)(2,1)}, bf16[128,4096]{1,0:T(8,128)(2,1)}, u32[]{:S(2)}, u32[]{:S(2)}) collective-permute-start(bf16[128,4096]{1,0:T(8,128)(2,1)} %get-tuple-element.1078), channel_id=1, source_target_pairs={{0,16},{4,20},{8,24},{12,28},{16,0},{20,4},{24,8},{28,12},{1,17},{... | collective-permute-start | bytes 3145736 | tf_op jit(solution)/shard_map/ppermute | solution.py:21
  194.5 46.3 %collective-permute-start.51 = (bf16[128,4096]{1,0:T(8,128)(2,1)}, bf16[128,4096]{1,0:T(8,128)(2,1)}, u32[]{:S(2)}, u32[]{:S(2)}) collective-permute-start(bf16[128,4096]{1,0:T(8,128)(2,1)} %get-tuple-element.1079), channel_id=1, source_target_pairs={{0,24},{4,28},{8,16},{12,20},{16,8},{20,12},{24,0},{28,4},{1,25},{... | collective-permute-start | bytes 3145736 | tf_op jit(solution)/shard_map/ppermute | solution.py:21
  203.6 4.3 %collective-permute-start.43 = (f32[8,1024]{1,0:T(8,128)}, f32[8,1024]{1,0:T(8,128)S(1)}, u32[]{:S(2)}, u32[]{:S(2)}) collective-permute-start(f32[8,1024]{1,0:T(8,128)} %get-tuple-element.1058.refs_1_), channel_id=1, source_target_pairs={{0,1},{1,0},{2,3},{3,2},{4,5},{5,4},{6,7},{7,6},{8,9},{9,8},{10,11... | collective-permute-start | bytes 98312 | tf_op jit(solution)/shard_map/ppermute | solution.py:32
  208.6 7.4 %collective-permute-start.44 = (f32[16,1024]{1,0:T(8,128)S(1)}, f32[16,1024]{1,0:T(8,128)S(1)}, u32[]{:S(2)}, u32[]{:S(2)}) collective-permute-start(f32[16,1024]{1,0:T(8,128)S(1)} %pad_maximum_fusion.1), channel_id=1, source_target_pairs={{0,2},{1,3},{2,0},{3,1},{4,6},{5,7},{6,4},{7,5},{8,10},{9,11},{10,... | collective-permute-start | bytes 196616 | tf_op jit(solution)/shard_map/ppermute | solution.py:32
  211.0 9.4 %collective-permute-start.45 = (bf16[256,512]{1,0:T(8,128)(2,1)}, bf16[256,512]{1,0:T(8,128)(2,1)S(1)}, u32[]{:S(2)}, u32[]{:S(2)}) collective-permute-start(bf16[256,512]{1,0:T(8,128)(2,1)} %get-tuple-element.1066.refs_1_), channel_id=1, source_target_pairs={{0,4},{4,0},{8,12},{12,8},{16,20},{20,16},{24,28},{28,24},{1,5},{5... | collective-permute-start | bytes 786440 | tf_op jit(solution)/shard_map/ppermute | solution.py:21
  216.1 5.7 %collective-permute-start.46 = (bf16[256,512]{1,0:T(8,128)(2,1)}, bf16[256,512]{1,0:T(8,128)(2,1)S(1)}, u32[]{:S(2)}, u32[]{:S(2)}) collective-permute-start(bf16[256,512]{1,0:T(8,128)(2,1)} %get-tuple-element.1067.refs_2_), channel_id=1, source_target_pairs={{0,4},{4,0},{8,12},{12,8},{16,20},{20,16},{24,28},{28,24},{1,5},{5... | collective-permute-start | bytes 786440 | tf_op jit(solution)/shard_map/ppermute | solution.py:21
  220.4 14.2 %collective-permute-start.47 = (bf16[256,512]{1,0:T(8,128)(2,1)}, bf16[256,512]{1,0:T(8,128)(2,1)S(1)}, u32[]{:S(2)}, u32[]{:S(2)}) collective-permute-start(bf16[256,512]{1,0:T(8,128)(2,1)} %get-tuple-element.1063.refs_16_.refs_5_), channel_id=1, source_target_pairs={{0,4},{4,0},{8,12},{12,8},{16,20},{20,16},{24,28},{28,24},{1,5},{5... | collective-permute-start | bytes 786440 | tf_op jit(solution)/shard_map/ppermute | solution.py:21
  221.7 12.9 %collective-permute-start.48 = (bf16[256,512]{1,0:T(8,128)(2,1)}, bf16[256,512]{1,0:T(8,128)(2,1)}, u32[]{:S(2)}, u32[]{:S(2)}) collective-permute-start(bf16[256,512]{1,0:T(8,128)(2,1)} %get-tuple-element.1064.refs_17_.refs_6_), channel_id=1, source_target_pairs={{0,4},{4,0},{8,12},{12,8},{16,20},{20,16},{24,28},{28,24},{1,5},{5... | collective-permute-start | bytes 786440 | tf_op jit(solution)/shard_map/ppermute | solution.py:21
  240.8 94.5 %reduce-scatter.8.cloned.1.call-start = ((), (), s32[]{:S(2)}) async-start(), calls=%async_computation.7 | async-start | bytes 1638400 | tf_op jit(solution)/shard_map/reduce_scatter | solution.py:1179
  240.9 9.1 %collective-permute-start.52 = (bf16[2,256,1024]{2,1,0:T(8,128)(2,1)}, bf16[2,256,1024]{2,1,0:T(8,128)(2,1)}, u32[]{:S(2)}, u32[]{:S(2)}) collective-permute-start(bf16[2,256,1024]{2,1,0:T(8,128)(2,1)} %get-tuple-element.1140.refs_3_), channel_id=1, source_target_pairs={{0,4},{4,0},{8,12},{12,8},{16,20},{20,16},{24,28},{28,24},{1,5},{5... | collective-permute-start | bytes 3145736 | tf_op jit(solution)/shard_map/ppermute | solution.py:21
  242.4 7.6 %collective-permute-start.53 = (f32[2,1024]{1,0:T(2,128)S(1)}, f32[2,1024]{1,0:T(2,128)S(1)}, u32[]{:S(2)}, u32[]{:S(2)}) collective-permute-start(f32[2,1024]{1,0:T(2,128)S(1)} %copy-done.30), channel_id=1, source_target_pairs={{1,0},{2,1},{3,2},{5,4},{6,5},{7,6},{9,8},{10,9},{11,10},{13,12},{... | collective-permute-start | bytes 24584 | tf_op jit(solution)/shard_map/ppermute | solution.py:27
  252.2 15.1 %collective-permute-start.54 = (bf16[128,1024]{1,0:T(8,128)(2,1)}, bf16[128,1024]{1,0:T(8,128)(2,1)S(1)}, u32[]{:S(2)}, u32[]{:S(2)}) collective-permute-start(bf16[128,1024]{1,0:T(8,128)(2,1)} %get-tuple-element.1267), channel_id=1, source_target_pairs={{0,8},{4,12},{8,0},{12,4},{16,24},{20,28},{24,16},{28,20},{1,9},{5... | collective-permute-start | bytes 786440 | tf_op jit(solution)/shard_map/ppermute | solution.py:21
  253.5 13.8 %collective-permute-start.55 = (bf16[128,1024]{1,0:T(8,128)(2,1)}, bf16[128,1024]{1,0:T(8,128)(2,1)S(1)}, u32[]{:S(2)}, u32[]{:S(2)}) collective-permute-start(bf16[128,1024]{1,0:T(8,128)(2,1)} %get-tuple-element.1266), channel_id=1, source_target_pairs={{0,16},{4,20},{8,24},{12,28},{16,0},{20,4},{24,8},{28,12},{1,17},{... | collective-permute-start | bytes 786440 | tf_op jit(solution)/shard_map/ppermute | solution.py:21
  254.6 12.7 %collective-permute-start.56 = (bf16[128,1024]{1,0:T(8,128)(2,1)}, bf16[128,1024]{1,0:T(8,128)(2,1)}, u32[]{:S(2)}, u32[]{:S(2)}) collective-permute-start(bf16[128,1024]{1,0:T(8,128)(2,1)} %get-tuple-element.1265), channel_id=1, source_target_pairs={{0,24},{4,28},{8,16},{12,20},{16,8},{20,12},{24,0},{28,4},{1,25},{... | collective-permute-start | bytes 786440 | tf_op jit(solution)/shard_map/ppermute | solution.py:21
  268.0 16.6 %collective-permute-start.57 = (bf16[272,1024]{1,0:T(8,128)(2,1)}, bf16[272,1024]{1,0:T(8,128)(2,1)S(1)}, u32[]{:S(2)}, u32[]{:S(2)}) collective-permute-start(bf16[272,1024]{1,0:T(8,128)(2,1)} %get-tuple-element.1152), channel_id=1, source_target_pairs={{0,8},{4,12},{8,0},{12,4},{16,24},{20,28},{24,16},{28,20},{1,9},{5... | collective-permute-start | bytes 1671176 | tf_op jit(solution)/shard_map/ppermute | solution.py:21
  269.3 15.3 %collective-permute-start.58 = (bf16[272,1024]{1,0:T(8,128)(2,1)}, bf16[272,1024]{1,0:T(8,128)(2,1)}, u32[]{:S(2)}, u32[]{:S(2)}) collective-permute-start(bf16[272,1024]{1,0:T(8,128)(2,1)} %get-tuple-element.1153), channel_id=1, source_target_pairs={{0,16},{4,20},{8,24},{12,28},{16,0},{20,4},{24,8},{28,12},{1,17},{... | collective-permute-start | bytes 1671176 | tf_op jit(solution)/shard_map/ppermute | solution.py:21
  270.5 23.7 %collective-permute-start.59 = (bf16[272,1024]{1,0:T(8,128)(2,1)}, bf16[272,1024]{1,0:T(8,128)(2,1)}, u32[]{:S(2)}, u32[]{:S(2)}) collective-permute-start(bf16[272,1024]{1,0:T(8,128)(2,1)} %get-tuple-element.1154), channel_id=1, source_target_pairs={{0,24},{4,28},{8,16},{12,20},{16,8},{20,12},{24,0},{28,4},{1,25},{... | collective-permute-start | bytes 1671176 | tf_op jit(solution)/shard_map/ppermute | solution.py:21
  296.2 5.9 %collective-permute-start.60 = (bf16[64,1024]{1,0:T(8,128)(2,1)}, bf16[64,1024]{1,0:T(8,128)(2,1)S(1)}, u32[]{:S(2)}, u32[]{:S(2)}) collective-permute-start(bf16[64,1024]{1,0:T(8,128)(2,1)} %get-tuple-element.1270), channel_id=1, source_target_pairs={{0,8},{4,12},{8,0},{12,4},{16,24},{20,28},{24,16},{28,20},{1,9},{5... | collective-permute-start | bytes 393224 | tf_op jit(solution)/shard_map/ppermute | solution.py:21
  297.2 5.8 %collective-permute-start.61 = (bf16[64,1024]{1,0:T(8,128)(2,1)}, bf16[64,1024]{1,0:T(8,128)(2,1)S(1)}, u32[]{:S(2)}, u32[]{:S(2)}) collective-permute-start(bf16[64,1024]{1,0:T(8,128)(2,1)} %get-tuple-element.1269), channel_id=1, source_target_pairs={{0,16},{4,20},{8,24},{12,28},{16,0},{20,4},{24,8},{28,12},{1,17},{... | collective-permute-start | bytes 393224 | tf_op jit(solution)/shard_map/ppermute | solution.py:21
  297.5 5.5 %collective-permute-start.62 = (bf16[64,1024]{1,0:T(8,128)(2,1)}, bf16[64,1024]{1,0:T(8,128)(2,1)}, u32[]{:S(2)}, u32[]{:S(2)}) collective-permute-start(bf16[64,1024]{1,0:T(8,128)(2,1)} %get-tuple-element.1268), channel_id=1, source_target_pairs={{0,24},{4,28},{8,16},{12,20},{16,8},{20,12},{24,0},{28,4},{1,25},{... | collective-permute-start | bytes 393224 | tf_op jit(solution)/shard_map/ppermute | solution.py:21
  303.0 12.5 %collective-permute-start.63 = (bf16[80,1024]{1,0:T(8,128)(2,1)}, bf16[80,1024]{1,0:T(8,128)(2,1)S(1)}, u32[]{:S(2)}, u32[]{:S(2)}) collective-permute-start(bf16[80,1024]{1,0:T(8,128)(2,1)} %get-tuple-element.1191), channel_id=1, source_target_pairs={{0,1},{1,0},{2,3},{3,2},{4,5},{5,4},{6,7},{7,6},{8,9},{9,8},{10,11... | collective-permute-start | bytes 491528 | tf_op jit(solution)/shard_map/ppermute | solution.py:32
  303.0 15.7 %collective-permute-start.64 = (bf16[80,1024]{1,0:T(8,128)(2,1)}, bf16[80,1024]{1,0:T(8,128)(2,1)S(1)}, u32[]{:S(2)}, u32[]{:S(2)}) collective-permute-start(bf16[80,1024]{1,0:T(8,128)(2,1)} %get-tuple-element.1192), channel_id=1, source_target_pairs={{0,2},{1,3},{2,0},{3,1},{4,6},{5,7},{6,4},{7,5},{8,10},{9,11},{10,... | collective-permute-start | bytes 491528 | tf_op jit(solution)/shard_map/ppermute | solution.py:32
  304.4 26.3 %collective-permute-start.65 = (bf16[80,1024]{1,0:T(8,128)(2,1)}, bf16[80,1024]{1,0:T(8,128)(2,1)S(1)}, u32[]{:S(2)}, u32[]{:S(2)}) collective-permute-start(bf16[80,1024]{1,0:T(8,128)(2,1)} %get-tuple-element.1193), channel_id=1, source_target_pairs={{0,3},{1,2},{2,1},{3,0},{4,7},{5,6},{6,5},{7,4},{8,11},{9,10},{10,... | collective-permute-start | bytes 491528 | tf_op jit(solution)/shard_map/ppermute | solution.py:32
  331.5 3.2 collective-permute-start.66
  (41 other events, 297.1 us)
Sparse Core Ops, SparseCore 0:
  12.9 37.5 all-gather.6
  52.8 62.6 all-gather.8
  158.7 79.5 reduce-scatter.3
  241.0 43.6 reduce-scatter.5
  286.8 39.8 reduce-scatter.7
